TPU v7x, 128 devices: a whole 4x4x4 slice. The times are simulated.
128 devices in a mesh: ctx: 64 (over y, x, z_lo, core), head: 2 (over z_hi).
Axes of the slice: x: 4, y: 4, z: 4 (z_hi: 2, z_lo: 2; z = z_hi * 2 + z_lo), core: 2. Of those that a mesh axis runs over, the one named last changes fastest.
Arguments:
- queries: bfloat16 [16384, 4096], P(('ctx', 'head')), may hold values from -80 to 80
- input_key_rows: bfloat16 [16384, 1024], P(('ctx', 'head')), may hold values from -4 to 4
- input_value_rows: bfloat16 [16384, 1024], P(('ctx', 'head')), may hold values from -6 to 6
- attention_output_gradient: bfloat16 [16384, 4096], P(('ctx', 'head')), may hold values from -6 to 6
- level_offsets: int32 [5, 8], P(None, 'head'), may hold values from 0 to 15, as said below
Outputs:
- attended: bfloat16 [16384, 4096], P(('ctx', 'head'))
- grad_queries: bfloat16 [16384, 4096], P(('ctx', 'head'))
- grad_keys: bfloat16 [16384, 1024], P(('ctx', 'head'))
- grad_values: bfloat16 [16384, 1024], P(('ctx', 'head'))
Inputs may be any that keep to these rules, and one draw needn't show every extreme that they name: level_offsets[k, g] lies in 0 .. 2^k - 1.
All inputs are finite; a program needn't handle non-finite values.
Results may differ from a plain program's by a relative error of at most 0.018.
Values may be sent and summed in bfloat16 or wider, within the bound.
No kernel may reach another device: no remote copies, remote signals or barrier semaphores. Data moves between devices by JAX's collectives and lax.ppermute only.
A program may use at most 128 MiB of HBM per device.

v0:
```python
import functools

import jax
import jax.numpy as jnp
from jax import lax
from jax.experimental import pallas as pl
from jax.experimental.pallas import tpu as pltpu
from jax.sharding import PartitionSpec as P

D = 128
GROUPS = 8
HEADS = 4
TOKENS = 128
WIDE = HEADS * D
SCALE = D ** (-0.5)
LOG2E = 1.4426950408889634
AXES = ("ctx", "head")
BF = jnp.bfloat16
F32 = jnp.float32
ANY_ROWS = ((0, 64, 1), (64, 96, 2), (96, 112, 3), (112, 120, 4))
VMEM_LIMIT = 56 * 1024 * 1024


def dot(a, b):
    return lax.dot_general(a, b, (((1,), (0,)), ((), ())), preferred_element_type=F32)


def dot_nt(a, b):
    return lax.dot_general(a, b, (((1,), (1,)), ((), ())), preferred_element_type=F32)


def one_hot(mask):
    return jnp.where(mask, 1.0, 0.0).astype(BF)


def selected_token(row, offs, group):
    token = jnp.full(row.shape, -1, jnp.int32)
    for start, stop, level in ANY_ROWS:
        inside = (row >= start) & (row < stop)
        token = jnp.where(inside, (row - start) * 2**level + offs[level, group], token)
    return token


def selector(offs, group):
    shape = (128, TOKENS)
    row = lax.broadcasted_iota(jnp.int32, shape, 0)
    return one_hot(selected_token(row, offs, group) == lax.broadcasted_iota(jnp.int32, shape, 1))


def placer(offs, group):
    shape = (TOKENS, 128)
    row = lax.broadcasted_iota(jnp.int32, shape, 1)
    return one_hot(selected_token(row, offs, group) == lax.broadcasted_iota(jnp.int32, shape, 0))


def group_rows(keys_ref, values_ref, group):
    lanes = slice(group * D, (group + 1) * D)
    return jnp.concatenate([keys_ref[:, lanes], values_ref[:, lanes]], 1)


def select_kernel(offs, keys, values, first, middle, tail, last):
    for g in range(GROUPS):
        rows = dot(selector(offs, g), group_rows(keys, values, g))
        first[g] = rows[0:64].astype(BF)
        middle[g] = rows[64:128].astype(BF)
        tail[g] = rows[96:128].astype(BF)
        last[g] = rows[112:128].astype(BF)


def compact_kernel(one, two, three, packed):
    for g in range(GROUPS):
        a, b, c = one[g].astype(F32), two[g].astype(F32), three[g].astype(F32)
        packed[g] = jnp.concatenate([a[:24], b[:8], c[:8], jnp.zeros((8, 2 * D), F32)], 0).astype(BF)


def assemble_kernel(
    offs, first, mid_own, x_own, keys, values, x_far, mid_up, x_up, mid_down, x_down, held
):
    for g in range(GROUPS):
        far = dot(selector(offs, g), group_rows(keys, values, g))
        mids = [mid_own[g].astype(F32), far[64:128], mid_up[g].astype(F32), mid_down[g].astype(F32)]
        extras = [ref[g].astype(F32) for ref in (x_own, x_far, x_up, x_down)]
        rows = [first[g].astype(F32), far[0:64]]
        rows += [m[0:32] for m in mids]
        for m, x in zip(mids, extras):
            rows += [m[32:48], x[0:16]]
        for m, x in zip(mids, extras):
            rows += [m[48:56], x[16:40]]
        held[g] = jnp.concatenate(rows, 0).astype(BF)


def by_level(rows):
    parts = []
    for start, stop in ((0, 64), (64, 96), (96, 112), (112, 120), (120, 128)):
        parts += [rows[start:stop, h * D : (h + 1) * D] for h in range(HEADS)]
    return jnp.concatenate(parts, 0)


def by_selection(rows):
    heads = []
    for h in range(HEADS):
        parts = []
        base = 0
        for count in (64, 32, 16, 8, 8):
            parts.append(rows[base + h * count : base + (h + 1) * count])
            base += HEADS * count
        heads.append(jnp.concatenate(parts, 0))
    return jnp.concatenate(heads, 1)


def split3(x):
    high = x.astype(BF)
    rest = x - high.astype(F32)
    mid = rest.astype(BF)
    low = (rest - mid.astype(F32)).astype(BF)
    return [high.astype(F32), mid.astype(F32), low.astype(F32)]


def attention_kernel(
    offs, q_ref, g_ref, k_ref, v_ref, kp_ref, vp_ref, own_ref, other_ref,
    att_ref, dq_ref, d0_ref, down_ref, dother_ref,
):
    group = pl.program_id(0)
    eye = one_hot(
        lax.broadcasted_iota(jnp.int32, (D, D), 0) == lax.broadcasted_iota(jnp.int32, (D, D), 1)
    )
    pick = selector(offs, group)
    place = placer(offs, group)
    q_rows = q_ref[...]
    g_rows = g_ref[...]
    q0 = jnp.concatenate([q_rows[:, h * D : (h + 1) * D] for h in range(HEADS)], 0)
    g0 = jnp.concatenate([g_rows[:, h * D : (h + 1) * D] for h in range(HEADS)], 0)
    qs = by_level(dot(pick, q_rows)).astype(BF)
    gs = by_level(dot(pick, g_rows)).astype(BF)

    shape = (512, WIDE)
    row = lax.broadcasted_iota(jnp.int32, shape, 0)
    target = jnp.full(shape, -1, jnp.int32)
    base = 0
    for count, level in ((64, 1), (32, 2), (16, 3), (8, 4)):
        r = row - base
        shift = count.bit_length() - 1
        value = (r >> shift) * TOKENS + (r & (count - 1)) * 2**level + offs[level, group]
        target = jnp.where((r >= 0) & (r < HEADS * count), value, target)
        base += HEADS * count
    spread = one_hot(target == lax.broadcasted_iota(jnp.int32, shape, 1))

    own = own_ref[0]
    other = other_ref[0]

    def both(start, lanes):
        return [own[start : start + 128, lanes], other[start : start + 128, lanes]]

    k_lanes, v_lanes = slice(0, D), slice(D, 2 * D)
    keys = [
        jnp.concatenate([k_ref[...], kp_ref[...]], 0),
        jnp.concatenate(both(0, k_lanes), 0),
        jnp.concatenate(both(128, k_lanes), 0),
        jnp.concatenate(both(256, k_lanes) + both(384, k_lanes), 0),
    ]
    values = [
        jnp.concatenate([v_ref[...], vp_ref[...]], 0),
        jnp.concatenate(both(0, v_lanes), 0),
        jnp.concatenate(both(128, v_lanes), 0),
        jnp.concatenate(both(256, v_lanes) + both(384, v_lanes), 0),
    ]
    queries = [q0, qs[0:256], qs[256:384], qs[384:512]]
    grads = [g0, gs[0:256], gs[256:384], gs[384:512]]

    raised, peaks, lses, outs = [], [], [], []
    for i in range(4):
        scores = dot_nt(keys[i], queries[i]) * (SCALE * LOG2E)
        if i == 3:
            shape = (512, 128)
            third = lax.broadcasted_iota(jnp.int32, shape, 0) < 256
            column = lax.broadcasted_iota(jnp.int32, shape, 1) < 64
            scores = jnp.where(third == column, scores, -jnp.inf)
        peak = jnp.max(scores, 0, keepdims=True)
        power = jnp.exp2(scores - peak)
        total = jnp.sum(power, 0, keepdims=True)
        raised.append(power)
        peaks.append(peak)
        lses.append(peak + jnp.log2(total))
        flipped = dot_nt(eye, values[i]).astype(BF)
        outs.append(dot(flipped, power.astype(BF)))

    lse_first = lses[0]
    lse_rest = jnp.concatenate(lses[1:], 1)
    lane = lax.broadcasted_iota(jnp.int32, (1, 512), 1)
    rows = []
    for start, stop in ((0, 256), (256, 384), (384, 448), (448, 480)):
        inside = (lane >= start) & (lane < stop)
        rows += [jnp.where(inside, part, 0.0) for part in split3(lse_rest)]
        rows.append(jnp.where(inside, 1.0, 0.0))
    placed = dot(jnp.concatenate(rows, 0).astype(BF), spread)
    merged_peak = lse_first
    level_lse = []
    for k in range(4):
        part = placed[4 * k : 4 * k + 1] + placed[4 * k + 1 : 4 * k + 2] + placed[4 * k + 2 : 4 * k + 3]
        member = placed[4 * k + 3 : 4 * k + 4] > 0.5
        level_lse.append((part, member))
        merged_peak = jnp.maximum(merged_peak, jnp.where(member, part, lse_first))
    row_total = jnp.exp2(lse_first - merged_peak)
    for part, member in level_lse:
        row_total = row_total + jnp.where(member, jnp.exp2(part - merged_peak), 0.0)
    merged = merged_peak + jnp.log2(row_total)

    def at_selection(x):
        parts = split3(x) + [jnp.zeros((13, WIDE), F32)]
        got = dot_nt(jnp.concatenate(parts, 0).astype(BF), spread)
        return got[0:1] + got[1:2] + got[2:3]

    merged_sel = at_selection(merged)
    bounds = ((0, 256), (256, 384), (384, 512))
    factors = [jnp.exp2(peaks[0] - merged)]
    factors += [jnp.exp2(peaks[i + 1] - merged_sel[:, a:b]) for i, (a, b) in enumerate(bounds)]

    def to_rows(flat):
        flat = flat.astype(BF)
        return [dot_nt(eye, flat[:, c : c + 128]) for c in range(0, flat.shape[1], 128)]

    def gather_levels(first, rest):
        level0 = jnp.concatenate(to_rows(first), 1)
        rows = jnp.concatenate(sum([to_rows(part) for part in rest], []), 0)
        return level0 + dot(place, by_selection(rows).astype(BF))

    scaled = [outs[i] * factors[i] for i in range(4)]
    attended = gather_levels(scaled[0], scaled[1:]).astype(BF)
    att_ref[...] = attended

    product = g_rows.astype(F32) * attended.astype(F32)
    high = product.astype(BF)
    low = (product - high.astype(F32)).astype(BF)
    ones = jnp.ones((16, D), BF)
    delta = jnp.concatenate(
        [
            (dot_nt(ones, high[:, h * D : (h + 1) * D]) + dot_nt(ones, low[:, h * D : (h + 1) * D]))[0:1]
            for h in range(HEADS)
        ],
        1,
    )
    delta_sel = at_selection(delta)
    deltas = [delta] + [delta_sel[:, a:b] for a, b in bounds]

    dqs = []
    for i in range(4):
        probs = raised[i] * factors[i]
        grad_weights = dot_nt(values[i], grads[i])
        grad_scores = (probs * (grad_weights - deltas[i])).astype(BF)
        grad_values = dot(probs.astype(BF), grads[i])
        grad_keys = dot(grad_scores, queries[i]) * SCALE
        flipped = dot_nt(eye, keys[i]).astype(BF)
        dqs.append(dot(flipped, grad_scores) * SCALE)
        pair = jnp.concatenate([grad_keys, grad_values], 1).astype(BF)
        if i == 0:
            d0_ref[0] = pair
        else:
            start = 128 * (i - 1)
            for part in range(pair.shape[0] // 256):
                at = start + 128 * part
                down_ref[0, at : at + 128] = pair[256 * part : 256 * part + 128]
                dother_ref[0, at : at + 128] = pair[256 * part + 128 : 256 * part + 256]
    dq_ref[...] = gather_levels(dqs[0], dqs[1:]).astype(BF)


def reduce_kernel(offs, d0, mine, theirs, kept, far, up, down, x_far, x_kept):
    for g in range(GROUPS):
        total = mine[g].astype(F32) + theirs[g].astype(F32)
        place = placer(offs, g)
        zero = jnp.zeros((8, 2 * D), F32)
        for z in range(4):
            middle = [
                total[128 + 32 * z : 160 + 32 * z],
                total[256 + 32 * z : 272 + 32 * z],
                total[384 + 32 * z : 392 + 32 * z],
                zero,
            ]
            extra = [total[272 + 32 * z : 288 + 32 * z], total[392 + 32 * z : 416 + 32 * z], zero]
            if z < 2:
                rows = jnp.concatenate([total[64 * z : 64 * z + 64]] + middle, 0).astype(BF)
                whole = d0[g, 128 * z : 128 * z + 128].astype(F32) + dot(place, rows)
                if z == 0:
                    kept[g] = whole
                    x_kept[g] = jnp.concatenate(extra, 0)
                else:
                    far[g] = whole.astype(BF)
                    x_far[g] = jnp.concatenate(extra, 0).astype(BF)
            else:
                ref = up if z == 2 else down
                ref[g] = jnp.concatenate(middle + extra, 0).astype(BF)


def cross_kernel(kept, far, up, down, one, two, three):
    for g in range(GROUPS):
        total = kept[g] + far[g].astype(F32) + up[g, 64:112].astype(F32) + down[g, 64:112].astype(F32)
        zero = jnp.zeros((8, 2 * D), F32)
        one[g] = jnp.concatenate([total[0:24], zero], 0).astype(BF)
        two[g] = jnp.concatenate([total[24:32], zero], 0).astype(BF)
        three[g] = jnp.concatenate([total[32:40], zero], 0).astype(BF)


def finish_kernel(offs, kept, far, up, down, one, two, three, dk_ref, dv_ref):
    for g in range(GROUPS):
        middle = up[g, 0:64].astype(F32) + down[g, 0:64].astype(F32)
        a, b, c = one[g].astype(F32), two[g].astype(F32), three[g].astype(F32)
        rows = jnp.concatenate(
            [
                jnp.zeros((64, 2 * D), F32),
                middle[0:32],
                middle[32:48] + a[0:16],
                middle[48:56] + a[16:24] + b[0:8] + c[0:8],
                jnp.zeros((8, 2 * D), F32),
            ],
            0,
        ).astype(BF)
        whole = kept[g] + far[g].astype(F32) + dot(placer(offs, g), rows)
        dk_ref[:, g * D : (g + 1) * D] = whole[:, :D].astype(BF)
        dv_ref[:, g * D : (g + 1) * D] = whole[:, D:].astype(BF)


def whole_call(body, name, outs, offs, *arrays):
    specs = [pl.BlockSpec(memory_space=pltpu.VMEM)] * len(arrays)
    if offs is not None:
        specs = [pl.BlockSpec(memory_space=pltpu.SMEM)] + specs
        arrays = (offs,) + arrays
    shapes = [jax.ShapeDtypeStruct(shape, dtype) for shape, dtype in outs]
    return pl.pallas_call(
        body,
        name=name,
        out_shape=shapes,
        in_specs=specs,
        out_specs=[pl.BlockSpec(memory_space=pltpu.VMEM)] * len(shapes),
        compiler_params=pltpu.CompilerParams(vmem_limit_bytes=VMEM_LIMIT),
    )(*arrays)


def attention(offs, q, g, k, v, kp, vp, own, other):
    lanes = lambda width: pl.BlockSpec((TOKENS, width), lambda i: (0, i))
    block = lambda rows: pl.BlockSpec((1, rows, 2 * D), lambda i: (i, 0, 0))
    return pl.pallas_call(
        attention_kernel,
        name="attention",
        grid=(GROUPS,),
        in_specs=[pl.BlockSpec(memory_space=pltpu.SMEM)]
        + [lanes(WIDE), lanes(WIDE), lanes(D), lanes(D), lanes(D), lanes(D), block(512), block(512)],
        out_specs=[lanes(WIDE), lanes(WIDE), block(256), block(512), block(512)],
        out_shape=[
            jax.ShapeDtypeStruct((TOKENS, GROUPS * WIDE), BF),
            jax.ShapeDtypeStruct((TOKENS, GROUPS * WIDE), BF),
            jax.ShapeDtypeStruct((GROUPS, 256, 2 * D), BF),
            jax.ShapeDtypeStruct((GROUPS, 512, 2 * D), BF),
            jax.ShapeDtypeStruct((GROUPS, 512, 2 * D), BF),
        ],
        compiler_params=pltpu.CompilerParams(vmem_limit_bytes=VMEM_LIMIT),
    )(offs, q, g, k, v, kp, vp, own, other)


def routes(count):
    def along_z(i, step):
        z = ((i & 1) * 2 + (i >> 2 & 1) + step) % 4
        return (i & ~5) | (z & 1) << 2 | z >> 1

    table = {
        "head": lambda i: i ^ 1,
        "core": lambda i: i ^ 2,
        "up": lambda i: along_z(i, 1),
        "down": lambda i: along_z(i, -1),
        "x1": lambda i: i ^ 8,
        "x2": lambda i: i ^ 16,
        "x3": lambda i: i ^ 24,
    }
    return {name: [(i, to(i)) for i in range(count)] for name, to in table.items()}


def shards(count, queries, key_rows, value_rows, gradient, level_offsets):
    route = routes(count)

    def send(x, name):
        return lax.ppermute(x, AXES, route[name])

    other_offsets = send(level_offsets, "head")
    low = lax.axis_index("head") == 0
    offs = jnp.where(
        low,
        jnp.concatenate([level_offsets, other_offsets], 1),
        jnp.concatenate([other_offsets, level_offsets], 1),
    )
    far_keys = send(key_rows, "head")
    far_values = send(value_rows, "head")

    rows = lambda n, dtype=BF: ((GROUPS, n, 2 * D), dtype)
    first, middle, tail, last = whole_call(
        select_kernel, "select", [rows(64), rows(64), rows(32), rows(16)], offs, key_rows, value_rows
    )
    middle_down = send(middle, "up")
    middle_up = send(middle, "down")
    (extra,) = whole_call(
        compact_kernel, "compact", [rows(48)], None, send(tail, "x1"), send(last, "x2"), send(last, "x3")
    )
    extra_down = send(extra, "up")
    extra_up = send(extra, "down")
    extra_far = send(extra, "head")
    (own,) = whole_call(
        assemble_kernel, "assemble", [rows(512)], offs, first, middle, extra, far_keys, far_values,
        extra_far, middle_up, extra_up, middle_down, extra_down,
    )
    other = send(own, "core")
    attended, grad_queries, d0, down_own, down_other = attention(
        offs, queries, gradient, key_rows, value_rows, far_keys, far_values, own, other
    )
    theirs = send(down_other, "core")
    kept, far, up, down, x_far, x_kept = whole_call(
        reduce_kernel, "reduce", [rows(128, F32), rows(128), rows(112), rows(112), rows(48), rows(48, F32)],
        offs, d0, down_own, theirs,
    )
    from_down = send(up, "up")
    from_up = send(down, "down")
    x_far = send(x_far, "head")
    far = send(far, "head")
    one, two, three = whole_call(
        cross_kernel, "cross", [rows(32), rows(16), rows(16)], None, x_kept, x_far, from_up, from_down
    )
    one, two, three = send(one, "x1"), send(two, "x2"), send(three, "x3")
    out = ((TOKENS, GROUPS * D), BF)
    grad_keys, grad_values = whole_call(
        finish_kernel, "finish", [out, out], offs, kept, far, from_up, from_down, one, two, three
    )
    return (attended, grad_queries, grad_keys, grad_values)


def solution(mesh):
    rows = P(AXES, None)
    return jax.shard_map(
        functools.partial(shards, mesh.size),
        mesh=mesh,
        in_specs=(rows, rows, rows, rows, P(None, "head")),
        out_specs=(rows, rows, rows, rows),
        check_vma=False,
    )
```

profile of v0, /device:TPU:0, one launch (start us, length us, event | category | flops | bytes accessed | tf_op | source)
XLA Modules:
  0.0 144.9 jit_solution(5829140826858476719)
XLA Ops:
  0.6 4.0 %collective-permute-start.1 = (bf16[128,1024]{1,0:T(8,128)(2,1)}, bf16[128,1024]{1,0:T(8,128)(2,1)S(1)}, u32[]{:S(2)}, u32[]{:S(2)}) collective-permute-start(bf16[128,1024]{1,0:T(8,128)(2,1)} %k_ref.1), channel_id=1, source_target_pairs={{0,1},{1,0},{2,3},{3,2},{4,5},{5,4},{6,7},{7,6},{8,9},{9,8},{10,11... | collective-permute-start | bytes 786440 | tf_op jit(solution)/shard_map/ppermute | solution.py:379
  4.7 0.1 collective-permute-start.2
  4.8 0.8 copy.10
  5.5 3.4 %collective-permute-start = (s32[5,4]{1,0:T(8,128)S(1)}, s32[5,4]{1,0:T(8,128)S(1)}, u32[]{:S(2)}, u32[]{:S(2)}) collective-permute-start(s32[5,4]{1,0:T(8,128)S(1)} %copy.10), channel_id=1, source_target_pairs={{0,1},{1,0},{2,3},{3,2},{4,5},{5,4},{6,7},{7,6},{8,9},{9,8},{10,11... | collective-permute-start | bytes 248 | tf_op jit(solution)/shard_map/ppermute | solution.py:379
  9.0 7.9 %collective-permute-done = s32[5,4]{1,0:T(8,128)S(1)} collective-permute-done((s32[5,4]{1,0:T(8,128)S(1)}, s32[5,4]{1,0:T(8,128)S(1)}, u32[]{:S(2)}, u32[]{:S(2)}) %collective-permute-start) | collective-permute-done | bytes 112 | tf_op jit(solution)/shard_map/ppermute | solution.py:379
  16.9 0.7 add_select_fusion.offs
  17.6 2.2 %select.1 = (bf16[8,64,256]{2,1,0:T(8,128)(2,1)}, bf16[8,64,256]{2,1,0:T(8,128)(2,1)}, bf16[8,32,256]{2,1,0:T(8,128)(2,1)}, bf16[8,16,256]{2,1,0:T(8,128)(2,1)}) custom-call(s32[5,8]{1,0:T(8,128)} %add_select_fusion.offs, bf16[128,1024]{1,0:T(8,128)(2,1)} %k_ref.1, bf16[128,1024]{1,0:T(8,128)(2,1)} %v_ref.1), custom_call_target="tpu_custom_call" | custom-call | tf_op jit(solution)/shard_map/select/pallas_call | solution.py:327
  19.7 2.8 %collective-permute-start.5 = (bf16[8,16,256]{2,1,0:T(8,128)(2,1)}, bf16[8,16,256]{2,1,0:T(8,128)(2,1)S(1)}, u32[]{:S(2)}, u32[]{:S(2)}) collective-permute-start(bf16[8,16,256]{2,1,0:T(8,128)(2,1)} %get-tuple-element.27), channel_id=1, source_target_pairs={{0,24},{1,25},{2,26},{3,27},{4,28},{5,29},{6,30},{7,31},{8,16},{9,... | collective-permute-start | bytes 196616 | tf_op jit(solution)/shard_map/ppermute | solution.py:379
  22.5 0.2 collective-permute-start.3
  22.7 1.7 %collective-permute-start.4 = (bf16[8,16,256]{2,1,0:T(8,128)(2,1)}, bf16[8,16,256]{2,1,0:T(8,128)(2,1)S(1)}, u32[]{:S(2)}, u32[]{:S(2)}) collective-permute-start(bf16[8,16,256]{2,1,0:T(8,128)(2,1)} %get-tuple-element.27), channel_id=1, source_target_pairs={{0,16},{1,17},{2,18},{3,19},{4,20},{5,21},{6,22},{7,23},{8,24},{9,... | collective-permute-start | bytes 196616 | tf_op jit(solution)/shard_map/ppermute | solution.py:379
  24.4 1.0 collective-permute-done.5.three
  25.4 1.3 collective-permute-start.9
  26.7 2.0 %collective-permute-done.4.two = bf16[8,16,256]{2,1,0:T(8,128)(2,1)S(1)} collective-permute-done((bf16[8,16,256]{2,1,0:T(8,128)(2,1)}, bf16[8,16,256]{2,1,0:T(8,128)(2,1)S(1)}, u32[]{:S(2)}, u32[]{:S(2)}) %collective-permute-start.4) | collective-permute-done | bytes 65568 | tf_op jit(solution)/shard_map/ppermute | solution.py:379
  28.7 3.4 %collective-permute-start.7 = (bf16[8,64,256]{2,1,0:T(8,128)(2,1)}, bf16[8,64,256]{2,1,0:T(8,128)(2,1)S(1)}, u32[]{:S(2)}, u32[]{:S(2)}) collective-permute-start(bf16[8,64,256]{2,1,0:T(8,128)(2,1)} %get-tuple-element.25.mid_own), channel_id=1, source_target_pairs={{0,5},{1,4},{2,7},{3,6},{4,0},{5,1},{6,2},{7,3},{8,13},{9,12},{10,... | collective-permute-start | bytes 786440 | tf_op jit(solution)/shard_map/ppermute | solution.py:379
  32.1 0.0 collective-permute-done.3.one
  32.1 0.0 copy-start.13
  32.1 0.6 copy-done.13
  32.8 1.6 %compact.1.x_own = bf16[8,48,256]{2,1,0:T(8,128)(2,1)} custom-call(bf16[8,32,256]{2,1,0:T(8,128)(2,1)} %copy-done.13, bf16[8,16,256]{2,1,0:T(8,128)(2,1)} %copy-done.18, bf16[8,16,256]{2,1,0:T(8,128)(2,1)} %copy-done.16), custom_call_target="tpu_custom_call" | custom-call | tf_op jit(solution)/shard_map/compact/pallas_call | solution.py:327
  34.4 0.0 collective-permute-start.10
  34.4 3.2 %collective-permute-start.8 = (bf16[8,48,256]{2,1,0:T(8,128)(2,1)}, bf16[8,48,256]{2,1,0:T(8,128)(2,1)S(1)}, u32[]{:S(2)}, u32[]{:S(2)}) collective-permute-start(bf16[8,48,256]{2,1,0:T(8,128)(2,1)} %compact.1.x_own), channel_id=1, source_target_pairs={{0,5},{1,4},{2,7},{3,6},{4,0},{5,1},{6,2},{7,3},{8,13},{9,12},{10,... | collective-permute-start | bytes 589832 | tf_op jit(solution)/shard_map/ppermute | solution.py:379
  37.7 1.7 %collective-permute-done.7.mid_up = bf16[8,64,256]{2,1,0:T(8,128)(2,1)S(1)} collective-permute-done((bf16[8,64,256]{2,1,0:T(8,128)(2,1)}, bf16[8,64,256]{2,1,0:T(8,128)(2,1)S(1)}, u32[]{:S(2)}, u32[]{:S(2)}) %collective-permute-start.7) | collective-permute-done | bytes 262176 | tf_op jit(solution)/shard_map/ppermute | solution.py:379
  39.3 5.9 %collective-permute-done.10.x_down = bf16[8,48,256]{2,1,0:T(8,128)(2,1)S(1)} collective-permute-done((bf16[8,48,256]{2,1,0:T(8,128)(2,1)}, bf16[8,48,256]{2,1,0:T(8,128)(2,1)S(1)}, u32[]{:S(2)}, u32[]{:S(2)}) %collective-permute-start.10) | collective-permute-done | bytes 196640 | tf_op jit(solution)/shard_map/ppermute | solution.py:379
  45.3 0.6 copy-done.9
  45.9 0.1 copy-done.10
  46.0 0.1 copy-done.11
  46.1 3.3 %assemble.1.own_ref = bf16[8,512,256]{2,1,0:T(8,128)(2,1)} custom-call(s32[5,8]{1,0:T(8,128)} %add_select_fusion.offs, bf16[8,64,256]{2,1,0:T(8,128)(2,1)} %get-tuple-element.24.first, bf16[8,64,256]{2,1,0:T(8,128)(2,1)} %get-tuple-element.25.mid_own, bf16[8,48,256]{2,1,0:T(8,128)(2,1)} %compact.1.x_own, bf16[128,1024]{1,0:T(8,128)(2,1)} %copy-done.4, ...), custom_call_target="tpu_custom_call" | custom-call | tf_op jit(solution)/shard_map/assemble/pallas_call | solution.py:327
  49.4 4.4 %collective-permute-done.11.other_ref = bf16[8,512,256]{2,1,0:T(8,128)(2,1)S(1)} collective-permute-done((bf16[8,512,256]{2,1,0:T(8,128)(2,1)}, bf16[8,512,256]{2,1,0:T(8,128)(2,1)S(1)}, u32[]{:S(2)}, u32[]{:S(2)}) %collective-permute-start.11) | collective-permute-done | bytes 2097184 | tf_op jit(solution)/shard_map/ppermute | solution.py:379
  53.7 1.4 copy-done
  55.1 31.3 %attention.1 = (bf16[128,4096]{1,0:T(8,128)(2,1)}, bf16[128,4096]{1,0:T(8,128)(2,1)}, bf16[8,256,256]{2,1,0:T(8,128)(2,1)}, bf16[8,512,256]{2,1,0:T(8,128)(2,1)}, bf16[8,512,256]{2,1,0:T(8,128)(2,1)}) custom-call(s32[5,8]{1,0:T(8,128)} %add_select_fusion.offs, bf16[128,4096]{1,0:T(8,128)(2,1)} %q_ref.1, bf16[128,4096]{1,0:T(8,128)(2,1)} %g_ref.1, ...), custom_call_target="tpu_custom_call" | custom-call | tf_op jit(solution)/shard_map/attention/pallas_call | solution.py:340
  86.4 0.2 collective-permute-start.12
  86.6 4.2 %collective-permute-done.12.theirs = bf16[8,512,256]{2,1,0:T(8,128)(2,1)S(1)} collective-permute-done((bf16[8,512,256]{2,1,0:T(8,128)(2,1)}, bf16[8,512,256]{2,1,0:T(8,128)(2,1)S(1)}, u32[]{:S(2)}, u32[]{:S(2)}) %collective-permute-start.12) | collective-permute-done | bytes 2097184 | tf_op jit(solution)/shard_map/ppermute | solution.py:379
  90.8 1.4 copy-done.1
  92.2 4.7 %reduce.1 = (f32[8,128,256]{2,1,0:T(8,128)}, bf16[8,128,256]{2,1,0:T(8,128)(2,1)}, bf16[8,112,256]{2,1,0:T(8,128)(2,1)}, bf16[8,112,256]{2,1,0:T(8,128)(2,1)}, b...) custom-call(s32[5,8]{1,0:T(8,128)} %add_select_fusion.offs, bf16[8,256,256]{2,1,0:T(8,128)(2,1)} %get-tuple-element.30.d0, ...), custom_call_target="tpu_custom_call" | custom-call | tf_op jit(solution)/shard_map/reduce/pallas_call | solution.py:327
  96.9 3.0 %collective-permute-start.14 = (bf16[8,112,256]{2,1,0:T(8,128)(2,1)}, bf16[8,112,256]{2,1,0:T(8,128)(2,1)S(1)}, u32[]{:S(2)}, u32[]{:S(2)}) collective-permute-start(bf16[8,112,256]{2,1,0:T(8,128)(2,1)} %get-tuple-element.35), channel_id=1, source_target_pairs={{0,5},{1,4},{2,7},{3,6},{4,0},{5,1},{6,2},{7,3},{8,13},{9,12},{10,... | collective-permute-start | bytes 1376264 | tf_op jit(solution)/shard_map/ppermute | solution.py:379
  99.9 1.5 %collective-permute-start.13 = (bf16[8,128,256]{2,1,0:T(8,128)(2,1)}, bf16[8,128,256]{2,1,0:T(8,128)(2,1)S(1)}, u32[]{:S(2)}, u32[]{:S(2)}) collective-permute-start(bf16[8,128,256]{2,1,0:T(8,128)(2,1)} %get-tuple-element.34), channel_id=1, source_target_pairs={{0,1},{1,0},{2,3},{3,2},{4,5},{5,4},{6,7},{7,6},{8,9},{9,8},{10,11... | collective-permute-start | bytes 1572872 | tf_op jit(solution)/shard_map/ppermute | solution.py:379
  101.4 2.1 %collective-permute-start.16 = (bf16[8,48,256]{2,1,0:T(8,128)(2,1)}, bf16[8,48,256]{2,1,0:T(8,128)(2,1)S(1)}, u32[]{:S(2)}, u32[]{:S(2)}) collective-permute-start(bf16[8,48,256]{2,1,0:T(8,128)(2,1)} %get-tuple-element.38), channel_id=1, source_target_pairs={{0,1},{1,0},{2,3},{3,2},{4,5},{5,4},{6,7},{7,6},{8,9},{9,8},{10,11... | collective-permute-start | bytes 589832 | tf_op jit(solution)/shard_map/ppermute | solution.py:379
  103.4 24.2 %collective-permute-done.16.far = bf16[8,48,256]{2,1,0:T(8,128)(2,1)S(1)} collective-permute-done((bf16[8,48,256]{2,1,0:T(8,128)(2,1)}, bf16[8,48,256]{2,1,0:T(8,128)(2,1)S(1)}, u32[]{:S(2)}, u32[]{:S(2)}) %collective-permute-start.16) | collective-permute-done | bytes 196640 | tf_op jit(solution)/shard_map/ppermute | solution.py:379
  127.7 1.4 collective-permute-done.15.down
  129.0 0.8 copy-done.3
  129.8 2.1 %cross.1 = (bf16[8,32,256]{2,1,0:T(8,128)(2,1)}, bf16[8,16,256]{2,1,0:T(8,128)(2,1)}, bf16[8,16,256]{2,1,0:T(8,128)(2,1)}) custom-call(f32[8,48,256]{2,1,0:T(8,128)} %get-tuple-element.37.kept, bf16[8,48,256]{2,1,0:T(8,128)(2,1)} %copy-done.12, bf16[8,112,256]{2,1,0:T(8,128)(2,1)} %copy-done.2, bf16[8,112,256]{2,1,0:T(8,128)(2,1)} %copy-done.3), custom_call_target="tpu_custom_call" | custom-call | tf_op jit(solution)/shard_map/cross/pallas_call | solution.py:327
  131.9 1.8 %collective-permute-start.17 = (bf16[8,32,256]{2,1,0:T(8,128)(2,1)}, bf16[8,32,256]{2,1,0:T(8,128)(2,1)S(1)}, u32[]{:S(2)}, u32[]{:S(2)}) collective-permute-start(bf16[8,32,256]{2,1,0:T(8,128)(2,1)} %get-tuple-element.39), channel_id=1, source_target_pairs={{0,8},{1,9},{2,10},{3,11},{4,12},{5,13},{6,14},{7,15},{8,0},{9,1},... | collective-permute-start | bytes 393224 | tf_op jit(solution)/shard_map/ppermute | solution.py:379
  133.7 2.0 %collective-permute-start.18 = (bf16[8,16,256]{2,1,0:T(8,128)(2,1)}, bf16[8,16,256]{2,1,0:T(8,128)(2,1)S(1)}, u32[]{:S(2)}, u32[]{:S(2)}) collective-permute-start(bf16[8,16,256]{2,1,0:T(8,128)(2,1)} %get-tuple-element.40), channel_id=1, source_target_pairs={{0,16},{1,17},{2,18},{3,19},{4,20},{5,21},{6,22},{7,23},{8,24},{9,... | collective-permute-start | bytes 196616 | tf_op jit(solution)/shard_map/ppermute | solution.py:379
  135.7 0.9 collective-permute-start.19
  136.6 3.1 %collective-permute-done.18.two = bf16[8,16,256]{2,1,0:T(8,128)(2,1)S(1)} collective-permute-done((bf16[8,16,256]{2,1,0:T(8,128)(2,1)}, bf16[8,16,256]{2,1,0:T(8,128)(2,1)S(1)}, u32[]{:S(2)}, u32[]{:S(2)}) %collective-permute-start.18) | collective-permute-done | bytes 65568 | tf_op jit(solution)/shard_map/ppermute | solution.py:379
  139.7 1.7 %collective-permute-done.19.three = bf16[8,16,256]{2,1,0:T(8,128)(2,1)S(1)} collective-permute-done((bf16[8,16,256]{2,1,0:T(8,128)(2,1)}, bf16[8,16,256]{2,1,0:T(8,128)(2,1)S(1)}, u32[]{:S(2)}, u32[]{:S(2)}) %collective-permute-start.19) | collective-permute-done | bytes 65568 | tf_op jit(solution)/shard_map/ppermute | solution.py:379
  141.4 0.6 copy-done.17
  142.0 0.1 copy-done.14
  142.1 2.8 %finish.1 = (bf16[128,1024]{1,0:T(8,128)(2,1)}, bf16[128,1024]{1,0:T(8,128)(2,1)}) custom-call(s32[5,8]{1,0:T(8,128)} %add_select_fusion.offs, f32[8,128,256]{2,1,0:T(8,128)} %get-tuple-element.33.kept, bf16[8,128,256]{2,1,0:T(8,128)(2,1)} %copy-done.6, bf16[8,112,256]{2,1,0:T(8,128)(2,1)} %copy-done.2, bf16[8,112,256]{2,1,0:T(8,128)(2,1)} %copy-done.3, ...), custom_call_target="tpu_custom_call" | custom-call | tf_op jit(solution)/shard_map/finish/pallas_call | solution.py:327
  (39 shorter events, 0.1 us)
Async XLA Ops:
  0.6 33.8 %collective-permute-start.1 = (bf16[128,1024]{1,0:T(8,128)(2,1)}, bf16[128,1024]{1,0:T(8,128)(2,1)S(1)}, u32[]{:S(2)}, u32[]{:S(2)}) collective-permute-start(bf16[128,1024]{1,0:T(8,128)(2,1)} %k_ref.1), channel_id=1, source_target_pairs={{0,1},{1,0},{2,3},{3,2},{4,5},{5,4},{6,7},{7,6},{8,9},{9,8},{10,11... | collective-permute-start | bytes 786440 | tf_op jit(solution)/shard_map/ppermute | solution.py:379
  4.7 33.0 %collective-permute-start.2 = (bf16[128,1024]{1,0:T(8,128)(2,1)}, bf16[128,1024]{1,0:T(8,128)(2,1)S(1)}, u32[]{:S(2)}, u32[]{:S(2)}) collective-permute-start(bf16[128,1024]{1,0:T(8,128)(2,1)} %v_ref.1), channel_id=1, source_target_pairs={{0,1},{1,0},{2,3},{3,2},{4,5},{5,4},{6,7},{7,6},{8,9},{9,8},{10,11... | collective-permute-start | bytes 786440 | tf_op jit(solution)/shard_map/ppermute | solution.py:379
  5.5 11.4 %collective-permute-start = (s32[5,4]{1,0:T(8,128)S(1)}, s32[5,4]{1,0:T(8,128)S(1)}, u32[]{:S(2)}, u32[]{:S(2)}) collective-permute-start(s32[5,4]{1,0:T(8,128)S(1)} %copy.10), channel_id=1, source_target_pairs={{0,1},{1,0},{2,3},{3,2},{4,5},{5,4},{6,7},{7,6},{8,9},{9,8},{10,11... | collective-permute-start | bytes 248 | tf_op jit(solution)/shard_map/ppermute | solution.py:379
  19.7 5.7 %collective-permute-start.5 = (bf16[8,16,256]{2,1,0:T(8,128)(2,1)}, bf16[8,16,256]{2,1,0:T(8,128)(2,1)S(1)}, u32[]{:S(2)}, u32[]{:S(2)}) collective-permute-start(bf16[8,16,256]{2,1,0:T(8,128)(2,1)} %get-tuple-element.27), channel_id=1, source_target_pairs={{0,24},{1,25},{2,26},{3,27},{4,28},{5,29},{6,30},{7,31},{8,16},{9,... | collective-permute-start | bytes 196616 | tf_op jit(solution)/shard_map/ppermute | solution.py:379
  22.5 9.6 %collective-permute-start.3 = (bf16[8,32,256]{2,1,0:T(8,128)(2,1)}, bf16[8,32,256]{2,1,0:T(8,128)(2,1)S(1)}, u32[]{:S(2)}, u32[]{:S(2)}) collective-permute-start(bf16[8,32,256]{2,1,0:T(8,128)(2,1)} %get-tuple-element.26), channel_id=1, source_target_pairs={{0,8},{1,9},{2,10},{3,11},{4,12},{5,13},{6,14},{7,15},{8,0},{9,1},... | collective-permute-start | bytes 393224 | tf_op jit(solution)/shard_map/ppermute | solution.py:379
  22.7 6.0 %collective-permute-start.4 = (bf16[8,16,256]{2,1,0:T(8,128)(2,1)}, bf16[8,16,256]{2,1,0:T(8,128)(2,1)S(1)}, u32[]{:S(2)}, u32[]{:S(2)}) collective-permute-start(bf16[8,16,256]{2,1,0:T(8,128)(2,1)} %get-tuple-element.27), channel_id=1, source_target_pairs={{0,16},{1,17},{2,18},{3,19},{4,20},{5,21},{6,22},{7,23},{8,24},{9,... | collective-permute-start | bytes 196616 | tf_op jit(solution)/shard_map/ppermute | solution.py:379
  25.4 6.7 %copy-start.16 = (bf16[8,16,256]{2,1,0:T(8,128)(2,1)}, bf16[8,16,256]{2,1,0:T(8,128)(2,1)S(1)}, u32[]{:S(2)}) copy-start(bf16[8,16,256]{2,1,0:T(8,128)(2,1)S(1)} %collective-permute-done.5.three) | copy-start | bytes 196612
  25.4 12.2 %collective-permute-start.9 = (bf16[8,64,256]{2,1,0:T(8,128)(2,1)}, bf16[8,64,256]{2,1,0:T(8,128)(2,1)S(1)}, u32[]{:S(2)}, u32[]{:S(2)}) collective-permute-start(bf16[8,64,256]{2,1,0:T(8,128)(2,1)} %get-tuple-element.25.mid_own), channel_id=1, source_target_pairs={{0,4},{1,5},{2,6},{3,7},{4,1},{5,0},{6,3},{7,2},{8,12},{9,13},{10,... | collective-permute-start | bytes 786440 | tf_op jit(solution)/shard_map/ppermute | solution.py:379
  28.7 3.4 %copy-start.18 = (bf16[8,16,256]{2,1,0:T(8,128)(2,1)}, bf16[8,16,256]{2,1,0:T(8,128)(2,1)S(1)}, u32[]{:S(2)}) copy-start(bf16[8,16,256]{2,1,0:T(8,128)(2,1)S(1)} %collective-permute-done.4.two) | copy-start | bytes 196612
  28.7 10.6 %collective-permute-start.7 = (bf16[8,64,256]{2,1,0:T(8,128)(2,1)}, bf16[8,64,256]{2,1,0:T(8,128)(2,1)S(1)}, u32[]{:S(2)}, u32[]{:S(2)}) collective-permute-start(bf16[8,64,256]{2,1,0:T(8,128)(2,1)} %get-tuple-element.25.mid_own), channel_id=1, source_target_pairs={{0,5},{1,4},{2,7},{3,6},{4,0},{5,1},{6,2},{7,3},{8,13},{9,12},{10,... | collective-permute-start | bytes 786440 | tf_op jit(solution)/shard_map/ppermute | solution.py:379
  32.1 0.7 copy-start.13
  34.4 10.8 %collective-permute-start.10 = (bf16[8,48,256]{2,1,0:T(8,128)(2,1)}, bf16[8,48,256]{2,1,0:T(8,128)(2,1)S(1)}, u32[]{:S(2)}, u32[]{:S(2)}) collective-permute-start(bf16[8,48,256]{2,1,0:T(8,128)(2,1)} %compact.1.x_own), channel_id=1, source_target_pairs={{0,4},{1,5},{2,6},{3,7},{4,1},{5,0},{6,3},{7,2},{8,12},{9,13},{10,... | collective-permute-start | bytes 589832 | tf_op jit(solution)/shard_map/ppermute | solution.py:379
  34.4 10.9 %copy-start.4 = (bf16[128,1024]{1,0:T(8,128)(2,1)}, bf16[128,1024]{1,0:T(8,128)(2,1)S(1)}, u32[]{:S(2)}) copy-start(bf16[128,1024]{1,0:T(8,128)(2,1)S(1)} %collective-permute-done.1.keys.kp_ref) | copy-start | bytes 786436
  34.4 10.8 %collective-permute-start.8 = (bf16[8,48,256]{2,1,0:T(8,128)(2,1)}, bf16[8,48,256]{2,1,0:T(8,128)(2,1)S(1)}, u32[]{:S(2)}, u32[]{:S(2)}) collective-permute-start(bf16[8,48,256]{2,1,0:T(8,128)(2,1)} %compact.1.x_own), channel_id=1, source_target_pairs={{0,5},{1,4},{2,7},{3,6},{4,0},{5,1},{6,2},{7,3},{8,13},{9,12},{10,... | collective-permute-start | bytes 589832 | tf_op jit(solution)/shard_map/ppermute | solution.py:379
  37.6 7.6 %copy-start.5 = (bf16[128,1024]{1,0:T(8,128)(2,1)}, bf16[128,1024]{1,0:T(8,128)(2,1)S(1)}, u32[]{:S(2)}) copy-start(bf16[128,1024]{1,0:T(8,128)(2,1)S(1)} %collective-permute-done.2.values.vp_ref) | copy-start | bytes 786436
  37.6 7.6 %collective-permute-start.6 = (bf16[8,48,256]{2,1,0:T(8,128)(2,1)}, bf16[8,48,256]{2,1,0:T(8,128)(2,1)S(1)}, u32[]{:S(2)}, u32[]{:S(2)}) collective-permute-start(bf16[8,48,256]{2,1,0:T(8,128)(2,1)} %compact.1.x_own), channel_id=1, source_target_pairs={{0,1},{1,0},{2,3},{3,2},{4,5},{5,4},{6,7},{7,6},{8,9},{9,8},{10,11... | collective-permute-start | bytes 589832 | tf_op jit(solution)/shard_map/ppermute | solution.py:379
  37.7 7.6 %copy-start.7 = (bf16[8,64,256]{2,1,0:T(8,128)(2,1)}, bf16[8,64,256]{2,1,0:T(8,128)(2,1)S(1)}, u32[]{:S(2)}) copy-start(bf16[8,64,256]{2,1,0:T(8,128)(2,1)S(1)} %collective-permute-done.9.mid_down) | copy-start | bytes 786436
  39.3 6.0 %copy-start.8 = (bf16[8,64,256]{2,1,0:T(8,128)(2,1)}, bf16[8,64,256]{2,1,0:T(8,128)(2,1)S(1)}, u32[]{:S(2)}) copy-start(bf16[8,64,256]{2,1,0:T(8,128)(2,1)S(1)} %collective-permute-done.7.mid_up) | copy-start | bytes 786436
  45.2 0.7 copy-start.9
  45.2 0.7 copy-start.10
  45.3 0.8 copy-start.11
  49.3 4.4 %collective-permute-start.11 = (bf16[8,512,256]{2,1,0:T(8,128)(2,1)}, bf16[8,512,256]{2,1,0:T(8,128)(2,1)S(1)}, u32[]{:S(2)}, u32[]{:S(2)}) collective-permute-start(bf16[8,512,256]{2,1,0:T(8,128)(2,1)} %assemble.1.own_ref), channel_id=1, source_target_pairs={{0,2},{1,3},{2,0},{3,1},{4,6},{5,7},{6,4},{7,5},{8,10},{9,11},{10,... | collective-permute-start | bytes 6291464 | tf_op jit(solution)/shard_map/ppermute | solution.py:379
  53.7 1.4 copy-start
  86.4 4.5 %collective-permute-start.12 = (bf16[8,512,256]{2,1,0:T(8,128)(2,1)}, bf16[8,512,256]{2,1,0:T(8,128)(2,1)S(1)}, u32[]{:S(2)}, u32[]{:S(2)}) collective-permute-start(bf16[8,512,256]{2,1,0:T(8,128)(2,1)} %get-tuple-element.32), channel_id=1, source_target_pairs={{0,2},{1,3},{2,0},{3,1},{4,6},{5,7},{6,4},{7,5},{8,10},{9,11},{10,... | collective-permute-start | bytes 6291464 | tf_op jit(solution)/shard_map/ppermute | solution.py:379
  90.8 1.4 copy-start.1
  96.9 30.8 %collective-permute-start.14 = (bf16[8,112,256]{2,1,0:T(8,128)(2,1)}, bf16[8,112,256]{2,1,0:T(8,128)(2,1)S(1)}, u32[]{:S(2)}, u32[]{:S(2)}) collective-permute-start(bf16[8,112,256]{2,1,0:T(8,128)(2,1)} %get-tuple-element.35), channel_id=1, source_target_pairs={{0,5},{1,4},{2,7},{3,6},{4,0},{5,1},{6,2},{7,3},{8,13},{9,12},{10,... | collective-permute-start | bytes 1376264 | tf_op jit(solution)/shard_map/ppermute | solution.py:379
  99.9 29.2 %collective-permute-start.15 = (bf16[8,112,256]{2,1,0:T(8,128)(2,1)}, bf16[8,112,256]{2,1,0:T(8,128)(2,1)S(1)}, u32[]{:S(2)}, u32[]{:S(2)}) collective-permute-start(bf16[8,112,256]{2,1,0:T(8,128)(2,1)} %get-tuple-element.36), channel_id=1, source_target_pairs={{0,4},{1,5},{2,6},{3,7},{4,1},{5,0},{6,3},{7,2},{8,12},{9,13},{10,... | collective-permute-start | bytes 1376264 | tf_op jit(solution)/shard_map/ppermute | solution.py:379
  99.9 36.7 %collective-permute-start.13 = (bf16[8,128,256]{2,1,0:T(8,128)(2,1)}, bf16[8,128,256]{2,1,0:T(8,128)(2,1)S(1)}, u32[]{:S(2)}, u32[]{:S(2)}) collective-permute-start(bf16[8,128,256]{2,1,0:T(8,128)(2,1)} %get-tuple-element.34), channel_id=1, source_target_pairs={{0,1},{1,0},{2,3},{3,2},{4,5},{5,4},{6,7},{7,6},{8,9},{9,8},{10,11... | collective-permute-start | bytes 1572872 | tf_op jit(solution)/shard_map/ppermute | solution.py:379
  101.4 26.3 %collective-permute-start.16 = (bf16[8,48,256]{2,1,0:T(8,128)(2,1)}, bf16[8,48,256]{2,1,0:T(8,128)(2,1)S(1)}, u32[]{:S(2)}, u32[]{:S(2)}) collective-permute-start(bf16[8,48,256]{2,1,0:T(8,128)(2,1)} %get-tuple-element.38), channel_id=1, source_target_pairs={{0,1},{1,0},{2,3},{3,2},{4,5},{5,4},{6,7},{7,6},{8,9},{9,8},{10,11... | collective-permute-start | bytes 589832 | tf_op jit(solution)/shard_map/ppermute | solution.py:379
  127.7 1.4 copy-start.12
  127.7 1.4 copy-start.2
  129.0 0.8 copy-start.3
  131.9 9.5 %collective-permute-start.17 = (bf16[8,32,256]{2,1,0:T(8,128)(2,1)}, bf16[8,32,256]{2,1,0:T(8,128)(2,1)S(1)}, u32[]{:S(2)}, u32[]{:S(2)}) collective-permute-start(bf16[8,32,256]{2,1,0:T(8,128)(2,1)} %get-tuple-element.39), channel_id=1, source_target_pairs={{0,8},{1,9},{2,10},{3,11},{4,12},{5,13},{6,14},{7,15},{8,0},{9,1},... | collective-permute-start | bytes 393224 | tf_op jit(solution)/shard_map/ppermute | solution.py:379
  133.7 6.0 %collective-permute-start.18 = (bf16[8,16,256]{2,1,0:T(8,128)(2,1)}, bf16[8,16,256]{2,1,0:T(8,128)(2,1)S(1)}, u32[]{:S(2)}, u32[]{:S(2)}) collective-permute-start(bf16[8,16,256]{2,1,0:T(8,128)(2,1)} %get-tuple-element.40), channel_id=1, source_target_pairs={{0,16},{1,17},{2,18},{3,19},{4,20},{5,21},{6,22},{7,23},{8,24},{9,... | collective-permute-start | bytes 196616 | tf_op jit(solution)/shard_map/ppermute | solution.py:379
  135.7 5.7 %collective-permute-start.19 = (bf16[8,16,256]{2,1,0:T(8,128)(2,1)}, bf16[8,16,256]{2,1,0:T(8,128)(2,1)S(1)}, u32[]{:S(2)}, u32[]{:S(2)}) collective-permute-start(bf16[8,16,256]{2,1,0:T(8,128)(2,1)} %get-tuple-element.41), channel_id=1, source_target_pairs={{0,24},{1,25},{2,26},{3,27},{4,28},{5,29},{6,30},{7,31},{8,16},{9,... | collective-permute-start | bytes 196616 | tf_op jit(solution)/shard_map/ppermute | solution.py:379
  136.6 4.8 %copy-start.6 = (bf16[8,128,256]{2,1,0:T(8,128)(2,1)}, bf16[8,128,256]{2,1,0:T(8,128)(2,1)S(1)}, u32[]{:S(2)}) copy-start(bf16[8,128,256]{2,1,0:T(8,128)(2,1)S(1)} %collective-permute-done.13.far) | copy-start | bytes 1572868
  139.7 1.7 %copy-start.15 = (bf16[8,16,256]{2,1,0:T(8,128)(2,1)}, bf16[8,16,256]{2,1,0:T(8,128)(2,1)S(1)}, u32[]{:S(2)}) copy-start(bf16[8,16,256]{2,1,0:T(8,128)(2,1)S(1)} %collective-permute-done.18.two) | copy-start | bytes 196612
  141.4 0.6 copy-start.17
  141.4 0.7 copy-start.14
where the time goes:
time: 145 us
  waiting for transfers between devices  57.5 us (40%)
  Pallas kernels  47.9 us (33%)
  starting transfers between devices  31.6 us (22%)
  local copies, waits for them, and re-layouts  6.39 us (4%)
    ppermute x20, waiting for transfers between devices, send(): return lax.ppermute(x, AXES, route[name])  57.5 us
    ppermute x20, starting transfers between devices, send(): return lax.ppermute(x, AXES, route[name])  31.6 us
    pallas_call x1, Pallas kernels, attention(): pl.pallas_call(attention_kernel, name='attention', grid=(GROUPS,), in_spe...  31.3 us
    pallas_call x6, Pallas kernels, whole_call(): pl.pallas_call(body, name=name, out_shape=shapes, in_specs=specs, out_spe...  16.6 us
    unnamed x39, local copies, waits for them, and re-layouts  6.39 us
  transfers between devices with their start and end apart: 20, of which 11 were waited for; matrix products, arithmetic and copies ran while one was open for 1% of the time, Pallas kernels for 4%

commit v1 on v0

v1 whole, which is shorter than its diff:
```python
import functools

import jax
import jax.numpy as jnp
from jax import lax
from jax.experimental import pallas as pl
from jax.experimental.pallas import tpu as pltpu
from jax.sharding import PartitionSpec as P

D = 128
GROUPS = 8
HEADS = 4
TOKENS = 128
TOGETHER = 1
WIDE = HEADS * D
SCALE = D ** (-0.5)
LOG2E = 1.4426950408889634
AXES = ("ctx", "head")
BF = jnp.bfloat16
F32 = jnp.float32
ANY_ROWS = ((0, 64, 1), (64, 96, 2), (96, 112, 3), (112, 120, 4))
VMEM_LIMIT = 24 * 1024 * 1024


def dot(a, b):
    return lax.dot_general(a, b, (((1,), (0,)), ((), ())), preferred_element_type=F32)


def dot_nt(a, b):
    return lax.dot_general(a, b, (((1,), (1,)), ((), ())), preferred_element_type=F32)


def dot_tn(a, b):
    return lax.dot_general(a, b, (((0,), (0,)), ((), ())), preferred_element_type=F32)


def one_hot(mask):
    return jnp.where(mask, 1.0, 0.0).astype(BF)


def selected_token(row, offs, group):
    token = jnp.full(row.shape, -1, jnp.int32)
    for start, stop, level in ANY_ROWS:
        inside = (row >= start) & (row < stop)
        token = jnp.where(inside, (row - start) * 2**level + offs[level, group], token)
    return token


def selector(offs, group):
    shape = (128, TOKENS)
    row = lax.broadcasted_iota(jnp.int32, shape, 0)
    return one_hot(selected_token(row, offs, group) == lax.broadcasted_iota(jnp.int32, shape, 1))


def placer(offs, group):
    shape = (TOKENS, 128)
    row = lax.broadcasted_iota(jnp.int32, shape, 1)
    return one_hot(selected_token(row, offs, group) == lax.broadcasted_iota(jnp.int32, shape, 0))


def group_rows(keys_ref, values_ref, group):
    lanes = slice(group * D, (group + 1) * D)
    return jnp.concatenate([keys_ref[:, lanes], values_ref[:, lanes]], 1)


def select_kernel(offs, keys, values, first, middle, tail, last):
    for g in range(GROUPS):
        rows = dot(selector(offs, g), group_rows(keys, values, g))
        first[g] = rows[0:64].astype(BF)
        middle[g] = rows[64:128].astype(BF)
        tail[g] = rows[96:128].astype(BF)
        last[g] = rows[112:128].astype(BF)


def compact_kernel(one, two, three, packed):
    for g in range(GROUPS):
        a, b, c = one[g].astype(F32), two[g].astype(F32), three[g].astype(F32)
        packed[g] = jnp.concatenate([a[:24], b[:8], c[:8], jnp.zeros((8, 2 * D), F32)], 0).astype(BF)


def assemble_kernel(
    offs, first, mid_own, x_own, keys, values, x_far, mid_up, x_up, mid_down, x_down, held
):
    for g in range(GROUPS):
        far = dot(selector(offs, g), group_rows(keys, values, g))
        mids = [mid_own[g].astype(F32), far[64:128], mid_up[g].astype(F32), mid_down[g].astype(F32)]
        extras = [ref[g].astype(F32) for ref in (x_own, x_far, x_up, x_down)]
        rows = [first[g].astype(F32), far[0:64]]
        rows += [m[0:32] for m in mids]
        for m, x in zip(mids, extras):
            rows += [m[32:48], x[0:16]]
        for m, x in zip(mids, extras):
            rows += [m[48:56], x[16:40]]
        held[g] = jnp.concatenate(rows, 0).astype(BF)


def by_level(rows):
    parts = []
    for start, stop in ((0, 64), (64, 96), (96, 112), (112, 120), (120, 128)):
        parts += [rows[start:stop, h * D : (h + 1) * D] for h in range(HEADS)]
    return jnp.concatenate(parts, 0)


def by_selection(rows):
    heads = []
    for h in range(HEADS):
        parts = []
        base = 0
        for count in (64, 32, 16, 8, 8):
            parts.append(rows[base + h * count : base + (h + 1) * count])
            base += HEADS * count
        heads.append(jnp.concatenate(parts, 0))
    return jnp.concatenate(heads, 1)


def replicated(column, lanes):
    return jnp.broadcast_to(column, (column.shape[0], lanes))


def heads_to_lanes(column):
    count = column.shape[0] // HEADS
    wide = replicated(column, 128)
    lane = lax.broadcasted_iota(jnp.int32, (count, 128), 1)
    out = wide[(HEADS - 1) * count :]
    for h in range(HEADS - 1):
        out = jnp.where(lane == h, wide[h * count : (h + 1) * count], out)
    return out


def lanes_to_heads(x):
    return jnp.concatenate([x[:, h : h + 1] for h in range(HEADS)], 0)


def attention_kernel(
    offs, q_ref, g_ref, k_ref, v_ref, kp_ref, vp_ref, own_ref, other_ref,
    att_ref, dq_ref, d0_ref, down_ref, dother_ref, level_ref, token_ref, delta_ref,
):
    members = range(TOGETHER)
    first_group = pl.program_id(0) * TOGETHER
    ones = jnp.ones((256, D), BF)
    bounds = ((0, 256), (256, 384), (384, 448), (448, 480))
    starts = [[(offs[k, first_group + j], 128 >> k) for k in range(1, 5)] for j in members]

    def load(j):
        wide, lanes = slice(j * WIDE, (j + 1) * WIDE), slice(j * D, (j + 1) * D)
        pick = selector(offs, first_group + j)
        q_rows, g_rows = q_ref[:, wide], g_ref[:, wide]
        qs = by_level(dot(pick, q_rows)).astype(BF)
        gs = by_level(dot(pick, g_rows)).astype(BF)
        own, other = own_ref[j], other_ref[j]
        queries = [jnp.concatenate([q_rows[:, h * D : (h + 1) * D] for h in range(HEADS)], 0)]
        grads = [jnp.concatenate([g_rows[:, h * D : (h + 1) * D] for h in range(HEADS)], 0)]
        keys = [jnp.concatenate([k_ref[:, lanes], kp_ref[:, lanes]], 0)]
        values = [jnp.concatenate([v_ref[:, lanes], vp_ref[:, lanes]], 0)]
        for k, (a, b) in enumerate(bounds):
            queries.append(qs[a:b])
            grads.append(gs[a:b])
            both = jnp.concatenate([own[128 * k : 128 * k + 128], other[128 * k : 128 * k + 128]], 0)
            keys.append(both[:, :D])
            values.append(both[:, D:])
        return queries, grads, keys, values

    def forward(state):
        queries, _, keys, values = state
        raised, peaks, lses, outs = [], [], [], []
        for k in range(5):
            scores = dot_nt(queries[k], keys[k]) * (SCALE * LOG2E)
            peak = jnp.max(scores, 1, keepdims=True)
            power = jnp.exp2(scores - peak).astype(BF)
            out = dot(power, jnp.concatenate([values[k], ones], 1))
            raised.append(power)
            peaks.append(peak)
            lses.append(peak + jnp.log2(out[:, D : D + 1]))
            outs.append(out[:, :D])
        return raised, peaks, lses, outs

    def for_levels(j, ref, x):
        ref[j] = x
        columns = [lanes_to_heads(x)]
        for k, (start, count) in enumerate(starts[j]):
            columns.append(lanes_to_heads(ref[j, pl.ds(start, count, 2 ** (k + 1)), :]))
        return columns

    def merge(j, lses, peaks):
        for k, (start, count) in enumerate(starts[j]):
            level_ref[j, k, pl.ds(start, count, 2 ** (k + 1)), :] = heads_to_lanes(lses[k + 1])
        first = heads_to_lanes(lses[0])
        merged_peak = first
        for k in range(4):
            merged_peak = jnp.maximum(merged_peak, level_ref[j, k])
        row_total = jnp.exp2(first - merged_peak)
        for k in range(4):
            row_total = row_total + jnp.exp2(level_ref[j, k] - merged_peak)
        merged = merged_peak + jnp.log2(row_total)
        return [jnp.exp2(p - m) for p, m in zip(peaks, for_levels(j, token_ref, merged))]

    def gather_levels(j, parts):
        level0 = jnp.concatenate([parts[0][h * 128 : h * 128 + 128] for h in range(HEADS)], 1)
        rows = jnp.concatenate(parts[1:] + [jnp.zeros((32, D), F32)], 0)
        return level0 + dot(placer(offs, first_group + j), by_selection(rows).astype(BF))

    def attend(j, outs, factors):
        wide = slice(j * WIDE, (j + 1) * WIDE)
        attended = gather_levels(j, [out * factor for out, factor in zip(outs, factors)]).astype(BF)
        att_ref[:, wide] = attended
        product = g_ref[:, wide].astype(F32) * attended.astype(F32)
        delta = jnp.concatenate(
            [jnp.sum(product[:, h * D : (h + 1) * D], 1, keepdims=True) for h in range(HEADS)], 0
        )
        return for_levels(j, delta_ref, heads_to_lanes(delta))

    def backward(j, k, state, raised, factors, deltas):
        queries, grads, keys, values = state
        probs = raised[k].astype(F32) * factors[k]
        grad_weights = dot_nt(grads[k], values[k])
        grad_scores = (probs * (grad_weights - deltas[k])).astype(BF)
        grad_values = dot_tn(probs.astype(BF), grads[k])
        grad_keys = dot_tn(grad_scores, queries[k]) * SCALE
        pair = jnp.concatenate([grad_keys, grad_values], 1).astype(BF)
        if k == 0:
            d0_ref[j] = pair
        else:
            at = 128 * (k - 1)
            down_ref[j, at : at + 128] = pair[:128]
            dother_ref[j, at : at + 128] = pair[128:]
        return dot(grad_scores, keys[k]) * SCALE

    level_ref[...] = jnp.full(level_ref.shape, -1e30, F32)
    states = [load(j) for j in members]
    results = [forward(states[j]) for j in members]
    factors = [merge(j, results[j][2], results[j][1]) for j in members]
    deltas = [attend(j, results[j][3], factors[j]) for j in members]
    for j in members:
        dqs = [backward(j, k, states[j], results[j][0], factors[j], deltas[j]) for k in range(5)]
        dq_ref[:, j * WIDE : (j + 1) * WIDE] = gather_levels(j, dqs).astype(BF)


def middle_and_extra(total, z):
    zero = jnp.zeros((8, 2 * D), F32)
    middle = [
        total[128 + 32 * z : 160 + 32 * z],
        total[256 + 32 * z : 272 + 32 * z],
        total[384 + 32 * z : 392 + 32 * z],
        zero,
    ]
    return middle, [total[272 + 32 * z : 288 + 32 * z], total[392 + 32 * z : 416 + 32 * z], zero]


def reduce_kernel(mine, theirs, rows_kept, rows_far, up, down, x_far, x_kept):
    for g in range(GROUPS):
        total = mine[g].astype(F32) + theirs[g].astype(F32)
        for z, ref in enumerate((rows_kept, rows_far, up, down)):
            middle, extra = middle_and_extra(total, z)
            if z < 2:
                ref[g] = jnp.concatenate([total[64 * z : 64 * z + 64]] + middle, 0).astype(BF)
            else:
                ref[g] = jnp.concatenate(middle + extra, 0).astype(BF)
            if z == 0:
                x_kept[g] = jnp.concatenate(extra, 0)
            if z == 1:
                x_far[g] = jnp.concatenate(extra, 0).astype(BF)


def place_kernel(offs, d0, rows_far, _, far):
    for g in range(GROUPS):
        far[g] = (d0[g, 128:256].astype(F32) + dot(placer(offs, g), rows_far[g])).astype(BF)


def cross_kernel(kept, far, up, down, one, two, three):
    for g in range(GROUPS):
        total = kept[g] + far[g].astype(F32) + up[g, 64:112].astype(F32) + down[g, 64:112].astype(F32)
        zero = jnp.zeros((8, 2 * D), F32)
        one[g] = jnp.concatenate([total[0:24], zero], 0).astype(BF)
        two[g] = jnp.concatenate([total[24:32], zero], 0).astype(BF)
        three[g] = jnp.concatenate([total[32:40], zero], 0).astype(BF)


def finish_kernel(offs, d0, rows_kept, far, up, down, one, two, three, dk_ref, dv_ref):
    for g in range(GROUPS):
        kept = rows_kept[g].astype(F32)
        middle = up[g, 0:64].astype(F32) + down[g, 0:64].astype(F32) + kept[64:128]
        a, b, c = one[g].astype(F32), two[g].astype(F32), three[g].astype(F32)
        rows = jnp.concatenate(
            [
                kept[0:64],
                middle[0:32],
                middle[32:48] + a[0:16],
                middle[48:56] + a[16:24] + b[0:8] + c[0:8],
                jnp.zeros((8, 2 * D), F32),
            ],
            0,
        ).astype(BF)
        whole = d0[g, 0:128].astype(F32) + far[g].astype(F32) + dot(placer(offs, g), rows)
        dk_ref[:, g * D : (g + 1) * D] = whole[:, :D].astype(BF)
        dv_ref[:, g * D : (g + 1) * D] = whole[:, D:].astype(BF)


def whole_call(body, name, outs, offs, *arrays, after=()):
    specs = [pl.BlockSpec(memory_space=pltpu.VMEM)] * len(arrays)
    specs += [pl.BlockSpec(memory_space=pl.ANY)] * len(after)
    arrays = arrays + tuple(after)
    if offs is not None:
        specs = [pl.BlockSpec(memory_space=pltpu.SMEM)] + specs
        arrays = (offs,) + arrays
    shapes = [jax.ShapeDtypeStruct(shape, dtype) for shape, dtype in outs]
    return pl.pallas_call(
        body,
        name=name,
        out_shape=shapes,
        in_specs=specs,
        out_specs=[pl.BlockSpec(memory_space=pltpu.VMEM)] * len(shapes),
        cost_estimate=pl.CostEstimate(flops=0, bytes_accessed=4 * 10**6, transcendentals=0),
        compiler_params=pltpu.CompilerParams(vmem_limit_bytes=VMEM_LIMIT),
    )(*arrays)


def attention(offs, q, g, k, v, kp, vp, own, other):
    lanes = lambda width: pl.BlockSpec((TOKENS, TOGETHER * width), lambda i: (0, i))
    block = lambda rows: pl.BlockSpec((TOGETHER, rows, 2 * D), lambda i: (i, 0, 0))
    return pl.pallas_call(
        attention_kernel,
        name="attention",
        grid=(GROUPS // TOGETHER,),
        in_specs=[pl.BlockSpec(memory_space=pltpu.SMEM)]
        + [lanes(WIDE), lanes(WIDE), lanes(D), lanes(D), lanes(D), lanes(D), block(512), block(512)],
        out_specs=[lanes(WIDE), lanes(WIDE), block(256), block(512), block(512)],
        out_shape=[
            jax.ShapeDtypeStruct((TOKENS, GROUPS * WIDE), BF),
            jax.ShapeDtypeStruct((TOKENS, GROUPS * WIDE), BF),
            jax.ShapeDtypeStruct((GROUPS, 256, 2 * D), BF),
            jax.ShapeDtypeStruct((GROUPS, 512, 2 * D), BF),
            jax.ShapeDtypeStruct((GROUPS, 512, 2 * D), BF),
        ],
        scratch_shapes=[
            pltpu.VMEM((TOGETHER, 4, TOKENS, 128), F32),
            pltpu.VMEM((TOGETHER, TOKENS, 128), F32),
            pltpu.VMEM((TOGETHER, TOKENS, 128), F32),
        ],
        compiler_params=pltpu.CompilerParams(vmem_limit_bytes=62 * 1024 * 1024),
    )(offs, q, g, k, v, kp, vp, own, other)


def routes(count):
    def along_z(i, step):
        z = ((i & 1) * 2 + (i >> 2 & 1) + step) % 4
        return (i & ~5) | (z & 1) << 2 | z >> 1

    table = {
        "head": lambda i: i ^ 1,
        "core": lambda i: i ^ 2,
        "up": lambda i: along_z(i, 1),
        "down": lambda i: along_z(i, -1),
        "x1": lambda i: i ^ 8,
        "x2": lambda i: i ^ 16,
        "x3": lambda i: i ^ 24,
    }
    return {name: [(i, to(i)) for i in range(count)] for name, to in table.items()}


def shards(count, queries, key_rows, value_rows, gradient, level_offsets):
    route = routes(count)

    def send(x, name):
        return lax.ppermute(x, AXES, route[name])

    other_offsets = send(level_offsets, "head")
    low = lax.axis_index("head") == 0
    offs = jnp.where(
        low,
        jnp.concatenate([level_offsets, other_offsets], 1),
        jnp.concatenate([other_offsets, level_offsets], 1),
    )
    key_swap, value_swap, other_offsets = lax.optimization_barrier((key_rows, value_rows, other_offsets))
    far_keys = send(key_swap, "head")
    far_values = send(value_swap, "head")

    rows = lambda n, dtype=BF: ((GROUPS, n, 2 * D), dtype)
    first, middle, tail, last = whole_call(
        select_kernel, "select", [rows(64), rows(64), rows(32), rows(16)], offs, key_rows, value_rows
    )
    middle_down = send(middle, "up")
    middle_up = send(middle, "down")
    (extra,) = whole_call(
        compact_kernel, "compact", [rows(48)], None, send(tail, "x1"), send(last, "x2"), send(last, "x3")
    )
    extra_down = send(extra, "up")
    extra_up = send(extra, "down")
    extra_far = send(extra, "head")
    (own,) = whole_call(
        assemble_kernel, "assemble", [rows(512)], offs, first, middle, extra, far_keys, far_values,
        extra_far, middle_up, extra_up, middle_down, extra_down,
    )
    other = send(own, "core")
    attended, grad_queries, d0, down_own, down_other = attention(
        offs, queries, gradient, key_rows, value_rows, far_keys, far_values, own, other
    )
    theirs = send(down_other, "core")
    rows_kept, rows_far, up, down, x_far, x_kept = whole_call(
        reduce_kernel, "reduce", [rows(128), rows(128), rows(112), rows(112), rows(48), rows(48, F32)],
        None, down_own, theirs,
    )
    from_down = send(up, "up")
    from_up = send(down, "down")
    x_far = send(x_far, "head")
    (far,) = whole_call(place_kernel, "place", [rows(128)], offs, d0, rows_far, after=(x_far,))
    far = send(far, "head")
    one, two, three = whole_call(
        cross_kernel, "cross", [rows(32), rows(16), rows(16)], None, x_kept, x_far, from_up, from_down
    )
    one, two, three = send(one, "x1"), send(two, "x2"), send(three, "x3")
    out = ((TOKENS, GROUPS * D), BF)
    grad_keys, grad_values = whole_call(
        finish_kernel, "finish", [out, out], offs, d0, rows_kept, far, from_up, from_down, one, two, three
    )
    return (attended, grad_queries, grad_keys, grad_values)


def solution(mesh):
    rows = P(AXES, None)
    return jax.shard_map(
        functools.partial(shards, mesh.size),
        mesh=mesh,
        in_specs=(rows, rows, rows, rows, P(None, "head")),
        out_specs=(rows, rows, rows, rows),
        check_vma=False,
    )
```

time: 145 us -> 111 us (0.77)
  waiting for transfers between devices: 57.5 us -> 37.3 us
  Pallas kernels: 47.9 us -> 33.1 us
    ppermute x20, waiting for transfers between devices: 57.5 us -> 37.3 us  [send(): return lax.ppermute(x, AXES, route[name])]
    pallas_call x6 -> x7, Pallas kernels: 16.6 us -> 5.01 us  [whole_call(): pl.pallas_call(body, name=name, out_shape=shapes, in_specs=specs, out_spe...]
    pallas_call x1, Pallas kernels: 31.3 us -> 28.1 us  [attention(): pl.pallas_call(attention_kernel, name='attention', grid=(GROUPS // TOGETH...]
    unnamed x39 -> x19, local copies, waits for them, and re-layouts: 6.39 us -> 5.63 us
  transfers between devices with their start and end apart: 20 -> 20, of which waited for: 11 -> 12; matrix products, arithmetic and copies ran while one was open for 1% -> 0% of each run, Pallas kernels for 4% -> 2%
where the time goes in v1:
time: 111 us; the launch traced here: 110 us
  waiting for transfers between devices  37.3 us (34%)
  Pallas kernels  33.1 us (30%)
  starting transfers between devices  32.8 us (30%)
  local copies, waits for them, and re-layouts  5.63 us (5%)
    ppermute x20, waiting for transfers between devices, send(): return lax.ppermute(x, AXES, route[name])  37.3 us
    ppermute x20, starting transfers between devices, send(): return lax.ppermute(x, AXES, route[name])  32.8 us
    pallas_call x1, Pallas kernels, attention(): pl.pallas_call(attention_kernel, name='attention', grid=(GROUPS // TOGETH...  28.1 us
    unnamed x19, local copies, waits for them, and re-layouts  5.63 us
    pallas_call x7, Pallas kernels, whole_call(): pl.pallas_call(body, name=name, out_shape=shapes, in_specs=specs, out_spe...  5.01 us
  transfers between devices with their start and end apart: 20, of which 12 were waited for; matrix products, arithmetic and copies ran while one was open for 0% of the time, Pallas kernels for 2%

profile of v1, /device:TPU:0, one launch (start us, length us, event | category | flops | bytes accessed | tf_op | source)
XLA Modules:
  0.0 109.7 jit_solution(2954066408046553395)
XLA Ops:
  0.6 0.8 copy.10
  1.4 4.0 %collective-permute-start = (s32[5,4]{1,0:T(8,128)S(1)}, s32[5,4]{1,0:T(8,128)S(1)}, u32[]{:S(2)}, u32[]{:S(2)}) collective-permute-start(s32[5,4]{1,0:T(8,128)S(1)} %copy.10), channel_id=1, source_target_pairs={{0,1},{1,0},{2,3},{3,2},{4,5},{5,4},{6,7},{7,6},{8,9},{9,8},{10,11... | collective-permute-start | bytes 248 | tf_op jit(solution)/shard_map/ppermute | solution.py:364
  5.4 1.6 %collective-permute-done = s32[5,4]{1,0:T(8,128)S(1)} collective-permute-done((s32[5,4]{1,0:T(8,128)S(1)}, s32[5,4]{1,0:T(8,128)S(1)}, u32[]{:S(2)}, u32[]{:S(2)}) %collective-permute-start) | collective-permute-done | bytes 112 | tf_op jit(solution)/shard_map/ppermute | solution.py:364
  6.9 3.5 %collective-permute-start.1 = (bf16[128,1024]{1,0:T(8,128)(2,1)}, bf16[128,1024]{1,0:T(8,128)(2,1)S(1)}, u32[]{:S(2)}, u32[]{:S(2)}) collective-permute-start(bf16[128,1024]{1,0:T(8,128)(2,1)} %k_ref.1), channel_id=1, source_target_pairs={{0,1},{1,0},{2,3},{3,2},{4,5},{5,4},{6,7},{7,6},{8,9},{9,8},{10,11... | collective-permute-start | bytes 786440 | tf_op jit(solution)/shard_map/ppermute | solution.py:364
  10.5 0.0 collective-permute-start.2
  10.5 0.1 add_select_fusion.offs
  10.6 0.9 copy-done.5
  11.5 0.9 copy-done.6
  12.5 0.9 select.1
  13.4 2.8 %collective-permute-start.5 = (bf16[8,16,256]{2,1,0:T(8,128)(2,1)S(1)}, bf16[8,16,256]{2,1,0:T(8,128)(2,1)S(1)}, u32[]{:S(2)}, u32[]{:S(2)}) collective-permute-start(bf16[8,16,256]{2,1,0:T(8,128)(2,1)S(1)} %get-tuple-element.31), channel_id=1, source_target_pairs={{0,24},{1,25},{2,26},{3,27},{4,28},{5,29},{6,30},{7,31},{8,16},{9,... | collective-permute-start | bytes 196616 | tf_op jit(solution)/shard_map/ppermute | solution.py:364
  16.2 0.2 collective-permute-start.3
  16.4 1.7 %collective-permute-start.4 = (bf16[8,16,256]{2,1,0:T(8,128)(2,1)S(1)}, bf16[8,16,256]{2,1,0:T(8,128)(2,1)S(1)}, u32[]{:S(2)}, u32[]{:S(2)}) collective-permute-start(bf16[8,16,256]{2,1,0:T(8,128)(2,1)S(1)} %get-tuple-element.31), channel_id=1, source_target_pairs={{0,16},{1,17},{2,18},{3,19},{4,20},{5,21},{6,22},{7,23},{8,24},{9,... | collective-permute-start | bytes 196616 | tf_op jit(solution)/shard_map/ppermute | solution.py:364
  18.2 1.5 %collective-permute-done.5.three = bf16[8,16,256]{2,1,0:T(8,128)(2,1)S(1)} collective-permute-done((bf16[8,16,256]{2,1,0:T(8,128)(2,1)S(1)}, bf16[8,16,256]{2,1,0:T(8,128)(2,1)S(1)}, u32[]{:S(2)}, u32[]{:S(2)}) %collective-permute-start.5) | collective-permute-done | bytes 65568 | tf_op jit(solution)/shard_map/ppermute | solution.py:364
  19.6 1.5 %collective-permute-start.9 = (bf16[8,64,256]{2,1,0:T(8,128)(2,1)S(1)}, bf16[8,64,256]{2,1,0:T(8,128)(2,1)S(1)}, u32[]{:S(2)}, u32[]{:S(2)}) collective-permute-start(bf16[8,64,256]{2,1,0:T(8,128)(2,1)S(1)} %get-tuple-element.29.mid_own), channel_id=1, source_target_pairs={{0,4},{1,5},{2,6},{3,7},{4,1},{5,0},{6,3},{7,2},{8,12},{9,13},{10,... | collective-permute-start | bytes 786440 | tf_op jit(solution)/shard_map/ppermute | solution.py:364
  21.1 1.1 %collective-permute-done.4.two = bf16[8,16,256]{2,1,0:T(8,128)(2,1)S(1)} collective-permute-done((bf16[8,16,256]{2,1,0:T(8,128)(2,1)S(1)}, bf16[8,16,256]{2,1,0:T(8,128)(2,1)S(1)}, u32[]{:S(2)}, u32[]{:S(2)}) %collective-permute-start.4) | collective-permute-done | bytes 65568 | tf_op jit(solution)/shard_map/ppermute | solution.py:364
  22.2 3.7 %collective-permute-start.7 = (bf16[8,64,256]{2,1,0:T(8,128)(2,1)S(1)}, bf16[8,64,256]{2,1,0:T(8,128)(2,1)S(1)}, u32[]{:S(2)}, u32[]{:S(2)}) collective-permute-start(bf16[8,64,256]{2,1,0:T(8,128)(2,1)S(1)} %get-tuple-element.29.mid_own), channel_id=1, source_target_pairs={{0,5},{1,4},{2,7},{3,6},{4,0},{5,1},{6,2},{7,3},{8,13},{9,12},{10,... | collective-permute-start | bytes 786440 | tf_op jit(solution)/shard_map/ppermute | solution.py:364
  25.9 0.0 collective-permute-done.3.one
  25.9 0.1 collective-permute-start.10
  26.0 0.0 collective-permute-done.1.keys.kp_ref
  26.0 0.0 copy-start.3
  26.0 3.2 %collective-permute-start.8 = (bf16[8,48,256]{2,1,0:T(8,128)(2,1)S(1)}, bf16[8,48,256]{2,1,0:T(8,128)(2,1)S(1)}, u32[]{:S(2)}, u32[]{:S(2)}) collective-permute-start(bf16[8,48,256]{2,1,0:T(8,128)(2,1)S(1)} %compact.1.x_own), channel_id=1, source_target_pairs={{0,5},{1,4},{2,7},{3,6},{4,0},{5,1},{6,2},{7,3},{8,13},{9,12},{10,... | collective-permute-start | bytes 589832 | tf_op jit(solution)/shard_map/ppermute | solution.py:364
  29.2 0.0 collective-permute-start.6
  29.2 0.0 collective-permute-done.9.mid_down
  29.2 3.4 %collective-permute-done.7.mid_up = bf16[8,64,256]{2,1,0:T(8,128)(2,1)S(1)} collective-permute-done((bf16[8,64,256]{2,1,0:T(8,128)(2,1)S(1)}, bf16[8,64,256]{2,1,0:T(8,128)(2,1)S(1)}, u32[]{:S(2)}, u32[]{:S(2)}) %collective-permute-start.7) | collective-permute-done | bytes 262176 | tf_op jit(solution)/shard_map/ppermute | solution.py:364
  32.6 1.6 %collective-permute-done.10.x_down = bf16[8,48,256]{2,1,0:T(8,128)(2,1)S(1)} collective-permute-done((bf16[8,48,256]{2,1,0:T(8,128)(2,1)S(1)}, bf16[8,48,256]{2,1,0:T(8,128)(2,1)S(1)}, u32[]{:S(2)}, u32[]{:S(2)}) %collective-permute-start.10) | collective-permute-done | bytes 196640 | tf_op jit(solution)/shard_map/ppermute | solution.py:364
  34.2 2.6 %collective-permute-done.8.x_up = bf16[8,48,256]{2,1,0:T(8,128)(2,1)S(1)} collective-permute-done((bf16[8,48,256]{2,1,0:T(8,128)(2,1)S(1)}, bf16[8,48,256]{2,1,0:T(8,128)(2,1)S(1)}, u32[]{:S(2)}, u32[]{:S(2)}) %collective-permute-start.8) | collective-permute-done | bytes 196640 | tf_op jit(solution)/shard_map/ppermute | solution.py:364
  36.8 0.9 assemble.1.own_ref
  37.8 1.3 %copy-done = bf16[8,512,256]{2,1,0:T(8,128)(2,1)} copy-done((bf16[8,512,256]{2,1,0:T(8,128)(2,1)}, bf16[8,512,256]{2,1,0:T(8,128)(2,1)S(1)}, u32[]{:S(2)}) %copy-start) | copy-done | bytes 2097176
  39.1 4.3 %collective-permute-done.11.other_ref = bf16[8,512,256]{2,1,0:T(8,128)(2,1)} collective-permute-done((bf16[8,512,256]{2,1,0:T(8,128)(2,1)S(1)}, bf16[8,512,256]{2,1,0:T(8,128)(2,1)}, u32[]{:S(2)}, u32[]{:S(2)}) %collective-permute-start.11) | collective-permute-done | bytes 2097184 | tf_op jit(solution)/shard_map/ppermute | solution.py:364
  43.4 28.1 %attention.1 = (bf16[128,4096]{1,0:T(8,128)(2,1)}, bf16[128,4096]{1,0:T(8,128)(2,1)}, bf16[8,256,256]{2,1,0:T(8,128)(2,1)}, bf16[8,512,256]{2,1,0:T(8,128)(2,1)}, bf16[8,512,256]{2,1,0:T(8,128)(2,1)}) custom-call(s32[5,8]{1,0:T(8,128)} %copy-done.7, bf16[128,4096]{1,0:T(8,128)(2,1)} %q_ref.1, bf16[128,4096]{1,0:T(8,128)(2,1)} %g_ref.1, ...), custom_call_target="tpu_custom_call" | custom-call | tf_op jit(solution)/shard_map/attention/pallas_call | solution.py:320
  71.5 0.2 collective-permute-start.12
  71.8 4.2 %collective-permute-done.12.theirs = bf16[8,512,256]{2,1,0:T(8,128)(2,1)S(1)} collective-permute-done((bf16[8,512,256]{2,1,0:T(8,128)(2,1)}, bf16[8,512,256]{2,1,0:T(8,128)(2,1)S(1)}, u32[]{:S(2)}, u32[]{:S(2)}) %collective-permute-start.12) | collective-permute-done | bytes 2097184 | tf_op jit(solution)/shard_map/ppermute | solution.py:364
  76.0 1.6 %copy-done.2 = bf16[8,512,256]{2,1,0:T(8,128)(2,1)S(1)} copy-done((bf16[8,512,256]{2,1,0:T(8,128)(2,1)S(1)}, bf16[8,512,256]{2,1,0:T(8,128)(2,1)}, u32[]{:S(2)}) %copy-start.2) | copy-done | bytes 2097176
  77.6 0.5 reduce.1
  78.1 2.0 %collective-permute-start.13 = (bf16[8,48,256]{2,1,0:T(8,128)(2,1)S(1)}, bf16[8,48,256]{2,1,0:T(8,128)(2,1)S(1)}, u32[]{:S(2)}, u32[]{:S(2)}) collective-permute-start(bf16[8,48,256]{2,1,0:T(8,128)(2,1)S(1)} %get-tuple-element.39), channel_id=1, source_target_pairs={{0,1},{1,0},{2,3},{3,2},{4,5},{5,4},{6,7},{7,6},{8,9},{9,8},{10,11... | collective-permute-start | bytes 589832 | tf_op jit(solution)/shard_map/ppermute | solution.py:364
  80.1 2.3 %collective-permute-start.15 = (bf16[8,112,256]{2,1,0:T(8,128)(2,1)S(1)}, bf16[8,112,256]{2,1,0:T(8,128)(2,1)S(1)}, u32[]{:S(2)}, u32[]{:S(2)}) collective-permute-start(bf16[8,112,256]{2,1,0:T(8,128)(2,1)S(1)} %get-tuple-element.40), channel_id=1, source_target_pairs={{0,5},{1,4},{2,7},{3,6},{4,0},{5,1},{6,2},{7,3},{8,13},{9,12},{10,... | collective-permute-start | bytes 1376264 | tf_op jit(solution)/shard_map/ppermute | solution.py:364
  82.4 0.3 collective-permute-start.16
  82.7 4.7 %collective-permute-done.13._.far = bf16[8,48,256]{2,1,0:T(8,128)(2,1)S(1)} collective-permute-done((bf16[8,48,256]{2,1,0:T(8,128)(2,1)S(1)}, bf16[8,48,256]{2,1,0:T(8,128)(2,1)S(1)}, u32[]{:S(2)}, u32[]{:S(2)}) %collective-permute-start.13) | collective-permute-done | bytes 196640 | tf_op jit(solution)/shard_map/ppermute | solution.py:364
  87.4 0.9 place.1
  88.3 2.0 %collective-permute-start.14 = (bf16[8,128,256]{2,1,0:T(8,128)(2,1)S(1)}, bf16[8,128,256]{2,1,0:T(8,128)(2,1)S(1)}, u32[]{:S(2)}, u32[]{:S(2)}) collective-permute-start(bf16[8,128,256]{2,1,0:T(8,128)(2,1)S(1)} %place.1), channel_id=1, source_target_pairs={{0,1},{1,0},{2,3},{3,2},{4,5},{5,4},{6,7},{7,6},{8,9},{9,8},{10,11... | collective-permute-start | bytes 1572872 | tf_op jit(solution)/shard_map/ppermute | solution.py:364
  90.3 8.0 %collective-permute-done.15.up = bf16[8,112,256]{2,1,0:T(8,128)(2,1)S(1)} collective-permute-done((bf16[8,112,256]{2,1,0:T(8,128)(2,1)S(1)}, bf16[8,112,256]{2,1,0:T(8,128)(2,1)S(1)}, u32[]{:S(2)}, u32[]{:S(2)}) %collective-permute-start.15) | collective-permute-done | bytes 458784 | tf_op jit(solution)/shard_map/ppermute | solution.py:364
  98.3 0.1 cross.1
  98.4 2.5 %collective-permute-start.17 = (bf16[8,32,256]{2,1,0:T(8,128)(2,1)S(1)}, bf16[8,32,256]{2,1,0:T(8,128)(2,1)S(1)}, u32[]{:S(2)}, u32[]{:S(2)}) collective-permute-start(bf16[8,32,256]{2,1,0:T(8,128)(2,1)S(1)} %get-tuple-element.43), channel_id=1, source_target_pairs={{0,8},{1,9},{2,10},{3,11},{4,12},{5,13},{6,14},{7,15},{8,0},{9,1},... | collective-permute-start | bytes 393224 | tf_op jit(solution)/shard_map/ppermute | solution.py:364
  100.8 1.7 %collective-permute-start.18 = (bf16[8,16,256]{2,1,0:T(8,128)(2,1)S(1)}, bf16[8,16,256]{2,1,0:T(8,128)(2,1)S(1)}, u32[]{:S(2)}, u32[]{:S(2)}) collective-permute-start(bf16[8,16,256]{2,1,0:T(8,128)(2,1)S(1)} %get-tuple-element.44), channel_id=1, source_target_pairs={{0,16},{1,17},{2,18},{3,19},{4,20},{5,21},{6,22},{7,23},{8,24},{9,... | collective-permute-start | bytes 196616 | tf_op jit(solution)/shard_map/ppermute | solution.py:364
  102.5 1.1 %collective-permute-start.19 = (bf16[8,16,256]{2,1,0:T(8,128)(2,1)S(1)}, bf16[8,16,256]{2,1,0:T(8,128)(2,1)S(1)}, u32[]{:S(2)}, u32[]{:S(2)}) collective-permute-start(bf16[8,16,256]{2,1,0:T(8,128)(2,1)S(1)} %get-tuple-element.45), channel_id=1, source_target_pairs={{0,24},{1,25},{2,26},{3,27},{4,28},{5,29},{6,30},{7,31},{8,16},{9,... | collective-permute-start | bytes 196616 | tf_op jit(solution)/shard_map/ppermute | solution.py:364
  103.6 3.0 %collective-permute-done.18.two = bf16[8,16,256]{2,1,0:T(8,128)(2,1)S(1)} collective-permute-done((bf16[8,16,256]{2,1,0:T(8,128)(2,1)S(1)}, bf16[8,16,256]{2,1,0:T(8,128)(2,1)S(1)}, u32[]{:S(2)}, u32[]{:S(2)}) %collective-permute-start.18) | collective-permute-done | bytes 65568 | tf_op jit(solution)/shard_map/ppermute | solution.py:364
  106.6 1.4 %collective-permute-done.19.three = bf16[8,16,256]{2,1,0:T(8,128)(2,1)S(1)} collective-permute-done((bf16[8,16,256]{2,1,0:T(8,128)(2,1)S(1)}, bf16[8,16,256]{2,1,0:T(8,128)(2,1)S(1)}, u32[]{:S(2)}, u32[]{:S(2)}) %collective-permute-start.19) | collective-permute-done | bytes 65568 | tf_op jit(solution)/shard_map/ppermute | solution.py:364
  108.0 1.7 %finish.1 = (bf16[128,1024]{1,0:T(8,128)(2,1)}, bf16[128,1024]{1,0:T(8,128)(2,1)}) custom-call(s32[5,8]{1,0:T(8,128)S(1)} %copy-done.8, bf16[8,256,256]{2,1,0:T(8,128)(2,1)S(1)} %copy-done.1, bf16[8,128,256]{2,1,0:T(8,128)(2,1)S(1)} %get-tuple-element.37.rows_kept, bf16[8,128,256]{2,1,0:T(8,128)(2,1)S(1)} %collective-permute-done.14.far, ...), custom_call_target="tpu_custom_call" | custom-call | bytes 4000000 | tf_op jit(solution)/shard_map/finish/pallas_call | solution.py:306
  (20 shorter events, 0.1 us)
Async XLA Ops:
  1.4 5.5 %collective-permute-start = (s32[5,4]{1,0:T(8,128)S(1)}, s32[5,4]{1,0:T(8,128)S(1)}, u32[]{:S(2)}, u32[]{:S(2)}) collective-permute-start(s32[5,4]{1,0:T(8,128)S(1)} %copy.10), channel_id=1, source_target_pairs={{0,1},{1,0},{2,3},{3,2},{4,5},{5,4},{6,7},{7,6},{8,9},{9,8},{10,11... | collective-permute-start | bytes 248 | tf_op jit(solution)/shard_map/ppermute | solution.py:364
  6.9 19.0 %collective-permute-start.1 = (bf16[128,1024]{1,0:T(8,128)(2,1)}, bf16[128,1024]{1,0:T(8,128)(2,1)S(1)}, u32[]{:S(2)}, u32[]{:S(2)}) collective-permute-start(bf16[128,1024]{1,0:T(8,128)(2,1)} %k_ref.1), channel_id=1, source_target_pairs={{0,1},{1,0},{2,3},{3,2},{4,5},{5,4},{6,7},{7,6},{8,9},{9,8},{10,11... | collective-permute-start | bytes 786440 | tf_op jit(solution)/shard_map/ppermute | solution.py:364
  10.5 18.7 %collective-permute-start.2 = (bf16[128,1024]{1,0:T(8,128)(2,1)}, bf16[128,1024]{1,0:T(8,128)(2,1)S(1)}, u32[]{:S(2)}, u32[]{:S(2)}) collective-permute-start(bf16[128,1024]{1,0:T(8,128)(2,1)} %v_ref.1), channel_id=1, source_target_pairs={{0,1},{1,0},{2,3},{3,2},{4,5},{5,4},{6,7},{7,6},{8,9},{9,8},{10,11... | collective-permute-start | bytes 786440 | tf_op jit(solution)/shard_map/ppermute | solution.py:364
  10.6 1.0 copy-start.5
  11.5 0.9 copy-start.6
  12.5 25.3 %copy-start.7 = (s32[5,8]{1,0:T(8,128)}, s32[5,8]{1,0:T(8,128)S(1)}, u32[]{:S(2)}) copy-start(s32[5,8]{1,0:T(8,128)S(1)} %add_select_fusion.offs) | copy-start | bytes 484
  13.4 6.3 %collective-permute-start.5 = (bf16[8,16,256]{2,1,0:T(8,128)(2,1)S(1)}, bf16[8,16,256]{2,1,0:T(8,128)(2,1)S(1)}, u32[]{:S(2)}, u32[]{:S(2)}) collective-permute-start(bf16[8,16,256]{2,1,0:T(8,128)(2,1)S(1)} %get-tuple-element.31), channel_id=1, source_target_pairs={{0,24},{1,25},{2,26},{3,27},{4,28},{5,29},{6,30},{7,31},{8,16},{9,... | collective-permute-start | bytes 196616 | tf_op jit(solution)/shard_map/ppermute | solution.py:364
  16.2 9.7 %collective-permute-start.3 = (bf16[8,32,256]{2,1,0:T(8,128)(2,1)S(1)}, bf16[8,32,256]{2,1,0:T(8,128)(2,1)S(1)}, u32[]{:S(2)}, u32[]{:S(2)}) collective-permute-start(bf16[8,32,256]{2,1,0:T(8,128)(2,1)S(1)} %get-tuple-element.30), channel_id=1, source_target_pairs={{0,8},{1,9},{2,10},{3,11},{4,12},{5,13},{6,14},{7,15},{8,0},{9,1},... | collective-permute-start | bytes 393224 | tf_op jit(solution)/shard_map/ppermute | solution.py:364
  16.4 5.8 %collective-permute-start.4 = (bf16[8,16,256]{2,1,0:T(8,128)(2,1)S(1)}, bf16[8,16,256]{2,1,0:T(8,128)(2,1)S(1)}, u32[]{:S(2)}, u32[]{:S(2)}) collective-permute-start(bf16[8,16,256]{2,1,0:T(8,128)(2,1)S(1)} %get-tuple-element.31), channel_id=1, source_target_pairs={{0,16},{1,17},{2,18},{3,19},{4,20},{5,21},{6,22},{7,23},{8,24},{9,... | collective-permute-start | bytes 196616 | tf_op jit(solution)/shard_map/ppermute | solution.py:364
  19.6 9.6 %collective-permute-start.9 = (bf16[8,64,256]{2,1,0:T(8,128)(2,1)S(1)}, bf16[8,64,256]{2,1,0:T(8,128)(2,1)S(1)}, u32[]{:S(2)}, u32[]{:S(2)}) collective-permute-start(bf16[8,64,256]{2,1,0:T(8,128)(2,1)S(1)} %get-tuple-element.29.mid_own), channel_id=1, source_target_pairs={{0,4},{1,5},{2,6},{3,7},{4,1},{5,0},{6,3},{7,2},{8,12},{9,13},{10,... | collective-permute-start | bytes 786440 | tf_op jit(solution)/shard_map/ppermute | solution.py:364
  22.2 10.4 %collective-permute-start.7 = (bf16[8,64,256]{2,1,0:T(8,128)(2,1)S(1)}, bf16[8,64,256]{2,1,0:T(8,128)(2,1)S(1)}, u32[]{:S(2)}, u32[]{:S(2)}) collective-permute-start(bf16[8,64,256]{2,1,0:T(8,128)(2,1)S(1)} %get-tuple-element.29.mid_own), channel_id=1, source_target_pairs={{0,5},{1,4},{2,7},{3,6},{4,0},{5,1},{6,2},{7,3},{8,13},{9,12},{10,... | collective-permute-start | bytes 786440 | tf_op jit(solution)/shard_map/ppermute | solution.py:364
  25.9 8.3 %collective-permute-start.10 = (bf16[8,48,256]{2,1,0:T(8,128)(2,1)S(1)}, bf16[8,48,256]{2,1,0:T(8,128)(2,1)S(1)}, u32[]{:S(2)}, u32[]{:S(2)}) collective-permute-start(bf16[8,48,256]{2,1,0:T(8,128)(2,1)S(1)} %compact.1.x_own), channel_id=1, source_target_pairs={{0,4},{1,5},{2,6},{3,7},{4,1},{5,0},{6,3},{7,2},{8,12},{9,13},{10,... | collective-permute-start | bytes 589832 | tf_op jit(solution)/shard_map/ppermute | solution.py:364
  26.0 11.8 %copy-start.3 = (bf16[128,1024]{1,0:T(8,128)(2,1)}, bf16[128,1024]{1,0:T(8,128)(2,1)S(1)}, u32[]{:S(2)}) copy-start(bf16[128,1024]{1,0:T(8,128)(2,1)S(1)} %collective-permute-done.1.keys.kp_ref) | copy-start | bytes 786436
  26.0 10.8 %collective-permute-start.8 = (bf16[8,48,256]{2,1,0:T(8,128)(2,1)S(1)}, bf16[8,48,256]{2,1,0:T(8,128)(2,1)S(1)}, u32[]{:S(2)}, u32[]{:S(2)}) collective-permute-start(bf16[8,48,256]{2,1,0:T(8,128)(2,1)S(1)} %compact.1.x_own), channel_id=1, source_target_pairs={{0,5},{1,4},{2,7},{3,6},{4,0},{5,1},{6,2},{7,3},{8,13},{9,12},{10,... | collective-permute-start | bytes 589832 | tf_op jit(solution)/shard_map/ppermute | solution.py:364
  29.2 8.6 %copy-start.4 = (bf16[128,1024]{1,0:T(8,128)(2,1)}, bf16[128,1024]{1,0:T(8,128)(2,1)S(1)}, u32[]{:S(2)}) copy-start(bf16[128,1024]{1,0:T(8,128)(2,1)S(1)} %collective-permute-done.2.values.vp_ref) | copy-start | bytes 786436
  29.2 7.6 %collective-permute-start.6 = (bf16[8,48,256]{2,1,0:T(8,128)(2,1)S(1)}, bf16[8,48,256]{2,1,0:T(8,128)(2,1)S(1)}, u32[]{:S(2)}, u32[]{:S(2)}) collective-permute-start(bf16[8,48,256]{2,1,0:T(8,128)(2,1)S(1)} %compact.1.x_own), channel_id=1, source_target_pairs={{0,1},{1,0},{2,3},{3,2},{4,5},{5,4},{6,7},{7,6},{8,9},{9,8},{10,11... | collective-permute-start | bytes 589832 | tf_op jit(solution)/shard_map/ppermute | solution.py:364
  37.8 1.4 %copy-start = (bf16[8,512,256]{2,1,0:T(8,128)(2,1)}, bf16[8,512,256]{2,1,0:T(8,128)(2,1)S(1)}, u32[]{:S(2)}) copy-start(bf16[8,512,256]{2,1,0:T(8,128)(2,1)S(1)} %assemble.1.own_ref) | copy-start | bytes 6291460
  39.1 4.3 %collective-permute-start.11 = (bf16[8,512,256]{2,1,0:T(8,128)(2,1)S(1)}, bf16[8,512,256]{2,1,0:T(8,128)(2,1)}, u32[]{:S(2)}, u32[]{:S(2)}) collective-permute-start(bf16[8,512,256]{2,1,0:T(8,128)(2,1)S(1)} %assemble.1.own_ref), channel_id=1, source_target_pairs={{0,2},{1,3},{2,0},{3,1},{4,6},{5,7},{6,4},{7,5},{8,10},{9,11},{10,... | collective-permute-start | bytes 6291464 | tf_op jit(solution)/shard_map/ppermute | solution.py:364
  71.5 4.5 %collective-permute-start.12 = (bf16[8,512,256]{2,1,0:T(8,128)(2,1)}, bf16[8,512,256]{2,1,0:T(8,128)(2,1)S(1)}, u32[]{:S(2)}, u32[]{:S(2)}) collective-permute-start(bf16[8,512,256]{2,1,0:T(8,128)(2,1)} %get-tuple-element.36), channel_id=1, source_target_pairs={{0,2},{1,3},{2,0},{3,1},{4,6},{5,7},{6,4},{7,5},{8,10},{9,11},{10,... | collective-permute-start | bytes 6291464 | tf_op jit(solution)/shard_map/ppermute | solution.py:364
  76.0 1.6 %copy-start.2 = (bf16[8,512,256]{2,1,0:T(8,128)(2,1)S(1)}, bf16[8,512,256]{2,1,0:T(8,128)(2,1)}, u32[]{:S(2)}) copy-start(bf16[8,512,256]{2,1,0:T(8,128)(2,1)} %get-tuple-element.35.mine) | copy-start | bytes 6291460
  77.6 9.8 %copy-start.1 = (bf16[8,256,256]{2,1,0:T(8,128)(2,1)S(1)}, bf16[8,256,256]{2,1,0:T(8,128)(2,1)}, u32[]{:S(2)}) copy-start(bf16[8,256,256]{2,1,0:T(8,128)(2,1)} %get-tuple-element.34.d0) | copy-start | bytes 3145732
  77.6 9.8 %copy-start.8 = (s32[5,8]{1,0:T(8,128)S(1)}, s32[5,8]{1,0:T(8,128)}, u32[]{:S(2)}) copy-start(s32[5,8]{1,0:T(8,128)} %copy-done.7) | copy-start | bytes 484
  78.1 9.3 %collective-permute-start.13 = (bf16[8,48,256]{2,1,0:T(8,128)(2,1)S(1)}, bf16[8,48,256]{2,1,0:T(8,128)(2,1)S(1)}, u32[]{:S(2)}, u32[]{:S(2)}) collective-permute-start(bf16[8,48,256]{2,1,0:T(8,128)(2,1)S(1)} %get-tuple-element.39), channel_id=1, source_target_pairs={{0,1},{1,0},{2,3},{3,2},{4,5},{5,4},{6,7},{7,6},{8,9},{9,8},{10,11... | collective-permute-start | bytes 589832 | tf_op jit(solution)/shard_map/ppermute | solution.py:364
  80.1 18.2 %collective-permute-start.15 = (bf16[8,112,256]{2,1,0:T(8,128)(2,1)S(1)}, bf16[8,112,256]{2,1,0:T(8,128)(2,1)S(1)}, u32[]{:S(2)}, u32[]{:S(2)}) collective-permute-start(bf16[8,112,256]{2,1,0:T(8,128)(2,1)S(1)} %get-tuple-element.40), channel_id=1, source_target_pairs={{0,5},{1,4},{2,7},{3,6},{4,0},{5,1},{6,2},{7,3},{8,13},{9,12},{10,... | collective-permute-start | bytes 1376264 | tf_op jit(solution)/shard_map/ppermute | solution.py:364
  82.4 15.9 %collective-permute-start.16 = (bf16[8,112,256]{2,1,0:T(8,128)(2,1)S(1)}, bf16[8,112,256]{2,1,0:T(8,128)(2,1)S(1)}, u32[]{:S(2)}, u32[]{:S(2)}) collective-permute-start(bf16[8,112,256]{2,1,0:T(8,128)(2,1)S(1)} %get-tuple-element.41), channel_id=1, source_target_pairs={{0,4},{1,5},{2,6},{3,7},{4,1},{5,0},{6,3},{7,2},{8,12},{9,13},{10,... | collective-permute-start | bytes 1376264 | tf_op jit(solution)/shard_map/ppermute | solution.py:364
  88.3 19.7 %collective-permute-start.14 = (bf16[8,128,256]{2,1,0:T(8,128)(2,1)S(1)}, bf16[8,128,256]{2,1,0:T(8,128)(2,1)S(1)}, u32[]{:S(2)}, u32[]{:S(2)}) collective-permute-start(bf16[8,128,256]{2,1,0:T(8,128)(2,1)S(1)} %place.1), channel_id=1, source_target_pairs={{0,1},{1,0},{2,3},{3,2},{4,5},{5,4},{6,7},{7,6},{8,9},{9,8},{10,11... | collective-permute-start | bytes 1572872 | tf_op jit(solution)/shard_map/ppermute | solution.py:364
  98.4 9.6 %collective-permute-start.17 = (bf16[8,32,256]{2,1,0:T(8,128)(2,1)S(1)}, bf16[8,32,256]{2,1,0:T(8,128)(2,1)S(1)}, u32[]{:S(2)}, u32[]{:S(2)}) collective-permute-start(bf16[8,32,256]{2,1,0:T(8,128)(2,1)S(1)} %get-tuple-element.43), channel_id=1, source_target_pairs={{0,8},{1,9},{2,10},{3,11},{4,12},{5,13},{6,14},{7,15},{8,0},{9,1},... | collective-permute-start | bytes 393224 | tf_op jit(solution)/shard_map/ppermute | solution.py:364
  100.8 5.8 %collective-permute-start.18 = (bf16[8,16,256]{2,1,0:T(8,128)(2,1)S(1)}, bf16[8,16,256]{2,1,0:T(8,128)(2,1)S(1)}, u32[]{:S(2)}, u32[]{:S(2)}) collective-permute-start(bf16[8,16,256]{2,1,0:T(8,128)(2,1)S(1)} %get-tuple-element.44), channel_id=1, source_target_pairs={{0,16},{1,17},{2,18},{3,19},{4,20},{5,21},{6,22},{7,23},{8,24},{9,... | collective-permute-start | bytes 196616 | tf_op jit(solution)/shard_map/ppermute | solution.py:364
  102.5 5.5 %collective-permute-start.19 = (bf16[8,16,256]{2,1,0:T(8,128)(2,1)S(1)}, bf16[8,16,256]{2,1,0:T(8,128)(2,1)S(1)}, u32[]{:S(2)}, u32[]{:S(2)}) collective-permute-start(bf16[8,16,256]{2,1,0:T(8,128)(2,1)S(1)} %get-tuple-element.45), channel_id=1, source_target_pairs={{0,24},{1,25},{2,26},{3,27},{4,28},{5,29},{6,30},{7,31},{8,16},{9,... | collective-permute-start | bytes 196616 | tf_op jit(solution)/shard_map/ppermute | solution.py:364

commit v2 on v1

v2 whole, which is shorter than its diff:
```python
import functools

import jax
import jax.numpy as jnp
from jax import lax
from jax.experimental import pallas as pl
from jax.experimental.pallas import tpu as pltpu
from jax.sharding import PartitionSpec as P

D = 128
GROUPS = 8
HEADS = 4
TOKENS = 128
PARTS = 2
SHARE = GROUPS // PARTS
WIDE = HEADS * D
SCALE = D ** (-0.5)
LOG2E = 1.4426950408889634
AXES = ("ctx", "head")
BF = jnp.bfloat16
F32 = jnp.float32
ANY_ROWS = ((0, 64, 1), (64, 96, 2), (96, 112, 3), (112, 120, 4))
VMEM_LIMIT = 24 * 1024 * 1024


def dot(a, b):
    return lax.dot_general(a, b, (((1,), (0,)), ((), ())), preferred_element_type=F32)


def dot_nt(a, b):
    return lax.dot_general(a, b, (((1,), (1,)), ((), ())), preferred_element_type=F32)


def dot_tn(a, b):
    return lax.dot_general(a, b, (((0,), (0,)), ((), ())), preferred_element_type=F32)


def one_hot(mask):
    return jnp.where(mask, 1.0, 0.0).astype(BF)


def selected_token(row, offs, group):
    token = jnp.full(row.shape, -1, jnp.int32)
    for start, stop, level in ANY_ROWS:
        inside = (row >= start) & (row < stop)
        token = jnp.where(inside, (row - start) * 2**level + offs[level, group], token)
    return token


def selector(offs, group):
    shape = (128, TOKENS)
    row = lax.broadcasted_iota(jnp.int32, shape, 0)
    return one_hot(selected_token(row, offs, group) == lax.broadcasted_iota(jnp.int32, shape, 1))


def placer(offs, group):
    shape = (TOKENS, 128)
    row = lax.broadcasted_iota(jnp.int32, shape, 1)
    return one_hot(selected_token(row, offs, group) == lax.broadcasted_iota(jnp.int32, shape, 0))


def group_rows(pair_ref, member):
    k, v = member * D, (SHARE + member) * D
    return jnp.concatenate([pair_ref[:, k : k + D], pair_ref[:, v : v + D]], 1)


def select_kernel(base, offs, pair, first, middle, tail, last):
    for g in range(SHARE):
        rows = dot(selector(offs, base + g), group_rows(pair, g))
        first[g] = rows[0:64].astype(BF)
        middle[g] = rows[64:128].astype(BF)
        tail[g] = rows[96:128].astype(BF)
        last[g] = rows[112:128].astype(BF)


def compact_kernel(one, two, three, _, packed):
    for g in range(SHARE):
        a, b, c = one[g].astype(F32), two[g].astype(F32), three[g].astype(F32)
        packed[g] = jnp.concatenate([a[:24], b[:8], c[:8], jnp.zeros((8, 2 * D), F32)], 0).astype(BF)


def assemble_kernel(
    base, offs, first, mid_own, x_own, pair, x_far, mid_up, x_up, mid_down, x_down, *refs
):
    held = refs[-1]
    for g in range(SHARE):
        far = dot(selector(offs, base + g), group_rows(pair, g))
        mids = [mid_own[g].astype(F32), far[64:128], mid_up[g].astype(F32), mid_down[g].astype(F32)]
        extras = [ref[g].astype(F32) for ref in (x_own, x_far, x_up, x_down)]
        rows = [first[g].astype(F32), far[0:64]]
        rows += [m[0:32] for m in mids]
        for m, x in zip(mids, extras):
            rows += [m[32:48], x[0:16]]
        for m, x in zip(mids, extras):
            rows += [m[48:56], x[16:40]]
        held[g] = jnp.concatenate(rows, 0).astype(BF)


def by_level(rows):
    parts = []
    for start, stop in ((0, 64), (64, 96), (96, 112), (112, 120), (120, 128)):
        parts += [rows[start:stop, h * D : (h + 1) * D] for h in range(HEADS)]
    return jnp.concatenate(parts, 0)


def by_selection(rows):
    heads = []
    for h in range(HEADS):
        parts = []
        base = 0
        for count in (64, 32, 16, 8, 8):
            parts.append(rows[base + h * count : base + (h + 1) * count])
            base += HEADS * count
        heads.append(jnp.concatenate(parts, 0))
    return jnp.concatenate(heads, 1)


def heads_to_lanes(x):
    count = x.shape[0] // HEADS
    lane = lax.broadcasted_iota(jnp.int32, (count, 128), 1) & (HEADS - 1)
    out = x[(HEADS - 1) * count :]
    for h in range(HEADS - 1):
        out = jnp.where(lane == h, x[h * count : (h + 1) * count], out)
    return out


def attention_kernel(
    base, offs, q_ref, g_ref, pair_ref, far_ref, own_ref, other_ref, *refs
):
    att_ref, dq_ref, d0_ref, down_ref, dother_ref, level_ref, token_ref, delta_ref = refs[-8:]
    members = range(SHARE)
    ones = jnp.ones((256, D), BF)
    bounds = ((0, 256), (256, 384), (384, 448), (448, 480))
    starts = [[(offs[k, base + j], 128 >> k) for k in range(1, 5)] for j in members]

    def load(j):
        wide = slice(j * WIDE, (j + 1) * WIDE)
        own_pair, far_pair = group_rows(pair_ref, j), group_rows(far_ref, j)
        pick = selector(offs, base + j)
        q_rows, g_rows = q_ref[:, wide], g_ref[:, wide]
        qs = by_level(dot(pick, q_rows)).astype(BF)
        gs = by_level(dot(pick, g_rows)).astype(BF)
        own, other = own_ref[j], other_ref[j]
        queries = [jnp.concatenate([q_rows[:, h * D : (h + 1) * D] for h in range(HEADS)], 0)]
        grads = [jnp.concatenate([g_rows[:, h * D : (h + 1) * D] for h in range(HEADS)], 0)]
        keys = [jnp.concatenate([own_pair[:, :D], far_pair[:, :D]], 0)]
        values = [jnp.concatenate([own_pair[:, D:], far_pair[:, D:]], 0)]
        for k, (a, b) in enumerate(bounds):
            queries.append(qs[a:b])
            grads.append(gs[a:b])
            both = jnp.concatenate([own[128 * k : 128 * k + 128], other[128 * k : 128 * k + 128]], 0)
            keys.append(both[:, :D])
            values.append(both[:, D:])
        return queries, grads, keys, values

    def forward(states):
        results = [([], [], [], []) for _ in states]
        for k in range(5):
            scores = [dot_nt(st[0][k], st[2][k]) * (SCALE * LOG2E) for st in states]
            peaks = [jnp.max(x, 1, keepdims=True) for x in scores]
            powers = [jnp.exp2(x - p).astype(BF) for x, p in zip(scores, peaks)]
            outs = [dot(p, jnp.concatenate([st[3][k], ones], 1)) for p, st in zip(powers, states)]
            for r, power, peak, out in zip(results, powers, peaks, outs):
                peak = heads_to_lanes(jnp.broadcast_to(peak, (peak.shape[0], 128)))
                r[0].append(power)
                r[1].append(peak)
                r[2].append(peak + jnp.log2(heads_to_lanes(out[:, D:])))
                r[3].append(out[:, :D])
        return results

    def for_levels(ref, xs):
        for j, x in enumerate(xs):
            ref[j] = x
        columns = [[x] for x in xs]
        for k in range(4):
            for j in members:
                start, count = starts[j][k]
                columns[j].append(ref[j, pl.ds(start, count, 2 ** (k + 1)), :])
        return columns

    def merge(results):
        for k in range(4):
            for j in members:
                start, count = starts[j][k]
                level_ref[j, k, pl.ds(start, count, 2 ** (k + 1)), :] = results[j][2][k + 1]
        firsts = [r[2][0] for r in results]
        tops = [functools.reduce(jnp.maximum, [level_ref[j, k] for k in range(4)], firsts[j]) for j in members]
        sums = [
            jnp.exp2(firsts[j] - tops[j]) + sum(jnp.exp2(level_ref[j, k] - tops[j]) for k in range(4))
            for j in members
        ]
        columns = for_levels(token_ref, [top + jnp.log2(x) for top, x in zip(tops, sums)])
        return [[jnp.exp2(p - m) for p, m in zip(r[1], c)] for r, c in zip(results, columns)]

    def expand(x):
        return jnp.concatenate([jnp.broadcast_to(x[:, h : h + 1], x.shape) for h in range(HEADS)], 0)

    def beside(x):
        high = x.astype(BF).astype(F32)
        lane = lax.broadcasted_iota(jnp.int32, x.shape, 1)
        both = jnp.where(lane < 64, high, x - high)
        return jnp.concatenate(
            [jnp.where((lane & (HEADS - 1)) == h, both, 0.0) for h in range(HEADS)], 0
        ).astype(BF)

    def gather_levels(parts):
        level0 = [jnp.concatenate([p[0][h * 128 : h * 128 + 128] for h in range(HEADS)], 1) for p in parts]
        rows = [jnp.concatenate(p[1:] + [jnp.zeros((32, D), F32)], 0) for p in parts]
        rows = [by_selection(x).astype(BF) for x in rows]
        return [x + dot(placer(offs, base + j), r) for j, (x, r) in enumerate(zip(level0, rows))]

    def attend(results, spread):
        parts = [[out * f for out, f in zip(r[3], fs)] for r, fs in zip(results, spread)]
        attended = [x.astype(BF) for x in gather_levels(parts)]
        deltas = []
        for j, x in enumerate(attended):
            wide = slice(j * WIDE, (j + 1) * WIDE)
            att_ref[:, wide] = x
            product = g_ref[:, wide].astype(F32) * x.astype(F32)
            sums = [
                jnp.broadcast_to(jnp.sum(product[:, h * D : (h + 1) * D], 1, keepdims=True), (TOKENS, 128))
                for h in range(HEADS)
            ]
            deltas.append(heads_to_lanes(jnp.concatenate(sums, 0)))
        return for_levels(delta_ref, deltas)

    def backward(k, states, results, scaled, deltas):
        probs = [r[0][k] for r in results]
        weights = [
            dot_nt(
                jnp.concatenate([g[k], beside(d[k])], 1),
                jnp.concatenate([st[3][k], minus], 1),
            )
            for g, d, st in zip(scaled, deltas, states)
        ]
        scores = [(p.astype(F32) * w).astype(BF) for p, w in zip(probs, weights)]
        grad_values = [dot_tn(g[k], p).T for g, p in zip(scaled, probs)]
        grad_keys = [dot_tn(st[0][k], x).T * SCALE for x, st in zip(scores, states)]
        for j in members:
            pair = jnp.concatenate([grad_keys[j], grad_values[j]], 1).astype(BF)
            if k == 0:
                d0_ref[j] = pair
            else:
                at = 128 * (k - 1)
                down_ref[j, at : at + 128] = pair[:128]
                dother_ref[j, at : at + 128] = pair[128:]
        return [dot(x, st[2][k]) * SCALE for x, st in zip(scores, states)]

    shape = (2 * D, WIDE)
    row = lax.broadcasted_iota(jnp.int32, shape, 0) & (D - 1)
    widen = one_hot(row == lax.broadcasted_iota(jnp.int32, shape, 1) // D)
    lane = lax.broadcasted_iota(jnp.int32, (2 * D, D), 1)
    minus = jnp.where((lane & 63) < HEADS, -1.0, 0.0).astype(BF)
    level_ref[...] = jnp.full(level_ref.shape, -1e30, F32)
    states = [load(j) for j in members]
    results = forward(states)
    factors = merge(results)
    spread = [[expand(f) for f in fs] for fs in factors]
    deltas = attend(results, spread)
    deltas = [[f * d for f, d in zip(fs, ds)] for fs, ds in zip(factors, deltas)]
    scaled = [
        [(g.astype(F32) * f).astype(BF) for g, f in zip(st[1], fs)] for st, fs in zip(states, spread)
    ]
    dqs = [backward(k, states, results, scaled, deltas) for k in range(5)]
    for j, x in enumerate(gather_levels([[d[j] for d in dqs] for j in members])):
        dq_ref[:, j * WIDE : (j + 1) * WIDE] = x.astype(BF)


def middle_and_extra(total, z):
    zero = jnp.zeros((8, 2 * D), F32)
    middle = [
        total[128 + 32 * z : 160 + 32 * z],
        total[256 + 32 * z : 272 + 32 * z],
        total[384 + 32 * z : 392 + 32 * z],
        zero,
    ]
    return middle, [total[272 + 32 * z : 288 + 32 * z], total[392 + 32 * z : 416 + 32 * z], zero]


def reduce_kernel(mine, theirs, *refs):
    rows_kept, rows_far, up, down, x_far, x_kept = refs[-6:]
    for g in range(SHARE):
        total = mine[g].astype(F32) + theirs[g].astype(F32)
        for z, ref in enumerate((rows_kept, rows_far, up, down)):
            middle, extra = middle_and_extra(total, z)
            if z < 2:
                ref[g] = jnp.concatenate([total[64 * z : 64 * z + 64]] + middle, 0).astype(BF)
            else:
                ref[g] = jnp.concatenate(middle + extra, 0).astype(BF)
            if z == 0:
                x_kept[g] = jnp.concatenate(extra, 0)
            if z == 1:
                x_far[g] = jnp.concatenate(extra, 0).astype(BF)


def place_kernel(base, offs, d0, rows_far, _, far):
    for g in range(SHARE):
        far[g] = (d0[g, 128:256].astype(F32) + dot(placer(offs, base + g), rows_far[g])).astype(BF)


def cross_kernel(kept, far, up, down, one, two, three):
    for g in range(SHARE):
        total = kept[g] + far[g].astype(F32) + up[g, 64:112].astype(F32) + down[g, 64:112].astype(F32)
        zero = jnp.zeros((8, 2 * D), F32)
        one[g] = jnp.concatenate([total[0:24], zero], 0).astype(BF)
        two[g] = jnp.concatenate([total[24:32], zero], 0).astype(BF)
        three[g] = jnp.concatenate([total[32:40], zero], 0).astype(BF)


def finish_kernel(base, offs, d0, rows_kept, far, up, down, one, two, three, *refs):
    dk_ref, dv_ref = refs[-2:]
    if base:
        before_k, before_v = refs[:2]
        dk_ref[:, : base * D] = before_k[...]
        dv_ref[:, : base * D] = before_v[...]
    for g in range(SHARE):
        kept = rows_kept[g].astype(F32)
        middle = up[g, 0:64].astype(F32) + down[g, 0:64].astype(F32) + kept[64:128]
        a, b, c = one[g].astype(F32), two[g].astype(F32), three[g].astype(F32)
        rows = jnp.concatenate(
            [
                kept[0:64],
                middle[0:32],
                middle[32:48] + a[0:16],
                middle[48:56] + a[16:24] + b[0:8] + c[0:8],
                jnp.zeros((8, 2 * D), F32),
            ],
            0,
        ).astype(BF)
        whole = d0[g, 0:128].astype(F32) + far[g].astype(F32) + dot(placer(offs, base + g), rows)
        lanes = slice((base + g) * D, (base + g + 1) * D)
        dk_ref[:, lanes] = whole[:, :D].astype(BF)
        dv_ref[:, lanes] = whole[:, D:].astype(BF)


def whole_call(body, name, outs, offs, *arrays, after=()):
    specs = [pl.BlockSpec(memory_space=pltpu.VMEM)] * len(arrays)
    specs += [pl.BlockSpec(memory_space=pl.ANY)] * len(after)
    arrays = arrays + tuple(after)
    if offs is not None:
        specs = [pl.BlockSpec(memory_space=pltpu.SMEM)] + specs
        arrays = (offs,) + arrays
    shapes = [jax.ShapeDtypeStruct(shape, dtype) for shape, dtype in outs]
    return pl.pallas_call(
        body,
        name=name,
        out_shape=shapes,
        in_specs=specs,
        out_specs=[pl.BlockSpec(memory_space=pltpu.VMEM)] * len(shapes),
        cost_estimate=pl.CostEstimate(flops=0, bytes_accessed=4 * 10**6, transcendentals=0),
        compiler_params=pltpu.CompilerParams(vmem_limit_bytes=VMEM_LIMIT),
    )(*arrays)


def attention(base, offs, q, g, pair, far, own, other, before, after):
    part = base // SHARE
    lanes = pl.BlockSpec((TOKENS, SHARE * WIDE), lambda i: (0, part))
    whole = lambda *shape: pl.BlockSpec(shape, lambda i: (0,) * len(shape))
    pairs = whole(TOKENS, SHARE * 2 * D)
    rows = lambda n: whole(SHARE, n, 2 * D)
    return pl.pallas_call(
        functools.partial(attention_kernel, base),
        name="attention",
        grid=(1,),
        in_specs=[pl.BlockSpec(memory_space=pltpu.SMEM), lanes, lanes, pairs, pairs, rows(512), rows(512)]
        + [pl.BlockSpec(memory_space=pl.ANY)] * (len(before) + len(after)),
        out_specs=[lanes, lanes, rows(256), rows(512), rows(512)],
        out_shape=[
            jax.ShapeDtypeStruct((TOKENS, GROUPS * WIDE), BF),
            jax.ShapeDtypeStruct((TOKENS, GROUPS * WIDE), BF),
            jax.ShapeDtypeStruct((SHARE, 256, 2 * D), BF),
            jax.ShapeDtypeStruct((SHARE, 512, 2 * D), BF),
            jax.ShapeDtypeStruct((SHARE, 512, 2 * D), BF),
        ],
        scratch_shapes=[
            pltpu.VMEM((SHARE, 4, TOKENS, 128), F32),
            pltpu.VMEM((SHARE, TOKENS, 128), F32),
            pltpu.VMEM((SHARE, TOKENS, 128), F32),
        ],
        input_output_aliases={7 + i: i for i in range(len(before))},
        cost_estimate=pl.CostEstimate(flops=16 * 10**9, bytes_accessed=60 * 10**6, transcendentals=4 * 10**6),
        compiler_params=pltpu.CompilerParams(vmem_limit_bytes=48 * 1024 * 1024),
    )(offs, q, g, pair, far, own, other, *before, *after)


def routes(count):
    def along_z(i, step):
        z = ((i & 1) * 2 + (i >> 2 & 1) + step) % 4
        return (i & ~5) | (z & 1) << 2 | z >> 1

    table = {
        "head": lambda i: i ^ 1,
        "core": lambda i: i ^ 2,
        "up": lambda i: along_z(i, 1),
        "down": lambda i: along_z(i, -1),
        "x1": lambda i: i ^ 8,
        "x2": lambda i: i ^ 16,
        "x3": lambda i: i ^ 24,
    }
    return {name: [(i, to(i)) for i in range(count)] for name, to in table.items()}


def shards(count, queries, key_rows, value_rows, gradient, level_offsets):
    route = routes(count)

    def send(x, name):
        return lax.ppermute(x, AXES, route[name])

    other_offsets = send(level_offsets, "head")
    low = lax.axis_index("head") == 0
    offs = jnp.where(
        low,
        jnp.concatenate([level_offsets, other_offsets], 1),
        jnp.concatenate([other_offsets, level_offsets], 1),
    )
    rows = lambda n, dtype=BF: ((SHARE, n, 2 * D), dtype)
    bases = [part * SHARE for part in range(PARTS)]
    span = SHARE * D
    pairs = [
        jnp.concatenate([x[:, part * span : (part + 1) * span] for x in (key_rows, value_rows)], 1)
        for part in range(PARTS)
    ]

    gathered = []
    follow = offs
    for base, pair in zip(bases, pairs):
        pair_sent, _ = lax.optimization_barrier((pair, follow))
        far_pair = send(pair_sent, "head")
        first, middle, tail, last = whole_call(
            functools.partial(select_kernel, base), "select", [rows(64), rows(64), rows(32), rows(16)], offs, pair
        )
        follow = middle
        gathered.append((far_pair, first, middle, send(tail, "x1"), send(last, "x2"), send(last, "x3")))

    packed = []
    last_middle = gathered[-1][2]
    for _, first, middle, one, two, three in gathered:
        middle_down = send(middle, "up")
        middle_up = send(middle, "down")
        (extra,) = whole_call(compact_kernel, "compact", [rows(48)], None, one, two, three, after=(last_middle,))
        received = (send(extra, "head"), middle_up, send(extra, "down"), middle_down, send(extra, "up"))
        packed.append((first, middle, extra, received))

    before, after, turn, first_done = (), (packed[-1][2],), (), ()
    returned = []
    for base, pair, (far_pair, *_), (first, middle, extra, received) in zip(bases, pairs, gathered, packed):
        (own,) = whole_call(
            functools.partial(assemble_kernel, base), "assemble", [rows(512)], offs, first, middle, extra,
            far_pair, *received, after=first_done,
        )
        other = send(own, "core")
        attended, grad_queries, d0, down_own, down_other = attention(
            base, offs, queries, gradient, pair, far_pair, own, other, before, after
        )
        before, first_done = (attended, grad_queries), (d0,)
        down_other, _ = lax.optimization_barrier((down_other, turn))
        theirs = send(down_other, "core")
        rows_kept, rows_far, up, down, x_far, x_kept = whole_call(
            reduce_kernel, "reduce", [rows(128), rows(128), rows(112), rows(112), rows(48), rows(48, F32)],
            None, down_own, theirs,
        )
        from_down = send(up, "up")
        from_up = send(down, "down")
        x_far = send(x_far, "head")
        (far,) = whole_call(
            functools.partial(place_kernel, base), "place", [rows(128)], offs, d0, rows_far, after=(x_far,)
        )
        after = (far,)
        far = send(far, "head")
        turn = (from_down, from_up)
        one, two, three = whole_call(
            cross_kernel, "cross", [rows(32), rows(16), rows(16)], None, x_kept, x_far, from_up, from_down
        )
        one, two, three = send(one, "x1"), send(two, "x2"), send(three, "x3")
        returned.append((d0, rows_kept, far, from_up, from_down, one, two, three))

    grads = ()
    for base, arrays in zip(bases, returned):
        out = ((TOKENS, (base + SHARE) * D), BF)
        grads = whole_call(
            functools.partial(finish_kernel, base), "finish", [out, out], offs, *arrays, *grads
        )
    return (attended, grad_queries, *grads)


def solution(mesh):
    rows = P(AXES, None)
    return jax.shard_map(
        functools.partial(shards, mesh.size),
        mesh=mesh,
        in_specs=(rows, rows, rows, rows, P(None, "head")),
        out_specs=(rows, rows, rows, rows),
        check_vma=False,
    )
```

time: 111 us -> 109 us (0.982); the launches traced: 110 us -> 109 us
  starting transfers between devices: 32.8 us -> 46.3 us
  Pallas kernels: 33.1 us -> 25.7 us
  waiting for transfers between devices: 37.3 us -> 32.7 us
  local copies, waits for them, and re-layouts: 5.63 us -> 3.52 us
    ppermute x20 -> x37, starting transfers between devices: 32.8 us -> 46.3 us  [send(): return lax.ppermute(x, AXES, route[name])]
    pallas_call x1 -> x2, Pallas kernels: 28.1 us -> 17.7 us  [attention(): pl.pallas_call(functools.partial(attention_kernel, base), name='attention...]
    ppermute x20 -> x37, waiting for transfers between devices: 37.3 us -> 32.7 us  [send(): return lax.ppermute(x, AXES, route[name])]
    unnamed x19 -> x13, local copies, waits for them, and re-layouts: 5.63 us -> 2.39 us
    pallas_call x7 -> x14, Pallas kernels: 5.01 us -> 8.01 us  [whole_call(): pl.pallas_call(body, name=name, out_shape=shapes, in_specs=specs, out_spe...]
    slice x0 -> x1, local copies, waits for them, and re-layouts: none -> 1.13 us  [shards(): x[:, part * span:(part + 1) * span]]
  transfers between devices with their start and end apart: 20 -> 37, of which waited for: 12 -> 17; matrix products, arithmetic and copies ran while one was open for 0% -> 1% of each run, Pallas kernels for 2% -> 21%
where the time goes in v2:
time: 109 us
  starting transfers between devices  46.3 us (42%)
  waiting for transfers between devices  32.7 us (30%)
  Pallas kernels  25.7 us (24%)
  local copies, waits for them, and re-layouts  3.52 us (3%)
    ppermute x37, starting transfers between devices, send(): return lax.ppermute(x, AXES, route[name])  46.3 us
    ppermute x37, waiting for transfers between devices, send(): return lax.ppermute(x, AXES, route[name])  32.7 us
    pallas_call x2, Pallas kernels, attention(): pl.pallas_call(functools.partial(attention_kernel, base), name='attention...  17.7 us
    pallas_call x14, Pallas kernels, whole_call(): pl.pallas_call(body, name=name, out_shape=shapes, in_specs=specs, out_spe...  8.01 us
    unnamed x13, local copies, waits for them, and re-layouts  2.39 us
  transfers between devices with their start and end apart: 37, of which 17 were waited for; matrix products, arithmetic and copies ran while one was open for 1% of the time, Pallas kernels for 21%

profile of v2, /device:TPU:0, one launch (start us, length us, event | category | flops | bytes accessed | tf_op | source)
XLA Modules:
  0.0 109.2 jit_solution(6777479261966753982)
XLA Ops:
  1.4 4.0 %collective-permute-start = (s32[5,4]{1,0:T(8,128)S(1)}, s32[5,4]{1,0:T(8,128)S(1)}, u32[]{:S(2)}, u32[]{:S(2)}) collective-permute-start(s32[5,4]{1,0:T(8,128)S(1)} %copy.12), channel_id=1, source_target_pairs={{0,1},{1,0},{2,3},{3,2},{4,5},{5,4},{6,7},{7,6},{8,9},{9,8},{10,11... | collective-permute-start | bytes 248 | tf_op jit(solution)/shard_map/ppermute | solution.py:407
  5.4 1.1 %fusion = (bf16[128,512]{1,0:T(8,128)(2,1)S(1)}, bf16[128,512]{1,0:T(8,128)(2,1)S(1)}, bf16[128,512]{1,0:T(8,128)(2,1)S(1)}, bf16[128,512]{1,0:T(8,128)(2,1)S(1)}) fusion(bf16[128,1024]{1,0:T(8,128)(2,1)} %param.6, bf16[128,1024]{1,0:T(8,128)(2,1)} %param.7), kind=kLoop, calls=%fused_computation.3 | loop fusion | bytes 1048576 | tf_op jit(solution)/shard_map/slice | solution.py:420
  7.0 3.5 %collective-permute-start.10 = (bf16[128,1024]{1,0:T(8,128)(2,1)S(1)}, bf16[128,1024]{1,0:T(8,128)(2,1)S(1)}, u32[]{:S(2)}, u32[]{:S(2)}) collective-permute-start(bf16[128,1024]{1,0:T(8,128)(2,1)S(1)} %pad_maximum_fusion.1.pair.pair_ref), channel_id=1, source_target_pairs={{0,1},{1,0},{2,3},{3,2},{4,5},{5,4},{6,7},{7,6},{8,9},{9,8},{10,11... | collective-permute-start | bytes 786440 | tf_op jit(solution)/shard_map/ppermute | solution.py:407
  10.6 0.8 select.2
  11.4 3.1 %collective-permute-start.12 = (bf16[4,16,256]{2,1,0:T(8,128)(2,1)S(1)}, bf16[4,16,256]{2,1,0:T(8,128)(2,1)S(1)}, u32[]{:S(2)}, u32[]{:S(2)}) collective-permute-start(bf16[4,16,256]{2,1,0:T(8,128)(2,1)S(1)} %get-tuple-element.56), channel_id=1, source_target_pairs={{0,16},{1,17},{2,18},{3,19},{4,20},{5,21},{6,22},{7,23},{8,24},{9,... | collective-permute-start | bytes 98312 | tf_op jit(solution)/shard_map/ppermute | solution.py:407
  15.2 1.1 %collective-permute-start.13 = (bf16[4,16,256]{2,1,0:T(8,128)(2,1)S(1)}, bf16[4,16,256]{2,1,0:T(8,128)(2,1)S(1)}, u32[]{:S(2)}, u32[]{:S(2)}) collective-permute-start(bf16[4,16,256]{2,1,0:T(8,128)(2,1)S(1)} %get-tuple-element.56), channel_id=1, source_target_pairs={{0,24},{1,25},{2,26},{3,27},{4,28},{5,29},{6,30},{7,31},{8,16},{9,... | collective-permute-start | bytes 98312 | tf_op jit(solution)/shard_map/ppermute | solution.py:407
  16.3 1.3 %collective-permute-start.17 = (bf16[4,64,256]{2,1,0:T(8,128)(2,1)S(1)}, bf16[4,64,256]{2,1,0:T(8,128)(2,1)S(1)}, u32[]{:S(2)}, u32[]{:S(2)}) collective-permute-start(bf16[4,64,256]{2,1,0:T(8,128)(2,1)S(1)} %get-tuple-element.47.mid_own), channel_id=1, source_target_pairs={{0,4},{1,5},{2,6},{3,7},{4,1},{5,0},{6,3},{7,2},{8,12},{9,13},{10,... | collective-permute-start | bytes 393224 | tf_op jit(solution)/shard_map/ppermute | solution.py:407
  18.4 0.8 select.3
  19.2 1.1 %collective-permute-done.13.three = bf16[4,16,256]{2,1,0:T(8,128)(2,1)S(1)} collective-permute-done((bf16[4,16,256]{2,1,0:T(8,128)(2,1)S(1)}, bf16[4,16,256]{2,1,0:T(8,128)(2,1)S(1)}, u32[]{:S(2)}, u32[]{:S(2)}) %collective-permute-start.13) | collective-permute-done | bytes 32800 | tf_op jit(solution)/shard_map/ppermute | solution.py:407
  20.3 1.6 %collective-permute-done.11.one = bf16[4,32,256]{2,1,0:T(8,128)(2,1)S(1)} collective-permute-done((bf16[4,32,256]{2,1,0:T(8,128)(2,1)S(1)}, bf16[4,32,256]{2,1,0:T(8,128)(2,1)S(1)}, u32[]{:S(2)}, u32[]{:S(2)}) %collective-permute-start.11) | collective-permute-done | bytes 65568 | tf_op jit(solution)/shard_map/ppermute | solution.py:407
  21.9 1.1 %collective-permute-start.14 = (bf16[4,48,256]{2,1,0:T(8,128)(2,1)S(1)}, bf16[4,48,256]{2,1,0:T(8,128)(2,1)S(1)}, u32[]{:S(2)}, u32[]{:S(2)}) collective-permute-start(bf16[4,48,256]{2,1,0:T(8,128)(2,1)S(1)} %compact.3.x_own), channel_id=1, source_target_pairs={{0,1},{1,0},{2,3},{3,2},{4,5},{5,4},{6,7},{7,6},{8,9},{9,8},{10,11... | collective-permute-start | bytes 294920 | tf_op jit(solution)/shard_map/ppermute | solution.py:407
  23.1 2.6 %collective-permute-start.16 = (bf16[4,48,256]{2,1,0:T(8,128)(2,1)S(1)}, bf16[4,48,256]{2,1,0:T(8,128)(2,1)S(1)}, u32[]{:S(2)}, u32[]{:S(2)}) collective-permute-start(bf16[4,48,256]{2,1,0:T(8,128)(2,1)S(1)} %compact.3.x_own), channel_id=1, source_target_pairs={{0,5},{1,4},{2,7},{3,6},{4,0},{5,1},{6,2},{7,3},{8,13},{9,12},{10,... | collective-permute-start | bytes 294920 | tf_op jit(solution)/shard_map/ppermute | solution.py:407
  25.7 2.4 %collective-permute-done.14.x_far = bf16[4,48,256]{2,1,0:T(8,128)(2,1)S(1)} collective-permute-done((bf16[4,48,256]{2,1,0:T(8,128)(2,1)S(1)}, bf16[4,48,256]{2,1,0:T(8,128)(2,1)S(1)}, u32[]{:S(2)}, u32[]{:S(2)}) %collective-permute-start.14) | collective-permute-done | bytes 98336 | tf_op jit(solution)/shard_map/ppermute | solution.py:407
  28.4 3.1 %collective-permute-done.18.x_down = bf16[4,48,256]{2,1,0:T(8,128)(2,1)S(1)} collective-permute-done((bf16[4,48,256]{2,1,0:T(8,128)(2,1)S(1)}, bf16[4,48,256]{2,1,0:T(8,128)(2,1)S(1)}, u32[]{:S(2)}, u32[]{:S(2)}) %collective-permute-start.18) | collective-permute-done | bytes 98336 | tf_op jit(solution)/shard_map/ppermute | solution.py:407
  31.5 0.8 assemble.2.own_ref
  32.5 0.8 collective-permute-start.2
  33.3 2.8 %collective-permute-start.3 = (bf16[4,16,256]{2,1,0:T(8,128)(2,1)S(1)}, bf16[4,16,256]{2,1,0:T(8,128)(2,1)S(1)}, u32[]{:S(2)}, u32[]{:S(2)}) collective-permute-start(bf16[4,16,256]{2,1,0:T(8,128)(2,1)S(1)} %get-tuple-element.52), channel_id=1, source_target_pairs={{0,16},{1,17},{2,18},{3,19},{4,20},{5,21},{6,22},{7,23},{8,24},{9,... | collective-permute-start | bytes 98312 | tf_op jit(solution)/shard_map/ppermute | solution.py:407
  36.1 1.1 %collective-permute-start.4 = (bf16[4,16,256]{2,1,0:T(8,128)(2,1)S(1)}, bf16[4,16,256]{2,1,0:T(8,128)(2,1)S(1)}, u32[]{:S(2)}, u32[]{:S(2)}) collective-permute-start(bf16[4,16,256]{2,1,0:T(8,128)(2,1)S(1)} %get-tuple-element.52), channel_id=1, source_target_pairs={{0,24},{1,25},{2,26},{3,27},{4,28},{5,29},{6,30},{7,31},{8,16},{9,... | collective-permute-start | bytes 98312 | tf_op jit(solution)/shard_map/ppermute | solution.py:407
  37.3 2.0 %collective-permute-done.3.two = bf16[4,16,256]{2,1,0:T(8,128)(2,1)S(1)} collective-permute-done((bf16[4,16,256]{2,1,0:T(8,128)(2,1)S(1)}, bf16[4,16,256]{2,1,0:T(8,128)(2,1)S(1)}, u32[]{:S(2)}, u32[]{:S(2)}) %collective-permute-start.3) | collective-permute-done | bytes 32800 | tf_op jit(solution)/shard_map/ppermute | solution.py:407
  39.3 2.0 %collective-permute-done.4.three = bf16[4,16,256]{2,1,0:T(8,128)(2,1)S(1)} collective-permute-done((bf16[4,16,256]{2,1,0:T(8,128)(2,1)S(1)}, bf16[4,16,256]{2,1,0:T(8,128)(2,1)S(1)}, u32[]{:S(2)}, u32[]{:S(2)}) %collective-permute-start.4) | collective-permute-done | bytes 32800 | tf_op jit(solution)/shard_map/ppermute | solution.py:407
  41.3 3.6 %collective-permute-start.5 = (bf16[4,48,256]{2,1,0:T(8,128)(2,1)S(1)}, bf16[4,48,256]{2,1,0:T(8,128)(2,1)S(1)}, u32[]{:S(2)}, u32[]{:S(2)}) collective-permute-start(bf16[4,48,256]{2,1,0:T(8,128)(2,1)S(1)} %compact.2.refs_0_.x_own), channel_id=1, source_target_pairs={{0,1},{1,0},{2,3},{3,2},{4,5},{5,4},{6,7},{7,6},{8,9},{9,8},{10,11... | collective-permute-start | bytes 294920 | tf_op jit(solution)/shard_map/ppermute | solution.py:407
  44.9 1.2 %collective-permute-start.7 = (bf16[4,48,256]{2,1,0:T(8,128)(2,1)S(1)}, bf16[4,48,256]{2,1,0:T(8,128)(2,1)S(1)}, u32[]{:S(2)}, u32[]{:S(2)}) collective-permute-start(bf16[4,48,256]{2,1,0:T(8,128)(2,1)S(1)} %compact.2.refs_0_.x_own), channel_id=1, source_target_pairs={{0,5},{1,4},{2,7},{3,6},{4,0},{5,1},{6,2},{7,3},{8,13},{9,12},{10,... | collective-permute-start | bytes 294920 | tf_op jit(solution)/shard_map/ppermute | solution.py:407
  46.1 8.9 %attention.2 = (bf16[128,4096]{1,0:T(8,128)(2,1)}, bf16[128,4096]{1,0:T(8,128)(2,1)}, bf16[4,256,256]{2,1,0:T(8,128)(2,1)S(1)}, bf16[4,512,256]{2,1,0:T(8,128)(2,1)S(1)}, bf16[4,512,256]{2,1,0:T(8,128)(2,1)S(1)}) custom-call(s32[5,8]{1,0:T(8,128)S(1)} %add_select_fusion.offs, bf16[128,4096]{1,0:T(8,128)(2,1)S(1)} %copy-done.2, ...), custom_call_target="tpu_custom_call" | custom-call | flops 16000000000 | bytes 60000000 | tf_op jit(solution)/shard_map/attention/pallas_call | solution.py:361
  55.0 0.9 collective-permute-start.9
  55.9 5.5 %collective-permute-done.9.x_down = bf16[4,48,256]{2,1,0:T(8,128)(2,1)S(1)} collective-permute-done((bf16[4,48,256]{2,1,0:T(8,128)(2,1)S(1)}, bf16[4,48,256]{2,1,0:T(8,128)(2,1)S(1)}, u32[]{:S(2)}, u32[]{:S(2)}) %collective-permute-start.9) | collective-permute-done | bytes 98336 | tf_op jit(solution)/shard_map/ppermute | solution.py:407
  61.4 0.8 assemble.3.own_ref
  63.9 2.6 %collective-permute-start.24 = (bf16[4,112,256]{2,1,0:T(8,128)(2,1)S(1)}, bf16[4,112,256]{2,1,0:T(8,128)(2,1)S(1)}, u32[]{:S(2)}, u32[]{:S(2)}) collective-permute-start(bf16[4,112,256]{2,1,0:T(8,128)(2,1)S(1)} %get-tuple-element.70), channel_id=1, source_target_pairs={{0,5},{1,4},{2,7},{3,6},{4,0},{5,1},{6,2},{7,3},{8,13},{9,12},{10,... | collective-permute-start | bytes 688136 | tf_op jit(solution)/shard_map/ppermute | solution.py:407
  66.5 3.9 %collective-permute-done.22._.far = bf16[4,48,256]{2,1,0:T(8,128)(2,1)S(1)} collective-permute-done((bf16[4,48,256]{2,1,0:T(8,128)(2,1)S(1)}, bf16[4,48,256]{2,1,0:T(8,128)(2,1)S(1)}, u32[]{:S(2)}, u32[]{:S(2)}) %collective-permute-start.22) | collective-permute-done | bytes 98336 | tf_op jit(solution)/shard_map/ppermute | solution.py:407
  70.5 0.8 place.2.refs_2_
  71.3 1.0 copy-done.5
  72.3 8.8 %attention.3 = (bf16[128,4096]{1,0:T(8,128)(2,1)}, bf16[128,4096]{1,0:T(8,128)(2,1)}, bf16[4,256,256]{2,1,0:T(8,128)(2,1)S(1)}, bf16[4,512,256]{2,1,0:T(8,128)(2,1)S(1)}, bf16[4,512,256]{2,1,0:T(8,128)(2,1)S(1)}) custom-call(s32[5,8]{1,0:T(8,128)S(1)} %add_select_fusion.offs, ...), custom_call_target="tpu_custom_call", output_to_operand_aliasing={{0}: (7, {}), {1}: (8, {})} | custom-call | flops 16000000000 | bytes 60000000 | tf_op jit(solution)/shard_map/attention/pallas_call | solution.py:361
  81.2 2.6 %collective-permute-done.25.theirs = bf16[4,512,256]{2,1,0:T(8,128)(2,1)S(1)} collective-permute-done((bf16[4,512,256]{2,1,0:T(8,128)(2,1)S(1)}, bf16[4,512,256]{2,1,0:T(8,128)(2,1)S(1)}, u32[]{:S(2)}, u32[]{:S(2)}) %collective-permute-start.25) | collective-permute-done | bytes 1048608 | tf_op jit(solution)/shard_map/ppermute | solution.py:407
  84.2 1.9 %collective-permute-start.28 = (bf16[4,112,256]{2,1,0:T(8,128)(2,1)S(1)}, bf16[4,112,256]{2,1,0:T(8,128)(2,1)S(1)}, u32[]{:S(2)}, u32[]{:S(2)}) collective-permute-start(bf16[4,112,256]{2,1,0:T(8,128)(2,1)S(1)} %get-tuple-element.75), channel_id=1, source_target_pairs={{0,5},{1,4},{2,7},{3,6},{4,0},{5,1},{6,2},{7,3},{8,13},{9,12},{10,... | collective-permute-start | bytes 688136 | tf_op jit(solution)/shard_map/ppermute | solution.py:407
  86.3 3.4 %collective-permute-start.33 = (bf16[4,128,256]{2,1,0:T(8,128)(2,1)S(1)}, bf16[4,128,256]{2,1,0:T(8,128)(2,1)S(1)}, u32[]{:S(2)}, u32[]{:S(2)}) collective-permute-start(bf16[4,128,256]{2,1,0:T(8,128)(2,1)S(1)} %place.2.refs_2_), channel_id=1, source_target_pairs={{0,1},{1,0},{2,3},{3,2},{4,5},{5,4},{6,7},{7,6},{8,9},{9,8},{10,11... | collective-permute-start | bytes 786440 | tf_op jit(solution)/shard_map/ppermute | solution.py:407
  89.7 1.5 %collective-permute-done.26._.far = bf16[4,48,256]{2,1,0:T(8,128)(2,1)S(1)} collective-permute-done((bf16[4,48,256]{2,1,0:T(8,128)(2,1)S(1)}, bf16[4,48,256]{2,1,0:T(8,128)(2,1)S(1)}, u32[]{:S(2)}, u32[]{:S(2)}) %collective-permute-start.26) | collective-permute-done | bytes 98336 | tf_op jit(solution)/shard_map/ppermute | solution.py:407
  91.2 0.8 place.3
  92.2 0.9 collective-permute-start.34
  93.1 2.3 %collective-permute-start.35 = (bf16[4,16,256]{2,1,0:T(8,128)(2,1)S(1)}, bf16[4,16,256]{2,1,0:T(8,128)(2,1)S(1)}, u32[]{:S(2)}, u32[]{:S(2)}) collective-permute-start(bf16[4,16,256]{2,1,0:T(8,128)(2,1)S(1)} %get-tuple-element.84), channel_id=1, source_target_pairs={{0,16},{1,17},{2,18},{3,19},{4,20},{5,21},{6,22},{7,23},{8,24},{9,... | collective-permute-start | bytes 98312 | tf_op jit(solution)/shard_map/ppermute | solution.py:407
  95.3 0.9 collective-permute-done.29.down
  96.2 1.6 %collective-permute-start.36 = (bf16[4,16,256]{2,1,0:T(8,128)(2,1)S(1)}, bf16[4,16,256]{2,1,0:T(8,128)(2,1)S(1)}, u32[]{:S(2)}, u32[]{:S(2)}) collective-permute-start(bf16[4,16,256]{2,1,0:T(8,128)(2,1)S(1)} %get-tuple-element.85), channel_id=1, source_target_pairs={{0,24},{1,25},{2,26},{3,27},{4,28},{5,29},{6,30},{7,31},{8,16},{9,... | collective-permute-start | bytes 98312 | tf_op jit(solution)/shard_map/ppermute | solution.py:407
  98.5 1.2 %collective-permute-start.30 = (bf16[4,32,256]{2,1,0:T(8,128)(2,1)S(1)}, bf16[4,32,256]{2,1,0:T(8,128)(2,1)S(1)}, u32[]{:S(2)}, u32[]{:S(2)}) collective-permute-start(bf16[4,32,256]{2,1,0:T(8,128)(2,1)S(1)} %get-tuple-element.78), channel_id=1, source_target_pairs={{0,8},{1,9},{2,10},{3,11},{4,12},{5,13},{6,14},{7,15},{8,0},{9,1},... | collective-permute-start | bytes 196616 | tf_op jit(solution)/shard_map/ppermute | solution.py:407
  99.7 1.6 %collective-permute-done.36.three = bf16[4,16,256]{2,1,0:T(8,128)(2,1)S(1)} collective-permute-done((bf16[4,16,256]{2,1,0:T(8,128)(2,1)S(1)}, bf16[4,16,256]{2,1,0:T(8,128)(2,1)S(1)}, u32[]{:S(2)}, u32[]{:S(2)}) %collective-permute-start.36) | collective-permute-done | bytes 32800 | tf_op jit(solution)/shard_map/ppermute | solution.py:407
  101.3 1.1 %collective-permute-start.31 = (bf16[4,16,256]{2,1,0:T(8,128)(2,1)S(1)}, bf16[4,16,256]{2,1,0:T(8,128)(2,1)S(1)}, u32[]{:S(2)}, u32[]{:S(2)}) collective-permute-start(bf16[4,16,256]{2,1,0:T(8,128)(2,1)S(1)} %get-tuple-element.79), channel_id=1, source_target_pairs={{0,16},{1,17},{2,18},{3,19},{4,20},{5,21},{6,22},{7,23},{8,24},{9,... | collective-permute-start | bytes 98312 | tf_op jit(solution)/shard_map/ppermute | solution.py:407
  102.4 1.2 %collective-permute-start.32 = (bf16[4,16,256]{2,1,0:T(8,128)(2,1)S(1)}, bf16[4,16,256]{2,1,0:T(8,128)(2,1)S(1)}, u32[]{:S(2)}, u32[]{:S(2)}) collective-permute-start(bf16[4,16,256]{2,1,0:T(8,128)(2,1)S(1)} %get-tuple-element.80), channel_id=1, source_target_pairs={{0,24},{1,25},{2,26},{3,27},{4,28},{5,29},{6,30},{7,31},{8,16},{9,... | collective-permute-start | bytes 98312 | tf_op jit(solution)/shard_map/ppermute | solution.py:407
  103.6 0.8 finish.2
  104.4 2.3 %collective-permute-done.31.two = bf16[4,16,256]{2,1,0:T(8,128)(2,1)S(1)} collective-permute-done((bf16[4,16,256]{2,1,0:T(8,128)(2,1)S(1)}, bf16[4,16,256]{2,1,0:T(8,128)(2,1)S(1)}, u32[]{:S(2)}, u32[]{:S(2)}) %collective-permute-start.31) | collective-permute-done | bytes 32800 | tf_op jit(solution)/shard_map/ppermute | solution.py:407
  106.8 0.8 collective-permute-done.32.three
  107.6 1.6 %finish.3 = (bf16[128,1024]{1,0:T(8,128)(2,1)}, bf16[128,1024]{1,0:T(8,128)(2,1)}) custom-call(s32[5,8]{1,0:T(8,128)S(1)} %add_select_fusion.offs, bf16[4,256,256]{2,1,0:T(8,128)(2,1)S(1)} %get-tuple-element.66.d0, bf16[4,128,256]{2,1,0:T(8,128)(2,1)S(1)} %get-tuple-element.72.rows_kept, bf16[4,128,256]{2,1,0:T(8,128)(2,1)S(1)} %collective-permute-done.27.far, ...), custom_call_target="tpu_custom_call" | custom-call | bytes 4000000 | tf_op jit(solution)/shard_map/finish/pallas_call | solution.py:344
  (59 shorter events, 6.4 us)
Async XLA Ops:
  1.4 5.5 %collective-permute-start = (s32[5,4]{1,0:T(8,128)S(1)}, s32[5,4]{1,0:T(8,128)S(1)}, u32[]{:S(2)}, u32[]{:S(2)}) collective-permute-start(s32[5,4]{1,0:T(8,128)S(1)} %copy.12), channel_id=1, source_target_pairs={{0,1},{1,0},{2,3},{3,2},{4,5},{5,4},{6,7},{7,6},{8,9},{9,8},{10,11... | collective-permute-start | bytes 248 | tf_op jit(solution)/shard_map/ppermute | solution.py:407
  7.0 24.5 %collective-permute-start.10 = (bf16[128,1024]{1,0:T(8,128)(2,1)S(1)}, bf16[128,1024]{1,0:T(8,128)(2,1)S(1)}, u32[]{:S(2)}, u32[]{:S(2)}) collective-permute-start(bf16[128,1024]{1,0:T(8,128)(2,1)S(1)} %pad_maximum_fusion.1.pair.pair_ref), channel_id=1, source_target_pairs={{0,1},{1,0},{2,3},{3,2},{4,5},{5,4},{6,7},{7,6},{8,9},{9,8},{10,11... | collective-permute-start | bytes 786440 | tf_op jit(solution)/shard_map/ppermute | solution.py:407
  11.4 6.3 %collective-permute-start.12 = (bf16[4,16,256]{2,1,0:T(8,128)(2,1)S(1)}, bf16[4,16,256]{2,1,0:T(8,128)(2,1)S(1)}, u32[]{:S(2)}, u32[]{:S(2)}) collective-permute-start(bf16[4,16,256]{2,1,0:T(8,128)(2,1)S(1)} %get-tuple-element.56), channel_id=1, source_target_pairs={{0,16},{1,17},{2,18},{3,19},{4,20},{5,21},{6,22},{7,23},{8,24},{9,... | collective-permute-start | bytes 98312 | tf_op jit(solution)/shard_map/ppermute | solution.py:407
  14.5 11.2 %collective-permute-start.15 = (bf16[4,64,256]{2,1,0:T(8,128)(2,1)S(1)}, bf16[4,64,256]{2,1,0:T(8,128)(2,1)S(1)}, u32[]{:S(2)}, u32[]{:S(2)}) collective-permute-start(bf16[4,64,256]{2,1,0:T(8,128)(2,1)S(1)} %get-tuple-element.47.mid_own), channel_id=1, source_target_pairs={{0,5},{1,4},{2,7},{3,6},{4,0},{5,1},{6,2},{7,3},{8,13},{9,12},{10,... | collective-permute-start | bytes 393224 | tf_op jit(solution)/shard_map/ppermute | solution.py:407
  15.2 5.1 %collective-permute-start.13 = (bf16[4,16,256]{2,1,0:T(8,128)(2,1)S(1)}, bf16[4,16,256]{2,1,0:T(8,128)(2,1)S(1)}, u32[]{:S(2)}, u32[]{:S(2)}) collective-permute-start(bf16[4,16,256]{2,1,0:T(8,128)(2,1)S(1)} %get-tuple-element.56), channel_id=1, source_target_pairs={{0,24},{1,25},{2,26},{3,27},{4,28},{5,29},{6,30},{7,31},{8,16},{9,... | collective-permute-start | bytes 98312 | tf_op jit(solution)/shard_map/ppermute | solution.py:407
  16.3 9.4 %collective-permute-start.17 = (bf16[4,64,256]{2,1,0:T(8,128)(2,1)S(1)}, bf16[4,64,256]{2,1,0:T(8,128)(2,1)S(1)}, u32[]{:S(2)}, u32[]{:S(2)}) collective-permute-start(bf16[4,64,256]{2,1,0:T(8,128)(2,1)S(1)} %get-tuple-element.47.mid_own), channel_id=1, source_target_pairs={{0,4},{1,5},{2,6},{3,7},{4,1},{5,0},{6,3},{7,2},{8,12},{9,13},{10,... | collective-permute-start | bytes 393224 | tf_op jit(solution)/shard_map/ppermute | solution.py:407
  17.7 4.3 %collective-permute-start.11 = (bf16[4,32,256]{2,1,0:T(8,128)(2,1)S(1)}, bf16[4,32,256]{2,1,0:T(8,128)(2,1)S(1)}, u32[]{:S(2)}, u32[]{:S(2)}) collective-permute-start(bf16[4,32,256]{2,1,0:T(8,128)(2,1)S(1)} %get-tuple-element.55), channel_id=1, source_target_pairs={{0,8},{1,9},{2,10},{3,11},{4,12},{5,13},{6,14},{7,15},{8,0},{9,1},... | collective-permute-start | bytes 196616 | tf_op jit(solution)/shard_map/ppermute | solution.py:407
  21.9 6.2 %collective-permute-start.14 = (bf16[4,48,256]{2,1,0:T(8,128)(2,1)S(1)}, bf16[4,48,256]{2,1,0:T(8,128)(2,1)S(1)}, u32[]{:S(2)}, u32[]{:S(2)}) collective-permute-start(bf16[4,48,256]{2,1,0:T(8,128)(2,1)S(1)} %compact.3.x_own), channel_id=1, source_target_pairs={{0,1},{1,0},{2,3},{3,2},{4,5},{5,4},{6,7},{7,6},{8,9},{9,8},{10,11... | collective-permute-start | bytes 294920 | tf_op jit(solution)/shard_map/ppermute | solution.py:407
  23.1 5.4 %collective-permute-start.16 = (bf16[4,48,256]{2,1,0:T(8,128)(2,1)S(1)}, bf16[4,48,256]{2,1,0:T(8,128)(2,1)S(1)}, u32[]{:S(2)}, u32[]{:S(2)}) collective-permute-start(bf16[4,48,256]{2,1,0:T(8,128)(2,1)S(1)} %compact.3.x_own), channel_id=1, source_target_pairs={{0,5},{1,4},{2,7},{3,6},{4,0},{5,1},{6,2},{7,3},{8,13},{9,12},{10,... | collective-permute-start | bytes 294920 | tf_op jit(solution)/shard_map/ppermute | solution.py:407
  25.7 5.8 %collective-permute-start.18 = (bf16[4,48,256]{2,1,0:T(8,128)(2,1)S(1)}, bf16[4,48,256]{2,1,0:T(8,128)(2,1)S(1)}, u32[]{:S(2)}, u32[]{:S(2)}) collective-permute-start(bf16[4,48,256]{2,1,0:T(8,128)(2,1)S(1)} %compact.3.x_own), channel_id=1, source_target_pairs={{0,4},{1,5},{2,6},{3,7},{4,1},{5,0},{6,3},{7,2},{8,12},{9,13},{10,... | collective-permute-start | bytes 294920 | tf_op jit(solution)/shard_map/ppermute | solution.py:407
  31.5 14.6 %copy-start.2 = (bf16[128,4096]{1,0:T(8,128)(2,1)S(1)}, bf16[128,4096]{1,0:T(8,128)(2,1)}, u32[]{:S(2)}) copy-start(bf16[128,4096]{1,0:T(8,128)(2,1)} %q_ref.3) | copy-start | bytes 3145732
  31.5 14.6 %copy-start.3 = (bf16[128,4096]{1,0:T(8,128)(2,1)S(1)}, bf16[128,4096]{1,0:T(8,128)(2,1)}, u32[]{:S(2)}) copy-start(bf16[128,4096]{1,0:T(8,128)(2,1)} %g_ref.3) | copy-start | bytes 3145732
  32.4 13.7 %copy-start = (bf16[4,512,256]{2,1,0:T(8,128)(2,1)}, bf16[4,512,256]{2,1,0:T(8,128)(2,1)S(1)}, u32[]{:S(2)}) copy-start(bf16[4,512,256]{2,1,0:T(8,128)(2,1)S(1)} %assemble.2.own_ref) | copy-start | bytes 3145732
  32.4 12.5 %collective-permute-start.19 = (bf16[4,512,256]{2,1,0:T(8,128)(2,1)S(1)}, bf16[4,512,256]{2,1,0:T(8,128)(2,1)S(1)}, u32[]{:S(2)}, u32[]{:S(2)}) collective-permute-start(bf16[4,512,256]{2,1,0:T(8,128)(2,1)S(1)} %assemble.2.own_ref), channel_id=1, source_target_pairs={{0,2},{1,3},{2,0},{3,1},{4,6},{5,7},{6,4},{7,5},{8,10},{9,11},{10,... | collective-permute-start | bytes 3145736 | tf_op jit(solution)/shard_map/ppermute | solution.py:407
  32.5 8.8 %collective-permute-start.2 = (bf16[4,32,256]{2,1,0:T(8,128)(2,1)S(1)}, bf16[4,32,256]{2,1,0:T(8,128)(2,1)S(1)}, u32[]{:S(2)}, u32[]{:S(2)}) collective-permute-start(bf16[4,32,256]{2,1,0:T(8,128)(2,1)S(1)} %get-tuple-element.51), channel_id=1, source_target_pairs={{0,8},{1,9},{2,10},{3,11},{4,12},{5,13},{6,14},{7,15},{8,0},{9,1},... | collective-permute-start | bytes 196616 | tf_op jit(solution)/shard_map/ppermute | solution.py:407
  33.3 5.9 %collective-permute-start.3 = (bf16[4,16,256]{2,1,0:T(8,128)(2,1)S(1)}, bf16[4,16,256]{2,1,0:T(8,128)(2,1)S(1)}, u32[]{:S(2)}, u32[]{:S(2)}) collective-permute-start(bf16[4,16,256]{2,1,0:T(8,128)(2,1)S(1)} %get-tuple-element.52), channel_id=1, source_target_pairs={{0,16},{1,17},{2,18},{3,19},{4,20},{5,21},{6,22},{7,23},{8,24},{9,... | collective-permute-start | bytes 98312 | tf_op jit(solution)/shard_map/ppermute | solution.py:407
  36.1 5.1 %collective-permute-start.4 = (bf16[4,16,256]{2,1,0:T(8,128)(2,1)S(1)}, bf16[4,16,256]{2,1,0:T(8,128)(2,1)S(1)}, u32[]{:S(2)}, u32[]{:S(2)}) collective-permute-start(bf16[4,16,256]{2,1,0:T(8,128)(2,1)S(1)} %get-tuple-element.52), channel_id=1, source_target_pairs={{0,24},{1,25},{2,26},{3,27},{4,28},{5,29},{6,30},{7,31},{8,16},{9,... | collective-permute-start | bytes 98312 | tf_op jit(solution)/shard_map/ppermute | solution.py:407
  37.3 17.7 %collective-permute-start.6 = (bf16[4,64,256]{2,1,0:T(8,128)(2,1)S(1)}, bf16[4,64,256]{2,1,0:T(8,128)(2,1)S(1)}, u32[]{:S(2)}, u32[]{:S(2)}) collective-permute-start(bf16[4,64,256]{2,1,0:T(8,128)(2,1)S(1)} %get-tuple-element.50._.mid_own), channel_id=1, source_target_pairs={{0,5},{1,4},{2,7},{3,6},{4,0},{5,1},{6,2},{7,3},{8,13},{9,12},{10,... | collective-permute-start | bytes 393224 | tf_op jit(solution)/shard_map/ppermute | solution.py:407
  39.2 15.8 %collective-permute-start.8 = (bf16[4,64,256]{2,1,0:T(8,128)(2,1)S(1)}, bf16[4,64,256]{2,1,0:T(8,128)(2,1)S(1)}, u32[]{:S(2)}, u32[]{:S(2)}) collective-permute-start(bf16[4,64,256]{2,1,0:T(8,128)(2,1)S(1)} %get-tuple-element.50._.mid_own), channel_id=1, source_target_pairs={{0,4},{1,5},{2,6},{3,7},{4,1},{5,0},{6,3},{7,2},{8,12},{9,13},{10,... | collective-permute-start | bytes 393224 | tf_op jit(solution)/shard_map/ppermute | solution.py:407
  41.3 20.2 %collective-permute-start.1 = (bf16[128,1024]{1,0:T(8,128)(2,1)S(1)}, bf16[128,1024]{1,0:T(8,128)(2,1)S(1)}, u32[]{:S(2)}, u32[]{:S(2)}) collective-permute-start(bf16[128,1024]{1,0:T(8,128)(2,1)S(1)} %pad_maximum_fusion.pair.pair_ref), channel_id=1, source_target_pairs={{0,1},{1,0},{2,3},{3,2},{4,5},{5,4},{6,7},{7,6},{8,9},{9,8},{10,11... | collective-permute-start | bytes 786440 | tf_op jit(solution)/shard_map/ppermute | solution.py:407
  41.3 14.6 %collective-permute-start.5 = (bf16[4,48,256]{2,1,0:T(8,128)(2,1)S(1)}, bf16[4,48,256]{2,1,0:T(8,128)(2,1)S(1)}, u32[]{:S(2)}, u32[]{:S(2)}) collective-permute-start(bf16[4,48,256]{2,1,0:T(8,128)(2,1)S(1)} %compact.2.refs_0_.x_own), channel_id=1, source_target_pairs={{0,1},{1,0},{2,3},{3,2},{4,5},{5,4},{6,7},{7,6},{8,9},{9,8},{10,11... | collective-permute-start | bytes 294920 | tf_op jit(solution)/shard_map/ppermute | solution.py:407
  44.9 1.2 %copy-start.4 = (bf16[4,512,256]{2,1,0:T(8,128)(2,1)}, bf16[4,512,256]{2,1,0:T(8,128)(2,1)S(1)}, u32[]{:S(2)}) copy-start(bf16[4,512,256]{2,1,0:T(8,128)(2,1)S(1)} %collective-permute-done.19.other_ref) | copy-start | bytes 3145732
  44.9 11.0 %collective-permute-start.7 = (bf16[4,48,256]{2,1,0:T(8,128)(2,1)S(1)}, bf16[4,48,256]{2,1,0:T(8,128)(2,1)S(1)}, u32[]{:S(2)}, u32[]{:S(2)}) collective-permute-start(bf16[4,48,256]{2,1,0:T(8,128)(2,1)S(1)} %compact.2.refs_0_.x_own), channel_id=1, source_target_pairs={{0,5},{1,4},{2,7},{3,6},{4,0},{5,1},{6,2},{7,3},{8,13},{9,12},{10,... | collective-permute-start | bytes 294920 | tf_op jit(solution)/shard_map/ppermute | solution.py:407
  55.0 7.4 %collective-permute-start.21 = (bf16[4,512,256]{2,1,0:T(8,128)(2,1)S(1)}, bf16[4,512,256]{2,1,0:T(8,128)(2,1)S(1)}, u32[]{:S(2)}, u32[]{:S(2)}) collective-permute-start(bf16[4,512,256]{2,1,0:T(8,128)(2,1)S(1)} %get-tuple-element.61), channel_id=1, source_target_pairs={{0,2},{1,3},{2,0},{3,1},{4,6},{5,7},{6,4},{7,5},{8,10},{9,11},{10,... | collective-permute-start | bytes 3145736 | tf_op jit(solution)/shard_map/ppermute | solution.py:407
  55.0 6.4 %collective-permute-start.9 = (bf16[4,48,256]{2,1,0:T(8,128)(2,1)S(1)}, bf16[4,48,256]{2,1,0:T(8,128)(2,1)S(1)}, u32[]{:S(2)}, u32[]{:S(2)}) collective-permute-start(bf16[4,48,256]{2,1,0:T(8,128)(2,1)S(1)} %compact.2.refs_0_.x_own), channel_id=1, source_target_pairs={{0,4},{1,5},{2,6},{3,7},{4,1},{5,0},{6,3},{7,2},{8,12},{9,13},{10,... | collective-permute-start | bytes 294920 | tf_op jit(solution)/shard_map/ppermute | solution.py:407
  62.3 1.0 copy-start.1
  62.3 9.0 %collective-permute-start.20 = (bf16[4,512,256]{2,1,0:T(8,128)(2,1)S(1)}, bf16[4,512,256]{2,1,0:T(8,128)(2,1)S(1)}, u32[]{:S(2)}, u32[]{:S(2)}) collective-permute-start(bf16[4,512,256]{2,1,0:T(8,128)(2,1)S(1)} %assemble.3.own_ref), channel_id=1, source_target_pairs={{0,2},{1,3},{2,0},{3,1},{4,6},{5,7},{6,4},{7,5},{8,10},{9,11},{10,... | collective-permute-start | bytes 3145736 | tf_op jit(solution)/shard_map/ppermute | solution.py:407
  63.3 7.2 %collective-permute-start.22 = (bf16[4,48,256]{2,1,0:T(8,128)(2,1)S(1)}, bf16[4,48,256]{2,1,0:T(8,128)(2,1)S(1)}, u32[]{:S(2)}, u32[]{:S(2)}) collective-permute-start(bf16[4,48,256]{2,1,0:T(8,128)(2,1)S(1)} %get-tuple-element.63), channel_id=1, source_target_pairs={{0,1},{1,0},{2,3},{3,2},{4,5},{5,4},{6,7},{7,6},{8,9},{9,8},{10,11... | collective-permute-start | bytes 294920 | tf_op jit(solution)/shard_map/ppermute | solution.py:407
  63.3 17.8 %collective-permute-start.23 = (bf16[4,112,256]{2,1,0:T(8,128)(2,1)S(1)}, bf16[4,112,256]{2,1,0:T(8,128)(2,1)S(1)}, u32[]{:S(2)}, u32[]{:S(2)}) collective-permute-start(bf16[4,112,256]{2,1,0:T(8,128)(2,1)S(1)} %get-tuple-element.69), channel_id=1, source_target_pairs={{0,4},{1,5},{2,6},{3,7},{4,1},{5,0},{6,3},{7,2},{8,12},{9,13},{10,... | collective-permute-start | bytes 688136 | tf_op jit(solution)/shard_map/ppermute | solution.py:407
  63.9 17.2 %collective-permute-start.24 = (bf16[4,112,256]{2,1,0:T(8,128)(2,1)S(1)}, bf16[4,112,256]{2,1,0:T(8,128)(2,1)S(1)}, u32[]{:S(2)}, u32[]{:S(2)}) collective-permute-start(bf16[4,112,256]{2,1,0:T(8,128)(2,1)S(1)} %get-tuple-element.70), channel_id=1, source_target_pairs={{0,5},{1,4},{2,7},{3,6},{4,0},{5,1},{6,2},{7,3},{8,13},{9,12},{10,... | collective-permute-start | bytes 688136 | tf_op jit(solution)/shard_map/ppermute | solution.py:407
  71.3 1.0 copy-start.5
  81.1 2.7 %collective-permute-start.25 = (bf16[4,512,256]{2,1,0:T(8,128)(2,1)S(1)}, bf16[4,512,256]{2,1,0:T(8,128)(2,1)S(1)}, u32[]{:S(2)}, u32[]{:S(2)}) collective-permute-start(bf16[4,512,256]{2,1,0:T(8,128)(2,1)S(1)} %get-tuple-element.71), channel_id=1, source_target_pairs={{0,2},{1,3},{2,0},{3,1},{4,6},{5,7},{6,4},{7,5},{8,10},{9,11},{10,... | collective-permute-start | bytes 3145736 | tf_op jit(solution)/shard_map/ppermute | solution.py:407
  84.1 7.1 %collective-permute-start.26 = (bf16[4,48,256]{2,1,0:T(8,128)(2,1)S(1)}, bf16[4,48,256]{2,1,0:T(8,128)(2,1)S(1)}, u32[]{:S(2)}, u32[]{:S(2)}) collective-permute-start(bf16[4,48,256]{2,1,0:T(8,128)(2,1)S(1)} %get-tuple-element.74), channel_id=1, source_target_pairs={{0,1},{1,0},{2,3},{3,2},{4,5},{5,4},{6,7},{7,6},{8,9},{9,8},{10,11... | collective-permute-start | bytes 294920 | tf_op jit(solution)/shard_map/ppermute | solution.py:407
  84.2 8.9 %collective-permute-start.28 = (bf16[4,112,256]{2,1,0:T(8,128)(2,1)S(1)}, bf16[4,112,256]{2,1,0:T(8,128)(2,1)S(1)}, u32[]{:S(2)}, u32[]{:S(2)}) collective-permute-start(bf16[4,112,256]{2,1,0:T(8,128)(2,1)S(1)} %get-tuple-element.75), channel_id=1, source_target_pairs={{0,5},{1,4},{2,7},{3,6},{4,0},{5,1},{6,2},{7,3},{8,13},{9,12},{10,... | collective-permute-start | bytes 688136 | tf_op jit(solution)/shard_map/ppermute | solution.py:407
  86.0 10.2 %collective-permute-start.29 = (bf16[4,112,256]{2,1,0:T(8,128)(2,1)S(1)}, bf16[4,112,256]{2,1,0:T(8,128)(2,1)S(1)}, u32[]{:S(2)}, u32[]{:S(2)}) collective-permute-start(bf16[4,112,256]{2,1,0:T(8,128)(2,1)S(1)} %get-tuple-element.76), channel_id=1, source_target_pairs={{0,4},{1,5},{2,6},{3,7},{4,1},{5,0},{6,3},{7,2},{8,12},{9,13},{10,... | collective-permute-start | bytes 688136 | tf_op jit(solution)/shard_map/ppermute | solution.py:407
  86.3 17.3 %collective-permute-start.33 = (bf16[4,128,256]{2,1,0:T(8,128)(2,1)S(1)}, bf16[4,128,256]{2,1,0:T(8,128)(2,1)S(1)}, u32[]{:S(2)}, u32[]{:S(2)}) collective-permute-start(bf16[4,128,256]{2,1,0:T(8,128)(2,1)S(1)} %place.2.refs_2_), channel_id=1, source_target_pairs={{0,1},{1,0},{2,3},{3,2},{4,5},{5,4},{6,7},{7,6},{8,9},{9,8},{10,11... | collective-permute-start | bytes 786440 | tf_op jit(solution)/shard_map/ppermute | solution.py:407
  92.0 15.6 %collective-permute-start.27 = (bf16[4,128,256]{2,1,0:T(8,128)(2,1)S(1)}, bf16[4,128,256]{2,1,0:T(8,128)(2,1)S(1)}, u32[]{:S(2)}, u32[]{:S(2)}) collective-permute-start(bf16[4,128,256]{2,1,0:T(8,128)(2,1)S(1)} %place.3), channel_id=1, source_target_pairs={{0,1},{1,0},{2,3},{3,2},{4,5},{5,4},{6,7},{7,6},{8,9},{9,8},{10,11... | collective-permute-start | bytes 786440 | tf_op jit(solution)/shard_map/ppermute | solution.py:407
  92.2 10.2 %collective-permute-start.34 = (bf16[4,32,256]{2,1,0:T(8,128)(2,1)S(1)}, bf16[4,32,256]{2,1,0:T(8,128)(2,1)S(1)}, u32[]{:S(2)}, u32[]{:S(2)}) collective-permute-start(bf16[4,32,256]{2,1,0:T(8,128)(2,1)S(1)} %get-tuple-element.83), channel_id=1, source_target_pairs={{0,8},{1,9},{2,10},{3,11},{4,12},{5,13},{6,14},{7,15},{8,0},{9,1},... | collective-permute-start | bytes 196616 | tf_op jit(solution)/shard_map/ppermute | solution.py:407
  93.1 5.4 %collective-permute-start.35 = (bf16[4,16,256]{2,1,0:T(8,128)(2,1)S(1)}, bf16[4,16,256]{2,1,0:T(8,128)(2,1)S(1)}, u32[]{:S(2)}, u32[]{:S(2)}) collective-permute-start(bf16[4,16,256]{2,1,0:T(8,128)(2,1)S(1)} %get-tuple-element.84), channel_id=1, source_target_pairs={{0,16},{1,17},{2,18},{3,19},{4,20},{5,21},{6,22},{7,23},{8,24},{9,... | collective-permute-start | bytes 98312 | tf_op jit(solution)/shard_map/ppermute | solution.py:407
  96.2 5.1 %collective-permute-start.36 = (bf16[4,16,256]{2,1,0:T(8,128)(2,1)S(1)}, bf16[4,16,256]{2,1,0:T(8,128)(2,1)S(1)}, u32[]{:S(2)}, u32[]{:S(2)}) collective-permute-start(bf16[4,16,256]{2,1,0:T(8,128)(2,1)S(1)} %get-tuple-element.85), channel_id=1, source_target_pairs={{0,24},{1,25},{2,26},{3,27},{4,28},{5,29},{6,30},{7,31},{8,16},{9,... | collective-permute-start | bytes 98312 | tf_op jit(solution)/shard_map/ppermute | solution.py:407
  98.5 9.1 %collective-permute-start.30 = (bf16[4,32,256]{2,1,0:T(8,128)(2,1)S(1)}, bf16[4,32,256]{2,1,0:T(8,128)(2,1)S(1)}, u32[]{:S(2)}, u32[]{:S(2)}) collective-permute-start(bf16[4,32,256]{2,1,0:T(8,128)(2,1)S(1)} %get-tuple-element.78), channel_id=1, source_target_pairs={{0,8},{1,9},{2,10},{3,11},{4,12},{5,13},{6,14},{7,15},{8,0},{9,1},... | collective-permute-start | bytes 196616 | tf_op jit(solution)/shard_map/ppermute | solution.py:407
  101.3 5.4 %collective-permute-start.31 = (bf16[4,16,256]{2,1,0:T(8,128)(2,1)S(1)}, bf16[4,16,256]{2,1,0:T(8,128)(2,1)S(1)}, u32[]{:S(2)}, u32[]{:S(2)}) collective-permute-start(bf16[4,16,256]{2,1,0:T(8,128)(2,1)S(1)} %get-tuple-element.79), channel_id=1, source_target_pairs={{0,16},{1,17},{2,18},{3,19},{4,20},{5,21},{6,22},{7,23},{8,24},{9,... | collective-permute-start | bytes 98312 | tf_op jit(solution)/shard_map/ppermute | solution.py:407
  102.4 5.1 %collective-permute-start.32 = (bf16[4,16,256]{2,1,0:T(8,128)(2,1)S(1)}, bf16[4,16,256]{2,1,0:T(8,128)(2,1)S(1)}, u32[]{:S(2)}, u32[]{:S(2)}) collective-permute-start(bf16[4,16,256]{2,1,0:T(8,128)(2,1)S(1)} %get-tuple-element.80), channel_id=1, source_target_pairs={{0,24},{1,25},{2,26},{3,27},{4,28},{5,29},{6,30},{7,31},{8,16},{9,... | collective-permute-start | bytes 98312 | tf_op jit(solution)/shard_map/ppermute | solution.py:407

commit v3 on v1

v3 whole, which is shorter than its diff:
```python
import functools

import jax
import jax.numpy as jnp
from jax import lax
from jax.experimental import pallas as pl
from jax.experimental.pallas import tpu as pltpu
from jax.sharding import PartitionSpec as P

D = 128
GROUPS = 8
HEADS = 4
TOKENS = 128
TOGETHER = 4
WIDE = HEADS * D
SCALE = D ** (-0.5)
LOG2E = 1.4426950408889634
AXES = ("ctx", "head")
BF = jnp.bfloat16
F32 = jnp.float32
ANY_ROWS = ((0, 64, 1), (64, 96, 2), (96, 112, 3), (112, 120, 4))
VMEM_LIMIT = 24 * 1024 * 1024
GRID_LIMIT = 61 * 1024 * 1024


def dot(a, b):
    return lax.dot_general(a, b, (((1,), (0,)), ((), ())), preferred_element_type=F32)


def dot_nt(a, b):
    return lax.dot_general(a, b, (((1,), (1,)), ((), ())), preferred_element_type=F32)


def dot_tn(a, b):
    return lax.dot_general(a, b, (((0,), (0,)), ((), ())), preferred_element_type=F32)


def one_hot(mask):
    return jnp.where(mask, 1.0, 0.0).astype(BF)


def selected_token(row, offs, group):
    token = jnp.full(row.shape, -1, jnp.int32)
    for start, stop, level in ANY_ROWS:
        inside = (row >= start) & (row < stop)
        token = jnp.where(inside, (row - start) * 2**level + offs[level, group], token)
    return token


def selector(offs, group):
    shape = (128, TOKENS)
    row = lax.broadcasted_iota(jnp.int32, shape, 0)
    return one_hot(selected_token(row, offs, group) == lax.broadcasted_iota(jnp.int32, shape, 1))


def placer(offs, group):
    shape = (TOKENS, 128)
    row = lax.broadcasted_iota(jnp.int32, shape, 1)
    return one_hot(selected_token(row, offs, group) == lax.broadcasted_iota(jnp.int32, shape, 0))


def group_rows(keys_ref, values_ref, group):
    lanes = slice(group * D, (group + 1) * D)
    return jnp.concatenate([keys_ref[:, lanes], values_ref[:, lanes]], 1)


def select_kernel(offs, keys, values, first, middle, tail, last):
    for g in range(GROUPS):
        rows = dot(selector(offs, g), group_rows(keys, values, g))
        first[g] = rows[0:64].astype(BF)
        middle[g] = rows[64:128].astype(BF)
        tail[g] = rows[96:128].astype(BF)
        last[g] = rows[112:128].astype(BF)


def compact_kernel(middle, one, two, three, lift, extra):
    for g in range(GROUPS):
        mine, a, b, c = [ref[g].astype(F32) for ref in (middle, one, two, three)]
        last = [a[16:24], b[:8], c[:8]]
        lift[g] = jnp.concatenate([mine[0:48], a[0:16], mine[48:56]] + last, 0).astype(BF)
        extra[g] = jnp.concatenate([a[0:16]] + last + [jnp.zeros((8, 2 * D), F32)], 0).astype(BF)


def assemble_kernel(offs, first, lift, keys, values, x_far, lift_up, lift_down, _, held):
    for g in range(GROUPS):
        far = dot(selector(offs, g), group_rows(keys, values, g))
        extra = x_far[g].astype(F32)
        across = jnp.concatenate([far[64:112], extra[0:16], far[112:120], extra[16:40]], 0)
        lifts = [lift[g].astype(F32), across, lift_up[g].astype(F32), lift_down[g].astype(F32)]
        rows = [first[g].astype(F32), far[0:64]]
        for a, b in ((0, 32), (32, 64), (64, 96)):
            rows += [x[a:b] for x in lifts]
        held[g] = jnp.concatenate(rows, 0).astype(BF)


def by_level(rows):
    parts = []
    for start, stop in ((0, 64), (64, 96), (96, 112), (112, 120), (120, 128)):
        parts += [rows[start:stop, h * D : (h + 1) * D] for h in range(HEADS)]
    return jnp.concatenate(parts, 0)


def by_selection(rows):
    heads = []
    for h in range(HEADS):
        parts = []
        base = 0
        for count in (64, 32, 16, 8, 8):
            parts.append(rows[base + h * count : base + (h + 1) * count])
            base += HEADS * count
        heads.append(jnp.concatenate(parts, 0))
    return jnp.concatenate(heads, 1)


def heads_to_lanes(x):
    count = x.shape[0] // HEADS
    lane = lax.broadcasted_iota(jnp.int32, (count, 128), 1) & (HEADS - 1)
    out = x[(HEADS - 1) * count :]
    for h in range(HEADS - 1):
        out = jnp.where(lane == h, x[h * count : (h + 1) * count], out)
    return out


def wide_lanes(j):
    return slice(j * WIDE, (j + 1) * WIDE)


def by_head(rows):
    return jnp.concatenate([rows[:, h * D : (h + 1) * D] for h in range(HEADS)], 0)


def by_token(rows):
    count = rows.shape[0] // HEADS
    return jnp.concatenate([rows[h * count : (h + 1) * count] for h in range(HEADS)], 1)


def expand(x):
    return jnp.concatenate([jnp.broadcast_to(x[:, h : h + 1], x.shape) for h in range(HEADS)], 0)


def beside(x):
    high = x.astype(BF).astype(F32)
    lane = lax.broadcasted_iota(jnp.int32, x.shape, 1)
    both = jnp.where(lane < 64, high, x - high)
    return jnp.concatenate(
        [jnp.where((lane & (HEADS - 1)) == h, both, 0.0) for h in range(HEADS)], 0
    ).astype(BF)


def minus_lanes():
    lane = lax.broadcasted_iota(jnp.int32, (2 * D, D), 1)
    return jnp.where((lane & 63) < HEADS, -1.0, 0.0).astype(BF)


def forward(queries, keys, values):
    ones = jnp.ones((2 * D, D), BF)
    scores = [dot_nt(q, k) * (SCALE * LOG2E) for q, k in zip(queries, keys)]
    peaks = [jnp.max(x, 1, keepdims=True) for x in scores]
    powers = [jnp.exp2(x - p).astype(BF) for x, p in zip(scores, peaks)]
    outs = [dot(p, jnp.concatenate([v, ones], 1)) for p, v in zip(powers, values)]
    peaks = [heads_to_lanes(jnp.broadcast_to(p, (p.shape[0], 128))) for p in peaks]
    lses = [p + jnp.log2(heads_to_lanes(out[:, D:])) for p, out in zip(peaks, outs)]
    return powers, peaks, lses, [out[:, :D] for out in outs]


def backward(queries, scaled, keys, values, powers, shifts):
    minus = minus_lanes()
    weights = [
        dot_nt(jnp.concatenate([g, beside(d)], 1), jnp.concatenate([v, minus], 1))
        for g, d, v in zip(scaled, shifts, values)
    ]
    scores = [(p.astype(F32) * w).astype(BF) for p, w in zip(powers, weights)]
    grad_values = [dot_tn(g, p).T for g, p in zip(scaled, powers)]
    grad_keys = [dot_tn(q, x).T * SCALE for q, x in zip(queries, scores)]
    pairs = [jnp.concatenate(pair, 1).astype(BF) for pair in zip(grad_keys, grad_values)]
    return pairs, [dot(x, k) * SCALE for x, k in zip(scores, keys)]


def whole_rows(own_ref, far_ref, j):
    lanes = slice(j * D, (j + 1) * D)
    return jnp.concatenate([own_ref[:, lanes], far_ref[:, lanes]], 0)


def level0_kernel(q_ref, k_ref, v_ref, kp_ref, vp_ref, *refs):
    power_ref, peak_ref, lse_ref, out_ref = refs[-4:]
    members = range(TOGETHER)
    queries = [by_head(q_ref[:, wide_lanes(j)]) for j in members]
    keys = [whole_rows(k_ref, kp_ref, j) for j in members]
    values = [whole_rows(v_ref, vp_ref, j) for j in members]
    for j, (power, peak, lse, out) in enumerate(zip(*forward(queries, keys, values))):
        power_ref[j], peak_ref[j], lse_ref[j], out_ref[j] = power, peak, lse, out


def attention_kernel(
    offs, q_ref, g_ref, own_ref, other_ref, peak_ref, lse_ref, out_ref,
    att_ref, part_ref, down_ref, dother_ref, factor_ref, shift_ref, level_ref, token_ref, delta_ref,
):
    members = range(TOGETHER)
    first_group = pl.program_id(0) * TOGETHER
    bounds = ((0, 256), (256, 384), (384, 448), (448, 480))
    starts = [[(offs[k, first_group + j], 128 >> k) for k in range(1, 5)] for j in members]

    def selected(ref):
        rows = [dot(selector(offs, first_group + j), ref[:, wide_lanes(j)]) for j in members]
        rows = [by_level(x).astype(BF) for x in rows]
        return [[x[a:b] for x in rows] for a, b in bounds]

    def kept(k, lanes):
        at = slice(128 * k, 128 * k + 128)
        return [jnp.concatenate([own_ref[j, at, lanes], other_ref[j, at, lanes]], 0) for j in members]

    def for_levels(ref, xs):
        for j, x in enumerate(xs):
            ref[j] = x
        return [
            [ref[j, pl.ds(starts[j][k][0], starts[j][k][1], 2 ** (k + 1)), :] for j in members]
            for k in range(4)
        ]

    def place(parts):
        rows = [jnp.concatenate(list(p) + [jnp.zeros((32, D), F32)], 0) for p in zip(*parts)]
        rows = [by_selection(x).astype(BF) for x in rows]
        return [dot(placer(offs, first_group + j), r) for j, r in enumerate(rows)]

    level_ref[...] = jnp.full(level_ref.shape, -1e30, F32)
    queries, grads = selected(q_ref), selected(g_ref)
    keys = [kept(k, slice(0, D)) for k in range(4)]
    values = [kept(k, slice(D, 2 * D)) for k in range(4)]
    results = [forward(queries[k], keys[k], values[k]) for k in range(4)]

    for k in range(4):
        for j in members:
            start, count = starts[j][k]
            level_ref[j, k, pl.ds(start, count, 2 ** (k + 1)), :] = results[k][2][j]
    firsts = [lse_ref[j] for j in members]
    tops = [functools.reduce(jnp.maximum, [level_ref[j, k] for k in range(4)], firsts[j]) for j in members]
    sums = [
        jnp.exp2(firsts[j] - tops[j]) + sum(jnp.exp2(level_ref[j, k] - tops[j]) for k in range(4))
        for j in members
    ]
    merged = [top + jnp.log2(x) for top, x in zip(tops, sums)]
    factors = [
        [jnp.exp2(p - m) for p, m in zip(results[k][1], column)]
        for k, column in enumerate(for_levels(token_ref, merged))
    ]
    spread = [[expand(f) for f in fs] for fs in factors]
    placed = place([[out * f for out, f in zip(results[k][3], spread[k])] for k in range(4)])
    deltas = []
    for j in members:
        factor = jnp.exp2(peak_ref[j] - merged[j])
        attended = (placed[j] + by_token(out_ref[j] * expand(factor))).astype(BF)
        att_ref[:, wide_lanes(j)] = attended
        product = g_ref[:, wide_lanes(j)].astype(F32) * attended.astype(F32)
        total = [
            jnp.broadcast_to(jnp.sum(product[:, h * D : (h + 1) * D], 1, keepdims=True), (TOKENS, 128))
            for h in range(HEADS)
        ]
        deltas.append(heads_to_lanes(jnp.concatenate(total, 0)))
        factor_ref[j] = factor
        shift_ref[j] = factor * deltas[j]
    shifts = [
        [f * d for f, d in zip(factors[k], column)] for k, column in enumerate(for_levels(delta_ref, deltas))
    ]
    scaled = [
        [(g.astype(F32) * f).astype(BF) for g, f in zip(grads[k], spread[k])] for k in range(4)
    ]
    parts = []
    for k in range(4):
        pairs, part = backward(queries[k], scaled[k], keys[k], values[k], results[k][0], shifts[k])
        parts.append(part)
        for j in members:
            down_ref[j, 128 * k : 128 * k + 128] = pairs[j][:128]
            dother_ref[j, 128 * k : 128 * k + 128] = pairs[j][128:]
    for j, x in enumerate(place(parts)):
        part_ref[:, wide_lanes(j)] = x


def return0_kernel(
    q_ref, g_ref, k_ref, v_ref, kp_ref, vp_ref, power_ref, factor_ref, shift_ref, part_ref, *refs
):
    dq_ref, d0_ref = refs[-2:]
    members = range(TOGETHER)
    queries = [by_head(q_ref[:, wide_lanes(j)]) for j in members]
    keys = [whole_rows(k_ref, kp_ref, j) for j in members]
    values = [whole_rows(v_ref, vp_ref, j) for j in members]
    scaled = [
        (by_head(g_ref[:, wide_lanes(j)]).astype(F32) * expand(factor_ref[j])).astype(BF) for j in members
    ]
    powers, shifts = [power_ref[j] for j in members], [shift_ref[j] for j in members]
    pairs, parts = backward(queries, scaled, keys, values, powers, shifts)
    for j in members:
        d0_ref[j] = pairs[j]
        dq_ref[:, wide_lanes(j)] = (by_token(parts[j]) + part_ref[:, wide_lanes(j)]).astype(BF)


def reduce_kernel(mine, theirs, rows_kept, rows_far, up, down, x_far, x_kept):
    zero = jnp.zeros((8, 2 * D), F32)
    for g in range(GROUPS):
        total = mine[g].astype(F32) + theirs[g].astype(F32)
        for z, ref in enumerate((rows_kept, rows_far, up, down)):
            second, third, fourth = [total[s + 32 * z : s + 32 * z + 32] for s in (128, 256, 384)]
            if z >= 2:
                ref[g] = jnp.concatenate([second, third, fourth], 0).astype(BF)
                continue
            rows = [total[64 * z : 64 * z + 64], second, third[:16], fourth[:8], zero]
            ref[g] = jnp.concatenate(rows, 0).astype(BF)
            extra = jnp.concatenate([third[16:], fourth[8:], zero], 0)
            if z == 0:
                x_kept[g] = extra
            else:
                x_far[g] = extra.astype(BF)


def place_kernel(offs, d0, rows_far, far):
    for g in range(GROUPS):
        far[g] = (d0[g, 128:256].astype(F32) + dot(placer(offs, g), rows_far[g])).astype(BF)


def cross_kernel(kept, far, up, down, one, two, three):
    zero = jnp.zeros((8, 2 * D), F32)
    for g in range(GROUPS):
        sides = up[g].astype(F32) + down[g].astype(F32)
        total = kept[g] + far[g].astype(F32)
        third = total[0:16] + sides[48:64]
        fourth = total[16:40] + sides[72:96]
        one[g] = jnp.concatenate([third, fourth[0:8], zero], 0).astype(BF)
        two[g] = jnp.concatenate([fourth[8:16], zero], 0).astype(BF)
        three[g] = jnp.concatenate([fourth[16:24], zero], 0).astype(BF)


def finish_kernel(offs, d0, rows_kept, far, up, down, one, two, three, dk_ref, dv_ref):
    for g in range(GROUPS):
        kept = rows_kept[g].astype(F32)
        sides = up[g].astype(F32) + down[g].astype(F32)
        a, b, c = one[g].astype(F32), two[g].astype(F32), three[g].astype(F32)
        rows = jnp.concatenate(
            [
                kept[0:64],
                kept[64:96] + sides[0:32],
                kept[96:112] + sides[32:48] + a[0:16],
                kept[112:120] + sides[64:72] + a[16:24] + b[0:8] + c[0:8],
                jnp.zeros((8, 2 * D), F32),
            ],
            0,
        ).astype(BF)
        whole = d0[g, 0:128].astype(F32) + far[g].astype(F32) + dot(placer(offs, g), rows)
        dk_ref[:, g * D : (g + 1) * D] = whole[:, :D].astype(BF)
        dv_ref[:, g * D : (g + 1) * D] = whole[:, D:].astype(BF)


def whole_call(body, name, outs, offs, *arrays, after=()):
    specs = [pl.BlockSpec(memory_space=pltpu.VMEM)] * len(arrays)
    specs += [pl.BlockSpec(memory_space=pl.ANY)] * len(after)
    arrays = arrays + tuple(after)
    if offs is not None:
        specs = [pl.BlockSpec(memory_space=pltpu.SMEM)] + specs
        arrays = (offs,) + arrays
    shapes = [jax.ShapeDtypeStruct(shape, dtype) for shape, dtype in outs]
    return pl.pallas_call(
        body,
        name=name,
        out_shape=shapes,
        in_specs=specs,
        out_specs=[pl.BlockSpec(memory_space=pltpu.VMEM)] * len(shapes),
        cost_estimate=pl.CostEstimate(flops=0, bytes_accessed=4 * 10**6, transcendentals=0),
        compiler_params=pltpu.CompilerParams(vmem_limit_bytes=VMEM_LIMIT),
    )(*arrays)


def grid_call(body, name, offs, inputs, outs, scratch=(), after=()):
    def spec(shape):
        if len(shape) == 2:
            return pl.BlockSpec((TOKENS, shape[1] * TOGETHER // GROUPS), lambda i: (0, i))
        return pl.BlockSpec((TOGETHER,) + shape[1:], lambda i: (i, 0, 0))

    specs = [spec(x.shape) for x in inputs] + [pl.BlockSpec(memory_space=pl.ANY)] * len(after)
    arrays = tuple(inputs) + tuple(after)
    if offs is not None:
        specs = [pl.BlockSpec(memory_space=pltpu.SMEM)] + specs
        arrays = (offs,) + arrays
    return pl.pallas_call(
        body,
        name=name,
        grid=(GROUPS // TOGETHER,),
        in_specs=specs,
        out_specs=[spec(shape) for shape, _ in outs],
        out_shape=[jax.ShapeDtypeStruct(shape, dtype) for shape, dtype in outs],
        scratch_shapes=list(scratch),
        cost_estimate=pl.CostEstimate(flops=4 * 10**9, bytes_accessed=16 * 10**6, transcendentals=10**6),
        compiler_params=pltpu.CompilerParams(vmem_limit_bytes=GRID_LIMIT),
    )(*arrays)


def routes(count):
    def along_z(i, step):
        z = ((i & 1) * 2 + (i >> 2 & 1) + step) % 4
        return (i & ~5) | (z & 1) << 2 | z >> 1

    table = {
        "head": lambda i: i ^ 1,
        "core": lambda i: i ^ 2,
        "up": lambda i: along_z(i, 1),
        "down": lambda i: along_z(i, -1),
        "x1": lambda i: i ^ 8,
        "x2": lambda i: i ^ 16,
        "x3": lambda i: i ^ 24,
    }
    return {name: [(i, to(i)) for i in range(count)] for name, to in table.items()}


def shards(count, queries, key_rows, value_rows, gradient, level_offsets):
    route = routes(count)

    def send(x, name):
        return lax.ppermute(x, AXES, route[name])

    other_offsets = send(level_offsets, "head")
    low = lax.axis_index("head") == 0
    offs = jnp.where(
        low,
        jnp.concatenate([level_offsets, other_offsets], 1),
        jnp.concatenate([other_offsets, level_offsets], 1),
    )
    key_swap, value_swap, other_offsets = lax.optimization_barrier((key_rows, value_rows, other_offsets))
    far_keys = send(key_swap, "head")
    far_values = send(value_swap, "head")

    rows = lambda n, dtype=BF: ((GROUPS, n, 2 * D), dtype)
    packed = ((GROUPS, TOKENS, 128), F32)
    wide = lambda dtype: ((TOKENS, GROUPS * WIDE), dtype)
    first, middle, tail, last = whole_call(
        select_kernel, "select", [rows(64), rows(64), rows(32), rows(16)], offs, key_rows, value_rows
    )
    lift, extra = whole_call(
        compact_kernel, "compact", [rows(96), rows(48)], None,
        middle, send(tail, "x1"), send(last, "x2"), send(last, "x3"),
    )
    lift_down = send(lift, "up")
    lift_up = send(lift, "down")
    extra_far = send(extra, "head")
    power0, peak0, lse0, out0 = grid_call(
        level0_kernel, "level0", None, [queries, key_rows, value_rows, far_keys, far_values],
        [rows(512), packed, packed, ((GROUPS, 512, 128), F32)], after=(extra,),
    )
    (own,) = whole_call(
        assemble_kernel, "assemble", [rows(512)], offs, first, lift, far_keys, far_values,
        extra_far, lift_up, lift_down, after=(lse0,),
    )
    other = send(own, "core")
    stats = pltpu.VMEM((TOGETHER, TOKENS, 128), F32)
    attended, part, down_own, down_other, factor0, shift0 = grid_call(
        attention_kernel, "attention", offs, [queries, gradient, own, other, peak0, lse0, out0],
        [wide(BF), wide(F32), rows(512), rows(512), packed, packed],
        scratch=[pltpu.VMEM((TOGETHER, 4, TOKENS, 128), F32), stats, stats],
    )
    theirs = send(down_other, "core")
    rows_kept, rows_far, up, down, x_far, x_kept = whole_call(
        reduce_kernel, "reduce", [rows(128), rows(128), rows(96), rows(96), rows(48), rows(48, F32)],
        None, down_own, theirs,
    )
    from_down = send(up, "up")
    from_up = send(down, "down")
    x_far = send(x_far, "head")
    grad_queries, d0 = grid_call(
        return0_kernel, "return0", None,
        [queries, gradient, key_rows, value_rows, far_keys, far_values, power0, factor0, shift0, part],
        [wide(BF), rows(256)], after=(x_far,),
    )
    (far,) = whole_call(place_kernel, "place", [rows(128)], offs, d0, rows_far)
    far = send(far, "head")
    one, two, three = whole_call(
        cross_kernel, "cross", [rows(32), rows(16), rows(16)], None, x_kept, x_far, from_up, from_down
    )
    one, two, three = send(one, "x1"), send(two, "x2"), send(three, "x3")
    out = ((TOKENS, GROUPS * D), BF)
    grad_keys, grad_values = whole_call(
        finish_kernel, "finish", [out, out], offs, d0, rows_kept, far, from_up, from_down, one, two, three
    )
    return (attended, grad_queries, grad_keys, grad_values)


def solution(mesh):
    rows = P(AXES, None)
    return jax.shard_map(
        functools.partial(shards, mesh.size),
        mesh=mesh,
        in_specs=(rows, rows, rows, rows, P(None, "head")),
        out_specs=(rows, rows, rows, rows),
        check_vma=False,
    )
```

time: 111 us -> 106 us (0.955)
  local copies, waits for them, and re-layouts: 5.63 us -> 15.2 us
  starting transfers between devices: 32.8 us -> 26.5 us
  waiting for transfers between devices: 37.3 us -> 33.3 us
  Pallas kernels: 33.1 us -> 29.8 us
    unnamed x19 -> x45, local copies, waits for them, and re-layouts: 5.63 us -> 15.2 us
    ppermute x20 -> x18, starting transfers between devices: 32.8 us -> 26.5 us  [send(): return lax.ppermute(x, AXES, route[name])]
    ppermute x20 -> x18, waiting for transfers between devices: 37.3 us -> 33.3 us  [send(): return lax.ppermute(x, AXES, route[name])]
    pallas_call x1 -> x3, Pallas kernels: 28.1 us -> 24.2 us  [grid_call(): pl.pallas_call(body, name=name, grid=(GROUPS // TOGETHER,), in_specs=spec...]
  transfers between devices with their start and end apart: 20 -> 18, of which waited for: 12 -> 10; matrix products, arithmetic and copies ran while one was open for 0% -> 0% of each run, Pallas kernels for 2% -> 11%
where the time goes in v3:
time: 106 us
  waiting for transfers between devices  33.3 us (31%)
  Pallas kernels  29.8 us (28%)
  starting transfers between devices  26.5 us (25%)
  local copies, waits for them, and re-layouts  15.2 us (14%)
    ppermute x18, waiting for transfers between devices, send(): return lax.ppermute(x, AXES, route[name])  33.3 us
    ppermute x18, starting transfers between devices, send(): return lax.ppermute(x, AXES, route[name])  26.5 us
    pallas_call x3, Pallas kernels, grid_call(): pl.pallas_call(body, name=name, grid=(GROUPS // TOGETHER,), in_specs=spec...  24.2 us
    unnamed x45, local copies, waits for them, and re-layouts  15.2 us
    pallas_call x7, Pallas kernels, whole_call(): pl.pallas_call(body, name=name, out_shape=shapes, in_specs=specs, out_spe...  5.55 us
  transfers between devices with their start and end apart: 18, of which 10 were waited for; matrix products, arithmetic and copies ran while one was open for 0% of the time, Pallas kernels for 11%

profile of v3, /device:TPU:0, one launch (start us, length us, event | category | flops | bytes accessed | tf_op | source)
XLA Modules:
  0.0 105.7 jit_solution(5966014345767771133)
XLA Ops:
  0.6 0.8 copy.10
  1.4 4.0 %collective-permute-start = (s32[5,4]{1,0:T(8,128)S(1)}, s32[5,4]{1,0:T(8,128)S(1)}, u32[]{:S(2)}, u32[]{:S(2)}) collective-permute-start(s32[5,4]{1,0:T(8,128)S(1)} %copy.10), channel_id=1, source_target_pairs={{0,1},{1,0},{2,3},{3,2},{4,5},{5,4},{6,7},{7,6},{8,9},{9,8},{10,11... | collective-permute-start | bytes 248 | tf_op jit(solution)/shard_map/ppermute | solution.py:415
  5.4 1.6 %collective-permute-done = s32[5,4]{1,0:T(8,128)S(1)} collective-permute-done((s32[5,4]{1,0:T(8,128)S(1)}, s32[5,4]{1,0:T(8,128)S(1)}, u32[]{:S(2)}, u32[]{:S(2)}) %collective-permute-start) | collective-permute-done | bytes 112 | tf_op jit(solution)/shard_map/ppermute | solution.py:415
  6.9 3.5 %collective-permute-start.4 = (bf16[128,1024]{1,0:T(8,128)(2,1)}, bf16[128,1024]{1,0:T(8,128)(2,1)S(1)}, u32[]{:S(2)}, u32[]{:S(2)}) collective-permute-start(bf16[128,1024]{1,0:T(8,128)(2,1)} %k_ref.3), channel_id=1, source_target_pairs={{0,1},{1,0},{2,3},{3,2},{4,5},{5,4},{6,7},{7,6},{8,9},{9,8},{10,11... | collective-permute-start | bytes 786440 | tf_op jit(solution)/shard_map/ppermute | solution.py:415
  10.6 0.9 copy-done.7
  11.5 0.9 copy-done.8
  12.5 0.9 select.1
  13.4 1.6 %collective-permute-start.1 = (bf16[8,32,256]{2,1,0:T(8,128)(2,1)S(1)}, bf16[8,32,256]{2,1,0:T(8,128)(2,1)S(1)}, u32[]{:S(2)}, u32[]{:S(2)}) collective-permute-start(bf16[8,32,256]{2,1,0:T(8,128)(2,1)S(1)} %get-tuple-element.37), channel_id=1, source_target_pairs={{0,8},{1,9},{2,10},{3,11},{4,12},{5,13},{6,14},{7,15},{8,0},{9,1},... | collective-permute-start | bytes 393224 | tf_op jit(solution)/shard_map/ppermute | solution.py:415
  15.0 2.1 %collective-permute-start.3 = (bf16[8,16,256]{2,1,0:T(8,128)(2,1)S(1)}, bf16[8,16,256]{2,1,0:T(8,128)(2,1)S(1)}, u32[]{:S(2)}, u32[]{:S(2)}) collective-permute-start(bf16[8,16,256]{2,1,0:T(8,128)(2,1)S(1)} %get-tuple-element.38), channel_id=1, source_target_pairs={{0,24},{1,25},{2,26},{3,27},{4,28},{5,29},{6,30},{7,31},{8,16},{9,... | collective-permute-start | bytes 196616 | tf_op jit(solution)/shard_map/ppermute | solution.py:415
  17.1 0.6 collective-permute-start.2
  17.7 2.9 %collective-permute-done.3.three = bf16[8,16,256]{2,1,0:T(8,128)(2,1)S(1)} collective-permute-done((bf16[8,16,256]{2,1,0:T(8,128)(2,1)S(1)}, bf16[8,16,256]{2,1,0:T(8,128)(2,1)S(1)}, u32[]{:S(2)}, u32[]{:S(2)}) %collective-permute-start.3) | collective-permute-done | bytes 65568 | tf_op jit(solution)/shard_map/ppermute | solution.py:415
  20.7 2.2 %collective-permute-done.2.two = bf16[8,16,256]{2,1,0:T(8,128)(2,1)S(1)} collective-permute-done((bf16[8,16,256]{2,1,0:T(8,128)(2,1)S(1)}, bf16[8,16,256]{2,1,0:T(8,128)(2,1)S(1)}, u32[]{:S(2)}, u32[]{:S(2)}) %collective-permute-start.2) | collective-permute-done | bytes 65568 | tf_op jit(solution)/shard_map/ppermute | solution.py:415
  22.9 1.6 %collective-permute-start.8 = (bf16[8,96,256]{2,1,0:T(8,128)(2,1)S(1)}, bf16[8,96,256]{2,1,0:T(8,128)(2,1)S(1)}, u32[]{:S(2)}, u32[]{:S(2)}) collective-permute-start(bf16[8,96,256]{2,1,0:T(8,128)(2,1)S(1)} %get-tuple-element.39.lift), channel_id=1, source_target_pairs={{0,4},{1,5},{2,6},{3,7},{4,1},{5,0},{6,3},{7,2},{8,12},{9,13},{10,... | collective-permute-start | bytes 1179656 | tf_op jit(solution)/shard_map/ppermute | solution.py:415
  24.5 2.2 %collective-permute-start.7 = (bf16[8,96,256]{2,1,0:T(8,128)(2,1)S(1)}, bf16[8,96,256]{2,1,0:T(8,128)(2,1)S(1)}, u32[]{:S(2)}, u32[]{:S(2)}) collective-permute-start(bf16[8,96,256]{2,1,0:T(8,128)(2,1)S(1)} %get-tuple-element.39.lift), channel_id=1, source_target_pairs={{0,5},{1,4},{2,7},{3,6},{4,0},{5,1},{6,2},{7,3},{8,13},{9,12},{10,... | collective-permute-start | bytes 1179656 | tf_op jit(solution)/shard_map/ppermute | solution.py:415
  26.7 1.8 %collective-permute-start.6 = (bf16[8,48,256]{2,1,0:T(8,128)(2,1)S(1)}, bf16[8,48,256]{2,1,0:T(8,128)(2,1)S(1)}, u32[]{:S(2)}, u32[]{:S(2)}) collective-permute-start(bf16[8,48,256]{2,1,0:T(8,128)(2,1)S(1)} %get-tuple-element.42.refs_0_), channel_id=1, source_target_pairs={{0,1},{1,0},{2,3},{3,2},{4,5},{5,4},{6,7},{7,6},{8,9},{9,8},{10,11... | collective-permute-start | bytes 589832 | tf_op jit(solution)/shard_map/ppermute | solution.py:415
  28.5 0.7 copy-done.9
  29.2 0.7 copy-done.11
  29.9 4.4 %level0.1 = (bf16[8,512,256]{2,1,0:T(8,128)(2,1)}, f32[8,128,128]{2,1,0:T(8,128)}, f32[8,128,128]{2,1,0:T(8,128)}, f32[8,512,128]{2,1,0:T(8,128)}) custom-call(bf16[128,4096]{1,0:T(8,128)(2,1)} %q_ref.5, bf16[128,1024]{1,0:T(8,128)(2,1)} %k_ref.3, bf16[128,1024]{1,0:T(8,128)(2,1)} %v_ref.3, bf16[128,1024]{1,0:T(8,128)(2,1)} %copy-done.9, ...), custom_call_target="tpu_custom_call" | custom-call | flops 4000000000 | bytes 16000000 | tf_op jit(solution)/shard_map/level0/pallas_call | solution.py:381
  34.3 3.9 %collective-permute-done.6.x_far = bf16[8,48,256]{2,1,0:T(8,128)(2,1)S(1)} collective-permute-done((bf16[8,48,256]{2,1,0:T(8,128)(2,1)S(1)}, bf16[8,48,256]{2,1,0:T(8,128)(2,1)S(1)}, u32[]{:S(2)}, u32[]{:S(2)}) %collective-permute-start.6) | collective-permute-done | bytes 196640 | tf_op jit(solution)/shard_map/ppermute | solution.py:415
  38.3 0.7 copy-done.5
  39.0 1.0 copy-done.4
  40.1 1.0 copy-done.6
  41.1 0.9 copy-done.10
  42.0 0.9 copy-done.12
  43.0 0.9 copy-done.14
  43.9 0.7 copy-done.18
  44.6 0.9 assemble.1.own_ref
  45.6 4.1 %collective-permute-done.9.other_ref = bf16[8,512,256]{2,1,0:T(8,128)(2,1)S(1)} collective-permute-done((bf16[8,512,256]{2,1,0:T(8,128)(2,1)S(1)}, bf16[8,512,256]{2,1,0:T(8,128)(2,1)S(1)}, u32[]{:S(2)}, u32[]{:S(2)}) %collective-permute-start.9) | collective-permute-done | bytes 2097184 | tf_op jit(solution)/shard_map/ppermute | solution.py:415
  49.8 1.3 %copy-done.21 = bf16[8,512,256]{2,1,0:T(8,128)(2,1)} copy-done((bf16[8,512,256]{2,1,0:T(8,128)(2,1)}, bf16[8,512,256]{2,1,0:T(8,128)(2,1)S(1)}, u32[]{:S(2)}) %copy-start.21) | copy-done | bytes 2097176
  51.1 14.4 %attention.1 = (bf16[128,4096]{1,0:T(8,128)(2,1)}, f32[128,4096]{1,0:T(8,128)}, bf16[8,512,256]{2,1,0:T(8,128)(2,1)}, bf16[8,512,256]{2,1,0:T(8,128)(2,1)}, f32[...) custom-call(s32[5,8]{1,0:T(8,128)} %copy-done.17, bf16[128,4096]{1,0:T(8,128)(2,1)} %q_ref.5, bf16[128,4096]{1,0:T(8,128)(2,1)} %g_ref.3, ...), custom_call_target="tpu_custom_call" | custom-call | flops 4000000000 | bytes 16000000 | tf_op jit(solution)/shard_map/attention/pallas_call | solution.py:381
  65.5 0.2 collective-permute-start.10
  65.7 4.2 %collective-permute-done.10.theirs = bf16[8,512,256]{2,1,0:T(8,128)(2,1)S(1)} collective-permute-done((bf16[8,512,256]{2,1,0:T(8,128)(2,1)}, bf16[8,512,256]{2,1,0:T(8,128)(2,1)S(1)}, u32[]{:S(2)}, u32[]{:S(2)}) %collective-permute-start.10) | collective-permute-done | bytes 2097184 | tf_op jit(solution)/shard_map/ppermute | solution.py:415
  70.0 1.6 %copy-done.2 = bf16[8,512,256]{2,1,0:T(8,128)(2,1)S(1)} copy-done((bf16[8,512,256]{2,1,0:T(8,128)(2,1)S(1)}, bf16[8,512,256]{2,1,0:T(8,128)(2,1)}, u32[]{:S(2)}) %copy-start.2) | copy-done | bytes 2097176
  71.6 1.0 reduce.1
  72.7 3.7 %collective-permute-start.13 = (bf16[8,96,256]{2,1,0:T(8,128)(2,1)}, bf16[8,96,256]{2,1,0:T(8,128)(2,1)S(1)}, u32[]{:S(2)}, u32[]{:S(2)}) collective-permute-start(bf16[8,96,256]{2,1,0:T(8,128)(2,1)} %get-tuple-element.58), channel_id=1, source_target_pairs={{0,5},{1,4},{2,7},{3,6},{4,0},{5,1},{6,2},{7,3},{8,13},{9,12},{10,... | collective-permute-start | bytes 1179656 | tf_op jit(solution)/shard_map/ppermute | solution.py:415
  76.4 5.4 %collective-permute-done.11.refs_0_.far = bf16[8,48,256]{2,1,0:T(8,128)(2,1)S(1)} collective-permute-done((bf16[8,48,256]{2,1,0:T(8,128)(2,1)S(1)}, bf16[8,48,256]{2,1,0:T(8,128)(2,1)S(1)}, u32[]{:S(2)}, u32[]{:S(2)}) %collective-permute-start.11) | collective-permute-done | bytes 196640 | tf_op jit(solution)/shard_map/ppermute | solution.py:415
  81.8 0.7 copy-done.15
  82.5 5.4 %return0.1 = (bf16[128,4096]{1,0:T(8,128)(2,1)}, bf16[8,256,256]{2,1,0:T(8,128)(2,1)}) custom-call(bf16[128,4096]{1,0:T(8,128)(2,1)} %q_ref.5, bf16[128,4096]{1,0:T(8,128)(2,1)} %g_ref.3, bf16[128,1024]{1,0:T(8,128)(2,1)} %k_ref.3, bf16[128,1024]{1,0:T(8,128)(2,1)} %v_ref.3, bf16[128,1024]{1,0:T(8,128)(2,1)} %copy-done.9, bf16[128,1024]{1,0:T(8,128)(2,1)} %copy-done.11, ...), custom_call_target="tpu_custom_call" | custom-call | flops 4000000000 | bytes 16000000 | tf_op jit(solution)/shard_map/return0/pallas_call | solution.py:381
  87.9 1.2 %copy-done = bf16[8,256,256]{2,1,0:T(8,128)(2,1)S(1)} copy-done((bf16[8,256,256]{2,1,0:T(8,128)(2,1)S(1)}, bf16[8,256,256]{2,1,0:T(8,128)(2,1)}, u32[]{:S(2)}) %copy-start) | copy-done | bytes 1048600
  89.1 0.9 place.1
  90.0 0.2 collective-permute-start.12
  90.3 1.3 %collective-permute-start.15 = (bf16[8,32,256]{2,1,0:T(8,128)(2,1)S(1)}, bf16[8,32,256]{2,1,0:T(8,128)(2,1)S(1)}, u32[]{:S(2)}, u32[]{:S(2)}) collective-permute-start(bf16[8,32,256]{2,1,0:T(8,128)(2,1)S(1)} %get-tuple-element.61), channel_id=1, source_target_pairs={{0,8},{1,9},{2,10},{3,11},{4,12},{5,13},{6,14},{7,15},{8,0},{9,1},... | collective-permute-start | bytes 393224 | tf_op jit(solution)/shard_map/ppermute | solution.py:415
  91.6 2.2 %collective-permute-start.16 = (bf16[8,16,256]{2,1,0:T(8,128)(2,1)S(1)}, bf16[8,16,256]{2,1,0:T(8,128)(2,1)S(1)}, u32[]{:S(2)}, u32[]{:S(2)}) collective-permute-start(bf16[8,16,256]{2,1,0:T(8,128)(2,1)S(1)} %get-tuple-element.62), channel_id=1, source_target_pairs={{0,16},{1,17},{2,18},{3,19},{4,20},{5,21},{6,22},{7,23},{8,24},{9,... | collective-permute-start | bytes 196616 | tf_op jit(solution)/shard_map/ppermute | solution.py:415
  93.8 1.3 %collective-permute-start.17 = (bf16[8,16,256]{2,1,0:T(8,128)(2,1)S(1)}, bf16[8,16,256]{2,1,0:T(8,128)(2,1)S(1)}, u32[]{:S(2)}, u32[]{:S(2)}) collective-permute-start(bf16[8,16,256]{2,1,0:T(8,128)(2,1)S(1)} %get-tuple-element.63), channel_id=1, source_target_pairs={{0,24},{1,25},{2,26},{3,27},{4,28},{5,29},{6,30},{7,31},{8,16},{9,... | collective-permute-start | bytes 196616 | tf_op jit(solution)/shard_map/ppermute | solution.py:415
  95.0 2.4 %collective-permute-done.16.two = bf16[8,16,256]{2,1,0:T(8,128)(2,1)S(1)} collective-permute-done((bf16[8,16,256]{2,1,0:T(8,128)(2,1)S(1)}, bf16[8,16,256]{2,1,0:T(8,128)(2,1)S(1)}, u32[]{:S(2)}, u32[]{:S(2)}) %collective-permute-start.16) | collective-permute-done | bytes 65568 | tf_op jit(solution)/shard_map/ppermute | solution.py:415
  97.4 1.8 %collective-permute-done.17.three = bf16[8,16,256]{2,1,0:T(8,128)(2,1)S(1)} collective-permute-done((bf16[8,16,256]{2,1,0:T(8,128)(2,1)S(1)}, bf16[8,16,256]{2,1,0:T(8,128)(2,1)S(1)}, u32[]{:S(2)}, u32[]{:S(2)}) %collective-permute-start.17) | collective-permute-done | bytes 65568 | tf_op jit(solution)/shard_map/ppermute | solution.py:415
  99.2 4.7 %collective-permute-done.12.far = bf16[8,128,256]{2,1,0:T(8,128)(2,1)S(1)} collective-permute-done((bf16[8,128,256]{2,1,0:T(8,128)(2,1)S(1)}, bf16[8,128,256]{2,1,0:T(8,128)(2,1)S(1)}, u32[]{:S(2)}, u32[]{:S(2)}) %collective-permute-start.12) | collective-permute-done | bytes 524320 | tf_op jit(solution)/shard_map/ppermute | solution.py:415
  103.9 1.7 %finish.1 = (bf16[128,1024]{1,0:T(8,128)(2,1)}, bf16[128,1024]{1,0:T(8,128)(2,1)}) custom-call(s32[5,8]{1,0:T(8,128)S(1)} %copy-done.19, bf16[8,256,256]{2,1,0:T(8,128)(2,1)S(1)} %copy-done.1, bf16[8,128,256]{2,1,0:T(8,128)(2,1)S(1)} %get-tuple-element.56.rows_kept, bf16[8,128,256]{2,1,0:T(8,128)(2,1)S(1)} %collective-permute-done.12.far, ...), custom_call_target="tpu_custom_call" | custom-call | bytes 4000000 | tf_op jit(solution)/shard_map/finish/pallas_call | solution.py:359
  (44 shorter events, 0.5 us)
Async XLA Ops:
  1.4 5.5 %collective-permute-start = (s32[5,4]{1,0:T(8,128)S(1)}, s32[5,4]{1,0:T(8,128)S(1)}, u32[]{:S(2)}, u32[]{:S(2)}) collective-permute-start(s32[5,4]{1,0:T(8,128)S(1)} %copy.10), channel_id=1, source_target_pairs={{0,1},{1,0},{2,3},{3,2},{4,5},{5,4},{6,7},{7,6},{8,9},{9,8},{10,11... | collective-permute-start | bytes 248 | tf_op jit(solution)/shard_map/ppermute | solution.py:415
  6.9 21.5 %collective-permute-start.4 = (bf16[128,1024]{1,0:T(8,128)(2,1)}, bf16[128,1024]{1,0:T(8,128)(2,1)S(1)}, u32[]{:S(2)}, u32[]{:S(2)}) collective-permute-start(bf16[128,1024]{1,0:T(8,128)(2,1)} %k_ref.3), channel_id=1, source_target_pairs={{0,1},{1,0},{2,3},{3,2},{4,5},{5,4},{6,7},{7,6},{8,9},{9,8},{10,11... | collective-permute-start | bytes 786440 | tf_op jit(solution)/shard_map/ppermute | solution.py:415
  10.5 18.0 %collective-permute-start.5 = (bf16[128,1024]{1,0:T(8,128)(2,1)}, bf16[128,1024]{1,0:T(8,128)(2,1)S(1)}, u32[]{:S(2)}, u32[]{:S(2)}) collective-permute-start(bf16[128,1024]{1,0:T(8,128)(2,1)} %v_ref.3), channel_id=1, source_target_pairs={{0,1},{1,0},{2,3},{3,2},{4,5},{5,4},{6,7},{7,6},{8,9},{9,8},{10,11... | collective-permute-start | bytes 786440 | tf_op jit(solution)/shard_map/ppermute | solution.py:415
  10.6 1.0 copy-start.7
  11.5 0.9 copy-start.8
  12.5 16.0 %copy-start.17 = (s32[5,8]{1,0:T(8,128)}, s32[5,8]{1,0:T(8,128)S(1)}, u32[]{:S(2)}) copy-start(s32[5,8]{1,0:T(8,128)S(1)} %add_select_fusion.offs) | copy-start | bytes 484
  13.4 15.1 %copy-start.13 = (bf16[8,64,256]{2,1,0:T(8,128)(2,1)}, bf16[8,64,256]{2,1,0:T(8,128)(2,1)S(1)}, u32[]{:S(2)}) copy-start(bf16[8,64,256]{2,1,0:T(8,128)(2,1)S(1)} %get-tuple-element.35.first) | copy-start | bytes 786436
  13.4 9.4 %collective-permute-start.1 = (bf16[8,32,256]{2,1,0:T(8,128)(2,1)S(1)}, bf16[8,32,256]{2,1,0:T(8,128)(2,1)S(1)}, u32[]{:S(2)}, u32[]{:S(2)}) collective-permute-start(bf16[8,32,256]{2,1,0:T(8,128)(2,1)S(1)} %get-tuple-element.37), channel_id=1, source_target_pairs={{0,8},{1,9},{2,10},{3,11},{4,12},{5,13},{6,14},{7,15},{8,0},{9,1},... | collective-permute-start | bytes 393224 | tf_op jit(solution)/shard_map/ppermute | solution.py:415
  15.0 5.7 %collective-permute-start.3 = (bf16[8,16,256]{2,1,0:T(8,128)(2,1)S(1)}, bf16[8,16,256]{2,1,0:T(8,128)(2,1)S(1)}, u32[]{:S(2)}, u32[]{:S(2)}) collective-permute-start(bf16[8,16,256]{2,1,0:T(8,128)(2,1)S(1)} %get-tuple-element.38), channel_id=1, source_target_pairs={{0,24},{1,25},{2,26},{3,27},{4,28},{5,29},{6,30},{7,31},{8,16},{9,... | collective-permute-start | bytes 196616 | tf_op jit(solution)/shard_map/ppermute | solution.py:415
  17.1 5.8 %collective-permute-start.2 = (bf16[8,16,256]{2,1,0:T(8,128)(2,1)S(1)}, bf16[8,16,256]{2,1,0:T(8,128)(2,1)S(1)}, u32[]{:S(2)}, u32[]{:S(2)}) collective-permute-start(bf16[8,16,256]{2,1,0:T(8,128)(2,1)S(1)} %get-tuple-element.38), channel_id=1, source_target_pairs={{0,16},{1,17},{2,18},{3,19},{4,20},{5,21},{6,22},{7,23},{8,24},{9,... | collective-permute-start | bytes 196616 | tf_op jit(solution)/shard_map/ppermute | solution.py:415
  22.9 5.6 %copy-start.20 = (bf16[8,48,256]{2,1,0:T(8,128)(2,1)}, bf16[8,48,256]{2,1,0:T(8,128)(2,1)S(1)}, u32[]{:S(2)}) copy-start(bf16[8,48,256]{2,1,0:T(8,128)(2,1)S(1)} %get-tuple-element.42.refs_0_) | copy-start | bytes 589828
  22.9 15.4 %collective-permute-start.8 = (bf16[8,96,256]{2,1,0:T(8,128)(2,1)S(1)}, bf16[8,96,256]{2,1,0:T(8,128)(2,1)S(1)}, u32[]{:S(2)}, u32[]{:S(2)}) collective-permute-start(bf16[8,96,256]{2,1,0:T(8,128)(2,1)S(1)} %get-tuple-element.39.lift), channel_id=1, source_target_pairs={{0,4},{1,5},{2,6},{3,7},{4,1},{5,0},{6,3},{7,2},{8,12},{9,13},{10,... | collective-permute-start | bytes 1179656 | tf_op jit(solution)/shard_map/ppermute | solution.py:415
  24.5 13.8 %collective-permute-start.7 = (bf16[8,96,256]{2,1,0:T(8,128)(2,1)S(1)}, bf16[8,96,256]{2,1,0:T(8,128)(2,1)S(1)}, u32[]{:S(2)}, u32[]{:S(2)}) collective-permute-start(bf16[8,96,256]{2,1,0:T(8,128)(2,1)S(1)} %get-tuple-element.39.lift), channel_id=1, source_target_pairs={{0,5},{1,4},{2,7},{3,6},{4,0},{5,1},{6,2},{7,3},{8,13},{9,12},{10,... | collective-permute-start | bytes 1179656 | tf_op jit(solution)/shard_map/ppermute | solution.py:415
  26.7 11.6 %collective-permute-start.6 = (bf16[8,48,256]{2,1,0:T(8,128)(2,1)S(1)}, bf16[8,48,256]{2,1,0:T(8,128)(2,1)S(1)}, u32[]{:S(2)}, u32[]{:S(2)}) collective-permute-start(bf16[8,48,256]{2,1,0:T(8,128)(2,1)S(1)} %get-tuple-element.42.refs_0_), channel_id=1, source_target_pairs={{0,1},{1,0},{2,3},{3,2},{4,5},{5,4},{6,7},{7,6},{8,9},{9,8},{10,11... | collective-permute-start | bytes 589832 | tf_op jit(solution)/shard_map/ppermute | solution.py:415
  28.5 0.7 copy-start.9
  29.2 0.7 copy-start.11
  38.3 0.7 copy-start.5
  39.0 1.0 copy-start.4
  40.1 1.0 copy-start.6
  41.1 0.9 copy-start.10
  42.0 0.9 copy-start.12
  43.0 0.9 copy-start.14
  43.9 0.7 copy-start.18
  45.5 5.6 %copy-start.3 = (bf16[8,512,256]{2,1,0:T(8,128)(2,1)}, bf16[8,512,256]{2,1,0:T(8,128)(2,1)S(1)}, u32[]{:S(2)}) copy-start(bf16[8,512,256]{2,1,0:T(8,128)(2,1)S(1)} %assemble.1.own_ref) | copy-start | bytes 6291460
  45.5 4.2 %collective-permute-start.9 = (bf16[8,512,256]{2,1,0:T(8,128)(2,1)S(1)}, bf16[8,512,256]{2,1,0:T(8,128)(2,1)S(1)}, u32[]{:S(2)}, u32[]{:S(2)}) collective-permute-start(bf16[8,512,256]{2,1,0:T(8,128)(2,1)S(1)} %assemble.1.own_ref), channel_id=1, source_target_pairs={{0,2},{1,3},{2,0},{3,1},{4,6},{5,7},{6,4},{7,5},{8,10},{9,11},{10,... | collective-permute-start | bytes 6291464 | tf_op jit(solution)/shard_map/ppermute | solution.py:415
  49.8 1.3 %copy-start.21 = (bf16[8,512,256]{2,1,0:T(8,128)(2,1)}, bf16[8,512,256]{2,1,0:T(8,128)(2,1)S(1)}, u32[]{:S(2)}) copy-start(bf16[8,512,256]{2,1,0:T(8,128)(2,1)S(1)} %collective-permute-done.9.other_ref) | copy-start | bytes 6291460
  65.5 4.5 %collective-permute-start.10 = (bf16[8,512,256]{2,1,0:T(8,128)(2,1)}, bf16[8,512,256]{2,1,0:T(8,128)(2,1)S(1)}, u32[]{:S(2)}, u32[]{:S(2)}) collective-permute-start(bf16[8,512,256]{2,1,0:T(8,128)(2,1)} %get-tuple-element.52), channel_id=1, source_target_pairs={{0,2},{1,3},{2,0},{3,1},{4,6},{5,7},{6,4},{7,5},{8,10},{9,11},{10,... | collective-permute-start | bytes 6291464 | tf_op jit(solution)/shard_map/ppermute | solution.py:415
  70.0 1.6 %copy-start.2 = (bf16[8,512,256]{2,1,0:T(8,128)(2,1)S(1)}, bf16[8,512,256]{2,1,0:T(8,128)(2,1)}, u32[]{:S(2)}) copy-start(bf16[8,512,256]{2,1,0:T(8,128)(2,1)} %get-tuple-element.51.mine) | copy-start | bytes 6291460
  72.6 9.2 %collective-permute-start.11 = (bf16[8,48,256]{2,1,0:T(8,128)(2,1)S(1)}, bf16[8,48,256]{2,1,0:T(8,128)(2,1)S(1)}, u32[]{:S(2)}, u32[]{:S(2)}) collective-permute-start(bf16[8,48,256]{2,1,0:T(8,128)(2,1)S(1)} %get-tuple-element.53), channel_id=1, source_target_pairs={{0,1},{1,0},{2,3},{3,2},{4,5},{5,4},{6,7},{7,6},{8,9},{9,8},{10,11... | collective-permute-start | bytes 589832 | tf_op jit(solution)/shard_map/ppermute | solution.py:415
  72.7 17.5 %collective-permute-start.13 = (bf16[8,96,256]{2,1,0:T(8,128)(2,1)}, bf16[8,96,256]{2,1,0:T(8,128)(2,1)S(1)}, u32[]{:S(2)}, u32[]{:S(2)}) collective-permute-start(bf16[8,96,256]{2,1,0:T(8,128)(2,1)} %get-tuple-element.58), channel_id=1, source_target_pairs={{0,5},{1,4},{2,7},{3,6},{4,0},{5,1},{6,2},{7,3},{8,13},{9,12},{10,... | collective-permute-start | bytes 1179656 | tf_op jit(solution)/shard_map/ppermute | solution.py:415
  76.4 13.8 %collective-permute-start.14 = (bf16[8,96,256]{2,1,0:T(8,128)(2,1)S(1)}, bf16[8,96,256]{2,1,0:T(8,128)(2,1)S(1)}, u32[]{:S(2)}, u32[]{:S(2)}) collective-permute-start(bf16[8,96,256]{2,1,0:T(8,128)(2,1)S(1)} %get-tuple-element.59), channel_id=1, source_target_pairs={{0,4},{1,5},{2,6},{3,7},{4,1},{5,0},{6,3},{7,2},{8,12},{9,13},{10,... | collective-permute-start | bytes 1179656 | tf_op jit(solution)/shard_map/ppermute | solution.py:415
  81.8 0.7 copy-start.15
  82.5 5.4 %copy-start.19 = (s32[5,8]{1,0:T(8,128)S(1)}, s32[5,8]{1,0:T(8,128)}, u32[]{:S(2)}) copy-start(s32[5,8]{1,0:T(8,128)} %copy-done.17) | copy-start | bytes 484
  87.9 1.2 %copy-start = (bf16[8,256,256]{2,1,0:T(8,128)(2,1)S(1)}, bf16[8,256,256]{2,1,0:T(8,128)(2,1)}, u32[]{:S(2)}) copy-start(bf16[8,256,256]{2,1,0:T(8,128)(2,1)} %get-tuple-element.55.d0) | copy-start | bytes 3145732
  89.1 1.1 %copy-start.16 = (bf16[8,48,256]{2,1,0:T(8,128)(2,1)S(1)}, bf16[8,48,256]{2,1,0:T(8,128)(2,1)}, u32[]{:S(2)}) copy-start(bf16[8,48,256]{2,1,0:T(8,128)(2,1)} %copy-done.15) | copy-start | bytes 589828
  89.1 14.8 %copy-start.1 = (bf16[8,256,256]{2,1,0:T(8,128)(2,1)S(1)}, bf16[8,256,256]{2,1,0:T(8,128)(2,1)}, u32[]{:S(2)}) copy-start(bf16[8,256,256]{2,1,0:T(8,128)(2,1)} %get-tuple-element.55.d0) | copy-start | bytes 3145732
  90.0 13.9 %collective-permute-start.12 = (bf16[8,128,256]{2,1,0:T(8,128)(2,1)S(1)}, bf16[8,128,256]{2,1,0:T(8,128)(2,1)S(1)}, u32[]{:S(2)}, u32[]{:S(2)}) collective-permute-start(bf16[8,128,256]{2,1,0:T(8,128)(2,1)S(1)} %place.1), channel_id=1, source_target_pairs={{0,1},{1,0},{2,3},{3,2},{4,5},{5,4},{6,7},{7,6},{8,9},{9,8},{10,11... | collective-permute-start | bytes 1572872 | tf_op jit(solution)/shard_map/ppermute | solution.py:415
  90.3 9.0 %collective-permute-start.15 = (bf16[8,32,256]{2,1,0:T(8,128)(2,1)S(1)}, bf16[8,32,256]{2,1,0:T(8,128)(2,1)S(1)}, u32[]{:S(2)}, u32[]{:S(2)}) collective-permute-start(bf16[8,32,256]{2,1,0:T(8,128)(2,1)S(1)} %get-tuple-element.61), channel_id=1, source_target_pairs={{0,8},{1,9},{2,10},{3,11},{4,12},{5,13},{6,14},{7,15},{8,0},{9,1},... | collective-permute-start | bytes 393224 | tf_op jit(solution)/shard_map/ppermute | solution.py:415
  91.6 5.8 %collective-permute-start.16 = (bf16[8,16,256]{2,1,0:T(8,128)(2,1)S(1)}, bf16[8,16,256]{2,1,0:T(8,128)(2,1)S(1)}, u32[]{:S(2)}, u32[]{:S(2)}) collective-permute-start(bf16[8,16,256]{2,1,0:T(8,128)(2,1)S(1)} %get-tuple-element.62), channel_id=1, source_target_pairs={{0,16},{1,17},{2,18},{3,19},{4,20},{5,21},{6,22},{7,23},{8,24},{9,... | collective-permute-start | bytes 196616 | tf_op jit(solution)/shard_map/ppermute | solution.py:415
  93.8 5.5 %collective-permute-start.17 = (bf16[8,16,256]{2,1,0:T(8,128)(2,1)S(1)}, bf16[8,16,256]{2,1,0:T(8,128)(2,1)S(1)}, u32[]{:S(2)}, u32[]{:S(2)}) collective-permute-start(bf16[8,16,256]{2,1,0:T(8,128)(2,1)S(1)} %get-tuple-element.63), channel_id=1, source_target_pairs={{0,24},{1,25},{2,26},{3,27},{4,28},{5,29},{6,30},{7,31},{8,16},{9,... | collective-permute-start | bytes 196616 | tf_op jit(solution)/shard_map/ppermute | solution.py:415

commit v4 on v3

--- a/solution.py
+++ b/solution.py
@@ -20,7 +20,7 @@
 F32 = jnp.float32
 ANY_ROWS = ((0, 64, 1), (64, 96, 2), (96, 112, 3), (112, 120, 4))
 VMEM_LIMIT = 24 * 1024 * 1024
-GRID_LIMIT = 61 * 1024 * 1024
+GRID_LIMIT = 32 * 1024 * 1024
 
 
 def dot(a, b):
@@ -65,12 +65,13 @@
 
 
 def select_kernel(offs, keys, values, first, middle, tail, last):
-    for g in range(GROUPS):
-        rows = dot(selector(offs, g), group_rows(keys, values, g))
-        first[g] = rows[0:64].astype(BF)
-        middle[g] = rows[64:128].astype(BF)
-        tail[g] = rows[96:128].astype(BF)
-        last[g] = rows[112:128].astype(BF)
+    first_group = pl.program_id(0) * TOGETHER
+    for j in range(TOGETHER):
+        rows = dot(selector(offs, first_group + j), group_rows(keys, values, j))
+        first[j] = rows[0:64].astype(BF)
+        middle[j] = rows[64:128].astype(BF)
+        tail[j] = rows[96:128].astype(BF)
+        last[j] = rows[112:128].astype(BF)
 
 
 def compact_kernel(middle, one, two, three, lift, extra):
@@ -293,7 +294,7 @@
         dq_ref[:, wide_lanes(j)] = (by_token(parts[j]) + part_ref[:, wide_lanes(j)]).astype(BF)
 
 
-def reduce_kernel(mine, theirs, rows_kept, rows_far, up, down, x_far, x_kept):
+def reduce_kernel(mine, theirs, _, rows_kept, rows_far, up, down, x_far, x_kept):
     zero = jnp.zeros((8, 2 * D), F32)
     for g in range(GROUPS):
         total = mine[g].astype(F32) + theirs[g].astype(F32)
@@ -311,7 +312,7 @@
                 x_far[g] = extra.astype(BF)
 
 
-def place_kernel(offs, d0, rows_far, far):
+def place_kernel(offs, d0, rows_far, _, far):
     for g in range(GROUPS):
         far[g] = (d0[g, 128:256].astype(F32) + dot(placer(offs, g), rows_far[g])).astype(BF)
 
@@ -368,12 +369,16 @@
 
 
 def grid_call(body, name, offs, inputs, outs, scratch=(), after=()):
-    def spec(shape):
+    def spec(shape, offset=0):
+        if offset:
+            return pl.BlockSpec((TOKENS, TOGETHER * D), lambda i: (0, i + offset - 1))
         if len(shape) == 2:
             return pl.BlockSpec((TOKENS, shape[1] * TOGETHER // GROUPS), lambda i: (0, i))
         return pl.BlockSpec((TOGETHER,) + shape[1:], lambda i: (i, 0, 0))
 
-    specs = [spec(x.shape) for x in inputs] + [pl.BlockSpec(memory_space=pl.ANY)] * len(after)
+    specs = [spec(x[0].shape, x[1]) if isinstance(x, tuple) else spec(x.shape) for x in inputs]
+    inputs = [x[0] if isinstance(x, tuple) else x for x in inputs]
+    specs += [pl.BlockSpec(memory_space=pl.ANY)] * len(after)
     arrays = tuple(inputs) + tuple(after)
     if offs is not None:
         specs = [pl.BlockSpec(memory_space=pltpu.SMEM)] + specs
@@ -428,8 +433,10 @@
     rows = lambda n, dtype=BF: ((GROUPS, n, 2 * D), dtype)
     packed = ((GROUPS, TOKENS, 128), F32)
     wide = lambda dtype: ((TOKENS, GROUPS * WIDE), dtype)
-    first, middle, tail, last = whole_call(
-        select_kernel, "select", [rows(64), rows(64), rows(32), rows(16)], offs, key_rows, value_rows
+    pair = jnp.concatenate([key_rows, value_rows], 1)
+    first, middle, tail, last = grid_call(
+        select_kernel, "select", offs, [(pair, 1), (pair, 1 + GROUPS // TOGETHER)],
+        [rows(64), rows(64), rows(32), rows(16)],
     )
     lift, extra = whole_call(
         compact_kernel, "compact", [rows(96), rows(48)], None,
@@ -454,19 +461,19 @@
         scratch=[pltpu.VMEM((TOGETHER, 4, TOKENS, 128), F32), stats, stats],
     )
     theirs = send(down_other, "core")
+    grad_queries, d0 = grid_call(
+        return0_kernel, "return0", None,
+        [queries, gradient, key_rows, value_rows, far_keys, far_values, power0, factor0, shift0, part],
+        [wide(BF), rows(256)],
+    )
     rows_kept, rows_far, up, down, x_far, x_kept = whole_call(
         reduce_kernel, "reduce", [rows(128), rows(128), rows(96), rows(96), rows(48), rows(48, F32)],
-        None, down_own, theirs,
+        None, down_own, theirs, after=(d0,),
     )
     from_down = send(up, "up")
     from_up = send(down, "down")
     x_far = send(x_far, "head")
-    grad_queries, d0 = grid_call(
-        return0_kernel, "return0", None,
-        [queries, gradient, key_rows, value_rows, far_keys, far_values, power0, factor0, shift0, part],
-        [wide(BF), rows(256)], after=(x_far,),
-    )
-    (far,) = whole_call(place_kernel, "place", [rows(128)], offs, d0, rows_far)
+    (far,) = whole_call(place_kernel, "place", [rows(128)], offs, d0, rows_far, after=(x_far,))
     far = send(far, "head")
     one, two, three = whole_call(
         cross_kernel, "cross", [rows(32), rows(16), rows(16)], None, x_kept, x_far, from_up, from_down

time: 106 us -> 88.3 us (0.83)
  local copies, waits for them, and re-layouts: 15.2 us -> 0.78 us
  Pallas kernels: 29.8 us -> 22.6 us
  waiting for transfers between devices: 33.3 us -> 35.3 us
    unnamed x45 -> x9, local copies, waits for them, and re-layouts: 15.2 us -> 0.78 us
    pallas_call x3 -> x4, Pallas kernels: 24.2 us -> 18.5 us  [grid_call(): pl.pallas_call(body, name=name, grid=(GROUPS // TOGETHER,), in_specs=spec...]
    ppermute x18, waiting for transfers between devices: 33.3 us -> 35.3 us  [send(): return lax.ppermute(x, AXES, route[name])]
    pallas_call x7 -> x6, Pallas kernels: 5.55 us -> 4.16 us  [whole_call(): pl.pallas_call(body, name=name, out_shape=shapes, in_specs=specs, out_spe...]
    concatenate x0 -> x1, other arithmetic: none -> 1.06 us  [shards(): pair = jnp.concatenate([key_rows, value_rows], 1)]
  transfers between devices with their start and end apart: 18 -> 18, of which waited for: 10 -> 12; matrix products, arithmetic and copies ran while one was open for 0% -> 1% of each run, Pallas kernels for 11% -> 9%
where the time goes in v4:
time: 88.3 us; the launch traced here: 88 us
  waiting for transfers between devices  35.3 us (40%)
  starting transfers between devices  27.3 us (31%)
  Pallas kernels  22.6 us (26%)
  other arithmetic  1.14 us (1%)
    ppermute x18, waiting for transfers between devices, send(): return lax.ppermute(x, AXES, route[name])  35.3 us
    ppermute x18, starting transfers between devices, send(): return lax.ppermute(x, AXES, route[name])  27.3 us
    pallas_call x4, Pallas kernels, grid_call(): pl.pallas_call(body, name=name, grid=(GROUPS // TOGETHER,), in_specs=spec...  18.5 us
    pallas_call x6, Pallas kernels, whole_call(): pl.pallas_call(body, name=name, out_shape=shapes, in_specs=specs, out_spe...  4.16 us
  transfers between devices with their start and end apart: 18, of which 12 were waited for; matrix products, arithmetic and copies ran while one was open for 1% of the time, Pallas kernels for 9%

profile of v4, /device:TPU:0, one launch (start us, length us, event | category | flops | bytes accessed | tf_op | source)
XLA Modules:
  0.0 88.0 jit_solution(12916668232133679763)
XLA Ops:
  0.6 0.8 copy.10
  1.4 4.0 %collective-permute-start = (s32[5,4]{1,0:T(8,128)S(1)}, s32[5,4]{1,0:T(8,128)S(1)}, u32[]{:S(2)}, u32[]{:S(2)}) collective-permute-start(s32[5,4]{1,0:T(8,128)S(1)} %copy.10), channel_id=1, source_target_pairs={{0,1},{1,0},{2,3},{3,2},{4,5},{5,4},{6,7},{7,6},{8,9},{9,8},{10,11... | collective-permute-start | bytes 248 | tf_op jit(solution)/shard_map/ppermute | solution.py:420
  5.4 1.1 %pad_maximum_fusion.keys.values = bf16[128,2048]{1,0:T(8,128)(2,1)S(1)} fusion(bf16[128,1024]{1,0:T(8,128)(2,1)} %v_ref.3, bf16[128,1024]{1,0:T(8,128)(2,1)} %k_ref.3), kind=kLoop, calls=%fused_computation | loop fusion | flops 1048576 | bytes 1048576 | tf_op jit(solution)/shard_map/concatenate | solution.py:436
  6.4 0.5 collective-permute-done
  6.9 3.5 %collective-permute-start.4 = (bf16[128,1024]{1,0:T(8,128)(2,1)}, bf16[128,1024]{1,0:T(8,128)(2,1)S(1)}, u32[]{:S(2)}, u32[]{:S(2)}) collective-permute-start(bf16[128,1024]{1,0:T(8,128)(2,1)} %k_ref.3), channel_id=1, source_target_pairs={{0,1},{1,0},{2,3},{3,2},{4,5},{5,4},{6,7},{7,6},{8,9},{9,8},{10,11... | collective-permute-start | bytes 786440 | tf_op jit(solution)/shard_map/ppermute | solution.py:420
  10.5 0.0 collective-permute-start.5
  10.5 0.1 add_select_fusion.offs
  10.6 1.1 %select.1 = (bf16[8,64,256]{2,1,0:T(8,128)(2,1)S(1)}, bf16[8,64,256]{2,1,0:T(8,128)(2,1)S(1)}, bf16[8,32,256]{2,1,0:T(8,128)(2,1)S(1)}, bf16[8,16,256]{2,1,0:T(8,128)(2,1)S(1)}) custom-call(s32[5,8]{1,0:T(8,128)S(1)} %add_select_fusion.offs, bf16[128,2048]{1,0:T(8,128)(2,1)S(1)} %pad_maximum_fusion.keys.values, bf16[128,2048]{1,0:T(8,128)(2,1)S(1)} %pad_maximum_fusion.keys.values), custom_call_target="tpu_custom_call" | custom-call | flops 4000000000 | bytes 16000000 | tf_op jit(solution)/shard_map/select/pallas_call | solution.py:386
  11.7 1.6 %collective-permute-start.1 = (bf16[8,32,256]{2,1,0:T(8,128)(2,1)S(1)}, bf16[8,32,256]{2,1,0:T(8,128)(2,1)S(1)}, u32[]{:S(2)}, u32[]{:S(2)}) collective-permute-start(bf16[8,32,256]{2,1,0:T(8,128)(2,1)S(1)} %get-tuple-element.37), channel_id=1, source_target_pairs={{0,8},{1,9},{2,10},{3,11},{4,12},{5,13},{6,14},{7,15},{8,0},{9,1},... | collective-permute-start | bytes 393224 | tf_op jit(solution)/shard_map/ppermute | solution.py:420
  13.3 2.1 %collective-permute-start.3 = (bf16[8,16,256]{2,1,0:T(8,128)(2,1)S(1)}, bf16[8,16,256]{2,1,0:T(8,128)(2,1)S(1)}, u32[]{:S(2)}, u32[]{:S(2)}) collective-permute-start(bf16[8,16,256]{2,1,0:T(8,128)(2,1)S(1)} %get-tuple-element.38), channel_id=1, source_target_pairs={{0,24},{1,25},{2,26},{3,27},{4,28},{5,29},{6,30},{7,31},{8,16},{9,... | collective-permute-start | bytes 196616 | tf_op jit(solution)/shard_map/ppermute | solution.py:420
  15.4 0.6 collective-permute-start.2
  16.0 3.1 %collective-permute-done.3.three = bf16[8,16,256]{2,1,0:T(8,128)(2,1)S(1)} collective-permute-done((bf16[8,16,256]{2,1,0:T(8,128)(2,1)S(1)}, bf16[8,16,256]{2,1,0:T(8,128)(2,1)S(1)}, u32[]{:S(2)}, u32[]{:S(2)}) %collective-permute-start.3) | collective-permute-done | bytes 65568 | tf_op jit(solution)/shard_map/ppermute | solution.py:420
  19.1 2.0 %collective-permute-done.2.two = bf16[8,16,256]{2,1,0:T(8,128)(2,1)S(1)} collective-permute-done((bf16[8,16,256]{2,1,0:T(8,128)(2,1)S(1)}, bf16[8,16,256]{2,1,0:T(8,128)(2,1)S(1)}, u32[]{:S(2)}, u32[]{:S(2)}) %collective-permute-start.2) | collective-permute-done | bytes 65568 | tf_op jit(solution)/shard_map/ppermute | solution.py:420
  21.2 0.0 collective-permute-done.1.one
  21.2 1.6 %collective-permute-start.8 = (bf16[8,96,256]{2,1,0:T(8,128)(2,1)S(1)}, bf16[8,96,256]{2,1,0:T(8,128)(2,1)S(1)}, u32[]{:S(2)}, u32[]{:S(2)}) collective-permute-start(bf16[8,96,256]{2,1,0:T(8,128)(2,1)S(1)} %get-tuple-element.39.lift), channel_id=1, source_target_pairs={{0,4},{1,5},{2,6},{3,7},{4,1},{5,0},{6,3},{7,2},{8,12},{9,13},{10,... | collective-permute-start | bytes 1179656 | tf_op jit(solution)/shard_map/ppermute | solution.py:420
  22.8 2.2 %collective-permute-start.7 = (bf16[8,96,256]{2,1,0:T(8,128)(2,1)S(1)}, bf16[8,96,256]{2,1,0:T(8,128)(2,1)S(1)}, u32[]{:S(2)}, u32[]{:S(2)}) collective-permute-start(bf16[8,96,256]{2,1,0:T(8,128)(2,1)S(1)} %get-tuple-element.39.lift), channel_id=1, source_target_pairs={{0,5},{1,4},{2,7},{3,6},{4,0},{5,1},{6,2},{7,3},{8,13},{9,12},{10,... | collective-permute-start | bytes 1179656 | tf_op jit(solution)/shard_map/ppermute | solution.py:420
  25.0 1.8 %collective-permute-start.6 = (bf16[8,48,256]{2,1,0:T(8,128)(2,1)S(1)}, bf16[8,48,256]{2,1,0:T(8,128)(2,1)S(1)}, u32[]{:S(2)}, u32[]{:S(2)}) collective-permute-start(bf16[8,48,256]{2,1,0:T(8,128)(2,1)S(1)} %get-tuple-element.42.refs_0_), channel_id=1, source_target_pairs={{0,1},{1,0},{2,3},{3,2},{4,5},{5,4},{6,7},{7,6},{8,9},{9,8},{10,11... | collective-permute-start | bytes 589832 | tf_op jit(solution)/shard_map/ppermute | solution.py:420
  26.8 0.0 collective-permute-done.4.kp_ref.keys
  26.8 0.0 collective-permute-done.5.vp_ref.values
  26.8 2.1 %level0.1 = (bf16[8,512,256]{2,1,0:T(8,128)(2,1)S(1)}, f32[8,128,128]{2,1,0:T(8,128)S(1)}, f32[8,128,128]{2,1,0:T(8,128)S(1)}, f32[8,512,128]{2,1,0:T(8,128)S(1)}) custom-call(bf16[128,4096]{1,0:T(8,128)(2,1)S(1)} %copy-done.2, bf16[128,1024]{1,0:T(8,128)(2,1)S(1)} %copy-done.1, bf16[128,1024]{1,0:T(8,128)(2,1)S(1)} %copy-done, ...), custom_call_target="tpu_custom_call" | custom-call | flops 4000000000 | bytes 16000000 | tf_op jit(solution)/shard_map/level0/pallas_call | solution.py:386
  28.9 7.6 %collective-permute-done.6.x_far = bf16[8,48,256]{2,1,0:T(8,128)(2,1)S(1)} collective-permute-done((bf16[8,48,256]{2,1,0:T(8,128)(2,1)S(1)}, bf16[8,48,256]{2,1,0:T(8,128)(2,1)S(1)}, u32[]{:S(2)}, u32[]{:S(2)}) %collective-permute-start.6) | collective-permute-done | bytes 196640 | tf_op jit(solution)/shard_map/ppermute | solution.py:420
  36.6 0.0 collective-permute-done.8.lift_down
  36.6 0.0 collective-permute-done.7.lift_up
  36.6 0.9 %assemble.1.own_ref = bf16[8,512,256]{2,1,0:T(8,128)(2,1)S(1)} custom-call(s32[5,8]{1,0:T(8,128)S(1)} %add_select_fusion.offs, bf16[8,64,256]{2,1,0:T(8,128)(2,1)S(1)} %get-tuple-element.35.first, bf16[8,96,256]{2,1,0:T(8,128)(2,1)S(1)} %get-tuple-element.39.lift, bf16[128,1024]{1,0:T(8,128)(2,1)S(1)} %collective-permute-done.4.kp_ref.keys, ...), custom_call_target="tpu_custom_call" | custom-call | bytes 4000000 | tf_op jit(solution)/shard_map/assemble/pallas_call | solution.py:360
  37.5 0.1 collective-permute-start.9
  37.6 4.1 %collective-permute-done.9.other_ref = bf16[8,512,256]{2,1,0:T(8,128)(2,1)S(1)} collective-permute-done((bf16[8,512,256]{2,1,0:T(8,128)(2,1)S(1)}, bf16[8,512,256]{2,1,0:T(8,128)(2,1)S(1)}, u32[]{:S(2)}, u32[]{:S(2)}) %collective-permute-start.9) | collective-permute-done | bytes 2097184 | tf_op jit(solution)/shard_map/ppermute | solution.py:420
  41.8 11.6 %attention.1 = (bf16[128,4096]{1,0:T(8,128)(2,1)}, f32[128,4096]{1,0:T(8,128)S(1)}, bf16[8,512,256]{2,1,0:T(8,128)(2,1)S(1)}, bf16[8,512,256]{2,1,0:T(8,128)(2,1...) custom-call(s32[5,8]{1,0:T(8,128)S(1)} %add_select_fusion.offs, bf16[128,4096]{1,0:T(8,128)(2,1)S(1)} %copy-done.2, ...), custom_call_target="tpu_custom_call" | custom-call | flops 4000000000 | bytes 16000000 | tf_op jit(solution)/shard_map/attention/pallas_call | solution.py:386
  53.4 0.1 collective-permute-start.10
  53.5 3.6 %return0.1 = (bf16[128,4096]{1,0:T(8,128)(2,1)}, bf16[8,256,256]{2,1,0:T(8,128)(2,1)S(1)}) custom-call(bf16[128,4096]{1,0:T(8,128)(2,1)S(1)} %copy-done.2, bf16[128,4096]{1,0:T(8,128)(2,1)S(1)} %copy-done.3, bf16[128,1024]{1,0:T(8,128)(2,1)S(1)} %copy-done.1, bf16[128,1024]{1,0:T(8,128)(2,1)S(1)} %copy-done, ...), custom_call_target="tpu_custom_call" | custom-call | flops 4000000000 | bytes 16000000 | tf_op jit(solution)/shard_map/return0/pallas_call | solution.py:386
  57.2 0.4 collective-permute-done.10.theirs
  57.6 0.5 reduce.1
  58.0 1.0 %collective-permute-start.11 = (bf16[8,48,256]{2,1,0:T(8,128)(2,1)S(1)}, bf16[8,48,256]{2,1,0:T(8,128)(2,1)S(1)}, u32[]{:S(2)}, u32[]{:S(2)}) collective-permute-start(bf16[8,48,256]{2,1,0:T(8,128)(2,1)S(1)} %get-tuple-element.57), channel_id=1, source_target_pairs={{0,1},{1,0},{2,3},{3,2},{4,5},{5,4},{6,7},{7,6},{8,9},{9,8},{10,11... | collective-permute-start | bytes 589832 | tf_op jit(solution)/shard_map/ppermute | solution.py:420
  59.0 2.9 %collective-permute-start.13 = (bf16[8,96,256]{2,1,0:T(8,128)(2,1)S(1)}, bf16[8,96,256]{2,1,0:T(8,128)(2,1)S(1)}, u32[]{:S(2)}, u32[]{:S(2)}) collective-permute-start(bf16[8,96,256]{2,1,0:T(8,128)(2,1)S(1)} %get-tuple-element.58), channel_id=1, source_target_pairs={{0,5},{1,4},{2,7},{3,6},{4,0},{5,1},{6,2},{7,3},{8,13},{9,12},{10,... | collective-permute-start | bytes 1179656 | tf_op jit(solution)/shard_map/ppermute | solution.py:420
  61.9 0.0 collective-permute-start.14
  61.9 5.4 %collective-permute-done.11._.far = bf16[8,48,256]{2,1,0:T(8,128)(2,1)S(1)} collective-permute-done((bf16[8,48,256]{2,1,0:T(8,128)(2,1)S(1)}, bf16[8,48,256]{2,1,0:T(8,128)(2,1)S(1)}, u32[]{:S(2)}, u32[]{:S(2)}) %collective-permute-start.11) | collective-permute-done | bytes 196640 | tf_op jit(solution)/shard_map/ppermute | solution.py:420
  67.4 0.9 %place.1 = bf16[8,128,256]{2,1,0:T(8,128)(2,1)S(1)} custom-call(s32[5,8]{1,0:T(8,128)S(1)} %add_select_fusion.offs, bf16[8,256,256]{2,1,0:T(8,128)(2,1)S(1)} %get-tuple-element.52._.d0, bf16[8,128,256]{2,1,0:T(8,128)(2,1)S(1)} %get-tuple-element.56.rows_far, bf16[8,48,256]{2,1,0:T(8,128)(2,1)S(1)} %collective-permute-done.11._.far), custom_call_target="tpu_custom_call" | custom-call | bytes 4000000 | tf_op jit(solution)/shard_map/place/pallas_call | solution.py:360
  68.2 1.0 %collective-permute-start.12 = (bf16[8,128,256]{2,1,0:T(8,128)(2,1)S(1)}, bf16[8,128,256]{2,1,0:T(8,128)(2,1)S(1)}, u32[]{:S(2)}, u32[]{:S(2)}) collective-permute-start(bf16[8,128,256]{2,1,0:T(8,128)(2,1)S(1)} %place.1), channel_id=1, source_target_pairs={{0,1},{1,0},{2,3},{3,2},{4,5},{5,4},{6,7},{7,6},{8,9},{9,8},{10,11... | collective-permute-start | bytes 1572872 | tf_op jit(solution)/shard_map/ppermute | solution.py:420
  69.3 5.7 %collective-permute-done.13.up = bf16[8,96,256]{2,1,0:T(8,128)(2,1)S(1)} collective-permute-done((bf16[8,96,256]{2,1,0:T(8,128)(2,1)S(1)}, bf16[8,96,256]{2,1,0:T(8,128)(2,1)S(1)}, u32[]{:S(2)}, u32[]{:S(2)}) %collective-permute-start.13) | collective-permute-done | bytes 393248 | tf_op jit(solution)/shard_map/ppermute | solution.py:420
  75.0 0.8 collective-permute-done.14.down
  75.8 0.1 cross.1
  75.9 1.0 %collective-permute-start.15 = (bf16[8,32,256]{2,1,0:T(8,128)(2,1)S(1)}, bf16[8,32,256]{2,1,0:T(8,128)(2,1)S(1)}, u32[]{:S(2)}, u32[]{:S(2)}) collective-permute-start(bf16[8,32,256]{2,1,0:T(8,128)(2,1)S(1)} %get-tuple-element.61), channel_id=1, source_target_pairs={{0,8},{1,9},{2,10},{3,11},{4,12},{5,13},{6,14},{7,15},{8,0},{9,1},... | collective-permute-start | bytes 393224 | tf_op jit(solution)/shard_map/ppermute | solution.py:420
  76.8 2.2 %collective-permute-start.16 = (bf16[8,16,256]{2,1,0:T(8,128)(2,1)S(1)}, bf16[8,16,256]{2,1,0:T(8,128)(2,1)S(1)}, u32[]{:S(2)}, u32[]{:S(2)}) collective-permute-start(bf16[8,16,256]{2,1,0:T(8,128)(2,1)S(1)} %get-tuple-element.62), channel_id=1, source_target_pairs={{0,16},{1,17},{2,18},{3,19},{4,20},{5,21},{6,22},{7,23},{8,24},{9,... | collective-permute-start | bytes 196616 | tf_op jit(solution)/shard_map/ppermute | solution.py:420
  79.0 1.7 %collective-permute-start.17 = (bf16[8,16,256]{2,1,0:T(8,128)(2,1)S(1)}, bf16[8,16,256]{2,1,0:T(8,128)(2,1)S(1)}, u32[]{:S(2)}, u32[]{:S(2)}) collective-permute-start(bf16[8,16,256]{2,1,0:T(8,128)(2,1)S(1)} %get-tuple-element.63), channel_id=1, source_target_pairs={{0,24},{1,25},{2,26},{3,27},{4,28},{5,29},{6,30},{7,31},{8,16},{9,... | collective-permute-start | bytes 196616 | tf_op jit(solution)/shard_map/ppermute | solution.py:420
  80.7 2.2 %collective-permute-done.16.two = bf16[8,16,256]{2,1,0:T(8,128)(2,1)S(1)} collective-permute-done((bf16[8,16,256]{2,1,0:T(8,128)(2,1)S(1)}, bf16[8,16,256]{2,1,0:T(8,128)(2,1)S(1)}, u32[]{:S(2)}, u32[]{:S(2)}) %collective-permute-start.16) | collective-permute-done | bytes 65568 | tf_op jit(solution)/shard_map/ppermute | solution.py:420
  82.8 1.6 %collective-permute-done.17.three = bf16[8,16,256]{2,1,0:T(8,128)(2,1)S(1)} collective-permute-done((bf16[8,16,256]{2,1,0:T(8,128)(2,1)S(1)}, bf16[8,16,256]{2,1,0:T(8,128)(2,1)S(1)}, u32[]{:S(2)}, u32[]{:S(2)}) %collective-permute-start.17) | collective-permute-done | bytes 65568 | tf_op jit(solution)/shard_map/ppermute | solution.py:420
  84.5 0.0 collective-permute-done.15.one
  84.5 1.7 %collective-permute-done.12.far = bf16[8,128,256]{2,1,0:T(8,128)(2,1)S(1)} collective-permute-done((bf16[8,128,256]{2,1,0:T(8,128)(2,1)S(1)}, bf16[8,128,256]{2,1,0:T(8,128)(2,1)S(1)}, u32[]{:S(2)}, u32[]{:S(2)}) %collective-permute-start.12) | collective-permute-done | bytes 524320 | tf_op jit(solution)/shard_map/ppermute | solution.py:420
  86.2 1.7 %finish.1 = (bf16[128,1024]{1,0:T(8,128)(2,1)}, bf16[128,1024]{1,0:T(8,128)(2,1)}) custom-call(s32[5,8]{1,0:T(8,128)S(1)} %add_select_fusion.offs, bf16[8,256,256]{2,1,0:T(8,128)(2,1)S(1)} %get-tuple-element.52._.d0, bf16[8,128,256]{2,1,0:T(8,128)(2,1)S(1)} %get-tuple-element.55.rows_kept, bf16[8,128,256]{2,1,0:T(8,128)(2,1)S(1)} %collective-permute-done.12.far, ...), custom_call_target="tpu_custom_call" | custom-call | bytes 4000000 | tf_op jit(solution)/shard_map/finish/pallas_call | solution.py:360
  (9 shorter events, 0.1 us)
Async XLA Ops:
  1.4 5.5 %collective-permute-start = (s32[5,4]{1,0:T(8,128)S(1)}, s32[5,4]{1,0:T(8,128)S(1)}, u32[]{:S(2)}, u32[]{:S(2)}) collective-permute-start(s32[5,4]{1,0:T(8,128)S(1)} %copy.10), channel_id=1, source_target_pairs={{0,1},{1,0},{2,3},{3,2},{4,5},{5,4},{6,7},{7,6},{8,9},{9,8},{10,11... | collective-permute-start | bytes 248 | tf_op jit(solution)/shard_map/ppermute | solution.py:420
  6.9 19.9 %collective-permute-start.4 = (bf16[128,1024]{1,0:T(8,128)(2,1)}, bf16[128,1024]{1,0:T(8,128)(2,1)S(1)}, u32[]{:S(2)}, u32[]{:S(2)}) collective-permute-start(bf16[128,1024]{1,0:T(8,128)(2,1)} %k_ref.3), channel_id=1, source_target_pairs={{0,1},{1,0},{2,3},{3,2},{4,5},{5,4},{6,7},{7,6},{8,9},{9,8},{10,11... | collective-permute-start | bytes 786440 | tf_op jit(solution)/shard_map/ppermute | solution.py:420
  10.5 16.3 %collective-permute-start.5 = (bf16[128,1024]{1,0:T(8,128)(2,1)}, bf16[128,1024]{1,0:T(8,128)(2,1)S(1)}, u32[]{:S(2)}, u32[]{:S(2)}) collective-permute-start(bf16[128,1024]{1,0:T(8,128)(2,1)} %v_ref.3), channel_id=1, source_target_pairs={{0,1},{1,0},{2,3},{3,2},{4,5},{5,4},{6,7},{7,6},{8,9},{9,8},{10,11... | collective-permute-start | bytes 786440 | tf_op jit(solution)/shard_map/ppermute | solution.py:420
  10.6 16.2 %copy-start = (bf16[128,1024]{1,0:T(8,128)(2,1)S(1)}, bf16[128,1024]{1,0:T(8,128)(2,1)}, u32[]{:S(2)}) copy-start(bf16[128,1024]{1,0:T(8,128)(2,1)} %v_ref.3) | copy-start | bytes 786436
  10.6 16.2 %copy-start.1 = (bf16[128,1024]{1,0:T(8,128)(2,1)S(1)}, bf16[128,1024]{1,0:T(8,128)(2,1)}, u32[]{:S(2)}) copy-start(bf16[128,1024]{1,0:T(8,128)(2,1)} %k_ref.3) | copy-start | bytes 786436
  10.6 16.2 %copy-start.2 = (bf16[128,4096]{1,0:T(8,128)(2,1)S(1)}, bf16[128,4096]{1,0:T(8,128)(2,1)}, u32[]{:S(2)}) copy-start(bf16[128,4096]{1,0:T(8,128)(2,1)} %q_ref.5) | copy-start | bytes 3145732
  11.7 9.4 %collective-permute-start.1 = (bf16[8,32,256]{2,1,0:T(8,128)(2,1)S(1)}, bf16[8,32,256]{2,1,0:T(8,128)(2,1)S(1)}, u32[]{:S(2)}, u32[]{:S(2)}) collective-permute-start(bf16[8,32,256]{2,1,0:T(8,128)(2,1)S(1)} %get-tuple-element.37), channel_id=1, source_target_pairs={{0,8},{1,9},{2,10},{3,11},{4,12},{5,13},{6,14},{7,15},{8,0},{9,1},... | collective-permute-start | bytes 393224 | tf_op jit(solution)/shard_map/ppermute | solution.py:420
  13.3 5.8 %collective-permute-start.3 = (bf16[8,16,256]{2,1,0:T(8,128)(2,1)S(1)}, bf16[8,16,256]{2,1,0:T(8,128)(2,1)S(1)}, u32[]{:S(2)}, u32[]{:S(2)}) collective-permute-start(bf16[8,16,256]{2,1,0:T(8,128)(2,1)S(1)} %get-tuple-element.38), channel_id=1, source_target_pairs={{0,24},{1,25},{2,26},{3,27},{4,28},{5,29},{6,30},{7,31},{8,16},{9,... | collective-permute-start | bytes 196616 | tf_op jit(solution)/shard_map/ppermute | solution.py:420
  15.4 5.8 %collective-permute-start.2 = (bf16[8,16,256]{2,1,0:T(8,128)(2,1)S(1)}, bf16[8,16,256]{2,1,0:T(8,128)(2,1)S(1)}, u32[]{:S(2)}, u32[]{:S(2)}) collective-permute-start(bf16[8,16,256]{2,1,0:T(8,128)(2,1)S(1)} %get-tuple-element.38), channel_id=1, source_target_pairs={{0,16},{1,17},{2,18},{3,19},{4,20},{5,21},{6,22},{7,23},{8,24},{9,... | collective-permute-start | bytes 196616 | tf_op jit(solution)/shard_map/ppermute | solution.py:420
  21.2 15.4 %collective-permute-start.8 = (bf16[8,96,256]{2,1,0:T(8,128)(2,1)S(1)}, bf16[8,96,256]{2,1,0:T(8,128)(2,1)S(1)}, u32[]{:S(2)}, u32[]{:S(2)}) collective-permute-start(bf16[8,96,256]{2,1,0:T(8,128)(2,1)S(1)} %get-tuple-element.39.lift), channel_id=1, source_target_pairs={{0,4},{1,5},{2,6},{3,7},{4,1},{5,0},{6,3},{7,2},{8,12},{9,13},{10,... | collective-permute-start | bytes 1179656 | tf_op jit(solution)/shard_map/ppermute | solution.py:420
  22.8 13.8 %collective-permute-start.7 = (bf16[8,96,256]{2,1,0:T(8,128)(2,1)S(1)}, bf16[8,96,256]{2,1,0:T(8,128)(2,1)S(1)}, u32[]{:S(2)}, u32[]{:S(2)}) collective-permute-start(bf16[8,96,256]{2,1,0:T(8,128)(2,1)S(1)} %get-tuple-element.39.lift), channel_id=1, source_target_pairs={{0,5},{1,4},{2,7},{3,6},{4,0},{5,1},{6,2},{7,3},{8,13},{9,12},{10,... | collective-permute-start | bytes 1179656 | tf_op jit(solution)/shard_map/ppermute | solution.py:420
  25.0 11.6 %collective-permute-start.6 = (bf16[8,48,256]{2,1,0:T(8,128)(2,1)S(1)}, bf16[8,48,256]{2,1,0:T(8,128)(2,1)S(1)}, u32[]{:S(2)}, u32[]{:S(2)}) collective-permute-start(bf16[8,48,256]{2,1,0:T(8,128)(2,1)S(1)} %get-tuple-element.42.refs_0_), channel_id=1, source_target_pairs={{0,1},{1,0},{2,3},{3,2},{4,5},{5,4},{6,7},{7,6},{8,9},{9,8},{10,11... | collective-permute-start | bytes 589832 | tf_op jit(solution)/shard_map/ppermute | solution.py:420
  36.6 5.2 %copy-start.3 = (bf16[128,4096]{1,0:T(8,128)(2,1)S(1)}, bf16[128,4096]{1,0:T(8,128)(2,1)}, u32[]{:S(2)}) copy-start(bf16[128,4096]{1,0:T(8,128)(2,1)} %g_ref.3) | copy-start | bytes 3145732
  37.5 4.2 %collective-permute-start.9 = (bf16[8,512,256]{2,1,0:T(8,128)(2,1)S(1)}, bf16[8,512,256]{2,1,0:T(8,128)(2,1)S(1)}, u32[]{:S(2)}, u32[]{:S(2)}) collective-permute-start(bf16[8,512,256]{2,1,0:T(8,128)(2,1)S(1)} %assemble.1.own_ref), channel_id=1, source_target_pairs={{0,2},{1,3},{2,0},{3,1},{4,6},{5,7},{6,4},{7,5},{8,10},{9,11},{10,... | collective-permute-start | bytes 6291464 | tf_op jit(solution)/shard_map/ppermute | solution.py:420
  53.4 4.2 %collective-permute-start.10 = (bf16[8,512,256]{2,1,0:T(8,128)(2,1)S(1)}, bf16[8,512,256]{2,1,0:T(8,128)(2,1)S(1)}, u32[]{:S(2)}, u32[]{:S(2)}) collective-permute-start(bf16[8,512,256]{2,1,0:T(8,128)(2,1)S(1)} %get-tuple-element.54), channel_id=1, source_target_pairs={{0,2},{1,3},{2,0},{3,1},{4,6},{5,7},{6,4},{7,5},{8,10},{9,11},{10,... | collective-permute-start | bytes 6291464 | tf_op jit(solution)/shard_map/ppermute | solution.py:420
  58.0 9.3 %collective-permute-start.11 = (bf16[8,48,256]{2,1,0:T(8,128)(2,1)S(1)}, bf16[8,48,256]{2,1,0:T(8,128)(2,1)S(1)}, u32[]{:S(2)}, u32[]{:S(2)}) collective-permute-start(bf16[8,48,256]{2,1,0:T(8,128)(2,1)S(1)} %get-tuple-element.57), channel_id=1, source_target_pairs={{0,1},{1,0},{2,3},{3,2},{4,5},{5,4},{6,7},{7,6},{8,9},{9,8},{10,11... | collective-permute-start | bytes 589832 | tf_op jit(solution)/shard_map/ppermute | solution.py:420
  59.0 15.9 %collective-permute-start.13 = (bf16[8,96,256]{2,1,0:T(8,128)(2,1)S(1)}, bf16[8,96,256]{2,1,0:T(8,128)(2,1)S(1)}, u32[]{:S(2)}, u32[]{:S(2)}) collective-permute-start(bf16[8,96,256]{2,1,0:T(8,128)(2,1)S(1)} %get-tuple-element.58), channel_id=1, source_target_pairs={{0,5},{1,4},{2,7},{3,6},{4,0},{5,1},{6,2},{7,3},{8,13},{9,12},{10,... | collective-permute-start | bytes 1179656 | tf_op jit(solution)/shard_map/ppermute | solution.py:420
  61.9 13.9 %collective-permute-start.14 = (bf16[8,96,256]{2,1,0:T(8,128)(2,1)S(1)}, bf16[8,96,256]{2,1,0:T(8,128)(2,1)S(1)}, u32[]{:S(2)}, u32[]{:S(2)}) collective-permute-start(bf16[8,96,256]{2,1,0:T(8,128)(2,1)S(1)} %get-tuple-element.59), channel_id=1, source_target_pairs={{0,4},{1,5},{2,6},{3,7},{4,1},{5,0},{6,3},{7,2},{8,12},{9,13},{10,... | collective-permute-start | bytes 1179656 | tf_op jit(solution)/shard_map/ppermute | solution.py:420
  68.2 18.0 %collective-permute-start.12 = (bf16[8,128,256]{2,1,0:T(8,128)(2,1)S(1)}, bf16[8,128,256]{2,1,0:T(8,128)(2,1)S(1)}, u32[]{:S(2)}, u32[]{:S(2)}) collective-permute-start(bf16[8,128,256]{2,1,0:T(8,128)(2,1)S(1)} %place.1), channel_id=1, source_target_pairs={{0,1},{1,0},{2,3},{3,2},{4,5},{5,4},{6,7},{7,6},{8,9},{9,8},{10,11... | collective-permute-start | bytes 1572872 | tf_op jit(solution)/shard_map/ppermute | solution.py:420
  75.9 8.6 %collective-permute-start.15 = (bf16[8,32,256]{2,1,0:T(8,128)(2,1)S(1)}, bf16[8,32,256]{2,1,0:T(8,128)(2,1)S(1)}, u32[]{:S(2)}, u32[]{:S(2)}) collective-permute-start(bf16[8,32,256]{2,1,0:T(8,128)(2,1)S(1)} %get-tuple-element.61), channel_id=1, source_target_pairs={{0,8},{1,9},{2,10},{3,11},{4,12},{5,13},{6,14},{7,15},{8,0},{9,1},... | collective-permute-start | bytes 393224 | tf_op jit(solution)/shard_map/ppermute | solution.py:420
  76.8 6.0 %collective-permute-start.16 = (bf16[8,16,256]{2,1,0:T(8,128)(2,1)S(1)}, bf16[8,16,256]{2,1,0:T(8,128)(2,1)S(1)}, u32[]{:S(2)}, u32[]{:S(2)}) collective-permute-start(bf16[8,16,256]{2,1,0:T(8,128)(2,1)S(1)} %get-tuple-element.62), channel_id=1, source_target_pairs={{0,16},{1,17},{2,18},{3,19},{4,20},{5,21},{6,22},{7,23},{8,24},{9,... | collective-permute-start | bytes 196616 | tf_op jit(solution)/shard_map/ppermute | solution.py:420
  79.0 5.5 %collective-permute-start.17 = (bf16[8,16,256]{2,1,0:T(8,128)(2,1)S(1)}, bf16[8,16,256]{2,1,0:T(8,128)(2,1)S(1)}, u32[]{:S(2)}, u32[]{:S(2)}) collective-permute-start(bf16[8,16,256]{2,1,0:T(8,128)(2,1)S(1)} %get-tuple-element.63), channel_id=1, source_target_pairs={{0,24},{1,25},{2,26},{3,27},{4,28},{5,29},{6,30},{7,31},{8,16},{9,... | collective-permute-start | bytes 196616 | tf_op jit(solution)/shard_map/ppermute | solution.py:420

commit v5 on v4

--- a/solution.py
+++ b/solution.py
@@ -182,33 +182,46 @@
     return jnp.concatenate([own_ref[:, lanes], far_ref[:, lanes]], 0)
 
 
-def level0_kernel(q_ref, k_ref, v_ref, kp_ref, vp_ref, *refs):
-    power_ref, peak_ref, lse_ref, out_ref = refs[-4:]
+def both_rows(own_ref, other_ref, j, at, lanes):
+    return jnp.concatenate([own_ref[j, at, lanes], other_ref[j, at, lanes]], 0)
+
+
+K_LANES, V_LANES, LEVEL1 = slice(0, D), slice(D, 2 * D), slice(0, 128)
+
+
+def early_kernel(offs, q_ref, g_ref, k_ref, v_ref, kp_ref, vp_ref, *refs):
+    qs_ref, gs_ref, power0, peak0, lse0, out0 = refs[-6:]
     members = range(TOGETHER)
+    first_group = pl.program_id(0) * TOGETHER
+    for j in members:
+        pick = selector(offs, first_group + j)
+        qs_ref[j] = by_level(dot(pick, q_ref[:, wide_lanes(j)])).astype(BF)
+        gs_ref[j] = by_level(dot(pick, g_ref[:, wide_lanes(j)])).astype(BF)
     queries = [by_head(q_ref[:, wide_lanes(j)]) for j in members]
     keys = [whole_rows(k_ref, kp_ref, j) for j in members]
     values = [whole_rows(v_ref, vp_ref, j) for j in members]
     for j, (power, peak, lse, out) in enumerate(zip(*forward(queries, keys, values))):
-        power_ref[j], peak_ref[j], lse_ref[j], out_ref[j] = power, peak, lse, out
+        power0[j], peak0[j], lse0[j], out0[j] = power, peak, lse, out
+
+
+def place_levels(offs, first_group, rows):
+    rows = [by_selection(x).astype(BF) for x in rows]
+    return [dot(placer(offs, first_group + j), r) for j, r in enumerate(rows)]
 
 
 def attention_kernel(
-    offs, q_ref, g_ref, own_ref, other_ref, peak_ref, lse_ref, out_ref,
-    att_ref, part_ref, down_ref, dother_ref, factor_ref, shift_ref, level_ref, token_ref, delta_ref,
+    offs, qs_ref, gs_ref, g_ref, own_ref, other_ref, peak0, lse0, out0,
+    att_ref, part_ref, down_ref, dother_ref, factor0, shift0, power1, factor1, shift1,
+    level_ref, token_ref, delta_ref,
 ):
     members = range(TOGETHER)
     first_group = pl.program_id(0) * TOGETHER
     bounds = ((0, 256), (256, 384), (384, 448), (448, 480))
     starts = [[(offs[k, first_group + j], 128 >> k) for k in range(1, 5)] for j in members]
 
-    def selected(ref):
-        rows = [dot(selector(offs, first_group + j), ref[:, wide_lanes(j)]) for j in members]
-        rows = [by_level(x).astype(BF) for x in rows]
-        return [[x[a:b] for x in rows] for a, b in bounds]
-
     def kept(k, lanes):
         at = slice(128 * k, 128 * k + 128)
-        return [jnp.concatenate([own_ref[j, at, lanes], other_ref[j, at, lanes]], 0) for j in members]
+        return [both_rows(own_ref, other_ref, j, at, lanes) for j in members]
 
     def for_levels(ref, xs):
         for j, x in enumerate(xs):
@@ -218,22 +231,18 @@
             for k in range(4)
         ]
 
-    def place(parts):
-        rows = [jnp.concatenate(list(p) + [jnp.zeros((32, D), F32)], 0) for p in zip(*parts)]
-        rows = [by_selection(x).astype(BF) for x in rows]
-        return [dot(placer(offs, first_group + j), r) for j, r in enumerate(rows)]
-
     level_ref[...] = jnp.full(level_ref.shape, -1e30, F32)
-    queries, grads = selected(q_ref), selected(g_ref)
-    keys = [kept(k, slice(0, D)) for k in range(4)]
-    values = [kept(k, slice(D, 2 * D)) for k in range(4)]
+    queries = [[qs_ref[j, a:b] for j in members] for a, b in bounds]
+    grads = [[gs_ref[j, a:b] for j in members] for a, b in bounds]
+    keys = [kept(k, K_LANES) for k in range(4)]
+    values = [kept(k, V_LANES) for k in range(4)]
     results = [forward(queries[k], keys[k], values[k]) for k in range(4)]
 
     for k in range(4):
         for j in members:
             start, count = starts[j][k]
             level_ref[j, k, pl.ds(start, count, 2 ** (k + 1)), :] = results[k][2][j]
-    firsts = [lse_ref[j] for j in members]
+    firsts = [lse0[j] for j in members]
     tops = [functools.reduce(jnp.maximum, [level_ref[j, k] for k in range(4)], firsts[j]) for j in members]
     sums = [
         jnp.exp2(firsts[j] - tops[j]) + sum(jnp.exp2(level_ref[j, k] - tops[j]) for k in range(4))
@@ -245,11 +254,13 @@
         for k, column in enumerate(for_levels(token_ref, merged))
     ]
     spread = [[expand(f) for f in fs] for fs in factors]
-    placed = place([[out * f for out, f in zip(results[k][3], spread[k])] for k in range(4)])
+    pad = [jnp.zeros((32, D), F32)]
+    parts = [[out * f for out, f in zip(results[k][3], spread[k])] for k in range(4)]
+    placed = place_levels(offs, first_group, [jnp.concatenate(list(p) + pad, 0) for p in zip(*parts)])
     deltas = []
     for j in members:
-        factor = jnp.exp2(peak_ref[j] - merged[j])
-        attended = (placed[j] + by_token(out_ref[j] * expand(factor))).astype(BF)
+        factor = jnp.exp2(peak0[j] - merged[j])
+        attended = (placed[j] + by_token(out0[j] * expand(factor))).astype(BF)
         att_ref[:, wide_lanes(j)] = attended
         product = g_ref[:, wide_lanes(j)].astype(F32) * attended.astype(F32)
         total = [
@@ -257,23 +268,21 @@
             for h in range(HEADS)
         ]
         deltas.append(heads_to_lanes(jnp.concatenate(total, 0)))
-        factor_ref[j] = factor
-        shift_ref[j] = factor * deltas[j]
+        factor0[j] = factor
+        shift0[j] = factor * deltas[j]
     shifts = [
         [f * d for f, d in zip(factors[k], column)] for k, column in enumerate(for_levels(delta_ref, deltas))
     ]
-    scaled = [
-        [(g.astype(F32) * f).astype(BF) for g, f in zip(grads[k], spread[k])] for k in range(4)
-    ]
-    parts = []
-    for k in range(4):
-        pairs, part = backward(queries[k], scaled[k], keys[k], values[k], results[k][0], shifts[k])
-        parts.append(part)
+    for j in members:
+        power1[j], factor1[j], shift1[j] = results[0][0][j], factors[0][j], shifts[0][j]
+    for k in range(1, 4):
+        scaled = [(g.astype(F32) * f).astype(BF) for g, f in zip(grads[k], spread[k])]
+        pairs, part = backward(queries[k], scaled, keys[k], values[k], results[k][0], shifts[k])
+        at = slice(128 * k - 128, 128 * k)
         for j in members:
-            down_ref[j, 128 * k : 128 * k + 128] = pairs[j][:128]
-            dother_ref[j, 128 * k : 128 * k + 128] = pairs[j][128:]
-    for j, x in enumerate(place(parts)):
-        part_ref[:, wide_lanes(j)] = x
+            down_ref[j, at] = pairs[j][:128]
+            dother_ref[j, at] = pairs[j][128:]
+            part_ref[j, bounds[k][0] - 256 : bounds[k][1] - 256] = part[j]
 
 
 def return0_kernel(
@@ -294,17 +303,35 @@
         dq_ref[:, wide_lanes(j)] = (by_token(parts[j]) + part_ref[:, wide_lanes(j)]).astype(BF)
 
 
-def reduce_kernel(mine, theirs, _, rows_kept, rows_far, up, down, x_far, x_kept):
+def return1_kernel(
+    offs, qs_ref, gs_ref, own_ref, other_ref, power_ref, factor_ref, shift_ref, part_ref,
+    dq_ref, down_ref, dother_ref,
+):
+    members = range(TOGETHER)
+    queries = [qs_ref[j, 0:256] for j in members]
+    keys = [both_rows(own_ref, other_ref, j, LEVEL1, K_LANES) for j in members]
+    values = [both_rows(own_ref, other_ref, j, LEVEL1, V_LANES) for j in members]
+    scaled = [(gs_ref[j, 0:256].astype(F32) * expand(factor_ref[j])).astype(BF) for j in members]
+    powers, shifts = [power_ref[j] for j in members], [shift_ref[j] for j in members]
+    pairs, parts = backward(queries, scaled, keys, values, powers, shifts)
+    pad = [jnp.zeros((32, D), F32)]
+    rows = [jnp.concatenate([parts[j], part_ref[j]] + pad, 0) for j in members]
+    for j, x in enumerate(place_levels(offs, pl.program_id(0) * TOGETHER, rows)):
+        down_ref[j] = pairs[j][:128]
+        dother_ref[j] = pairs[j][128:]
+        dq_ref[:, wide_lanes(j)] = x
+
+
+def reduce_kernel(mine, theirs, _, mid_kept, mid_far, up, down, x_far, x_kept):
     zero = jnp.zeros((8, 2 * D), F32)
     for g in range(GROUPS):
         total = mine[g].astype(F32) + theirs[g].astype(F32)
-        for z, ref in enumerate((rows_kept, rows_far, up, down)):
-            second, third, fourth = [total[s + 32 * z : s + 32 * z + 32] for s in (128, 256, 384)]
+        for z, ref in enumerate((mid_kept, mid_far, up, down)):
+            second, third, fourth = [total[s + 32 * z : s + 32 * z + 32] for s in (0, 128, 256)]
             if z >= 2:
                 ref[g] = jnp.concatenate([second, third, fourth], 0).astype(BF)
                 continue
-            rows = [total[64 * z : 64 * z + 64], second, third[:16], fourth[:8], zero]
-            ref[g] = jnp.concatenate(rows, 0).astype(BF)
+            ref[g] = jnp.concatenate([second, third[:16], fourth[:8], zero], 0).astype(BF)
             extra = jnp.concatenate([third[16:], fourth[8:], zero], 0)
             if z == 0:
                 x_kept[g] = extra
@@ -312,9 +339,12 @@
                 x_far[g] = extra.astype(BF)
 
 
-def place_kernel(offs, d0, rows_far, _, far):
+def place_kernel(offs, d0, mine, theirs, mid_far, _, *refs):
     for g in range(GROUPS):
-        far[g] = (d0[g, 128:256].astype(F32) + dot(placer(offs, g), rows_far[g])).astype(BF)
+        first = (mine[g, 64:128].astype(F32) + theirs[g, 64:128].astype(F32)).astype(BF)
+        rows = jnp.concatenate([first, mid_far[g]], 0)
+        whole = (d0[g, 128:256].astype(F32) + dot(placer(offs, g), rows)).astype(BF)
+        refs[g // TOGETHER][g % TOGETHER] = whole
 
 
 def cross_kernel(kept, far, up, down, one, two, three):
@@ -329,22 +359,24 @@
         three[g] = jnp.concatenate([fourth[16:24], zero], 0).astype(BF)
 
 
-def finish_kernel(offs, d0, rows_kept, far, up, down, one, two, three, dk_ref, dv_ref):
+def finish_kernel(offs, d0, mine, theirs, mid_kept, *refs):
+    *fars, up, down, one, two, three, dk_ref, dv_ref = refs
     for g in range(GROUPS):
-        kept = rows_kept[g].astype(F32)
+        kept = mid_kept[g].astype(F32)
         sides = up[g].astype(F32) + down[g].astype(F32)
         a, b, c = one[g].astype(F32), two[g].astype(F32), three[g].astype(F32)
         rows = jnp.concatenate(
             [
-                kept[0:64],
-                kept[64:96] + sides[0:32],
-                kept[96:112] + sides[32:48] + a[0:16],
-                kept[112:120] + sides[64:72] + a[16:24] + b[0:8] + c[0:8],
+                mine[g, 0:64].astype(F32) + theirs[g, 0:64].astype(F32),
+                kept[0:32] + sides[0:32],
+                kept[32:48] + sides[32:48] + a[0:16],
+                kept[48:56] + sides[64:72] + a[16:24] + b[0:8] + c[0:8],
                 jnp.zeros((8, 2 * D), F32),
             ],
             0,
         ).astype(BF)
-        whole = d0[g, 0:128].astype(F32) + far[g].astype(F32) + dot(placer(offs, g), rows)
+        far = fars[g // TOGETHER][g % TOGETHER].astype(F32)
+        whole = d0[g, 0:128].astype(F32) + far + dot(placer(offs, g), rows)
         dk_ref[:, g * D : (g + 1) * D] = whole[:, :D].astype(BF)
         dv_ref[:, g * D : (g + 1) * D] = whole[:, D:].astype(BF)
 
@@ -369,7 +401,9 @@
 
 
 def grid_call(body, name, offs, inputs, outs, scratch=(), after=()):
-    def spec(shape, offset=0):
+    def spec(shape, offset=None):
+        if offset == 0:
+            return pl.BlockSpec((TOGETHER, 128) + shape[2:], lambda i: (i, 0, 0))
         if offset:
             return pl.BlockSpec((TOKENS, TOGETHER * D), lambda i: (0, i + offset - 1))
         if len(shape) == 2:
@@ -426,14 +460,14 @@
         jnp.concatenate([level_offsets, other_offsets], 1),
         jnp.concatenate([other_offsets, level_offsets], 1),
     )
-    key_swap, value_swap, other_offsets = lax.optimization_barrier((key_rows, value_rows, other_offsets))
+    pair = jnp.concatenate([key_rows, value_rows], 1)
+    key_swap, value_swap, pair = lax.optimization_barrier((key_rows, value_rows, pair))
     far_keys = send(key_swap, "head")
     far_values = send(value_swap, "head")
 
     rows = lambda n, dtype=BF: ((GROUPS, n, 2 * D), dtype)
     packed = ((GROUPS, TOKENS, 128), F32)
     wide = lambda dtype: ((TOKENS, GROUPS * WIDE), dtype)
-    pair = jnp.concatenate([key_rows, value_rows], 1)
     first, middle, tail, last = grid_call(
         select_kernel, "select", offs, [(pair, 1), (pair, 1 + GROUPS // TOGETHER)],
         [rows(64), rows(64), rows(32), rows(16)],
@@ -445,9 +479,11 @@
     lift_down = send(lift, "up")
     lift_up = send(lift, "down")
     extra_far = send(extra, "head")
-    power0, peak0, lse0, out0 = grid_call(
-        level0_kernel, "level0", None, [queries, key_rows, value_rows, far_keys, far_values],
-        [rows(512), packed, packed, ((GROUPS, 512, 128), F32)], after=(extra,),
+    tall = lambda n, dtype=F32: ((GROUPS, n, D), dtype)
+    kv = [key_rows, value_rows, far_keys, far_values]
+    qs, gs, power0, peak0, lse0, out0 = grid_call(
+        early_kernel, "early", offs, [queries, gradient, *kv],
+        [tall(512, BF), tall(512, BF), rows(512), tall(128), tall(128), tall(512)], after=(extra,),
     )
     (own,) = whole_call(
         assemble_kernel, "assemble", [rows(512)], offs, first, lift, far_keys, far_values,
@@ -455,33 +491,42 @@
     )
     other = send(own, "core")
     stats = pltpu.VMEM((TOGETHER, TOKENS, 128), F32)
-    attended, part, down_own, down_other, factor0, shift0 = grid_call(
-        attention_kernel, "attention", offs, [queries, gradient, own, other, peak0, lse0, out0],
-        [wide(BF), wide(F32), rows(512), rows(512), packed, packed],
+    attended, part, down_own, down_other, factor0, shift0, power1, factor1, shift1 = grid_call(
+        attention_kernel, "attention", offs,
+        [qs, gs, gradient, own, other, peak0, lse0, out0],
+        [wide(BF), tall(224), rows(384), rows(384), tall(128), tall(128), rows(256), tall(64), tall(64)],
         scratch=[pltpu.VMEM((TOGETHER, 4, TOKENS, 128), F32), stats, stats],
     )
     theirs = send(down_other, "core")
-    grad_queries, d0 = grid_call(
-        return0_kernel, "return0", None,
-        [queries, gradient, key_rows, value_rows, far_keys, far_values, power0, factor0, shift0, part],
-        [wide(BF), rows(256)],
-    )
-    rows_kept, rows_far, up, down, x_far, x_kept = whole_call(
-        reduce_kernel, "reduce", [rows(128), rows(128), rows(96), rows(96), rows(48), rows(48, F32)],
-        None, down_own, theirs, after=(d0,),
+    placed, mine1, theirs1 = grid_call(
+        return1_kernel, "return1", offs, [qs, gs, (own, 0), (other, 0), power1, factor1, shift1, part],
+        [wide(F32), rows(128), rows(128)],
+    )
+    mid_kept, mid_far, up, down, x_far, x_kept = whole_call(
+        reduce_kernel, "reduce", [rows(64), rows(64), rows(96), rows(96), rows(48), rows(48, F32)],
+        None, down_own, theirs, after=(mine1,),
     )
     from_down = send(up, "up")
     from_up = send(down, "down")
     x_far = send(x_far, "head")
-    (far,) = whole_call(place_kernel, "place", [rows(128)], offs, d0, rows_far, after=(x_far,))
-    far = send(far, "head")
+    grad_queries, d0 = grid_call(
+        return0_kernel, "return0", None, [queries, gradient, *kv, power0, factor0, shift0, placed],
+        [wide(BF), rows(256)], after=(x_far,),
+    )
+    theirs1 = send(theirs1, "core")
+    half = ((TOGETHER, TOKENS, 2 * D), BF)
+    fars = whole_call(
+        place_kernel, "place", [half] * (GROUPS // TOGETHER), offs, d0, mine1, theirs1, mid_far, after=(x_far,)
+    )
+    fars = [send(far, "head") for far in fars]
     one, two, three = whole_call(
         cross_kernel, "cross", [rows(32), rows(16), rows(16)], None, x_kept, x_far, from_up, from_down
     )
     one, two, three = send(one, "x1"), send(two, "x2"), send(three, "x3")
     out = ((TOKENS, GROUPS * D), BF)
     grad_keys, grad_values = whole_call(
-        finish_kernel, "finish", [out, out], offs, d0, rows_kept, far, from_up, from_down, one, two, three
+        finish_kernel, "finish", [out, out], offs, d0, mine1, theirs1, mid_kept, *fars, from_up, from_down,
+        one, two, three,
     )
     return (attended, grad_queries, grad_keys, grad_values)
 

time: 88.3 us -> 84.3 us (0.955)
  waiting for transfers between devices: 35.3 us -> 29.2 us
  Pallas kernels: 22.6 us -> 24.6 us
    ppermute x18 -> x20, waiting for transfers between devices: 35.3 us -> 29.2 us  [send(): return lax.ppermute(x, AXES, route[name])]
    pallas_call x4 -> x5, Pallas kernels: 18.5 us -> 20.4 us  [grid_call(): pl.pallas_call(body, name=name, grid=(GROUPS // TOGETHER,), in_specs=spec...]
    ppermute x18 -> x20, starting transfers between devices: 27.3 us -> 27.7 us  [send(): return lax.ppermute(x, AXES, route[name])]
  transfers between devices with their start and end apart: 18 -> 20, of which waited for: 12 -> 10; matrix products, arithmetic and copies ran while one was open for 1% -> 1% of each run, Pallas kernels for 9% -> 14%
where the time goes in v5:
time: 84.3 us; the launch traced here: 84.2 us
  waiting for transfers between devices  29.2 us (35%)
  starting transfers between devices  27.7 us (33%)
  Pallas kernels  24.6 us (29%)
  other arithmetic  1.14 us (1%)
    ppermute x20, waiting for transfers between devices, send(): return lax.ppermute(x, AXES, route[name])  29.2 us
    ppermute x20, starting transfers between devices, send(): return lax.ppermute(x, AXES, route[name])  27.7 us
    pallas_call x5, Pallas kernels, grid_call(): pl.pallas_call(body, name=name, grid=(GROUPS // TOGETHER,), in_specs=spec...  20.4 us
    pallas_call x6, Pallas kernels, whole_call(): pl.pallas_call(body, name=name, out_shape=shapes, in_specs=specs, out_spe...  4.13 us
  transfers between devices with their start and end apart: 20, of which 10 were waited for; matrix products, arithmetic and copies ran while one was open for 1% of the time, Pallas kernels for 14%

profile of v5, /device:TPU:0, one launch (start us, length us, event | category | flops | bytes accessed | tf_op | source)
XLA Modules:
  0.0 84.2 jit_solution(8880143545597444104)
XLA Ops:
  0.6 0.8 copy.10
  1.4 4.0 %collective-permute-start = (s32[5,4]{1,0:T(8,128)S(1)}, s32[5,4]{1,0:T(8,128)S(1)}, u32[]{:S(2)}, u32[]{:S(2)}) collective-permute-start(s32[5,4]{1,0:T(8,128)S(1)} %copy.10), channel_id=1, source_target_pairs={{0,1},{1,0},{2,3},{3,2},{4,5},{5,4},{6,7},{7,6},{8,9},{9,8},{10,11... | collective-permute-start | bytes 248 | tf_op jit(solution)/shard_map/ppermute | solution.py:454
  5.4 1.1 %pad_maximum_fusion.keys.values = bf16[128,2048]{1,0:T(8,128)(2,1)S(1)} fusion(bf16[128,1024]{1,0:T(8,128)(2,1)} %v_ref.3, bf16[128,1024]{1,0:T(8,128)(2,1)} %k_ref.3), kind=kLoop, calls=%fused_computation | loop fusion | flops 1048576 | bytes 1048576 | tf_op jit(solution)/shard_map/concatenate | solution.py:463
  6.4 0.1 collective-permute-start.1
  6.5 3.5 %collective-permute-start.2 = (bf16[128,1024]{1,0:T(8,128)(2,1)}, bf16[128,1024]{1,0:T(8,128)(2,1)S(1)}, u32[]{:S(2)}, u32[]{:S(2)}) collective-permute-start(bf16[128,1024]{1,0:T(8,128)(2,1)} %v_ref.3), channel_id=1, source_target_pairs={{0,1},{1,0},{2,3},{3,2},{4,5},{5,4},{6,7},{7,6},{8,9},{9,8},{10,11... | collective-permute-start | bytes 786440 | tf_op jit(solution)/shard_map/ppermute | solution.py:454
  10.0 0.0 collective-permute-done
  10.0 0.1 add_select_fusion.offs
  10.1 1.1 %select.1 = (bf16[8,64,256]{2,1,0:T(8,128)(2,1)S(1)}, bf16[8,64,256]{2,1,0:T(8,128)(2,1)S(1)}, bf16[8,32,256]{2,1,0:T(8,128)(2,1)S(1)}, bf16[8,16,256]{2,1,0:T(8,128)(2,1)S(1)}) custom-call(s32[5,8]{1,0:T(8,128)S(1)} %add_select_fusion.offs, bf16[128,2048]{1,0:T(8,128)(2,1)S(1)} %pad_maximum_fusion.keys.values, bf16[128,2048]{1,0:T(8,128)(2,1)S(1)} %pad_maximum_fusion.keys.values), custom_call_target="tpu_custom_call" | custom-call | flops 4000000000 | bytes 16000000 | tf_op jit(solution)/shard_map/select/pallas_call | solution.py:420
  11.3 1.6 %collective-permute-start.3 = (bf16[8,32,256]{2,1,0:T(8,128)(2,1)S(1)}, bf16[8,32,256]{2,1,0:T(8,128)(2,1)S(1)}, u32[]{:S(2)}, u32[]{:S(2)}) collective-permute-start(bf16[8,32,256]{2,1,0:T(8,128)(2,1)S(1)} %get-tuple-element.50), channel_id=1, source_target_pairs={{0,8},{1,9},{2,10},{3,11},{4,12},{5,13},{6,14},{7,15},{8,0},{9,1},... | collective-permute-start | bytes 393224 | tf_op jit(solution)/shard_map/ppermute | solution.py:454
  12.8 2.1 %collective-permute-start.5 = (bf16[8,16,256]{2,1,0:T(8,128)(2,1)S(1)}, bf16[8,16,256]{2,1,0:T(8,128)(2,1)S(1)}, u32[]{:S(2)}, u32[]{:S(2)}) collective-permute-start(bf16[8,16,256]{2,1,0:T(8,128)(2,1)S(1)} %get-tuple-element.51), channel_id=1, source_target_pairs={{0,24},{1,25},{2,26},{3,27},{4,28},{5,29},{6,30},{7,31},{8,16},{9,... | collective-permute-start | bytes 196616 | tf_op jit(solution)/shard_map/ppermute | solution.py:454
  14.9 0.6 collective-permute-start.4
  15.6 3.3 %collective-permute-done.5.three = bf16[8,16,256]{2,1,0:T(8,128)(2,1)S(1)} collective-permute-done((bf16[8,16,256]{2,1,0:T(8,128)(2,1)S(1)}, bf16[8,16,256]{2,1,0:T(8,128)(2,1)S(1)}, u32[]{:S(2)}, u32[]{:S(2)}) %collective-permute-start.5) | collective-permute-done | bytes 65568 | tf_op jit(solution)/shard_map/ppermute | solution.py:454
  18.9 1.8 %collective-permute-done.4.two = bf16[8,16,256]{2,1,0:T(8,128)(2,1)S(1)} collective-permute-done((bf16[8,16,256]{2,1,0:T(8,128)(2,1)S(1)}, bf16[8,16,256]{2,1,0:T(8,128)(2,1)S(1)}, u32[]{:S(2)}, u32[]{:S(2)}) %collective-permute-start.4) | collective-permute-done | bytes 65568 | tf_op jit(solution)/shard_map/ppermute | solution.py:454
  20.7 0.0 collective-permute-done.3.one
  20.8 1.1 %collective-permute-start.8 = (bf16[8,96,256]{2,1,0:T(8,128)(2,1)S(1)}, bf16[8,96,256]{2,1,0:T(8,128)(2,1)S(1)}, u32[]{:S(2)}, u32[]{:S(2)}) collective-permute-start(bf16[8,96,256]{2,1,0:T(8,128)(2,1)S(1)} %get-tuple-element.56.lift), channel_id=1, source_target_pairs={{0,4},{1,5},{2,6},{3,7},{4,1},{5,0},{6,3},{7,2},{8,12},{9,13},{10,... | collective-permute-start | bytes 1179656 | tf_op jit(solution)/shard_map/ppermute | solution.py:454
  21.8 2.2 %collective-permute-start.7 = (bf16[8,96,256]{2,1,0:T(8,128)(2,1)S(1)}, bf16[8,96,256]{2,1,0:T(8,128)(2,1)S(1)}, u32[]{:S(2)}, u32[]{:S(2)}) collective-permute-start(bf16[8,96,256]{2,1,0:T(8,128)(2,1)S(1)} %get-tuple-element.56.lift), channel_id=1, source_target_pairs={{0,5},{1,4},{2,7},{3,6},{4,0},{5,1},{6,2},{7,3},{8,13},{9,12},{10,... | collective-permute-start | bytes 1179656 | tf_op jit(solution)/shard_map/ppermute | solution.py:454
  24.1 0.0 collective-permute-start.6
  24.1 0.0 collective-permute-done.1.kp_ref.keys
  24.1 3.2 %early.1 = (bf16[8,512,128]{2,1,0:T(8,128)(2,1)S(1)}, bf16[8,512,128]{2,1,0:T(8,128)(2,1)S(1)}, bf16[8,512,256]{2,1,0:T(8,128)(2,1)S(1)}, f32[8,128,128]{2,1,0:T...) custom-call(s32[5,8]{1,0:T(8,128)S(1)} %add_select_fusion.offs, bf16[128,4096]{1,0:T(8,128)(2,1)S(1)} %copy-done.2, ...), custom_call_target="tpu_custom_call" | custom-call | flops 4000000000 | bytes 16000000 | tf_op jit(solution)/shard_map/early/pallas_call | solution.py:420
  27.3 7.2 %collective-permute-done.6.x_far = bf16[8,48,256]{2,1,0:T(8,128)(2,1)S(1)} collective-permute-done((bf16[8,48,256]{2,1,0:T(8,128)(2,1)S(1)}, bf16[8,48,256]{2,1,0:T(8,128)(2,1)S(1)}, u32[]{:S(2)}, u32[]{:S(2)}) %collective-permute-start.6) | collective-permute-done | bytes 196640 | tf_op jit(solution)/shard_map/ppermute | solution.py:454
  34.5 0.9 %collective-permute-done.8.lift_down = bf16[8,96,256]{2,1,0:T(8,128)(2,1)S(1)} collective-permute-done((bf16[8,96,256]{2,1,0:T(8,128)(2,1)S(1)}, bf16[8,96,256]{2,1,0:T(8,128)(2,1)S(1)}, u32[]{:S(2)}, u32[]{:S(2)}) %collective-permute-start.8) | collective-permute-done | bytes 393248 | tf_op jit(solution)/shard_map/ppermute | solution.py:454
  35.5 0.0 collective-permute-done.7.lift_up
  35.5 0.9 %assemble.1.own_ref = bf16[8,512,256]{2,1,0:T(8,128)(2,1)S(1)} custom-call(s32[5,8]{1,0:T(8,128)S(1)} %add_select_fusion.offs, bf16[8,64,256]{2,1,0:T(8,128)(2,1)S(1)} %get-tuple-element.55.first, bf16[8,96,256]{2,1,0:T(8,128)(2,1)S(1)} %get-tuple-element.56.lift, bf16[128,1024]{1,0:T(8,128)(2,1)S(1)} %collective-permute-done.1.kp_ref.keys, ...), custom_call_target="tpu_custom_call" | custom-call | bytes 4000000 | tf_op jit(solution)/shard_map/assemble/pallas_call | solution.py:392
  36.4 0.1 collective-permute-start.9
  36.5 4.1 %collective-permute-done.9.other_ref = bf16[8,512,256]{2,1,0:T(8,128)(2,1)S(1)} collective-permute-done((bf16[8,512,256]{2,1,0:T(8,128)(2,1)S(1)}, bf16[8,512,256]{2,1,0:T(8,128)(2,1)S(1)}, u32[]{:S(2)}, u32[]{:S(2)}) %collective-permute-start.9) | collective-permute-done | bytes 2097184 | tf_op jit(solution)/shard_map/ppermute | solution.py:454
  40.6 9.8 %attention.1 = (bf16[128,4096]{1,0:T(8,128)(2,1)}, f32[8,224,128]{2,1,0:T(8,128)S(1)}, bf16[8,384,256]{2,1,0:T(8,128)(2,1)S(1)}, bf16[8,384,256]{2,1,0:T(8,128)(...) custom-call(s32[5,8]{1,0:T(8,128)S(1)} %add_select_fusion.offs, ...), custom_call_target="tpu_custom_call" | custom-call | flops 4000000000 | bytes 16000000 | tf_op jit(solution)/shard_map/attention/pallas_call | solution.py:420
  50.4 0.1 collective-permute-start.10
  50.5 2.7 %return1.1 = (f32[128,4096]{1,0:T(8,128)S(1)}, bf16[8,128,256]{2,1,0:T(8,128)(2,1)S(1)}, bf16[8,128,256]{2,1,0:T(8,128)(2,1)S(1)}) custom-call(s32[5,8]{1,0:T(8,128)S(1)} %add_select_fusion.offs, bf16[8,512,128]{2,1,0:T(8,128)(2,1)S(1)} %get-tuple-element.53.qs_ref, bf16[8,512,128]{2,1,0:T(8,128)(2,1)S(1)} %get-tuple-element.54.gs_ref, ...), custom_call_target="tpu_custom_call" | custom-call | flops 4000000000 | bytes 16000000 | tf_op jit(solution)/shard_map/return1/pallas_call | solution.py:420
  53.3 0.5 collective-permute-done.10.theirs
  53.8 0.4 reduce.1
  54.2 1.1 %collective-permute-start.11 = (bf16[8,48,256]{2,1,0:T(8,128)(2,1)S(1)}, bf16[8,48,256]{2,1,0:T(8,128)(2,1)S(1)}, u32[]{:S(2)}, u32[]{:S(2)}) collective-permute-start(bf16[8,48,256]{2,1,0:T(8,128)(2,1)S(1)} %get-tuple-element.72), channel_id=1, source_target_pairs={{0,1},{1,0},{2,3},{3,2},{4,5},{5,4},{6,7},{7,6},{8,9},{9,8},{10,11... | collective-permute-start | bytes 589832 | tf_op jit(solution)/shard_map/ppermute | solution.py:454
  55.3 0.0 collective-permute-start.12
  55.3 2.5 %collective-permute-start.15 = (bf16[8,96,256]{2,1,0:T(8,128)(2,1)S(1)}, bf16[8,96,256]{2,1,0:T(8,128)(2,1)S(1)}, u32[]{:S(2)}, u32[]{:S(2)}) collective-permute-start(bf16[8,96,256]{2,1,0:T(8,128)(2,1)S(1)} %get-tuple-element.80), channel_id=1, source_target_pairs={{0,5},{1,4},{2,7},{3,6},{4,0},{5,1},{6,2},{7,3},{8,13},{9,12},{10,... | collective-permute-start | bytes 1179656 | tf_op jit(solution)/shard_map/ppermute | solution.py:454
  57.8 0.3 collective-permute-start.16
  58.1 5.4 %collective-permute-done.11.refs_0_._.far = bf16[8,48,256]{2,1,0:T(8,128)(2,1)S(1)} collective-permute-done((bf16[8,48,256]{2,1,0:T(8,128)(2,1)S(1)}, bf16[8,48,256]{2,1,0:T(8,128)(2,1)S(1)}, u32[]{:S(2)}, u32[]{:S(2)}) %collective-permute-start.11) | collective-permute-done | bytes 196640 | tf_op jit(solution)/shard_map/ppermute | solution.py:454
  63.5 3.6 %return0.1 = (bf16[128,4096]{1,0:T(8,128)(2,1)}, bf16[8,256,256]{2,1,0:T(8,128)(2,1)S(1)}) custom-call(bf16[128,4096]{1,0:T(8,128)(2,1)S(1)} %copy-done.2, bf16[128,4096]{1,0:T(8,128)(2,1)S(1)} %copy-done.3, bf16[128,1024]{1,0:T(8,128)(2,1)S(1)} %copy-done, bf16[128,1024]{1,0:T(8,128)(2,1)S(1)} %copy-done.1, ...), custom_call_target="tpu_custom_call" | custom-call | flops 4000000000 | bytes 16000000 | tf_op jit(solution)/shard_map/return0/pallas_call | solution.py:420
  67.1 0.0 collective-permute-done.12.theirs
  67.1 0.9 %place.1 = (bf16[4,128,256]{2,1,0:T(8,128)(2,1)S(1)}, bf16[4,128,256]{2,1,0:T(8,128)(2,1)S(1)}) custom-call(s32[5,8]{1,0:T(8,128)S(1)} %add_select_fusion.offs, bf16[8,256,256]{2,1,0:T(8,128)(2,1)S(1)} %get-tuple-element.74.d0, bf16[8,128,256]{2,1,0:T(8,128)(2,1)S(1)} %get-tuple-element.71._.mine, bf16[8,128,256]{2,1,0:T(8,128)(2,1)S(1)} %collective-permute-done.12.theirs, ...), custom_call_target="tpu_custom_call" | custom-call | bytes 4000000 | tf_op jit(solution)/shard_map/place/pallas_call | solution.py:392
  68.0 1.1 %collective-permute-start.13 = (bf16[4,128,256]{2,1,0:T(8,128)(2,1)S(1)}, bf16[4,128,256]{2,1,0:T(8,128)(2,1)S(1)}, u32[]{:S(2)}, u32[]{:S(2)}) collective-permute-start(bf16[4,128,256]{2,1,0:T(8,128)(2,1)S(1)} %get-tuple-element.78), channel_id=1, source_target_pairs={{0,1},{1,0},{2,3},{3,2},{4,5},{5,4},{6,7},{7,6},{8,9},{9,8},{10,11... | collective-permute-start | bytes 786440 | tf_op jit(solution)/shard_map/ppermute | solution.py:454
  69.1 2.5 %collective-permute-start.14 = (bf16[4,128,256]{2,1,0:T(8,128)(2,1)S(1)}, bf16[4,128,256]{2,1,0:T(8,128)(2,1)S(1)}, u32[]{:S(2)}, u32[]{:S(2)}) collective-permute-start(bf16[4,128,256]{2,1,0:T(8,128)(2,1)S(1)} %get-tuple-element.79), channel_id=1, source_target_pairs={{0,1},{1,0},{2,3},{3,2},{4,5},{5,4},{6,7},{7,6},{8,9},{9,8},{10,11... | collective-permute-start | bytes 786440 | tf_op jit(solution)/shard_map/ppermute | solution.py:454
  71.6 0.2 collective-permute-done.15.up.refs_2_
  71.8 0.1 cross.1
  71.9 0.7 collective-permute-start.17
  72.6 2.6 %collective-permute-start.18 = (bf16[8,16,256]{2,1,0:T(8,128)(2,1)S(1)}, bf16[8,16,256]{2,1,0:T(8,128)(2,1)S(1)}, u32[]{:S(2)}, u32[]{:S(2)}) collective-permute-start(bf16[8,16,256]{2,1,0:T(8,128)(2,1)S(1)} %get-tuple-element.84), channel_id=1, source_target_pairs={{0,16},{1,17},{2,18},{3,19},{4,20},{5,21},{6,22},{7,23},{8,24},{9,... | collective-permute-start | bytes 196616 | tf_op jit(solution)/shard_map/ppermute | solution.py:454
  75.2 1.4 %collective-permute-start.19 = (bf16[8,16,256]{2,1,0:T(8,128)(2,1)S(1)}, bf16[8,16,256]{2,1,0:T(8,128)(2,1)S(1)}, u32[]{:S(2)}, u32[]{:S(2)}) collective-permute-start(bf16[8,16,256]{2,1,0:T(8,128)(2,1)S(1)} %get-tuple-element.85), channel_id=1, source_target_pairs={{0,24},{1,25},{2,26},{3,27},{4,28},{5,29},{6,30},{7,31},{8,16},{9,... | collective-permute-start | bytes 196616 | tf_op jit(solution)/shard_map/ppermute | solution.py:454
  76.7 2.2 %collective-permute-done.13.refs_0_ = bf16[4,128,256]{2,1,0:T(8,128)(2,1)S(1)} collective-permute-done((bf16[4,128,256]{2,1,0:T(8,128)(2,1)S(1)}, bf16[4,128,256]{2,1,0:T(8,128)(2,1)S(1)}, u32[]{:S(2)}, u32[]{:S(2)}) %collective-permute-start.13) | collective-permute-done | bytes 262176 | tf_op jit(solution)/shard_map/ppermute | solution.py:454
  78.8 3.5 %collective-permute-done.14.refs_1_ = bf16[4,128,256]{2,1,0:T(8,128)(2,1)S(1)} collective-permute-done((bf16[4,128,256]{2,1,0:T(8,128)(2,1)S(1)}, bf16[4,128,256]{2,1,0:T(8,128)(2,1)S(1)}, u32[]{:S(2)}, u32[]{:S(2)}) %collective-permute-start.14) | collective-permute-done | bytes 262176 | tf_op jit(solution)/shard_map/ppermute | solution.py:454
  82.4 1.8 %finish.1 = (bf16[128,1024]{1,0:T(8,128)(2,1)}, bf16[128,1024]{1,0:T(8,128)(2,1)}) custom-call(s32[5,8]{1,0:T(8,128)S(1)} %add_select_fusion.offs, bf16[8,256,256]{2,1,0:T(8,128)(2,1)S(1)} %get-tuple-element.74.d0, bf16[8,128,256]{2,1,0:T(8,128)(2,1)S(1)} %get-tuple-element.71._.mine, bf16[8,128,256]{2,1,0:T(8,128)(2,1)S(1)} %collective-permute-done.12.theirs, ...), custom_call_target="tpu_custom_call" | custom-call | bytes 4000000 | tf_op jit(solution)/shard_map/finish/pallas_call | solution.py:392
  (14 shorter events, 0.1 us)
Async XLA Ops:
  1.4 8.6 %collective-permute-start = (s32[5,4]{1,0:T(8,128)S(1)}, s32[5,4]{1,0:T(8,128)S(1)}, u32[]{:S(2)}, u32[]{:S(2)}) collective-permute-start(s32[5,4]{1,0:T(8,128)S(1)} %copy.10), channel_id=1, source_target_pairs={{0,1},{1,0},{2,3},{3,2},{4,5},{5,4},{6,7},{7,6},{8,9},{9,8},{10,11... | collective-permute-start | bytes 248 | tf_op jit(solution)/shard_map/ppermute | solution.py:454
  6.4 17.6 %collective-permute-start.1 = (bf16[128,1024]{1,0:T(8,128)(2,1)}, bf16[128,1024]{1,0:T(8,128)(2,1)S(1)}, u32[]{:S(2)}, u32[]{:S(2)}) collective-permute-start(bf16[128,1024]{1,0:T(8,128)(2,1)} %k_ref.3), channel_id=1, source_target_pairs={{0,1},{1,0},{2,3},{3,2},{4,5},{5,4},{6,7},{7,6},{8,9},{9,8},{10,11... | collective-permute-start | bytes 786440 | tf_op jit(solution)/shard_map/ppermute | solution.py:454
  6.5 17.6 %collective-permute-start.2 = (bf16[128,1024]{1,0:T(8,128)(2,1)}, bf16[128,1024]{1,0:T(8,128)(2,1)S(1)}, u32[]{:S(2)}, u32[]{:S(2)}) collective-permute-start(bf16[128,1024]{1,0:T(8,128)(2,1)} %v_ref.3), channel_id=1, source_target_pairs={{0,1},{1,0},{2,3},{3,2},{4,5},{5,4},{6,7},{7,6},{8,9},{9,8},{10,11... | collective-permute-start | bytes 786440 | tf_op jit(solution)/shard_map/ppermute | solution.py:454
  10.1 14.0 %copy-start = (bf16[128,1024]{1,0:T(8,128)(2,1)S(1)}, bf16[128,1024]{1,0:T(8,128)(2,1)}, u32[]{:S(2)}) copy-start(bf16[128,1024]{1,0:T(8,128)(2,1)} %k_ref.3) | copy-start | bytes 786436
  10.1 14.0 %copy-start.1 = (bf16[128,1024]{1,0:T(8,128)(2,1)S(1)}, bf16[128,1024]{1,0:T(8,128)(2,1)}, u32[]{:S(2)}) copy-start(bf16[128,1024]{1,0:T(8,128)(2,1)} %v_ref.3) | copy-start | bytes 786436
  10.1 14.0 %copy-start.2 = (bf16[128,4096]{1,0:T(8,128)(2,1)S(1)}, bf16[128,4096]{1,0:T(8,128)(2,1)}, u32[]{:S(2)}) copy-start(bf16[128,4096]{1,0:T(8,128)(2,1)} %q_ref.3) | copy-start | bytes 3145732
  10.1 14.0 %copy-start.3 = (bf16[128,4096]{1,0:T(8,128)(2,1)S(1)}, bf16[128,4096]{1,0:T(8,128)(2,1)}, u32[]{:S(2)}) copy-start(bf16[128,4096]{1,0:T(8,128)(2,1)} %g_ref.5) | copy-start | bytes 3145732
  11.3 9.4 %collective-permute-start.3 = (bf16[8,32,256]{2,1,0:T(8,128)(2,1)S(1)}, bf16[8,32,256]{2,1,0:T(8,128)(2,1)S(1)}, u32[]{:S(2)}, u32[]{:S(2)}) collective-permute-start(bf16[8,32,256]{2,1,0:T(8,128)(2,1)S(1)} %get-tuple-element.50), channel_id=1, source_target_pairs={{0,8},{1,9},{2,10},{3,11},{4,12},{5,13},{6,14},{7,15},{8,0},{9,1},... | collective-permute-start | bytes 393224 | tf_op jit(solution)/shard_map/ppermute | solution.py:454
  12.8 6.1 %collective-permute-start.5 = (bf16[8,16,256]{2,1,0:T(8,128)(2,1)S(1)}, bf16[8,16,256]{2,1,0:T(8,128)(2,1)S(1)}, u32[]{:S(2)}, u32[]{:S(2)}) collective-permute-start(bf16[8,16,256]{2,1,0:T(8,128)(2,1)S(1)} %get-tuple-element.51), channel_id=1, source_target_pairs={{0,24},{1,25},{2,26},{3,27},{4,28},{5,29},{6,30},{7,31},{8,16},{9,... | collective-permute-start | bytes 196616 | tf_op jit(solution)/shard_map/ppermute | solution.py:454
  14.9 5.8 %collective-permute-start.4 = (bf16[8,16,256]{2,1,0:T(8,128)(2,1)S(1)}, bf16[8,16,256]{2,1,0:T(8,128)(2,1)S(1)}, u32[]{:S(2)}, u32[]{:S(2)}) collective-permute-start(bf16[8,16,256]{2,1,0:T(8,128)(2,1)S(1)} %get-tuple-element.51), channel_id=1, source_target_pairs={{0,16},{1,17},{2,18},{3,19},{4,20},{5,21},{6,22},{7,23},{8,24},{9,... | collective-permute-start | bytes 196616 | tf_op jit(solution)/shard_map/ppermute | solution.py:454
  20.8 14.7 %collective-permute-start.8 = (bf16[8,96,256]{2,1,0:T(8,128)(2,1)S(1)}, bf16[8,96,256]{2,1,0:T(8,128)(2,1)S(1)}, u32[]{:S(2)}, u32[]{:S(2)}) collective-permute-start(bf16[8,96,256]{2,1,0:T(8,128)(2,1)S(1)} %get-tuple-element.56.lift), channel_id=1, source_target_pairs={{0,4},{1,5},{2,6},{3,7},{4,1},{5,0},{6,3},{7,2},{8,12},{9,13},{10,... | collective-permute-start | bytes 1179656 | tf_op jit(solution)/shard_map/ppermute | solution.py:454
  21.8 13.6 %collective-permute-start.7 = (bf16[8,96,256]{2,1,0:T(8,128)(2,1)S(1)}, bf16[8,96,256]{2,1,0:T(8,128)(2,1)S(1)}, u32[]{:S(2)}, u32[]{:S(2)}) collective-permute-start(bf16[8,96,256]{2,1,0:T(8,128)(2,1)S(1)} %get-tuple-element.56.lift), channel_id=1, source_target_pairs={{0,5},{1,4},{2,7},{3,6},{4,0},{5,1},{6,2},{7,3},{8,13},{9,12},{10,... | collective-permute-start | bytes 1179656 | tf_op jit(solution)/shard_map/ppermute | solution.py:454
  24.1 10.4 %collective-permute-start.6 = (bf16[8,48,256]{2,1,0:T(8,128)(2,1)S(1)}, bf16[8,48,256]{2,1,0:T(8,128)(2,1)S(1)}, u32[]{:S(2)}, u32[]{:S(2)}) collective-permute-start(bf16[8,48,256]{2,1,0:T(8,128)(2,1)S(1)} %get-tuple-element.52.refs_0_), channel_id=1, source_target_pairs={{0,1},{1,0},{2,3},{3,2},{4,5},{5,4},{6,7},{7,6},{8,9},{9,8},{10,11... | collective-permute-start | bytes 589832 | tf_op jit(solution)/shard_map/ppermute | solution.py:454
  36.4 4.2 %collective-permute-start.9 = (bf16[8,512,256]{2,1,0:T(8,128)(2,1)S(1)}, bf16[8,512,256]{2,1,0:T(8,128)(2,1)S(1)}, u32[]{:S(2)}, u32[]{:S(2)}) collective-permute-start(bf16[8,512,256]{2,1,0:T(8,128)(2,1)S(1)} %assemble.1.own_ref), channel_id=1, source_target_pairs={{0,2},{1,3},{2,0},{3,1},{4,6},{5,7},{6,4},{7,5},{8,10},{9,11},{10,... | collective-permute-start | bytes 6291464 | tf_op jit(solution)/shard_map/ppermute | solution.py:454
  50.4 3.4 %collective-permute-start.10 = (bf16[8,384,256]{2,1,0:T(8,128)(2,1)S(1)}, bf16[8,384,256]{2,1,0:T(8,128)(2,1)S(1)}, u32[]{:S(2)}, u32[]{:S(2)}) collective-permute-start(bf16[8,384,256]{2,1,0:T(8,128)(2,1)S(1)} %get-tuple-element.70), channel_id=1, source_target_pairs={{0,2},{1,3},{2,0},{3,1},{4,6},{5,7},{6,4},{7,5},{8,10},{9,11},{10,... | collective-permute-start | bytes 4718600 | tf_op jit(solution)/shard_map/ppermute | solution.py:454
  54.2 9.3 %collective-permute-start.11 = (bf16[8,48,256]{2,1,0:T(8,128)(2,1)S(1)}, bf16[8,48,256]{2,1,0:T(8,128)(2,1)S(1)}, u32[]{:S(2)}, u32[]{:S(2)}) collective-permute-start(bf16[8,48,256]{2,1,0:T(8,128)(2,1)S(1)} %get-tuple-element.72), channel_id=1, source_target_pairs={{0,1},{1,0},{2,3},{3,2},{4,5},{5,4},{6,7},{7,6},{8,9},{9,8},{10,11... | collective-permute-start | bytes 589832 | tf_op jit(solution)/shard_map/ppermute | solution.py:454
  55.3 11.8 %collective-permute-start.12 = (bf16[8,128,256]{2,1,0:T(8,128)(2,1)S(1)}, bf16[8,128,256]{2,1,0:T(8,128)(2,1)S(1)}, u32[]{:S(2)}, u32[]{:S(2)}) collective-permute-start(bf16[8,128,256]{2,1,0:T(8,128)(2,1)S(1)} %get-tuple-element.75), channel_id=1, source_target_pairs={{0,2},{1,3},{2,0},{3,1},{4,6},{5,7},{6,4},{7,5},{8,10},{9,11},{10,... | collective-permute-start | bytes 1572872 | tf_op jit(solution)/shard_map/ppermute | solution.py:454
  55.3 16.5 %collective-permute-start.15 = (bf16[8,96,256]{2,1,0:T(8,128)(2,1)S(1)}, bf16[8,96,256]{2,1,0:T(8,128)(2,1)S(1)}, u32[]{:S(2)}, u32[]{:S(2)}) collective-permute-start(bf16[8,96,256]{2,1,0:T(8,128)(2,1)S(1)} %get-tuple-element.80), channel_id=1, source_target_pairs={{0,5},{1,4},{2,7},{3,6},{4,0},{5,1},{6,2},{7,3},{8,13},{9,12},{10,... | collective-permute-start | bytes 1179656 | tf_op jit(solution)/shard_map/ppermute | solution.py:454
  57.8 14.0 %collective-permute-start.16 = (bf16[8,96,256]{2,1,0:T(8,128)(2,1)S(1)}, bf16[8,96,256]{2,1,0:T(8,128)(2,1)S(1)}, u32[]{:S(2)}, u32[]{:S(2)}) collective-permute-start(bf16[8,96,256]{2,1,0:T(8,128)(2,1)S(1)} %get-tuple-element.81), channel_id=1, source_target_pairs={{0,4},{1,5},{2,6},{3,7},{4,1},{5,0},{6,3},{7,2},{8,12},{9,13},{10,... | collective-permute-start | bytes 1179656 | tf_op jit(solution)/shard_map/ppermute | solution.py:454
  68.0 10.8 %collective-permute-start.13 = (bf16[4,128,256]{2,1,0:T(8,128)(2,1)S(1)}, bf16[4,128,256]{2,1,0:T(8,128)(2,1)S(1)}, u32[]{:S(2)}, u32[]{:S(2)}) collective-permute-start(bf16[4,128,256]{2,1,0:T(8,128)(2,1)S(1)} %get-tuple-element.78), channel_id=1, source_target_pairs={{0,1},{1,0},{2,3},{3,2},{4,5},{5,4},{6,7},{7,6},{8,9},{9,8},{10,11... | collective-permute-start | bytes 786440 | tf_op jit(solution)/shard_map/ppermute | solution.py:454
  69.1 13.2 %collective-permute-start.14 = (bf16[4,128,256]{2,1,0:T(8,128)(2,1)S(1)}, bf16[4,128,256]{2,1,0:T(8,128)(2,1)S(1)}, u32[]{:S(2)}, u32[]{:S(2)}) collective-permute-start(bf16[4,128,256]{2,1,0:T(8,128)(2,1)S(1)} %get-tuple-element.79), channel_id=1, source_target_pairs={{0,1},{1,0},{2,3},{3,2},{4,5},{5,4},{6,7},{7,6},{8,9},{9,8},{10,11... | collective-permute-start | bytes 786440 | tf_op jit(solution)/shard_map/ppermute | solution.py:454
  71.9 10.5 %collective-permute-start.17 = (bf16[8,32,256]{2,1,0:T(8,128)(2,1)S(1)}, bf16[8,32,256]{2,1,0:T(8,128)(2,1)S(1)}, u32[]{:S(2)}, u32[]{:S(2)}) collective-permute-start(bf16[8,32,256]{2,1,0:T(8,128)(2,1)S(1)} %get-tuple-element.83), channel_id=1, source_target_pairs={{0,8},{1,9},{2,10},{3,11},{4,12},{5,13},{6,14},{7,15},{8,0},{9,1},... | collective-permute-start | bytes 393224 | tf_op jit(solution)/shard_map/ppermute | solution.py:454
  72.6 9.7 %collective-permute-start.18 = (bf16[8,16,256]{2,1,0:T(8,128)(2,1)S(1)}, bf16[8,16,256]{2,1,0:T(8,128)(2,1)S(1)}, u32[]{:S(2)}, u32[]{:S(2)}) collective-permute-start(bf16[8,16,256]{2,1,0:T(8,128)(2,1)S(1)} %get-tuple-element.84), channel_id=1, source_target_pairs={{0,16},{1,17},{2,18},{3,19},{4,20},{5,21},{6,22},{7,23},{8,24},{9,... | collective-permute-start | bytes 196616 | tf_op jit(solution)/shard_map/ppermute | solution.py:454
  75.2 7.1 %collective-permute-start.19 = (bf16[8,16,256]{2,1,0:T(8,128)(2,1)S(1)}, bf16[8,16,256]{2,1,0:T(8,128)(2,1)S(1)}, u32[]{:S(2)}, u32[]{:S(2)}) collective-permute-start(bf16[8,16,256]{2,1,0:T(8,128)(2,1)S(1)} %get-tuple-element.85), channel_id=1, source_target_pairs={{0,24},{1,25},{2,26},{3,27},{4,28},{5,29},{6,30},{7,31},{8,16},{9,... | collective-permute-start | bytes 196616 | tf_op jit(solution)/shard_map/ppermute | solution.py:454

commit v6 on v5

--- a/solution.py
+++ b/solution.py
@@ -74,24 +74,38 @@
         last[j] = rows[112:128].astype(BF)
 
 
+def extra_rows(ref, group):
+    at = 40 * (group % 2)
+    return ref[group // 2].astype(F32)[at : at + 40]
+
+
 def compact_kernel(middle, one, two, three, lift, extra):
+    whole = []
     for g in range(GROUPS):
         mine, a, b, c = [ref[g].astype(F32) for ref in (middle, one, two, three)]
         last = [a[16:24], b[:8], c[:8]]
         lift[g] = jnp.concatenate([mine[0:48], a[0:16], mine[48:56]] + last, 0).astype(BF)
-        extra[g] = jnp.concatenate([a[0:16]] + last + [jnp.zeros((8, 2 * D), F32)], 0).astype(BF)
-
-
-def assemble_kernel(offs, first, lift, keys, values, x_far, lift_up, lift_down, _, held):
-    for g in range(GROUPS):
-        far = dot(selector(offs, g), group_rows(keys, values, g))
-        extra = x_far[g].astype(F32)
-        across = jnp.concatenate([far[64:112], extra[0:16], far[112:120], extra[16:40]], 0)
-        lifts = [lift[g].astype(F32), across, lift_up[g].astype(F32), lift_down[g].astype(F32)]
-        rows = [first[g].astype(F32), far[0:64]]
-        for a, b in ((0, 32), (32, 64), (64, 96)):
-            rows += [x[a:b] for x in lifts]
-        held[g] = jnp.concatenate(rows, 0).astype(BF)
+        whole += [a[0:16]] + last
+        if g % 2:
+            extra[g // 2] = jnp.concatenate(whole, 0).astype(BF)
+            whole = []
+
+
+def across_kernel(offs, first, keys, values, _, held, across):
+    for g in range(GROUPS):
+        far = dot(selector(offs, g), group_rows(keys, values, g)).astype(BF)
+        held[g] = jnp.concatenate([first[g], far[0:64]], 0)
+        across[g] = far[64:128]
+
+
+def assemble_kernel(held, across, lift, x_far, lift_up, lift_down, out):
+    for g in range(GROUPS):
+        far, extra = across[g].astype(F32), extra_rows(x_far, g)
+        far = jnp.concatenate([far[0:48], extra[0:16], far[48:56], extra[16:40]], 0).astype(BF)
+        lifts = [lift[g], far, lift_up[g], lift_down[g]]
+        out[g, 0:128] = held[g]
+        for i, (a, b) in enumerate(((0, 32), (32, 64), (64, 96))):
+            out[g, 128 * i + 128 : 128 * i + 256] = jnp.concatenate([x[a:b] for x in lifts], 0)
 
 
 def by_level(rows):
@@ -324,6 +338,7 @@
 
 def reduce_kernel(mine, theirs, _, mid_kept, mid_far, up, down, x_far, x_kept):
     zero = jnp.zeros((8, 2 * D), F32)
+    whole = [[], []]
     for g in range(GROUPS):
         total = mine[g].astype(F32) + theirs[g].astype(F32)
         for z, ref in enumerate((mid_kept, mid_far, up, down)):
@@ -332,11 +347,11 @@
                 ref[g] = jnp.concatenate([second, third, fourth], 0).astype(BF)
                 continue
             ref[g] = jnp.concatenate([second, third[:16], fourth[:8], zero], 0).astype(BF)
-            extra = jnp.concatenate([third[16:], fourth[8:], zero], 0)
-            if z == 0:
-                x_kept[g] = extra
-            else:
-                x_far[g] = extra.astype(BF)
+            whole[z] += [third[16:], fourth[8:]]
+        if g % 2:
+            x_kept[g // 2] = jnp.concatenate(whole[0], 0)
+            x_far[g // 2] = jnp.concatenate(whole[1], 0).astype(BF)
+            whole = [[], []]
 
 
 def place_kernel(offs, d0, mine, theirs, mid_far, _, *refs):
@@ -344,14 +359,14 @@
         first = (mine[g, 64:128].astype(F32) + theirs[g, 64:128].astype(F32)).astype(BF)
         rows = jnp.concatenate([first, mid_far[g]], 0)
         whole = (d0[g, 128:256].astype(F32) + dot(placer(offs, g), rows)).astype(BF)
-        refs[g // TOGETHER][g % TOGETHER] = whole
-
-
-def cross_kernel(kept, far, up, down, one, two, three):
+        refs[0][g] = whole
+
+
+def cross_kernel(kept, far, down, up, one, two, three):
     zero = jnp.zeros((8, 2 * D), F32)
     for g in range(GROUPS):
         sides = up[g].astype(F32) + down[g].astype(F32)
-        total = kept[g] + far[g].astype(F32)
+        total = extra_rows(kept, g) + extra_rows(far, g)
         third = total[0:16] + sides[48:64]
         fourth = total[16:40] + sides[72:96]
         one[g] = jnp.concatenate([third, fourth[0:8], zero], 0).astype(BF)
@@ -359,24 +374,28 @@
         three[g] = jnp.concatenate([fourth[16:24], zero], 0).astype(BF)
 
 
-def finish_kernel(offs, d0, mine, theirs, mid_kept, *refs):
-    *fars, up, down, one, two, three, dk_ref, dv_ref = refs
-    for g in range(GROUPS):
-        kept = mid_kept[g].astype(F32)
+def keep_kernel(offs, d0, mine, theirs, mid_kept, down, up, one, two, three, kept):
+    for g in range(GROUPS):
+        mid = mid_kept[g].astype(F32)
         sides = up[g].astype(F32) + down[g].astype(F32)
         a, b, c = one[g].astype(F32), two[g].astype(F32), three[g].astype(F32)
         rows = jnp.concatenate(
             [
                 mine[g, 0:64].astype(F32) + theirs[g, 0:64].astype(F32),
-                kept[0:32] + sides[0:32],
-                kept[32:48] + sides[32:48] + a[0:16],
-                kept[48:56] + sides[64:72] + a[16:24] + b[0:8] + c[0:8],
+                mid[0:32] + sides[0:32],
+                mid[32:48] + sides[32:48] + a[0:16],
+                mid[48:56] + sides[64:72] + a[16:24] + b[0:8] + c[0:8],
                 jnp.zeros((8, 2 * D), F32),
             ],
             0,
         ).astype(BF)
-        far = fars[g // TOGETHER][g % TOGETHER].astype(F32)
-        whole = d0[g, 0:128].astype(F32) + far + dot(placer(offs, g), rows)
+        kept[g] = d0[g, 0:128].astype(F32) + dot(placer(offs, g), rows)
+
+
+def finish_kernel(kept, *refs):
+    *fars, dk_ref, dv_ref = refs
+    for g in range(GROUPS):
+        whole = kept[g] + fars[0][g].astype(F32)
         dk_ref[:, g * D : (g + 1) * D] = whole[:, :D].astype(BF)
         dv_ref[:, g * D : (g + 1) * D] = whole[:, D:].astype(BF)
 
@@ -437,6 +456,7 @@
 
     table = {
         "head": lambda i: i ^ 1,
+        "near": lambda i: along_z(i, 1 if i & 4 else -1),
         "core": lambda i: i ^ 2,
         "up": lambda i: along_z(i, 1),
         "down": lambda i: along_z(i, -1),
@@ -453,7 +473,7 @@
     def send(x, name):
         return lax.ppermute(x, AXES, route[name])
 
-    other_offsets = send(level_offsets, "head")
+    other_offsets = send(level_offsets, "near")
     low = lax.axis_index("head") == 0
     offs = jnp.where(
         low,
@@ -461,19 +481,18 @@
         jnp.concatenate([other_offsets, level_offsets], 1),
     )
     pair = jnp.concatenate([key_rows, value_rows], 1)
-    key_swap, value_swap, pair = lax.optimization_barrier((key_rows, value_rows, pair))
-    far_keys = send(key_swap, "head")
-    far_values = send(value_swap, "head")
+    far_keys = send(key_rows, "head")
+    far_values = send(value_rows, "head")
 
     rows = lambda n, dtype=BF: ((GROUPS, n, 2 * D), dtype)
-    packed = ((GROUPS, TOKENS, 128), F32)
+    extras = lambda dtype: ((GROUPS // 2, 80, 2 * D), dtype)
     wide = lambda dtype: ((TOKENS, GROUPS * WIDE), dtype)
     first, middle, tail, last = grid_call(
         select_kernel, "select", offs, [(pair, 1), (pair, 1 + GROUPS // TOGETHER)],
         [rows(64), rows(64), rows(32), rows(16)],
     )
     lift, extra = whole_call(
-        compact_kernel, "compact", [rows(96), rows(48)], None,
+        compact_kernel, "compact", [rows(96), extras(BF)], None,
         middle, send(tail, "x1"), send(last, "x2"), send(last, "x3"),
     )
     lift_down = send(lift, "up")
@@ -485,9 +504,11 @@
         early_kernel, "early", offs, [queries, gradient, *kv],
         [tall(512, BF), tall(512, BF), rows(512), tall(128), tall(128), tall(512)], after=(extra,),
     )
+    held, across = whole_call(
+        across_kernel, "across", [rows(128), rows(64)], offs, first, far_keys, far_values, after=(lse0,)
+    )
     (own,) = whole_call(
-        assemble_kernel, "assemble", [rows(512)], offs, first, lift, far_keys, far_values,
-        extra_far, lift_up, lift_down, after=(lse0,),
+        assemble_kernel, "assemble", [rows(512)], None, held, across, lift, extra_far, lift_up, lift_down
     )
     other = send(own, "core")
     stats = pltpu.VMEM((TOGETHER, TOKENS, 128), F32)
@@ -503,31 +524,32 @@
         [wide(F32), rows(128), rows(128)],
     )
     mid_kept, mid_far, up, down, x_far, x_kept = whole_call(
-        reduce_kernel, "reduce", [rows(64), rows(64), rows(96), rows(96), rows(48), rows(48, F32)],
+        reduce_kernel, "reduce", [rows(64), rows(64), rows(96), rows(96), extras(BF), extras(F32)],
         None, down_own, theirs, after=(mine1,),
     )
     from_down = send(up, "up")
     from_up = send(down, "down")
     x_far = send(x_far, "head")
+    theirs1 = send(theirs1, "core")
     grad_queries, d0 = grid_call(
         return0_kernel, "return0", None, [queries, gradient, *kv, power0, factor0, shift0, placed],
-        [wide(BF), rows(256)], after=(x_far,),
-    )
-    theirs1 = send(theirs1, "core")
+        [wide(BF), rows(256)], after=(theirs1,),
+    )
     half = ((TOGETHER, TOKENS, 2 * D), BF)
     fars = whole_call(
-        place_kernel, "place", [half] * (GROUPS // TOGETHER), offs, d0, mine1, theirs1, mid_far, after=(x_far,)
+        place_kernel, "place", [rows(128)], offs, d0, mine1, theirs1, mid_far, after=(x_far,)
     )
     fars = [send(far, "head") for far in fars]
     one, two, three = whole_call(
-        cross_kernel, "cross", [rows(32), rows(16), rows(16)], None, x_kept, x_far, from_up, from_down
+        cross_kernel, "cross", [rows(32), rows(16), rows(16)], None, x_kept, x_far, from_down, from_up
     )
     one, two, three = send(one, "x1"), send(two, "x2"), send(three, "x3")
     out = ((TOKENS, GROUPS * D), BF)
-    grad_keys, grad_values = whole_call(
-        finish_kernel, "finish", [out, out], offs, d0, mine1, theirs1, mid_kept, *fars, from_up, from_down,
+    (kept,) = whole_call(
+        keep_kernel, "keep", [rows(128, F32)], offs, d0, mine1, theirs1, mid_kept, from_down, from_up,
         one, two, three,
     )
+    grad_keys, grad_values = whole_call(finish_kernel, "finish", [out, out], None, kept, *fars)
     return (attended, grad_queries, grad_keys, grad_values)
 
 

time: 84.3 us -> 81.6 us (0.968)
  starting transfers between devices: 27.7 us -> 25.6 us
  waiting for transfers between devices: 29.2 us -> 28.1 us
    ppermute x20 -> x19, starting transfers between devices: 27.7 us -> 25.6 us  [send(): return lax.ppermute(x, AXES, route[name])]
    ppermute x20 -> x19, waiting for transfers between devices: 29.2 us -> 28.1 us  [send(): return lax.ppermute(x, AXES, route[name])]
    pallas_call x6 -> x8, Pallas kernels: 4.13 us -> 4.34 us  [whole_call(): pl.pallas_call(body, name=name, out_shape=shapes, in_specs=specs, out_spe...]
  transfers between devices with their start and end apart: 20 -> 19, of which waited for: 10 -> 12; matrix products, arithmetic and copies ran while one was open for 1% -> 1% of each run, Pallas kernels for 14% -> 17%
where the time goes in v6:
time: 81.6 us; the launch traced here: 81.2 us
  waiting for transfers between devices  28.1 us (34%)
  starting transfers between devices  25.6 us (31%)
  Pallas kernels  24.8 us (30%)
  other arithmetic  1.14 us (1%)
    ppermute x19, waiting for transfers between devices, send(): return lax.ppermute(x, AXES, route[name])  28.1 us
    ppermute x19, starting transfers between devices, send(): return lax.ppermute(x, AXES, route[name])  25.6 us
    pallas_call x5, Pallas kernels, grid_call(): pl.pallas_call(body, name=name, grid=(GROUPS // TOGETHER,), in_specs=spec...  20.4 us
    pallas_call x8, Pallas kernels, whole_call(): pl.pallas_call(body, name=name, out_shape=shapes, in_specs=specs, out_spe...  4.34 us
  transfers between devices with their start and end apart: 19, of which 12 were waited for; matrix products, arithmetic and copies ran while one was open for 1% of the time, Pallas kernels for 17%

profile of v6, /device:TPU:0, one launch (start us, length us, event | category | flops | bytes accessed | tf_op | source)
XLA Modules:
  0.0 81.2 jit_solution(1313443592758394777)
XLA Ops:
  0.6 0.8 copy.10
  1.4 4.1 %collective-permute-start = (s32[5,4]{1,0:T(8,128)S(1)}, s32[5,4]{1,0:T(8,128)S(1)}, u32[]{:S(2)}, u32[]{:S(2)}) collective-permute-start(s32[5,4]{1,0:T(8,128)S(1)} %copy.10), channel_id=1, source_target_pairs={{0,5},{1,4},{2,7},{3,6},{4,1},{5,0},{6,3},{7,2},{8,13},{9,12},{10,... | collective-permute-start | bytes 248 | tf_op jit(solution)/shard_map/ppermute | solution.py:474
  5.5 0.0 collective-permute-start.1
  5.5 3.5 %collective-permute-start.2 = (bf16[128,1024]{1,0:T(8,128)(2,1)}, bf16[128,1024]{1,0:T(8,128)(2,1)S(1)}, u32[]{:S(2)}, u32[]{:S(2)}) collective-permute-start(bf16[128,1024]{1,0:T(8,128)(2,1)} %v_ref.3), channel_id=1, source_target_pairs={{0,1},{1,0},{2,3},{3,2},{4,5},{5,4},{6,7},{7,6},{8,9},{9,8},{10,11... | collective-permute-start | bytes 786440 | tf_op jit(solution)/shard_map/ppermute | solution.py:474
  9.1 1.1 %pad_maximum_fusion.keys.values = bf16[128,2048]{1,0:T(8,128)(2,1)S(1)} fusion(bf16[128,1024]{1,0:T(8,128)(2,1)} %v_ref.3, bf16[128,1024]{1,0:T(8,128)(2,1)} %k_ref.3), kind=kLoop, calls=%fused_computation | loop fusion | flops 1048576 | bytes 1048576 | tf_op jit(solution)/shard_map/concatenate | solution.py:483
  10.1 0.0 collective-permute-done
  10.1 0.1 add_select_fusion.offs
  10.2 1.1 %select.1 = (bf16[8,64,256]{2,1,0:T(8,128)(2,1)S(1)}, bf16[8,64,256]{2,1,0:T(8,128)(2,1)S(1)}, bf16[8,32,256]{2,1,0:T(8,128)(2,1)S(1)}, bf16[8,16,256]{2,1,0:T(8,128)(2,1)S(1)}) custom-call(s32[5,8]{1,0:T(8,128)S(1)} %add_select_fusion.offs, bf16[128,2048]{1,0:T(8,128)(2,1)S(1)} %pad_maximum_fusion.keys.values, bf16[128,2048]{1,0:T(8,128)(2,1)S(1)} %pad_maximum_fusion.keys.values), custom_call_target="tpu_custom_call" | custom-call | flops 4000000000 | bytes 16000000 | tf_op jit(solution)/shard_map/select/pallas_call | solution.py:439
  11.4 1.6 %collective-permute-start.3 = (bf16[8,32,256]{2,1,0:T(8,128)(2,1)S(1)}, bf16[8,32,256]{2,1,0:T(8,128)(2,1)S(1)}, u32[]{:S(2)}, u32[]{:S(2)}) collective-permute-start(bf16[8,32,256]{2,1,0:T(8,128)(2,1)S(1)} %get-tuple-element.44), channel_id=1, source_target_pairs={{0,8},{1,9},{2,10},{3,11},{4,12},{5,13},{6,14},{7,15},{8,0},{9,1},... | collective-permute-start | bytes 393224 | tf_op jit(solution)/shard_map/ppermute | solution.py:474
  12.9 2.1 %collective-permute-start.5 = (bf16[8,16,256]{2,1,0:T(8,128)(2,1)S(1)}, bf16[8,16,256]{2,1,0:T(8,128)(2,1)S(1)}, u32[]{:S(2)}, u32[]{:S(2)}) collective-permute-start(bf16[8,16,256]{2,1,0:T(8,128)(2,1)S(1)} %get-tuple-element.45), channel_id=1, source_target_pairs={{0,24},{1,25},{2,26},{3,27},{4,28},{5,29},{6,30},{7,31},{8,16},{9,... | collective-permute-start | bytes 196616 | tf_op jit(solution)/shard_map/ppermute | solution.py:474
  15.0 0.6 collective-permute-start.4
  15.7 3.3 %collective-permute-done.5.three = bf16[8,16,256]{2,1,0:T(8,128)(2,1)S(1)} collective-permute-done((bf16[8,16,256]{2,1,0:T(8,128)(2,1)S(1)}, bf16[8,16,256]{2,1,0:T(8,128)(2,1)S(1)}, u32[]{:S(2)}, u32[]{:S(2)}) %collective-permute-start.5) | collective-permute-done | bytes 65568 | tf_op jit(solution)/shard_map/ppermute | solution.py:474
  19.0 1.8 %collective-permute-done.4.two = bf16[8,16,256]{2,1,0:T(8,128)(2,1)S(1)} collective-permute-done((bf16[8,16,256]{2,1,0:T(8,128)(2,1)S(1)}, bf16[8,16,256]{2,1,0:T(8,128)(2,1)S(1)}, u32[]{:S(2)}, u32[]{:S(2)}) %collective-permute-start.4) | collective-permute-done | bytes 65568 | tf_op jit(solution)/shard_map/ppermute | solution.py:474
  20.8 0.0 collective-permute-done.3.one
  20.9 0.1 collective-permute-start.8
  20.9 3.2 %collective-permute-start.7 = (bf16[8,96,256]{2,1,0:T(8,128)(2,1)S(1)}, bf16[8,96,256]{2,1,0:T(8,128)(2,1)S(1)}, u32[]{:S(2)}, u32[]{:S(2)}) collective-permute-start(bf16[8,96,256]{2,1,0:T(8,128)(2,1)S(1)} %get-tuple-element.53.lift), channel_id=1, source_target_pairs={{0,5},{1,4},{2,7},{3,6},{4,0},{5,1},{6,2},{7,3},{8,13},{9,12},{10,... | collective-permute-start | bytes 1179656 | tf_op jit(solution)/shard_map/ppermute | solution.py:474
  24.2 3.2 %early.1 = (bf16[8,512,128]{2,1,0:T(8,128)(2,1)S(1)}, bf16[8,512,128]{2,1,0:T(8,128)(2,1)S(1)}, bf16[8,512,256]{2,1,0:T(8,128)(2,1)S(1)}, f32[8,128,128]{2,1,0:T...) custom-call(s32[5,8]{1,0:T(8,128)S(1)} %add_select_fusion.offs, bf16[128,4096]{1,0:T(8,128)(2,1)S(1)} %copy-done.2, ...), custom_call_target="tpu_custom_call" | custom-call | flops 4000000000 | bytes 16000000 | tf_op jit(solution)/shard_map/early/pallas_call | solution.py:439
  27.4 0.9 %across.1 = (bf16[8,128,256]{2,1,0:T(8,128)(2,1)S(1)}, bf16[8,64,256]{2,1,0:T(8,128)(2,1)S(1)}) custom-call(s32[5,8]{1,0:T(8,128)S(1)} %add_select_fusion.offs, bf16[8,64,256]{2,1,0:T(8,128)(2,1)S(1)} %get-tuple-element.49.first, bf16[128,1024]{1,0:T(8,128)(2,1)S(1)} %collective-permute-done.1.kp_ref.keys, ...), custom_call_target="tpu_custom_call" | custom-call | bytes 4000000 | tf_op jit(solution)/shard_map/across/pallas_call | solution.py:411
  28.3 5.2 %collective-permute-done.6.x_far = bf16[4,80,256]{2,1,0:T(8,128)(2,1)S(1)} collective-permute-done((bf16[4,80,256]{2,1,0:T(8,128)(2,1)S(1)}, bf16[4,80,256]{2,1,0:T(8,128)(2,1)S(1)}, u32[]{:S(2)}, u32[]{:S(2)}) %collective-permute-start.6) | collective-permute-done | bytes 163872 | tf_op jit(solution)/shard_map/ppermute | solution.py:474
  33.6 1.3 %collective-permute-done.8.lift_down = bf16[8,96,256]{2,1,0:T(8,128)(2,1)S(1)} collective-permute-done((bf16[8,96,256]{2,1,0:T(8,128)(2,1)S(1)}, bf16[8,96,256]{2,1,0:T(8,128)(2,1)S(1)}, u32[]{:S(2)}, u32[]{:S(2)}) %collective-permute-start.8) | collective-permute-done | bytes 393248 | tf_op jit(solution)/shard_map/ppermute | solution.py:474
  34.8 0.1 assemble.1.own_ref
  35.0 0.1 collective-permute-start.9
  35.1 4.1 %collective-permute-done.9.other_ref = bf16[8,512,256]{2,1,0:T(8,128)(2,1)S(1)} collective-permute-done((bf16[8,512,256]{2,1,0:T(8,128)(2,1)S(1)}, bf16[8,512,256]{2,1,0:T(8,128)(2,1)S(1)}, u32[]{:S(2)}, u32[]{:S(2)}) %collective-permute-start.9) | collective-permute-done | bytes 2097184 | tf_op jit(solution)/shard_map/ppermute | solution.py:474
  39.2 9.7 %attention.1 = (bf16[128,4096]{1,0:T(8,128)(2,1)}, f32[8,224,128]{2,1,0:T(8,128)S(1)}, bf16[8,384,256]{2,1,0:T(8,128)(2,1)S(1)}, bf16[8,384,256]{2,1,0:T(8,128)(...) custom-call(s32[5,8]{1,0:T(8,128)S(1)} %add_select_fusion.offs, ...), custom_call_target="tpu_custom_call" | custom-call | flops 4000000000 | bytes 16000000 | tf_op jit(solution)/shard_map/attention/pallas_call | solution.py:439
  49.0 0.1 collective-permute-start.11
  49.1 2.7 %return1.1 = (f32[128,4096]{1,0:T(8,128)S(1)}, bf16[8,128,256]{2,1,0:T(8,128)(2,1)S(1)}, bf16[8,128,256]{2,1,0:T(8,128)(2,1)S(1)}) custom-call(s32[5,8]{1,0:T(8,128)S(1)} %add_select_fusion.offs, bf16[8,512,128]{2,1,0:T(8,128)(2,1)S(1)} %get-tuple-element.47.qs_ref, bf16[8,512,128]{2,1,0:T(8,128)(2,1)S(1)} %get-tuple-element.48.gs_ref, ...), custom_call_target="tpu_custom_call" | custom-call | flops 4000000000 | bytes 16000000 | tf_op jit(solution)/shard_map/return1/pallas_call | solution.py:439
  51.8 0.5 collective-permute-start.10
  52.3 0.1 collective-permute-done.11.theirs
  52.4 0.4 reduce.1
  52.7 0.7 collective-permute-start.14
  53.4 3.2 %collective-permute-start.12 = (bf16[8,96,256]{2,1,0:T(8,128)(2,1)S(1)}, bf16[8,96,256]{2,1,0:T(8,128)(2,1)S(1)}, u32[]{:S(2)}, u32[]{:S(2)}) collective-permute-start(bf16[8,96,256]{2,1,0:T(8,128)(2,1)S(1)} %get-tuple-element.72), channel_id=1, source_target_pairs={{0,4},{1,5},{2,6},{3,7},{4,1},{5,0},{6,3},{7,2},{8,12},{9,13},{10,... | collective-permute-start | bytes 1179656 | tf_op jit(solution)/shard_map/ppermute | solution.py:474
  56.6 0.0 collective-permute-start.13
  56.6 0.0 collective-permute-done.10.refs_0_.theirs
  56.6 3.6 %return0.1 = (bf16[128,4096]{1,0:T(8,128)(2,1)}, bf16[8,256,256]{2,1,0:T(8,128)(2,1)S(1)}) custom-call(bf16[128,4096]{1,0:T(8,128)(2,1)S(1)} %copy-done.2, bf16[128,4096]{1,0:T(8,128)(2,1)S(1)} %copy-done.3, bf16[128,1024]{1,0:T(8,128)(2,1)S(1)} %copy-done, bf16[128,1024]{1,0:T(8,128)(2,1)S(1)} %copy-done.1, ...), custom_call_target="tpu_custom_call" | custom-call | flops 4000000000 | bytes 16000000 | tf_op jit(solution)/shard_map/return0/pallas_call | solution.py:439
  60.3 1.1 %collective-permute-done.14.far._ = bf16[4,80,256]{2,1,0:T(8,128)(2,1)S(1)} collective-permute-done((bf16[4,80,256]{2,1,0:T(8,128)(2,1)S(1)}, bf16[4,80,256]{2,1,0:T(8,128)(2,1)S(1)}, u32[]{:S(2)}, u32[]{:S(2)}) %collective-permute-start.14) | collective-permute-done | bytes 163872 | tf_op jit(solution)/shard_map/ppermute | solution.py:474
  61.4 0.9 %place.1 = bf16[8,128,256]{2,1,0:T(8,128)(2,1)S(1)} custom-call(s32[5,8]{1,0:T(8,128)S(1)} %add_select_fusion.offs, bf16[8,256,256]{2,1,0:T(8,128)(2,1)S(1)} %get-tuple-element.67.d0, bf16[8,128,256]{2,1,0:T(8,128)(2,1)S(1)} %get-tuple-element.68._.mine, bf16[8,128,256]{2,1,0:T(8,128)(2,1)S(1)} %collective-permute-done.10.refs_0_.theirs, ...), custom_call_target="tpu_custom_call" | custom-call | bytes 4000000 | tf_op jit(solution)/shard_map/place/pallas_call | solution.py:411
  62.3 1.0 %collective-permute-start.18 = (bf16[8,128,256]{2,1,0:T(8,128)(2,1)S(1)}, bf16[8,128,256]{2,1,0:T(8,128)(2,1)S(1)}, u32[]{:S(2)}, u32[]{:S(2)}) collective-permute-start(bf16[8,128,256]{2,1,0:T(8,128)(2,1)S(1)} %place.1), channel_id=1, source_target_pairs={{0,1},{1,0},{2,3},{3,2},{4,5},{5,4},{6,7},{7,6},{8,9},{9,8},{10,11... | collective-permute-start | bytes 1572872 | tf_op jit(solution)/shard_map/ppermute | solution.py:474
  63.3 6.4 %collective-permute-done.12.down = bf16[8,96,256]{2,1,0:T(8,128)(2,1)S(1)} collective-permute-done((bf16[8,96,256]{2,1,0:T(8,128)(2,1)S(1)}, bf16[8,96,256]{2,1,0:T(8,128)(2,1)S(1)}, u32[]{:S(2)}, u32[]{:S(2)}) %collective-permute-start.12) | collective-permute-done | bytes 393248 | tf_op jit(solution)/shard_map/ppermute | solution.py:474
  69.7 0.4 collective-permute-done.13.up
  70.1 0.1 cross.1
  70.2 0.8 collective-permute-start.15
  70.9 1.7 %collective-permute-start.16 = (bf16[8,16,256]{2,1,0:T(8,128)(2,1)S(1)}, bf16[8,16,256]{2,1,0:T(8,128)(2,1)S(1)}, u32[]{:S(2)}, u32[]{:S(2)}) collective-permute-start(bf16[8,16,256]{2,1,0:T(8,128)(2,1)S(1)} %get-tuple-element.77), channel_id=1, source_target_pairs={{0,16},{1,17},{2,18},{3,19},{4,20},{5,21},{6,22},{7,23},{8,24},{9,... | collective-permute-start | bytes 196616 | tf_op jit(solution)/shard_map/ppermute | solution.py:474
  72.6 2.3 %collective-permute-start.17 = (bf16[8,16,256]{2,1,0:T(8,128)(2,1)S(1)}, bf16[8,16,256]{2,1,0:T(8,128)(2,1)S(1)}, u32[]{:S(2)}, u32[]{:S(2)}) collective-permute-start(bf16[8,16,256]{2,1,0:T(8,128)(2,1)S(1)} %get-tuple-element.78), channel_id=1, source_target_pairs={{0,24},{1,25},{2,26},{3,27},{4,28},{5,29},{6,30},{7,31},{8,16},{9,... | collective-permute-start | bytes 196616 | tf_op jit(solution)/shard_map/ppermute | solution.py:474
  75.0 2.0 %collective-permute-done.16.two = bf16[8,16,256]{2,1,0:T(8,128)(2,1)S(1)} collective-permute-done((bf16[8,16,256]{2,1,0:T(8,128)(2,1)S(1)}, bf16[8,16,256]{2,1,0:T(8,128)(2,1)S(1)}, u32[]{:S(2)}, u32[]{:S(2)}) %collective-permute-start.16) | collective-permute-done | bytes 65568 | tf_op jit(solution)/shard_map/ppermute | solution.py:474
  77.0 1.1 %collective-permute-done.17.three = bf16[8,16,256]{2,1,0:T(8,128)(2,1)S(1)} collective-permute-done((bf16[8,16,256]{2,1,0:T(8,128)(2,1)S(1)}, bf16[8,16,256]{2,1,0:T(8,128)(2,1)S(1)}, u32[]{:S(2)}, u32[]{:S(2)}) %collective-permute-start.17) | collective-permute-done | bytes 65568 | tf_op jit(solution)/shard_map/ppermute | solution.py:474
  78.1 1.0 %keep.1.kept = f32[8,128,256]{2,1,0:T(8,128)S(1)} custom-call(s32[5,8]{1,0:T(8,128)S(1)} %add_select_fusion.offs, bf16[8,256,256]{2,1,0:T(8,128)(2,1)S(1)} %get-tuple-element.67.d0, bf16[8,128,256]{2,1,0:T(8,128)(2,1)S(1)} %get-tuple-element.68._.mine, bf16[8,128,256]{2,1,0:T(8,128)(2,1)S(1)} %collective-permute-done.10.refs_0_.theirs, ...), custom_call_target="tpu_custom_call" | custom-call | bytes 4000000 | tf_op jit(solution)/shard_map/keep/pallas_call | solution.py:411
  79.1 1.1 %collective-permute-done.18.refs_0_ = bf16[8,128,256]{2,1,0:T(8,128)(2,1)S(1)} collective-permute-done((bf16[8,128,256]{2,1,0:T(8,128)(2,1)S(1)}, bf16[8,128,256]{2,1,0:T(8,128)(2,1)S(1)}, u32[]{:S(2)}, u32[]{:S(2)}) %collective-permute-start.18) | collective-permute-done | bytes 524320 | tf_op jit(solution)/shard_map/ppermute | solution.py:474
  80.3 0.9 %finish.1 = (bf16[128,1024]{1,0:T(8,128)(2,1)}, bf16[128,1024]{1,0:T(8,128)(2,1)}) custom-call(f32[8,128,256]{2,1,0:T(8,128)S(1)} %keep.1.kept, bf16[8,128,256]{2,1,0:T(8,128)(2,1)S(1)} %collective-permute-done.18.refs_0_), custom_call_target="tpu_custom_call" | custom-call | bytes 4000000 | tf_op jit(solution)/shard_map/finish/pallas_call | solution.py:411
  (14 shorter events, 0.1 us)
Async XLA Ops:
  1.4 8.7 %collective-permute-start = (s32[5,4]{1,0:T(8,128)S(1)}, s32[5,4]{1,0:T(8,128)S(1)}, u32[]{:S(2)}, u32[]{:S(2)}) collective-permute-start(s32[5,4]{1,0:T(8,128)S(1)} %copy.10), channel_id=1, source_target_pairs={{0,5},{1,4},{2,7},{3,6},{4,1},{5,0},{6,3},{7,2},{8,13},{9,12},{10,... | collective-permute-start | bytes 248 | tf_op jit(solution)/shard_map/ppermute | solution.py:474
  5.5 18.6 %collective-permute-start.1 = (bf16[128,1024]{1,0:T(8,128)(2,1)}, bf16[128,1024]{1,0:T(8,128)(2,1)S(1)}, u32[]{:S(2)}, u32[]{:S(2)}) collective-permute-start(bf16[128,1024]{1,0:T(8,128)(2,1)} %k_ref.3), channel_id=1, source_target_pairs={{0,1},{1,0},{2,3},{3,2},{4,5},{5,4},{6,7},{7,6},{8,9},{9,8},{10,11... | collective-permute-start | bytes 786440 | tf_op jit(solution)/shard_map/ppermute | solution.py:474
  5.5 18.6 %collective-permute-start.2 = (bf16[128,1024]{1,0:T(8,128)(2,1)}, bf16[128,1024]{1,0:T(8,128)(2,1)S(1)}, u32[]{:S(2)}, u32[]{:S(2)}) collective-permute-start(bf16[128,1024]{1,0:T(8,128)(2,1)} %v_ref.3), channel_id=1, source_target_pairs={{0,1},{1,0},{2,3},{3,2},{4,5},{5,4},{6,7},{7,6},{8,9},{9,8},{10,11... | collective-permute-start | bytes 786440 | tf_op jit(solution)/shard_map/ppermute | solution.py:474
  10.2 14.0 %copy-start = (bf16[128,1024]{1,0:T(8,128)(2,1)S(1)}, bf16[128,1024]{1,0:T(8,128)(2,1)}, u32[]{:S(2)}) copy-start(bf16[128,1024]{1,0:T(8,128)(2,1)} %k_ref.3) | copy-start | bytes 786436
  10.2 14.0 %copy-start.1 = (bf16[128,1024]{1,0:T(8,128)(2,1)S(1)}, bf16[128,1024]{1,0:T(8,128)(2,1)}, u32[]{:S(2)}) copy-start(bf16[128,1024]{1,0:T(8,128)(2,1)} %v_ref.3) | copy-start | bytes 786436
  10.2 14.0 %copy-start.2 = (bf16[128,4096]{1,0:T(8,128)(2,1)S(1)}, bf16[128,4096]{1,0:T(8,128)(2,1)}, u32[]{:S(2)}) copy-start(bf16[128,4096]{1,0:T(8,128)(2,1)} %q_ref.3) | copy-start | bytes 3145732
  10.2 14.0 %copy-start.3 = (bf16[128,4096]{1,0:T(8,128)(2,1)S(1)}, bf16[128,4096]{1,0:T(8,128)(2,1)}, u32[]{:S(2)}) copy-start(bf16[128,4096]{1,0:T(8,128)(2,1)} %g_ref.5) | copy-start | bytes 3145732
  11.4 9.4 %collective-permute-start.3 = (bf16[8,32,256]{2,1,0:T(8,128)(2,1)S(1)}, bf16[8,32,256]{2,1,0:T(8,128)(2,1)S(1)}, u32[]{:S(2)}, u32[]{:S(2)}) collective-permute-start(bf16[8,32,256]{2,1,0:T(8,128)(2,1)S(1)} %get-tuple-element.44), channel_id=1, source_target_pairs={{0,8},{1,9},{2,10},{3,11},{4,12},{5,13},{6,14},{7,15},{8,0},{9,1},... | collective-permute-start | bytes 393224 | tf_op jit(solution)/shard_map/ppermute | solution.py:474
  12.9 6.1 %collective-permute-start.5 = (bf16[8,16,256]{2,1,0:T(8,128)(2,1)S(1)}, bf16[8,16,256]{2,1,0:T(8,128)(2,1)S(1)}, u32[]{:S(2)}, u32[]{:S(2)}) collective-permute-start(bf16[8,16,256]{2,1,0:T(8,128)(2,1)S(1)} %get-tuple-element.45), channel_id=1, source_target_pairs={{0,24},{1,25},{2,26},{3,27},{4,28},{5,29},{6,30},{7,31},{8,16},{9,... | collective-permute-start | bytes 196616 | tf_op jit(solution)/shard_map/ppermute | solution.py:474
  15.0 5.8 %collective-permute-start.4 = (bf16[8,16,256]{2,1,0:T(8,128)(2,1)S(1)}, bf16[8,16,256]{2,1,0:T(8,128)(2,1)S(1)}, u32[]{:S(2)}, u32[]{:S(2)}) collective-permute-start(bf16[8,16,256]{2,1,0:T(8,128)(2,1)S(1)} %get-tuple-element.45), channel_id=1, source_target_pairs={{0,16},{1,17},{2,18},{3,19},{4,20},{5,21},{6,22},{7,23},{8,24},{9,... | collective-permute-start | bytes 196616 | tf_op jit(solution)/shard_map/ppermute | solution.py:474
  20.9 14.0 %collective-permute-start.8 = (bf16[8,96,256]{2,1,0:T(8,128)(2,1)S(1)}, bf16[8,96,256]{2,1,0:T(8,128)(2,1)S(1)}, u32[]{:S(2)}, u32[]{:S(2)}) collective-permute-start(bf16[8,96,256]{2,1,0:T(8,128)(2,1)S(1)} %get-tuple-element.53.lift), channel_id=1, source_target_pairs={{0,4},{1,5},{2,6},{3,7},{4,1},{5,0},{6,3},{7,2},{8,12},{9,13},{10,... | collective-permute-start | bytes 1179656 | tf_op jit(solution)/shard_map/ppermute | solution.py:474
  20.9 13.9 %collective-permute-start.7 = (bf16[8,96,256]{2,1,0:T(8,128)(2,1)S(1)}, bf16[8,96,256]{2,1,0:T(8,128)(2,1)S(1)}, u32[]{:S(2)}, u32[]{:S(2)}) collective-permute-start(bf16[8,96,256]{2,1,0:T(8,128)(2,1)S(1)} %get-tuple-element.53.lift), channel_id=1, source_target_pairs={{0,5},{1,4},{2,7},{3,6},{4,0},{5,1},{6,2},{7,3},{8,13},{9,12},{10,... | collective-permute-start | bytes 1179656 | tf_op jit(solution)/shard_map/ppermute | solution.py:474
  24.2 9.4 %collective-permute-start.6 = (bf16[4,80,256]{2,1,0:T(8,128)(2,1)S(1)}, bf16[4,80,256]{2,1,0:T(8,128)(2,1)S(1)}, u32[]{:S(2)}, u32[]{:S(2)}) collective-permute-start(bf16[4,80,256]{2,1,0:T(8,128)(2,1)S(1)} %get-tuple-element.46.refs_0_), channel_id=1, source_target_pairs={{0,1},{1,0},{2,3},{3,2},{4,5},{5,4},{6,7},{7,6},{8,9},{9,8},{10,11... | collective-permute-start | bytes 491528 | tf_op jit(solution)/shard_map/ppermute | solution.py:474
  35.0 4.2 %collective-permute-start.9 = (bf16[8,512,256]{2,1,0:T(8,128)(2,1)S(1)}, bf16[8,512,256]{2,1,0:T(8,128)(2,1)S(1)}, u32[]{:S(2)}, u32[]{:S(2)}) collective-permute-start(bf16[8,512,256]{2,1,0:T(8,128)(2,1)S(1)} %assemble.1.own_ref), channel_id=1, source_target_pairs={{0,2},{1,3},{2,0},{3,1},{4,6},{5,7},{6,4},{7,5},{8,10},{9,11},{10,... | collective-permute-start | bytes 6291464 | tf_op jit(solution)/shard_map/ppermute | solution.py:474
  49.0 3.4 %collective-permute-start.11 = (bf16[8,384,256]{2,1,0:T(8,128)(2,1)S(1)}, bf16[8,384,256]{2,1,0:T(8,128)(2,1)S(1)}, u32[]{:S(2)}, u32[]{:S(2)}) collective-permute-start(bf16[8,384,256]{2,1,0:T(8,128)(2,1)S(1)} %get-tuple-element.70), channel_id=1, source_target_pairs={{0,2},{1,3},{2,0},{3,1},{4,6},{5,7},{6,4},{7,5},{8,10},{9,11},{10,... | collective-permute-start | bytes 4718600 | tf_op jit(solution)/shard_map/ppermute | solution.py:474
  51.8 4.8 %collective-permute-start.10 = (bf16[8,128,256]{2,1,0:T(8,128)(2,1)S(1)}, bf16[8,128,256]{2,1,0:T(8,128)(2,1)S(1)}, u32[]{:S(2)}, u32[]{:S(2)}) collective-permute-start(bf16[8,128,256]{2,1,0:T(8,128)(2,1)S(1)} %get-tuple-element.65), channel_id=1, source_target_pairs={{0,2},{1,3},{2,0},{3,1},{4,6},{5,7},{6,4},{7,5},{8,10},{9,11},{10,... | collective-permute-start | bytes 1572872 | tf_op jit(solution)/shard_map/ppermute | solution.py:474
  52.7 8.7 %collective-permute-start.14 = (bf16[4,80,256]{2,1,0:T(8,128)(2,1)S(1)}, bf16[4,80,256]{2,1,0:T(8,128)(2,1)S(1)}, u32[]{:S(2)}, u32[]{:S(2)}) collective-permute-start(bf16[4,80,256]{2,1,0:T(8,128)(2,1)S(1)} %get-tuple-element.75), channel_id=1, source_target_pairs={{0,1},{1,0},{2,3},{3,2},{4,5},{5,4},{6,7},{7,6},{8,9},{9,8},{10,11... | collective-permute-start | bytes 491528 | tf_op jit(solution)/shard_map/ppermute | solution.py:474
  53.4 16.3 %collective-permute-start.12 = (bf16[8,96,256]{2,1,0:T(8,128)(2,1)S(1)}, bf16[8,96,256]{2,1,0:T(8,128)(2,1)S(1)}, u32[]{:S(2)}, u32[]{:S(2)}) collective-permute-start(bf16[8,96,256]{2,1,0:T(8,128)(2,1)S(1)} %get-tuple-element.72), channel_id=1, source_target_pairs={{0,4},{1,5},{2,6},{3,7},{4,1},{5,0},{6,3},{7,2},{8,12},{9,13},{10,... | collective-permute-start | bytes 1179656 | tf_op jit(solution)/shard_map/ppermute | solution.py:474
  56.6 13.5 %collective-permute-start.13 = (bf16[8,96,256]{2,1,0:T(8,128)(2,1)S(1)}, bf16[8,96,256]{2,1,0:T(8,128)(2,1)S(1)}, u32[]{:S(2)}, u32[]{:S(2)}) collective-permute-start(bf16[8,96,256]{2,1,0:T(8,128)(2,1)S(1)} %get-tuple-element.73), channel_id=1, source_target_pairs={{0,5},{1,4},{2,7},{3,6},{4,0},{5,1},{6,2},{7,3},{8,13},{9,12},{10,... | collective-permute-start | bytes 1179656 | tf_op jit(solution)/shard_map/ppermute | solution.py:474
  62.3 18.0 %collective-permute-start.18 = (bf16[8,128,256]{2,1,0:T(8,128)(2,1)S(1)}, bf16[8,128,256]{2,1,0:T(8,128)(2,1)S(1)}, u32[]{:S(2)}, u32[]{:S(2)}) collective-permute-start(bf16[8,128,256]{2,1,0:T(8,128)(2,1)S(1)} %place.1), channel_id=1, source_target_pairs={{0,1},{1,0},{2,3},{3,2},{4,5},{5,4},{6,7},{7,6},{8,9},{9,8},{10,11... | collective-permute-start | bytes 1572872 | tf_op jit(solution)/shard_map/ppermute | solution.py:474
  70.2 7.9 %collective-permute-start.15 = (bf16[8,32,256]{2,1,0:T(8,128)(2,1)S(1)}, bf16[8,32,256]{2,1,0:T(8,128)(2,1)S(1)}, u32[]{:S(2)}, u32[]{:S(2)}) collective-permute-start(bf16[8,32,256]{2,1,0:T(8,128)(2,1)S(1)} %get-tuple-element.76), channel_id=1, source_target_pairs={{0,8},{1,9},{2,10},{3,11},{4,12},{5,13},{6,14},{7,15},{8,0},{9,1},... | collective-permute-start | bytes 393224 | tf_op jit(solution)/shard_map/ppermute | solution.py:474
  70.9 6.1 %collective-permute-start.16 = (bf16[8,16,256]{2,1,0:T(8,128)(2,1)S(1)}, bf16[8,16,256]{2,1,0:T(8,128)(2,1)S(1)}, u32[]{:S(2)}, u32[]{:S(2)}) collective-permute-start(bf16[8,16,256]{2,1,0:T(8,128)(2,1)S(1)} %get-tuple-element.77), channel_id=1, source_target_pairs={{0,16},{1,17},{2,18},{3,19},{4,20},{5,21},{6,22},{7,23},{8,24},{9,... | collective-permute-start | bytes 196616 | tf_op jit(solution)/shard_map/ppermute | solution.py:474
  72.6 5.5 %collective-permute-start.17 = (bf16[8,16,256]{2,1,0:T(8,128)(2,1)S(1)}, bf16[8,16,256]{2,1,0:T(8,128)(2,1)S(1)}, u32[]{:S(2)}, u32[]{:S(2)}) collective-permute-start(bf16[8,16,256]{2,1,0:T(8,128)(2,1)S(1)} %get-tuple-element.78), channel_id=1, source_target_pairs={{0,24},{1,25},{2,26},{3,27},{4,28},{5,29},{6,30},{7,31},{8,16},{9,... | collective-permute-start | bytes 196616 | tf_op jit(solution)/shard_map/ppermute | solution.py:474

commit v7 on v6

--- a/solution.py
+++ b/solution.py
@@ -91,21 +91,19 @@
             whole = []
 
 
-def across_kernel(offs, first, keys, values, _, held, across):
-    for g in range(GROUPS):
-        far = dot(selector(offs, g), group_rows(keys, values, g)).astype(BF)
-        held[g] = jnp.concatenate([first[g], far[0:64]], 0)
-        across[g] = far[64:128]
-
-
-def assemble_kernel(held, across, lift, x_far, lift_up, lift_down, out):
+def across_kernel(offs, keys, values, _, across):
+    for g in range(GROUPS):
+        across[g] = dot(selector(offs, g), group_rows(keys, values, g)).astype(BF)
+
+
+def assemble_kernel(across, x_far, lift_up, lift_down, _, __, out):
     for g in range(GROUPS):
         far, extra = across[g].astype(F32), extra_rows(x_far, g)
-        far = jnp.concatenate([far[0:48], extra[0:16], far[48:56], extra[16:40]], 0).astype(BF)
-        lifts = [lift[g], far, lift_up[g], lift_down[g]]
-        out[g, 0:128] = held[g]
-        for i, (a, b) in enumerate(((0, 32), (32, 64), (64, 96))):
-            out[g, 128 * i + 128 : 128 * i + 256] = jnp.concatenate([x[a:b] for x in lifts], 0)
+        far = jnp.concatenate([far[0:112], extra[0:16], far[112:120], extra[16:40]], 0).astype(BF)
+        out[g, 0:64] = far[0:64]
+        for i, at in enumerate((0, 32, 64)):
+            rows = [far[64 + at : 96 + at], lift_up[g, at : at + 32], lift_down[g, at : at + 32]]
+            out[g, 96 * i + 64 : 96 * i + 160] = jnp.concatenate(rows, 0)
 
 
 def by_level(rows):
@@ -196,11 +194,11 @@
     return jnp.concatenate([own_ref[:, lanes], far_ref[:, lanes]], 0)
 
 
-def both_rows(own_ref, other_ref, j, at, lanes):
-    return jnp.concatenate([own_ref[j, at, lanes], other_ref[j, at, lanes]], 0)
-
-
-K_LANES, V_LANES, LEVEL1 = slice(0, D), slice(D, 2 * D), slice(0, 128)
+def level1_rows(refs, j, lanes):
+    return jnp.concatenate([ref[j, 0:64, lanes] for ref in refs], 0)
+
+
+K_LANES, V_LANES = slice(0, D), slice(D, 2 * D)
 
 
 def early_kernel(offs, q_ref, g_ref, k_ref, v_ref, kp_ref, vp_ref, *refs):
@@ -224,7 +222,7 @@
 
 
 def attention_kernel(
-    offs, qs_ref, gs_ref, g_ref, own_ref, other_ref, peak0, lse0, out0,
+    offs, qs_ref, gs_ref, g_ref, first, lift, late, other_first, other_lift, other_late, peak0, lse0, out0,
     att_ref, part_ref, down_ref, dother_ref, factor0, shift0, power1, factor1, shift1,
     level_ref, token_ref, delta_ref,
 ):
@@ -234,8 +232,11 @@
     starts = [[(offs[k, first_group + j], 128 >> k) for k in range(1, 5)] for j in members]
 
     def kept(k, lanes):
-        at = slice(128 * k, 128 * k + 128)
-        return [both_rows(own_ref, other_ref, j, at, lanes) for j in members]
+        if k == 0:
+            return [level1_rows((first, late, other_first, other_late), j, lanes) for j in members]
+        mine, rest = slice(32 * k - 32, 32 * k), slice(96 * k - 32, 96 * k + 64)
+        parts = ((lift, mine), (late, rest), (other_lift, mine), (other_late, rest))
+        return [jnp.concatenate([ref[j, at, lanes] for ref, at in parts], 0) for j in members]
 
     def for_levels(ref, xs):
         for j, x in enumerate(xs):
@@ -318,13 +319,14 @@
 
 
 def return1_kernel(
-    offs, qs_ref, gs_ref, own_ref, other_ref, power_ref, factor_ref, shift_ref, part_ref,
+    offs, qs_ref, gs_ref, first, late, other_first, other_late, power_ref, factor_ref, shift_ref, part_ref,
     dq_ref, down_ref, dother_ref,
 ):
+    level1 = (first, late, other_first, other_late)
     members = range(TOGETHER)
     queries = [qs_ref[j, 0:256] for j in members]
-    keys = [both_rows(own_ref, other_ref, j, LEVEL1, K_LANES) for j in members]
-    values = [both_rows(own_ref, other_ref, j, LEVEL1, V_LANES) for j in members]
+    keys = [level1_rows(level1, j, K_LANES) for j in members]
+    values = [level1_rows(level1, j, V_LANES) for j in members]
     scaled = [(gs_ref[j, 0:256].astype(F32) * expand(factor_ref[j])).astype(BF) for j in members]
     powers, shifts = [power_ref[j] for j in members], [shift_ref[j] for j in members]
     pairs, parts = backward(queries, scaled, keys, values, powers, shifts)
@@ -422,7 +424,7 @@
 def grid_call(body, name, offs, inputs, outs, scratch=(), after=()):
     def spec(shape, offset=None):
         if offset == 0:
-            return pl.BlockSpec((TOGETHER, 128) + shape[2:], lambda i: (i, 0, 0))
+            return pl.BlockSpec((TOGETHER, 64) + shape[2:], lambda i: (i, 0, 0))
         if offset:
             return pl.BlockSpec((TOKENS, TOGETHER * D), lambda i: (0, i + offset - 1))
         if len(shape) == 2:
@@ -504,23 +506,27 @@
         early_kernel, "early", offs, [queries, gradient, *kv],
         [tall(512, BF), tall(512, BF), rows(512), tall(128), tall(128), tall(512)], after=(extra,),
     )
-    held, across = whole_call(
-        across_kernel, "across", [rows(128), rows(64)], offs, first, far_keys, far_values, after=(lse0,)
-    )
-    (own,) = whole_call(
-        assemble_kernel, "assemble", [rows(512)], None, held, across, lift, extra_far, lift_up, lift_down
-    )
-    other = send(own, "core")
+    (across,) = whole_call(
+        across_kernel, "across", [rows(128)], offs, far_keys, far_values, after=(lse0,)
+    )
+    first_sent, lift_sent, _ = lax.optimization_barrier((first, lift, (far_keys, far_values)))
+    other_first, other_lift = send(first_sent, "core"), send(lift_sent, "core")
+    (late,) = whole_call(
+        assemble_kernel, "assemble", [rows(352)], None, across, extra_far, lift_up, lift_down,
+        after=(other_first, other_lift),
+    )
+    other_late = send(late, "core")
+    near = [first, lift, late, other_first, other_lift, other_late]
     stats = pltpu.VMEM((TOGETHER, TOKENS, 128), F32)
     attended, part, down_own, down_other, factor0, shift0, power1, factor1, shift1 = grid_call(
         attention_kernel, "attention", offs,
-        [qs, gs, gradient, own, other, peak0, lse0, out0],
+        [qs, gs, gradient, *near, peak0, lse0, out0],
         [wide(BF), tall(224), rows(384), rows(384), tall(128), tall(128), rows(256), tall(64), tall(64)],
         scratch=[pltpu.VMEM((TOGETHER, 4, TOKENS, 128), F32), stats, stats],
     )
     theirs = send(down_other, "core")
     placed, mine1, theirs1 = grid_call(
-        return1_kernel, "return1", offs, [qs, gs, (own, 0), (other, 0), power1, factor1, shift1, part],
+        return1_kernel, "return1", offs, [qs, gs, first, (late, 0), other_first, (other_late, 0), power1, factor1, shift1, part],
         [wide(F32), rows(128), rows(128)],
     )
     mid_kept, mid_far, up, down, x_far, x_kept = whole_call(

time: 81.6 us -> 80.6 us (0.988)
  waiting for transfers between devices: 28.1 us -> 26.7 us
    ppermute x19 -> x21, waiting for transfers between devices: 28.1 us -> 26.7 us  [send(): return lax.ppermute(x, AXES, route[name])]
    ppermute x19 -> x21, starting transfers between devices: 25.6 us -> 26.1 us  [send(): return lax.ppermute(x, AXES, route[name])]
  transfers between devices with their start and end apart: 19 -> 21, of which waited for: 12 -> 12; matrix products, arithmetic and copies ran while one was open for 1% -> 1% of each run, Pallas kernels for 17% -> 17%
where the time goes in v7:
time: 80.6 us; the launch traced here: 80.3 us
  waiting for transfers between devices  26.7 us (33%)
  starting transfers between devices  26.1 us (32%)
  Pallas kernels  24.7 us (31%)
  other arithmetic  1.14 us (1%)
    ppermute x21, waiting for transfers between devices, send(): return lax.ppermute(x, AXES, route[name])  26.7 us
    ppermute x21, starting transfers between devices, send(): return lax.ppermute(x, AXES, route[name])  26.1 us
    pallas_call x5, Pallas kernels, grid_call(): pl.pallas_call(body, name=name, grid=(GROUPS // TOGETHER,), in_specs=spec...  20.4 us
    pallas_call x8, Pallas kernels, whole_call(): pl.pallas_call(body, name=name, out_shape=shapes, in_specs=specs, out_spe...  4.27 us
  transfers between devices with their start and end apart: 21, of which 12 were waited for; matrix products, arithmetic and copies ran while one was open for 1% of the time, Pallas kernels for 17%

profile of v7, /device:TPU:0, one launch (start us, length us, event | category | flops | bytes accessed | tf_op | source)
XLA Modules:
  0.0 80.3 jit_solution(12134804059815174039)
XLA Ops:
  0.6 0.8 copy.10
  1.4 4.1 %collective-permute-start = (s32[5,4]{1,0:T(8,128)S(1)}, s32[5,4]{1,0:T(8,128)S(1)}, u32[]{:S(2)}, u32[]{:S(2)}) collective-permute-start(s32[5,4]{1,0:T(8,128)S(1)} %copy.10), channel_id=1, source_target_pairs={{0,5},{1,4},{2,7},{3,6},{4,1},{5,0},{6,3},{7,2},{8,13},{9,12},{10,... | collective-permute-start | bytes 248 | tf_op jit(solution)/shard_map/ppermute | solution.py:476
  5.5 3.5 %collective-permute-start.2 = (bf16[128,1024]{1,0:T(8,128)(2,1)}, bf16[128,1024]{1,0:T(8,128)(2,1)S(1)}, u32[]{:S(2)}, u32[]{:S(2)}) collective-permute-start(bf16[128,1024]{1,0:T(8,128)(2,1)} %v_ref.3), channel_id=1, source_target_pairs={{0,1},{1,0},{2,3},{3,2},{4,5},{5,4},{6,7},{7,6},{8,9},{9,8},{10,11... | collective-permute-start | bytes 786440 | tf_op jit(solution)/shard_map/ppermute | solution.py:476
  9.1 1.1 %pad_maximum_fusion.keys.values = bf16[128,2048]{1,0:T(8,128)(2,1)S(1)} fusion(bf16[128,1024]{1,0:T(8,128)(2,1)} %v_ref.3, bf16[128,1024]{1,0:T(8,128)(2,1)} %k_ref.3), kind=kLoop, calls=%fused_computation | loop fusion | flops 1048576 | bytes 1048576 | tf_op jit(solution)/shard_map/concatenate | solution.py:485
  10.1 0.0 collective-permute-done
  10.1 0.1 add_select_fusion.offs
  10.2 1.1 %select.1 = (bf16[8,64,256]{2,1,0:T(8,128)(2,1)S(1)}, bf16[8,64,256]{2,1,0:T(8,128)(2,1)S(1)}, bf16[8,32,256]{2,1,0:T(8,128)(2,1)S(1)}, bf16[8,16,256]{2,1,0:T(8,128)(2,1)S(1)}) custom-call(s32[5,8]{1,0:T(8,128)S(1)} %add_select_fusion.offs, bf16[128,2048]{1,0:T(8,128)(2,1)S(1)} %pad_maximum_fusion.keys.values, bf16[128,2048]{1,0:T(8,128)(2,1)S(1)} %pad_maximum_fusion.keys.values), custom_call_target="tpu_custom_call" | custom-call | flops 4000000000 | bytes 16000000 | tf_op jit(solution)/shard_map/select/pallas_call | solution.py:441
  11.4 1.6 %collective-permute-start.3 = (bf16[8,32,256]{2,1,0:T(8,128)(2,1)S(1)}, bf16[8,32,256]{2,1,0:T(8,128)(2,1)S(1)}, u32[]{:S(2)}, u32[]{:S(2)}) collective-permute-start(bf16[8,32,256]{2,1,0:T(8,128)(2,1)S(1)} %get-tuple-element.44), channel_id=1, source_target_pairs={{0,8},{1,9},{2,10},{3,11},{4,12},{5,13},{6,14},{7,15},{8,0},{9,1},... | collective-permute-start | bytes 393224 | tf_op jit(solution)/shard_map/ppermute | solution.py:476
  12.9 2.1 %collective-permute-start.5 = (bf16[8,16,256]{2,1,0:T(8,128)(2,1)S(1)}, bf16[8,16,256]{2,1,0:T(8,128)(2,1)S(1)}, u32[]{:S(2)}, u32[]{:S(2)}) collective-permute-start(bf16[8,16,256]{2,1,0:T(8,128)(2,1)S(1)} %get-tuple-element.45), channel_id=1, source_target_pairs={{0,24},{1,25},{2,26},{3,27},{4,28},{5,29},{6,30},{7,31},{8,16},{9,... | collective-permute-start | bytes 196616 | tf_op jit(solution)/shard_map/ppermute | solution.py:476
  15.0 0.6 collective-permute-start.4
  15.7 3.3 %collective-permute-done.5.three = bf16[8,16,256]{2,1,0:T(8,128)(2,1)S(1)} collective-permute-done((bf16[8,16,256]{2,1,0:T(8,128)(2,1)S(1)}, bf16[8,16,256]{2,1,0:T(8,128)(2,1)S(1)}, u32[]{:S(2)}, u32[]{:S(2)}) %collective-permute-start.5) | collective-permute-done | bytes 65568 | tf_op jit(solution)/shard_map/ppermute | solution.py:476
  19.0 1.8 %collective-permute-done.4.two = bf16[8,16,256]{2,1,0:T(8,128)(2,1)S(1)} collective-permute-done((bf16[8,16,256]{2,1,0:T(8,128)(2,1)S(1)}, bf16[8,16,256]{2,1,0:T(8,128)(2,1)S(1)}, u32[]{:S(2)}, u32[]{:S(2)}) %collective-permute-start.4) | collective-permute-done | bytes 65568 | tf_op jit(solution)/shard_map/ppermute | solution.py:476
  20.8 0.0 collective-permute-done.3.one
  20.9 0.1 collective-permute-start.8
  20.9 3.2 %collective-permute-start.7 = (bf16[8,96,256]{2,1,0:T(8,128)(2,1)S(1)}, bf16[8,96,256]{2,1,0:T(8,128)(2,1)S(1)}, u32[]{:S(2)}, u32[]{:S(2)}) collective-permute-start(bf16[8,96,256]{2,1,0:T(8,128)(2,1)S(1)} %get-tuple-element.53.lift), channel_id=1, source_target_pairs={{0,5},{1,4},{2,7},{3,6},{4,0},{5,1},{6,2},{7,3},{8,13},{9,12},{10,... | collective-permute-start | bytes 1179656 | tf_op jit(solution)/shard_map/ppermute | solution.py:476
  24.2 0.1 collective-permute-start.6
  24.3 0.4 collective-permute-start.9
  24.7 3.2 %early.1 = (bf16[8,512,128]{2,1,0:T(8,128)(2,1)S(1)}, bf16[8,512,128]{2,1,0:T(8,128)(2,1)S(1)}, bf16[8,512,256]{2,1,0:T(8,128)(2,1)S(1)}, f32[8,128,128]{2,1,0:T...) custom-call(s32[5,8]{1,0:T(8,128)S(1)} %add_select_fusion.offs, bf16[128,4096]{1,0:T(8,128)(2,1)S(1)} %copy-done.2, ...), custom_call_target="tpu_custom_call" | custom-call | flops 4000000000 | bytes 16000000 | tf_op jit(solution)/shard_map/early/pallas_call | solution.py:441
  27.9 0.9 %across.1 = bf16[8,128,256]{2,1,0:T(8,128)(2,1)S(1)} custom-call(s32[5,8]{1,0:T(8,128)S(1)} %add_select_fusion.offs, bf16[128,1024]{1,0:T(8,128)(2,1)S(1)} %collective-permute-done.1.kp_ref.keys, bf16[128,1024]{1,0:T(8,128)(2,1)S(1)} %collective-permute-done.2.vp_ref.values, f32[8,128,128]{2,1,0:T(8,128)S(1)} %get-tuple-element.51._.lse0), custom_call_target="tpu_custom_call" | custom-call | bytes 4000000 | tf_op jit(solution)/shard_map/across/pallas_call | solution.py:413
  28.8 4.8 %collective-permute-done.6.x_far = bf16[4,80,256]{2,1,0:T(8,128)(2,1)S(1)} collective-permute-done((bf16[4,80,256]{2,1,0:T(8,128)(2,1)S(1)}, bf16[4,80,256]{2,1,0:T(8,128)(2,1)S(1)}, u32[]{:S(2)}, u32[]{:S(2)}) %collective-permute-start.6) | collective-permute-done | bytes 163872 | tf_op jit(solution)/shard_map/ppermute | solution.py:476
  33.6 1.3 %collective-permute-done.8.lift_down = bf16[8,96,256]{2,1,0:T(8,128)(2,1)S(1)} collective-permute-done((bf16[8,96,256]{2,1,0:T(8,128)(2,1)S(1)}, bf16[8,96,256]{2,1,0:T(8,128)(2,1)S(1)}, u32[]{:S(2)}, u32[]{:S(2)}) %collective-permute-start.8) | collective-permute-done | bytes 393248 | tf_op jit(solution)/shard_map/ppermute | solution.py:476
  34.9 0.1 assemble.1.late
  35.0 0.1 collective-permute-start.11
  35.1 3.2 %collective-permute-done.11.other_late = bf16[8,352,256]{2,1,0:T(8,128)(2,1)S(1)} collective-permute-done((bf16[8,352,256]{2,1,0:T(8,128)(2,1)S(1)}, bf16[8,352,256]{2,1,0:T(8,128)(2,1)S(1)}, u32[]{:S(2)}, u32[]{:S(2)}) %collective-permute-start.11) | collective-permute-done | bytes 1441824 | tf_op jit(solution)/shard_map/ppermute | solution.py:476
  38.3 9.8 %attention.1 = (bf16[128,4096]{1,0:T(8,128)(2,1)}, f32[8,224,128]{2,1,0:T(8,128)S(1)}, bf16[8,384,256]{2,1,0:T(8,128)(2,1)S(1)}, bf16[8,384,256]{2,1,0:T(8,128)(...) custom-call(s32[5,8]{1,0:T(8,128)S(1)} %add_select_fusion.offs, ...), custom_call_target="tpu_custom_call" | custom-call | flops 4000000000 | bytes 16000000 | tf_op jit(solution)/shard_map/attention/pallas_call | solution.py:441
  48.0 0.1 collective-permute-start.13
  48.2 2.7 %return1.1 = (f32[128,4096]{1,0:T(8,128)S(1)}, bf16[8,128,256]{2,1,0:T(8,128)(2,1)S(1)}, bf16[8,128,256]{2,1,0:T(8,128)(2,1)S(1)}) custom-call(s32[5,8]{1,0:T(8,128)S(1)} %add_select_fusion.offs, bf16[8,512,128]{2,1,0:T(8,128)(2,1)S(1)} %get-tuple-element.47.qs_ref, bf16[8,512,128]{2,1,0:T(8,128)(2,1)S(1)} %get-tuple-element.48.gs_ref, ...), custom_call_target="tpu_custom_call" | custom-call | flops 4000000000 | bytes 16000000 | tf_op jit(solution)/shard_map/return1/pallas_call | solution.py:441
  50.9 0.4 collective-permute-start.12
  51.3 0.1 collective-permute-done.13.theirs
  51.4 0.4 reduce.1
  51.8 0.7 collective-permute-start.16
  52.5 3.2 %collective-permute-start.14 = (bf16[8,96,256]{2,1,0:T(8,128)(2,1)S(1)}, bf16[8,96,256]{2,1,0:T(8,128)(2,1)S(1)}, u32[]{:S(2)}, u32[]{:S(2)}) collective-permute-start(bf16[8,96,256]{2,1,0:T(8,128)(2,1)S(1)} %get-tuple-element.72), channel_id=1, source_target_pairs={{0,4},{1,5},{2,6},{3,7},{4,1},{5,0},{6,3},{7,2},{8,12},{9,13},{10,... | collective-permute-start | bytes 1179656 | tf_op jit(solution)/shard_map/ppermute | solution.py:476
  55.7 0.0 collective-permute-start.15
  55.7 3.6 %return0.1 = (bf16[128,4096]{1,0:T(8,128)(2,1)}, bf16[8,256,256]{2,1,0:T(8,128)(2,1)S(1)}) custom-call(bf16[128,4096]{1,0:T(8,128)(2,1)S(1)} %copy-done.2, bf16[128,4096]{1,0:T(8,128)(2,1)S(1)} %copy-done.3, bf16[128,1024]{1,0:T(8,128)(2,1)S(1)} %copy-done, bf16[128,1024]{1,0:T(8,128)(2,1)S(1)} %copy-done.1, ...), custom_call_target="tpu_custom_call" | custom-call | flops 4000000000 | bytes 16000000 | tf_op jit(solution)/shard_map/return0/pallas_call | solution.py:441
  59.3 1.1 %collective-permute-done.16.far._ = bf16[4,80,256]{2,1,0:T(8,128)(2,1)S(1)} collective-permute-done((bf16[4,80,256]{2,1,0:T(8,128)(2,1)S(1)}, bf16[4,80,256]{2,1,0:T(8,128)(2,1)S(1)}, u32[]{:S(2)}, u32[]{:S(2)}) %collective-permute-start.16) | collective-permute-done | bytes 163872 | tf_op jit(solution)/shard_map/ppermute | solution.py:476
  60.5 0.9 %place.1 = bf16[8,128,256]{2,1,0:T(8,128)(2,1)S(1)} custom-call(s32[5,8]{1,0:T(8,128)S(1)} %add_select_fusion.offs, bf16[8,256,256]{2,1,0:T(8,128)(2,1)S(1)} %get-tuple-element.67.d0, bf16[8,128,256]{2,1,0:T(8,128)(2,1)S(1)} %get-tuple-element.68._.mine, bf16[8,128,256]{2,1,0:T(8,128)(2,1)S(1)} %collective-permute-done.12.refs_0_.theirs, ...), custom_call_target="tpu_custom_call" | custom-call | bytes 4000000 | tf_op jit(solution)/shard_map/place/pallas_call | solution.py:413
  61.4 1.0 %collective-permute-start.20 = (bf16[8,128,256]{2,1,0:T(8,128)(2,1)S(1)}, bf16[8,128,256]{2,1,0:T(8,128)(2,1)S(1)}, u32[]{:S(2)}, u32[]{:S(2)}) collective-permute-start(bf16[8,128,256]{2,1,0:T(8,128)(2,1)S(1)} %place.1), channel_id=1, source_target_pairs={{0,1},{1,0},{2,3},{3,2},{4,5},{5,4},{6,7},{7,6},{8,9},{9,8},{10,11... | collective-permute-start | bytes 1572872 | tf_op jit(solution)/shard_map/ppermute | solution.py:476
  62.4 6.4 %collective-permute-done.14.down = bf16[8,96,256]{2,1,0:T(8,128)(2,1)S(1)} collective-permute-done((bf16[8,96,256]{2,1,0:T(8,128)(2,1)S(1)}, bf16[8,96,256]{2,1,0:T(8,128)(2,1)S(1)}, u32[]{:S(2)}, u32[]{:S(2)}) %collective-permute-start.14) | collective-permute-done | bytes 393248 | tf_op jit(solution)/shard_map/ppermute | solution.py:476
  68.8 0.4 collective-permute-done.15.up
  69.2 0.1 cross.1
  69.2 0.7 collective-permute-start.17
  70.0 1.7 %collective-permute-start.18 = (bf16[8,16,256]{2,1,0:T(8,128)(2,1)S(1)}, bf16[8,16,256]{2,1,0:T(8,128)(2,1)S(1)}, u32[]{:S(2)}, u32[]{:S(2)}) collective-permute-start(bf16[8,16,256]{2,1,0:T(8,128)(2,1)S(1)} %get-tuple-element.77), channel_id=1, source_target_pairs={{0,16},{1,17},{2,18},{3,19},{4,20},{5,21},{6,22},{7,23},{8,24},{9,... | collective-permute-start | bytes 196616 | tf_op jit(solution)/shard_map/ppermute | solution.py:476
  71.7 2.3 %collective-permute-start.19 = (bf16[8,16,256]{2,1,0:T(8,128)(2,1)S(1)}, bf16[8,16,256]{2,1,0:T(8,128)(2,1)S(1)}, u32[]{:S(2)}, u32[]{:S(2)}) collective-permute-start(bf16[8,16,256]{2,1,0:T(8,128)(2,1)S(1)} %get-tuple-element.78), channel_id=1, source_target_pairs={{0,24},{1,25},{2,26},{3,27},{4,28},{5,29},{6,30},{7,31},{8,16},{9,... | collective-permute-start | bytes 196616 | tf_op jit(solution)/shard_map/ppermute | solution.py:476
  74.0 2.0 %collective-permute-done.18.two = bf16[8,16,256]{2,1,0:T(8,128)(2,1)S(1)} collective-permute-done((bf16[8,16,256]{2,1,0:T(8,128)(2,1)S(1)}, bf16[8,16,256]{2,1,0:T(8,128)(2,1)S(1)}, u32[]{:S(2)}, u32[]{:S(2)}) %collective-permute-start.18) | collective-permute-done | bytes 65568 | tf_op jit(solution)/shard_map/ppermute | solution.py:476
  76.0 1.1 %collective-permute-done.19.three = bf16[8,16,256]{2,1,0:T(8,128)(2,1)S(1)} collective-permute-done((bf16[8,16,256]{2,1,0:T(8,128)(2,1)S(1)}, bf16[8,16,256]{2,1,0:T(8,128)(2,1)S(1)}, u32[]{:S(2)}, u32[]{:S(2)}) %collective-permute-start.19) | collective-permute-done | bytes 65568 | tf_op jit(solution)/shard_map/ppermute | solution.py:476
  77.2 1.0 %keep.1.kept = f32[8,128,256]{2,1,0:T(8,128)S(1)} custom-call(s32[5,8]{1,0:T(8,128)S(1)} %add_select_fusion.offs, bf16[8,256,256]{2,1,0:T(8,128)(2,1)S(1)} %get-tuple-element.67.d0, bf16[8,128,256]{2,1,0:T(8,128)(2,1)S(1)} %get-tuple-element.68._.mine, bf16[8,128,256]{2,1,0:T(8,128)(2,1)S(1)} %collective-permute-done.12.refs_0_.theirs, ...), custom_call_target="tpu_custom_call" | custom-call | bytes 4000000 | tf_op jit(solution)/shard_map/keep/pallas_call | solution.py:413
  78.2 1.2 %collective-permute-done.20.refs_0_ = bf16[8,128,256]{2,1,0:T(8,128)(2,1)S(1)} collective-permute-done((bf16[8,128,256]{2,1,0:T(8,128)(2,1)S(1)}, bf16[8,128,256]{2,1,0:T(8,128)(2,1)S(1)}, u32[]{:S(2)}, u32[]{:S(2)}) %collective-permute-start.20) | collective-permute-done | bytes 524320 | tf_op jit(solution)/shard_map/ppermute | solution.py:476
  79.3 0.9 %finish.1 = (bf16[128,1024]{1,0:T(8,128)(2,1)}, bf16[128,1024]{1,0:T(8,128)(2,1)}) custom-call(f32[8,128,256]{2,1,0:T(8,128)S(1)} %keep.1.kept, bf16[8,128,256]{2,1,0:T(8,128)(2,1)S(1)} %collective-permute-done.20.refs_0_), custom_call_target="tpu_custom_call" | custom-call | bytes 4000000 | tf_op jit(solution)/shard_map/finish/pallas_call | solution.py:413
  (18 shorter events, 0.1 us)
Async XLA Ops:
  1.4 8.7 %collective-permute-start = (s32[5,4]{1,0:T(8,128)S(1)}, s32[5,4]{1,0:T(8,128)S(1)}, u32[]{:S(2)}, u32[]{:S(2)}) collective-permute-start(s32[5,4]{1,0:T(8,128)S(1)} %copy.10), channel_id=1, source_target_pairs={{0,5},{1,4},{2,7},{3,6},{4,1},{5,0},{6,3},{7,2},{8,13},{9,12},{10,... | collective-permute-start | bytes 248 | tf_op jit(solution)/shard_map/ppermute | solution.py:476
  5.5 18.6 %collective-permute-start.1 = (bf16[128,1024]{1,0:T(8,128)(2,1)}, bf16[128,1024]{1,0:T(8,128)(2,1)S(1)}, u32[]{:S(2)}, u32[]{:S(2)}) collective-permute-start(bf16[128,1024]{1,0:T(8,128)(2,1)} %k_ref.3), channel_id=1, source_target_pairs={{0,1},{1,0},{2,3},{3,2},{4,5},{5,4},{6,7},{7,6},{8,9},{9,8},{10,11... | collective-permute-start | bytes 786440 | tf_op jit(solution)/shard_map/ppermute | solution.py:476
  5.5 18.6 %collective-permute-start.2 = (bf16[128,1024]{1,0:T(8,128)(2,1)}, bf16[128,1024]{1,0:T(8,128)(2,1)S(1)}, u32[]{:S(2)}, u32[]{:S(2)}) collective-permute-start(bf16[128,1024]{1,0:T(8,128)(2,1)} %v_ref.3), channel_id=1, source_target_pairs={{0,1},{1,0},{2,3},{3,2},{4,5},{5,4},{6,7},{7,6},{8,9},{9,8},{10,11... | collective-permute-start | bytes 786440 | tf_op jit(solution)/shard_map/ppermute | solution.py:476
  10.2 14.5 %copy-start = (bf16[128,1024]{1,0:T(8,128)(2,1)S(1)}, bf16[128,1024]{1,0:T(8,128)(2,1)}, u32[]{:S(2)}) copy-start(bf16[128,1024]{1,0:T(8,128)(2,1)} %k_ref.3) | copy-start | bytes 786436
  10.2 14.5 %copy-start.1 = (bf16[128,1024]{1,0:T(8,128)(2,1)S(1)}, bf16[128,1024]{1,0:T(8,128)(2,1)}, u32[]{:S(2)}) copy-start(bf16[128,1024]{1,0:T(8,128)(2,1)} %v_ref.3) | copy-start | bytes 786436
  10.2 14.5 %copy-start.2 = (bf16[128,4096]{1,0:T(8,128)(2,1)S(1)}, bf16[128,4096]{1,0:T(8,128)(2,1)}, u32[]{:S(2)}) copy-start(bf16[128,4096]{1,0:T(8,128)(2,1)} %q_ref.3) | copy-start | bytes 3145732
  10.2 14.5 %copy-start.3 = (bf16[128,4096]{1,0:T(8,128)(2,1)S(1)}, bf16[128,4096]{1,0:T(8,128)(2,1)}, u32[]{:S(2)}) copy-start(bf16[128,4096]{1,0:T(8,128)(2,1)} %g_ref.5) | copy-start | bytes 3145732
  11.4 9.4 %collective-permute-start.3 = (bf16[8,32,256]{2,1,0:T(8,128)(2,1)S(1)}, bf16[8,32,256]{2,1,0:T(8,128)(2,1)S(1)}, u32[]{:S(2)}, u32[]{:S(2)}) collective-permute-start(bf16[8,32,256]{2,1,0:T(8,128)(2,1)S(1)} %get-tuple-element.44), channel_id=1, source_target_pairs={{0,8},{1,9},{2,10},{3,11},{4,12},{5,13},{6,14},{7,15},{8,0},{9,1},... | collective-permute-start | bytes 393224 | tf_op jit(solution)/shard_map/ppermute | solution.py:476
  12.9 6.1 %collective-permute-start.5 = (bf16[8,16,256]{2,1,0:T(8,128)(2,1)S(1)}, bf16[8,16,256]{2,1,0:T(8,128)(2,1)S(1)}, u32[]{:S(2)}, u32[]{:S(2)}) collective-permute-start(bf16[8,16,256]{2,1,0:T(8,128)(2,1)S(1)} %get-tuple-element.45), channel_id=1, source_target_pairs={{0,24},{1,25},{2,26},{3,27},{4,28},{5,29},{6,30},{7,31},{8,16},{9,... | collective-permute-start | bytes 196616 | tf_op jit(solution)/shard_map/ppermute | solution.py:476
  15.0 5.8 %collective-permute-start.4 = (bf16[8,16,256]{2,1,0:T(8,128)(2,1)S(1)}, bf16[8,16,256]{2,1,0:T(8,128)(2,1)S(1)}, u32[]{:S(2)}, u32[]{:S(2)}) collective-permute-start(bf16[8,16,256]{2,1,0:T(8,128)(2,1)S(1)} %get-tuple-element.45), channel_id=1, source_target_pairs={{0,16},{1,17},{2,18},{3,19},{4,20},{5,21},{6,22},{7,23},{8,24},{9,... | collective-permute-start | bytes 196616 | tf_op jit(solution)/shard_map/ppermute | solution.py:476
  20.9 14.0 %collective-permute-start.8 = (bf16[8,96,256]{2,1,0:T(8,128)(2,1)S(1)}, bf16[8,96,256]{2,1,0:T(8,128)(2,1)S(1)}, u32[]{:S(2)}, u32[]{:S(2)}) collective-permute-start(bf16[8,96,256]{2,1,0:T(8,128)(2,1)S(1)} %get-tuple-element.53.lift), channel_id=1, source_target_pairs={{0,4},{1,5},{2,6},{3,7},{4,1},{5,0},{6,3},{7,2},{8,12},{9,13},{10,... | collective-permute-start | bytes 1179656 | tf_op jit(solution)/shard_map/ppermute | solution.py:476
  20.9 13.9 %collective-permute-start.7 = (bf16[8,96,256]{2,1,0:T(8,128)(2,1)S(1)}, bf16[8,96,256]{2,1,0:T(8,128)(2,1)S(1)}, u32[]{:S(2)}, u32[]{:S(2)}) collective-permute-start(bf16[8,96,256]{2,1,0:T(8,128)(2,1)S(1)} %get-tuple-element.53.lift), channel_id=1, source_target_pairs={{0,5},{1,4},{2,7},{3,6},{4,0},{5,1},{6,2},{7,3},{8,13},{9,12},{10,... | collective-permute-start | bytes 1179656 | tf_op jit(solution)/shard_map/ppermute | solution.py:476
  24.2 10.7 %collective-permute-start.10 = (bf16[8,96,256]{2,1,0:T(8,128)(2,1)S(1)}, bf16[8,96,256]{2,1,0:T(8,128)(2,1)S(1)}, u32[]{:S(2)}, u32[]{:S(2)}) collective-permute-start(bf16[8,96,256]{2,1,0:T(8,128)(2,1)S(1)} %get-tuple-element.53.lift), channel_id=1, source_target_pairs={{0,2},{1,3},{2,0},{3,1},{4,6},{5,7},{6,4},{7,5},{8,10},{9,11},{10,... | collective-permute-start | bytes 1179656 | tf_op jit(solution)/shard_map/ppermute | solution.py:476
  24.2 9.4 %collective-permute-start.6 = (bf16[4,80,256]{2,1,0:T(8,128)(2,1)S(1)}, bf16[4,80,256]{2,1,0:T(8,128)(2,1)S(1)}, u32[]{:S(2)}, u32[]{:S(2)}) collective-permute-start(bf16[4,80,256]{2,1,0:T(8,128)(2,1)S(1)} %get-tuple-element.46.refs_0_), channel_id=1, source_target_pairs={{0,1},{1,0},{2,3},{3,2},{4,5},{5,4},{6,7},{7,6},{8,9},{9,8},{10,11... | collective-permute-start | bytes 491528 | tf_op jit(solution)/shard_map/ppermute | solution.py:476
  24.3 9.3 %collective-permute-start.9 = (bf16[8,64,256]{2,1,0:T(8,128)(2,1)S(1)}, bf16[8,64,256]{2,1,0:T(8,128)(2,1)S(1)}, u32[]{:S(2)}, u32[]{:S(2)}) collective-permute-start(bf16[8,64,256]{2,1,0:T(8,128)(2,1)S(1)} %get-tuple-element.52.first), channel_id=1, source_target_pairs={{0,2},{1,3},{2,0},{3,1},{4,6},{5,7},{6,4},{7,5},{8,10},{9,11},{10,... | collective-permute-start | bytes 786440 | tf_op jit(solution)/shard_map/ppermute | solution.py:476
  35.0 3.3 %collective-permute-start.11 = (bf16[8,352,256]{2,1,0:T(8,128)(2,1)S(1)}, bf16[8,352,256]{2,1,0:T(8,128)(2,1)S(1)}, u32[]{:S(2)}, u32[]{:S(2)}) collective-permute-start(bf16[8,352,256]{2,1,0:T(8,128)(2,1)S(1)} %assemble.1.late), channel_id=1, source_target_pairs={{0,2},{1,3},{2,0},{3,1},{4,6},{5,7},{6,4},{7,5},{8,10},{9,11},{10,... | collective-permute-start | bytes 4325384 | tf_op jit(solution)/shard_map/ppermute | solution.py:476
  48.0 3.4 %collective-permute-start.13 = (bf16[8,384,256]{2,1,0:T(8,128)(2,1)S(1)}, bf16[8,384,256]{2,1,0:T(8,128)(2,1)S(1)}, u32[]{:S(2)}, u32[]{:S(2)}) collective-permute-start(bf16[8,384,256]{2,1,0:T(8,128)(2,1)S(1)} %get-tuple-element.70), channel_id=1, source_target_pairs={{0,2},{1,3},{2,0},{3,1},{4,6},{5,7},{6,4},{7,5},{8,10},{9,11},{10,... | collective-permute-start | bytes 4718600 | tf_op jit(solution)/shard_map/ppermute | solution.py:476
  50.9 4.8 %collective-permute-start.12 = (bf16[8,128,256]{2,1,0:T(8,128)(2,1)S(1)}, bf16[8,128,256]{2,1,0:T(8,128)(2,1)S(1)}, u32[]{:S(2)}, u32[]{:S(2)}) collective-permute-start(bf16[8,128,256]{2,1,0:T(8,128)(2,1)S(1)} %get-tuple-element.65), channel_id=1, source_target_pairs={{0,2},{1,3},{2,0},{3,1},{4,6},{5,7},{6,4},{7,5},{8,10},{9,11},{10,... | collective-permute-start | bytes 1572872 | tf_op jit(solution)/shard_map/ppermute | solution.py:476
  51.8 8.7 %collective-permute-start.16 = (bf16[4,80,256]{2,1,0:T(8,128)(2,1)S(1)}, bf16[4,80,256]{2,1,0:T(8,128)(2,1)S(1)}, u32[]{:S(2)}, u32[]{:S(2)}) collective-permute-start(bf16[4,80,256]{2,1,0:T(8,128)(2,1)S(1)} %get-tuple-element.75), channel_id=1, source_target_pairs={{0,1},{1,0},{2,3},{3,2},{4,5},{5,4},{6,7},{7,6},{8,9},{9,8},{10,11... | collective-permute-start | bytes 491528 | tf_op jit(solution)/shard_map/ppermute | solution.py:476
  52.5 16.3 %collective-permute-start.14 = (bf16[8,96,256]{2,1,0:T(8,128)(2,1)S(1)}, bf16[8,96,256]{2,1,0:T(8,128)(2,1)S(1)}, u32[]{:S(2)}, u32[]{:S(2)}) collective-permute-start(bf16[8,96,256]{2,1,0:T(8,128)(2,1)S(1)} %get-tuple-element.72), channel_id=1, source_target_pairs={{0,4},{1,5},{2,6},{3,7},{4,1},{5,0},{6,3},{7,2},{8,12},{9,13},{10,... | collective-permute-start | bytes 1179656 | tf_op jit(solution)/shard_map/ppermute | solution.py:476
  55.7 13.5 %collective-permute-start.15 = (bf16[8,96,256]{2,1,0:T(8,128)(2,1)S(1)}, bf16[8,96,256]{2,1,0:T(8,128)(2,1)S(1)}, u32[]{:S(2)}, u32[]{:S(2)}) collective-permute-start(bf16[8,96,256]{2,1,0:T(8,128)(2,1)S(1)} %get-tuple-element.73), channel_id=1, source_target_pairs={{0,5},{1,4},{2,7},{3,6},{4,0},{5,1},{6,2},{7,3},{8,13},{9,12},{10,... | collective-permute-start | bytes 1179656 | tf_op jit(solution)/shard_map/ppermute | solution.py:476
  61.4 18.0 %collective-permute-start.20 = (bf16[8,128,256]{2,1,0:T(8,128)(2,1)S(1)}, bf16[8,128,256]{2,1,0:T(8,128)(2,1)S(1)}, u32[]{:S(2)}, u32[]{:S(2)}) collective-permute-start(bf16[8,128,256]{2,1,0:T(8,128)(2,1)S(1)} %place.1), channel_id=1, source_target_pairs={{0,1},{1,0},{2,3},{3,2},{4,5},{5,4},{6,7},{7,6},{8,9},{9,8},{10,11... | collective-permute-start | bytes 1572872 | tf_op jit(solution)/shard_map/ppermute | solution.py:476
  69.2 7.9 %collective-permute-start.17 = (bf16[8,32,256]{2,1,0:T(8,128)(2,1)S(1)}, bf16[8,32,256]{2,1,0:T(8,128)(2,1)S(1)}, u32[]{:S(2)}, u32[]{:S(2)}) collective-permute-start(bf16[8,32,256]{2,1,0:T(8,128)(2,1)S(1)} %get-tuple-element.76), channel_id=1, source_target_pairs={{0,8},{1,9},{2,10},{3,11},{4,12},{5,13},{6,14},{7,15},{8,0},{9,1},... | collective-permute-start | bytes 393224 | tf_op jit(solution)/shard_map/ppermute | solution.py:476
  70.0 6.1 %collective-permute-start.18 = (bf16[8,16,256]{2,1,0:T(8,128)(2,1)S(1)}, bf16[8,16,256]{2,1,0:T(8,128)(2,1)S(1)}, u32[]{:S(2)}, u32[]{:S(2)}) collective-permute-start(bf16[8,16,256]{2,1,0:T(8,128)(2,1)S(1)} %get-tuple-element.77), channel_id=1, source_target_pairs={{0,16},{1,17},{2,18},{3,19},{4,20},{5,21},{6,22},{7,23},{8,24},{9,... | collective-permute-start | bytes 196616 | tf_op jit(solution)/shard_map/ppermute | solution.py:476
  71.7 5.5 %collective-permute-start.19 = (bf16[8,16,256]{2,1,0:T(8,128)(2,1)S(1)}, bf16[8,16,256]{2,1,0:T(8,128)(2,1)S(1)}, u32[]{:S(2)}, u32[]{:S(2)}) collective-permute-start(bf16[8,16,256]{2,1,0:T(8,128)(2,1)S(1)} %get-tuple-element.78), channel_id=1, source_target_pairs={{0,24},{1,25},{2,26},{3,27},{4,28},{5,29},{6,30},{7,31},{8,16},{9,... | collective-permute-start | bytes 196616 | tf_op jit(solution)/shard_map/ppermute | solution.py:476

commit v8 on v7

--- a/solution.py
+++ b/solution.py
@@ -79,7 +79,7 @@
     return ref[group // 2].astype(F32)[at : at + 40]
 
 
-def compact_kernel(middle, one, two, three, lift, extra):
+def compact_kernel(middle, two, one, three, lift, extra):
     whole = []
     for g in range(GROUPS):
         mine, a, b, c = [ref[g].astype(F32) for ref in (middle, one, two, three)]
@@ -495,7 +495,7 @@
     )
     lift, extra = whole_call(
         compact_kernel, "compact", [rows(96), extras(BF)], None,
-        middle, send(tail, "x1"), send(last, "x2"), send(last, "x3"),
+        middle, send(last, "x2"), send(tail, "x1"), send(last, "x3"),
     )
     lift_down = send(lift, "up")
     lift_up = send(lift, "down")

time: 80.6 us -> 80.6 us (level)
  no operation moved by 1% of the time
where the time goes in v8:
time: 80.6 us; the launch traced here: 80.2 us
  waiting for transfers between devices  26.7 us (33%)
  starting transfers between devices  26.1 us (32%)
  Pallas kernels  24.7 us (31%)
  other arithmetic  1.14 us (1%)
    ppermute x21, waiting for transfers between devices, send(): return lax.ppermute(x, AXES, route[name])  26.7 us
    ppermute x21, starting transfers between devices, send(): return lax.ppermute(x, AXES, route[name])  26.1 us
    pallas_call x5, Pallas kernels, grid_call(): pl.pallas_call(body, name=name, grid=(GROUPS // TOGETHER,), in_specs=spec...  20.4 us
    pallas_call x8, Pallas kernels, whole_call(): pl.pallas_call(body, name=name, out_shape=shapes, in_specs=specs, out_spe...  4.27 us
  transfers between devices with their start and end apart: 21, of which 12 were waited for; matrix products, arithmetic and copies ran while one was open for 1% of the time, Pallas kernels for 17%

profile of v8, /device:TPU:0, one launch (start us, length us, event | category | flops | bytes accessed | tf_op | source)
XLA Modules:
  0.0 80.2 jit_solution(3861854968050280262)
XLA Ops:
  0.6 0.8 copy.10
  1.4 4.1 %collective-permute-start = (s32[5,4]{1,0:T(8,128)S(1)}, s32[5,4]{1,0:T(8,128)S(1)}, u32[]{:S(2)}, u32[]{:S(2)}) collective-permute-start(s32[5,4]{1,0:T(8,128)S(1)} %copy.10), channel_id=1, source_target_pairs={{0,5},{1,4},{2,7},{3,6},{4,1},{5,0},{6,3},{7,2},{8,13},{9,12},{10,... | collective-permute-start | bytes 248 | tf_op jit(solution)/shard_map/ppermute | solution.py:476
  5.5 3.5 %collective-permute-start.2 = (bf16[128,1024]{1,0:T(8,128)(2,1)}, bf16[128,1024]{1,0:T(8,128)(2,1)S(1)}, u32[]{:S(2)}, u32[]{:S(2)}) collective-permute-start(bf16[128,1024]{1,0:T(8,128)(2,1)} %v_ref.3), channel_id=1, source_target_pairs={{0,1},{1,0},{2,3},{3,2},{4,5},{5,4},{6,7},{7,6},{8,9},{9,8},{10,11... | collective-permute-start | bytes 786440 | tf_op jit(solution)/shard_map/ppermute | solution.py:476
  9.1 1.1 %pad_maximum_fusion.keys.values = bf16[128,2048]{1,0:T(8,128)(2,1)S(1)} fusion(bf16[128,1024]{1,0:T(8,128)(2,1)} %v_ref.3, bf16[128,1024]{1,0:T(8,128)(2,1)} %k_ref.3), kind=kLoop, calls=%fused_computation | loop fusion | flops 1048576 | bytes 1048576 | tf_op jit(solution)/shard_map/concatenate | solution.py:485
  10.1 0.0 collective-permute-done
  10.1 0.1 add_select_fusion.offs
  10.2 1.1 %select.1 = (bf16[8,64,256]{2,1,0:T(8,128)(2,1)S(1)}, bf16[8,64,256]{2,1,0:T(8,128)(2,1)S(1)}, bf16[8,32,256]{2,1,0:T(8,128)(2,1)S(1)}, bf16[8,16,256]{2,1,0:T(8,128)(2,1)S(1)}) custom-call(s32[5,8]{1,0:T(8,128)S(1)} %add_select_fusion.offs, bf16[128,2048]{1,0:T(8,128)(2,1)S(1)} %pad_maximum_fusion.keys.values, bf16[128,2048]{1,0:T(8,128)(2,1)S(1)} %pad_maximum_fusion.keys.values), custom_call_target="tpu_custom_call" | custom-call | flops 4000000000 | bytes 16000000 | tf_op jit(solution)/shard_map/select/pallas_call | solution.py:441
  11.4 1.6 %collective-permute-start.4 = (bf16[8,32,256]{2,1,0:T(8,128)(2,1)S(1)}, bf16[8,32,256]{2,1,0:T(8,128)(2,1)S(1)}, u32[]{:S(2)}, u32[]{:S(2)}) collective-permute-start(bf16[8,32,256]{2,1,0:T(8,128)(2,1)S(1)} %get-tuple-element.45), channel_id=1, source_target_pairs={{0,8},{1,9},{2,10},{3,11},{4,12},{5,13},{6,14},{7,15},{8,0},{9,1},... | collective-permute-start | bytes 393224 | tf_op jit(solution)/shard_map/ppermute | solution.py:476
  12.9 2.1 %collective-permute-start.5 = (bf16[8,16,256]{2,1,0:T(8,128)(2,1)S(1)}, bf16[8,16,256]{2,1,0:T(8,128)(2,1)S(1)}, u32[]{:S(2)}, u32[]{:S(2)}) collective-permute-start(bf16[8,16,256]{2,1,0:T(8,128)(2,1)S(1)} %get-tuple-element.44), channel_id=1, source_target_pairs={{0,24},{1,25},{2,26},{3,27},{4,28},{5,29},{6,30},{7,31},{8,16},{9,... | collective-permute-start | bytes 196616 | tf_op jit(solution)/shard_map/ppermute | solution.py:476
  15.0 0.6 collective-permute-start.3
  15.7 3.3 %collective-permute-done.5.three = bf16[8,16,256]{2,1,0:T(8,128)(2,1)S(1)} collective-permute-done((bf16[8,16,256]{2,1,0:T(8,128)(2,1)S(1)}, bf16[8,16,256]{2,1,0:T(8,128)(2,1)S(1)}, u32[]{:S(2)}, u32[]{:S(2)}) %collective-permute-start.5) | collective-permute-done | bytes 65568 | tf_op jit(solution)/shard_map/ppermute | solution.py:476
  19.0 1.8 %collective-permute-done.3.two = bf16[8,16,256]{2,1,0:T(8,128)(2,1)S(1)} collective-permute-done((bf16[8,16,256]{2,1,0:T(8,128)(2,1)S(1)}, bf16[8,16,256]{2,1,0:T(8,128)(2,1)S(1)}, u32[]{:S(2)}, u32[]{:S(2)}) %collective-permute-start.3) | collective-permute-done | bytes 65568 | tf_op jit(solution)/shard_map/ppermute | solution.py:476
  20.8 0.0 collective-permute-done.4.one
  20.9 0.1 collective-permute-start.8
  20.9 3.2 %collective-permute-start.7 = (bf16[8,96,256]{2,1,0:T(8,128)(2,1)S(1)}, bf16[8,96,256]{2,1,0:T(8,128)(2,1)S(1)}, u32[]{:S(2)}, u32[]{:S(2)}) collective-permute-start(bf16[8,96,256]{2,1,0:T(8,128)(2,1)S(1)} %get-tuple-element.53.lift), channel_id=1, source_target_pairs={{0,5},{1,4},{2,7},{3,6},{4,0},{5,1},{6,2},{7,3},{8,13},{9,12},{10,... | collective-permute-start | bytes 1179656 | tf_op jit(solution)/shard_map/ppermute | solution.py:476
  24.2 0.1 collective-permute-start.6
  24.3 0.4 collective-permute-start.9
  24.7 3.2 %early.1 = (bf16[8,512,128]{2,1,0:T(8,128)(2,1)S(1)}, bf16[8,512,128]{2,1,0:T(8,128)(2,1)S(1)}, bf16[8,512,256]{2,1,0:T(8,128)(2,1)S(1)}, f32[8,128,128]{2,1,0:T...) custom-call(s32[5,8]{1,0:T(8,128)S(1)} %add_select_fusion.offs, bf16[128,4096]{1,0:T(8,128)(2,1)S(1)} %copy-done.2, ...), custom_call_target="tpu_custom_call" | custom-call | flops 4000000000 | bytes 16000000 | tf_op jit(solution)/shard_map/early/pallas_call | solution.py:441
  27.9 0.9 %across.1 = bf16[8,128,256]{2,1,0:T(8,128)(2,1)S(1)} custom-call(s32[5,8]{1,0:T(8,128)S(1)} %add_select_fusion.offs, bf16[128,1024]{1,0:T(8,128)(2,1)S(1)} %collective-permute-done.1.kp_ref.keys, bf16[128,1024]{1,0:T(8,128)(2,1)S(1)} %collective-permute-done.2.vp_ref.values, f32[8,128,128]{2,1,0:T(8,128)S(1)} %get-tuple-element.51._.lse0), custom_call_target="tpu_custom_call" | custom-call | bytes 4000000 | tf_op jit(solution)/shard_map/across/pallas_call | solution.py:413
  28.8 4.8 %collective-permute-done.6.x_far = bf16[4,80,256]{2,1,0:T(8,128)(2,1)S(1)} collective-permute-done((bf16[4,80,256]{2,1,0:T(8,128)(2,1)S(1)}, bf16[4,80,256]{2,1,0:T(8,128)(2,1)S(1)}, u32[]{:S(2)}, u32[]{:S(2)}) %collective-permute-start.6) | collective-permute-done | bytes 163872 | tf_op jit(solution)/shard_map/ppermute | solution.py:476
  33.6 1.3 %collective-permute-done.8.lift_down = bf16[8,96,256]{2,1,0:T(8,128)(2,1)S(1)} collective-permute-done((bf16[8,96,256]{2,1,0:T(8,128)(2,1)S(1)}, bf16[8,96,256]{2,1,0:T(8,128)(2,1)S(1)}, u32[]{:S(2)}, u32[]{:S(2)}) %collective-permute-start.8) | collective-permute-done | bytes 393248 | tf_op jit(solution)/shard_map/ppermute | solution.py:476
  34.9 0.1 assemble.1.late
  35.0 0.1 collective-permute-start.11
  35.1 3.2 %collective-permute-done.11.other_late = bf16[8,352,256]{2,1,0:T(8,128)(2,1)S(1)} collective-permute-done((bf16[8,352,256]{2,1,0:T(8,128)(2,1)S(1)}, bf16[8,352,256]{2,1,0:T(8,128)(2,1)S(1)}, u32[]{:S(2)}, u32[]{:S(2)}) %collective-permute-start.11) | collective-permute-done | bytes 1441824 | tf_op jit(solution)/shard_map/ppermute | solution.py:476
  38.3 9.7 %attention.1 = (bf16[128,4096]{1,0:T(8,128)(2,1)}, f32[8,224,128]{2,1,0:T(8,128)S(1)}, bf16[8,384,256]{2,1,0:T(8,128)(2,1)S(1)}, bf16[8,384,256]{2,1,0:T(8,128)(...) custom-call(s32[5,8]{1,0:T(8,128)S(1)} %add_select_fusion.offs, ...), custom_call_target="tpu_custom_call" | custom-call | flops 4000000000 | bytes 16000000 | tf_op jit(solution)/shard_map/attention/pallas_call | solution.py:441
  48.0 0.1 collective-permute-start.13
  48.1 2.7 %return1.1 = (f32[128,4096]{1,0:T(8,128)S(1)}, bf16[8,128,256]{2,1,0:T(8,128)(2,1)S(1)}, bf16[8,128,256]{2,1,0:T(8,128)(2,1)S(1)}) custom-call(s32[5,8]{1,0:T(8,128)S(1)} %add_select_fusion.offs, bf16[8,512,128]{2,1,0:T(8,128)(2,1)S(1)} %get-tuple-element.47.qs_ref, bf16[8,512,128]{2,1,0:T(8,128)(2,1)S(1)} %get-tuple-element.48.gs_ref, ...), custom_call_target="tpu_custom_call" | custom-call | flops 4000000000 | bytes 16000000 | tf_op jit(solution)/shard_map/return1/pallas_call | solution.py:441
  50.9 0.4 collective-permute-start.12
  51.3 0.1 collective-permute-done.13.theirs
  51.4 0.4 reduce.1
  51.8 0.7 collective-permute-start.16
  52.5 3.2 %collective-permute-start.14 = (bf16[8,96,256]{2,1,0:T(8,128)(2,1)S(1)}, bf16[8,96,256]{2,1,0:T(8,128)(2,1)S(1)}, u32[]{:S(2)}, u32[]{:S(2)}) collective-permute-start(bf16[8,96,256]{2,1,0:T(8,128)(2,1)S(1)} %get-tuple-element.72), channel_id=1, source_target_pairs={{0,4},{1,5},{2,6},{3,7},{4,1},{5,0},{6,3},{7,2},{8,12},{9,13},{10,... | collective-permute-start | bytes 1179656 | tf_op jit(solution)/shard_map/ppermute | solution.py:476
  55.7 0.0 collective-permute-start.15
  55.7 3.6 %return0.1 = (bf16[128,4096]{1,0:T(8,128)(2,1)}, bf16[8,256,256]{2,1,0:T(8,128)(2,1)S(1)}) custom-call(bf16[128,4096]{1,0:T(8,128)(2,1)S(1)} %copy-done.2, bf16[128,4096]{1,0:T(8,128)(2,1)S(1)} %copy-done.3, bf16[128,1024]{1,0:T(8,128)(2,1)S(1)} %copy-done, bf16[128,1024]{1,0:T(8,128)(2,1)S(1)} %copy-done.1, ...), custom_call_target="tpu_custom_call" | custom-call | flops 4000000000 | bytes 16000000 | tf_op jit(solution)/shard_map/return0/pallas_call | solution.py:441
  59.3 1.1 %collective-permute-done.16.far._ = bf16[4,80,256]{2,1,0:T(8,128)(2,1)S(1)} collective-permute-done((bf16[4,80,256]{2,1,0:T(8,128)(2,1)S(1)}, bf16[4,80,256]{2,1,0:T(8,128)(2,1)S(1)}, u32[]{:S(2)}, u32[]{:S(2)}) %collective-permute-start.16) | collective-permute-done | bytes 163872 | tf_op jit(solution)/shard_map/ppermute | solution.py:476
  60.4 0.9 %place.1 = bf16[8,128,256]{2,1,0:T(8,128)(2,1)S(1)} custom-call(s32[5,8]{1,0:T(8,128)S(1)} %add_select_fusion.offs, bf16[8,256,256]{2,1,0:T(8,128)(2,1)S(1)} %get-tuple-element.67.d0, bf16[8,128,256]{2,1,0:T(8,128)(2,1)S(1)} %get-tuple-element.68._.mine, bf16[8,128,256]{2,1,0:T(8,128)(2,1)S(1)} %collective-permute-done.12.refs_0_.theirs, ...), custom_call_target="tpu_custom_call" | custom-call | bytes 4000000 | tf_op jit(solution)/shard_map/place/pallas_call | solution.py:413
  61.3 1.0 %collective-permute-start.20 = (bf16[8,128,256]{2,1,0:T(8,128)(2,1)S(1)}, bf16[8,128,256]{2,1,0:T(8,128)(2,1)S(1)}, u32[]{:S(2)}, u32[]{:S(2)}) collective-permute-start(bf16[8,128,256]{2,1,0:T(8,128)(2,1)S(1)} %place.1), channel_id=1, source_target_pairs={{0,1},{1,0},{2,3},{3,2},{4,5},{5,4},{6,7},{7,6},{8,9},{9,8},{10,11... | collective-permute-start | bytes 1572872 | tf_op jit(solution)/shard_map/ppermute | solution.py:476
  62.3 6.4 %collective-permute-done.14.down = bf16[8,96,256]{2,1,0:T(8,128)(2,1)S(1)} collective-permute-done((bf16[8,96,256]{2,1,0:T(8,128)(2,1)S(1)}, bf16[8,96,256]{2,1,0:T(8,128)(2,1)S(1)}, u32[]{:S(2)}, u32[]{:S(2)}) %collective-permute-start.14) | collective-permute-done | bytes 393248 | tf_op jit(solution)/shard_map/ppermute | solution.py:476
  68.8 0.4 collective-permute-done.15.up
  69.1 0.1 cross.1
  69.2 0.7 collective-permute-start.17
  70.0 1.7 %collective-permute-start.18 = (bf16[8,16,256]{2,1,0:T(8,128)(2,1)S(1)}, bf16[8,16,256]{2,1,0:T(8,128)(2,1)S(1)}, u32[]{:S(2)}, u32[]{:S(2)}) collective-permute-start(bf16[8,16,256]{2,1,0:T(8,128)(2,1)S(1)} %get-tuple-element.77), channel_id=1, source_target_pairs={{0,16},{1,17},{2,18},{3,19},{4,20},{5,21},{6,22},{7,23},{8,24},{9,... | collective-permute-start | bytes 196616 | tf_op jit(solution)/shard_map/ppermute | solution.py:476
  71.7 2.3 %collective-permute-start.19 = (bf16[8,16,256]{2,1,0:T(8,128)(2,1)S(1)}, bf16[8,16,256]{2,1,0:T(8,128)(2,1)S(1)}, u32[]{:S(2)}, u32[]{:S(2)}) collective-permute-start(bf16[8,16,256]{2,1,0:T(8,128)(2,1)S(1)} %get-tuple-element.78), channel_id=1, source_target_pairs={{0,24},{1,25},{2,26},{3,27},{4,28},{5,29},{6,30},{7,31},{8,16},{9,... | collective-permute-start | bytes 196616 | tf_op jit(solution)/shard_map/ppermute | solution.py:476
  74.0 2.0 %collective-permute-done.18.two = bf16[8,16,256]{2,1,0:T(8,128)(2,1)S(1)} collective-permute-done((bf16[8,16,256]{2,1,0:T(8,128)(2,1)S(1)}, bf16[8,16,256]{2,1,0:T(8,128)(2,1)S(1)}, u32[]{:S(2)}, u32[]{:S(2)}) %collective-permute-start.18) | collective-permute-done | bytes 65568 | tf_op jit(solution)/shard_map/ppermute | solution.py:476
  76.0 1.1 %collective-permute-done.19.three = bf16[8,16,256]{2,1,0:T(8,128)(2,1)S(1)} collective-permute-done((bf16[8,16,256]{2,1,0:T(8,128)(2,1)S(1)}, bf16[8,16,256]{2,1,0:T(8,128)(2,1)S(1)}, u32[]{:S(2)}, u32[]{:S(2)}) %collective-permute-start.19) | collective-permute-done | bytes 65568 | tf_op jit(solution)/shard_map/ppermute | solution.py:476
  77.2 1.0 %keep.1.kept = f32[8,128,256]{2,1,0:T(8,128)S(1)} custom-call(s32[5,8]{1,0:T(8,128)S(1)} %add_select_fusion.offs, bf16[8,256,256]{2,1,0:T(8,128)(2,1)S(1)} %get-tuple-element.67.d0, bf16[8,128,256]{2,1,0:T(8,128)(2,1)S(1)} %get-tuple-element.68._.mine, bf16[8,128,256]{2,1,0:T(8,128)(2,1)S(1)} %collective-permute-done.12.refs_0_.theirs, ...), custom_call_target="tpu_custom_call" | custom-call | bytes 4000000 | tf_op jit(solution)/shard_map/keep/pallas_call | solution.py:413
  78.2 1.1 %collective-permute-done.20.refs_0_ = bf16[8,128,256]{2,1,0:T(8,128)(2,1)S(1)} collective-permute-done((bf16[8,128,256]{2,1,0:T(8,128)(2,1)S(1)}, bf16[8,128,256]{2,1,0:T(8,128)(2,1)S(1)}, u32[]{:S(2)}, u32[]{:S(2)}) %collective-permute-start.20) | collective-permute-done | bytes 524320 | tf_op jit(solution)/shard_map/ppermute | solution.py:476
  79.3 0.9 %finish.1 = (bf16[128,1024]{1,0:T(8,128)(2,1)}, bf16[128,1024]{1,0:T(8,128)(2,1)}) custom-call(f32[8,128,256]{2,1,0:T(8,128)S(1)} %keep.1.kept, bf16[8,128,256]{2,1,0:T(8,128)(2,1)S(1)} %collective-permute-done.20.refs_0_), custom_call_target="tpu_custom_call" | custom-call | bytes 4000000 | tf_op jit(solution)/shard_map/finish/pallas_call | solution.py:413
  (18 shorter events, 0.1 us)
Async XLA Ops:
  1.4 8.7 %collective-permute-start = (s32[5,4]{1,0:T(8,128)S(1)}, s32[5,4]{1,0:T(8,128)S(1)}, u32[]{:S(2)}, u32[]{:S(2)}) collective-permute-start(s32[5,4]{1,0:T(8,128)S(1)} %copy.10), channel_id=1, source_target_pairs={{0,5},{1,4},{2,7},{3,6},{4,1},{5,0},{6,3},{7,2},{8,13},{9,12},{10,... | collective-permute-start | bytes 248 | tf_op jit(solution)/shard_map/ppermute | solution.py:476
  5.5 18.6 %collective-permute-start.1 = (bf16[128,1024]{1,0:T(8,128)(2,1)}, bf16[128,1024]{1,0:T(8,128)(2,1)S(1)}, u32[]{:S(2)}, u32[]{:S(2)}) collective-permute-start(bf16[128,1024]{1,0:T(8,128)(2,1)} %k_ref.3), channel_id=1, source_target_pairs={{0,1},{1,0},{2,3},{3,2},{4,5},{5,4},{6,7},{7,6},{8,9},{9,8},{10,11... | collective-permute-start | bytes 786440 | tf_op jit(solution)/shard_map/ppermute | solution.py:476
  5.5 18.6 %collective-permute-start.2 = (bf16[128,1024]{1,0:T(8,128)(2,1)}, bf16[128,1024]{1,0:T(8,128)(2,1)S(1)}, u32[]{:S(2)}, u32[]{:S(2)}) collective-permute-start(bf16[128,1024]{1,0:T(8,128)(2,1)} %v_ref.3), channel_id=1, source_target_pairs={{0,1},{1,0},{2,3},{3,2},{4,5},{5,4},{6,7},{7,6},{8,9},{9,8},{10,11... | collective-permute-start | bytes 786440 | tf_op jit(solution)/shard_map/ppermute | solution.py:476
  10.2 14.5 %copy-start = (bf16[128,1024]{1,0:T(8,128)(2,1)S(1)}, bf16[128,1024]{1,0:T(8,128)(2,1)}, u32[]{:S(2)}) copy-start(bf16[128,1024]{1,0:T(8,128)(2,1)} %k_ref.3) | copy-start | bytes 786436
  10.2 14.5 %copy-start.1 = (bf16[128,1024]{1,0:T(8,128)(2,1)S(1)}, bf16[128,1024]{1,0:T(8,128)(2,1)}, u32[]{:S(2)}) copy-start(bf16[128,1024]{1,0:T(8,128)(2,1)} %v_ref.3) | copy-start | bytes 786436
  10.2 14.5 %copy-start.2 = (bf16[128,4096]{1,0:T(8,128)(2,1)S(1)}, bf16[128,4096]{1,0:T(8,128)(2,1)}, u32[]{:S(2)}) copy-start(bf16[128,4096]{1,0:T(8,128)(2,1)} %q_ref.3) | copy-start | bytes 3145732
  10.2 14.5 %copy-start.3 = (bf16[128,4096]{1,0:T(8,128)(2,1)S(1)}, bf16[128,4096]{1,0:T(8,128)(2,1)}, u32[]{:S(2)}) copy-start(bf16[128,4096]{1,0:T(8,128)(2,1)} %g_ref.5) | copy-start | bytes 3145732
  11.4 9.4 %collective-permute-start.4 = (bf16[8,32,256]{2,1,0:T(8,128)(2,1)S(1)}, bf16[8,32,256]{2,1,0:T(8,128)(2,1)S(1)}, u32[]{:S(2)}, u32[]{:S(2)}) collective-permute-start(bf16[8,32,256]{2,1,0:T(8,128)(2,1)S(1)} %get-tuple-element.45), channel_id=1, source_target_pairs={{0,8},{1,9},{2,10},{3,11},{4,12},{5,13},{6,14},{7,15},{8,0},{9,1},... | collective-permute-start | bytes 393224 | tf_op jit(solution)/shard_map/ppermute | solution.py:476
  12.9 6.1 %collective-permute-start.5 = (bf16[8,16,256]{2,1,0:T(8,128)(2,1)S(1)}, bf16[8,16,256]{2,1,0:T(8,128)(2,1)S(1)}, u32[]{:S(2)}, u32[]{:S(2)}) collective-permute-start(bf16[8,16,256]{2,1,0:T(8,128)(2,1)S(1)} %get-tuple-element.44), channel_id=1, source_target_pairs={{0,24},{1,25},{2,26},{3,27},{4,28},{5,29},{6,30},{7,31},{8,16},{9,... | collective-permute-start | bytes 196616 | tf_op jit(solution)/shard_map/ppermute | solution.py:476
  15.0 5.8 %collective-permute-start.3 = (bf16[8,16,256]{2,1,0:T(8,128)(2,1)S(1)}, bf16[8,16,256]{2,1,0:T(8,128)(2,1)S(1)}, u32[]{:S(2)}, u32[]{:S(2)}) collective-permute-start(bf16[8,16,256]{2,1,0:T(8,128)(2,1)S(1)} %get-tuple-element.44), channel_id=1, source_target_pairs={{0,16},{1,17},{2,18},{3,19},{4,20},{5,21},{6,22},{7,23},{8,24},{9,... | collective-permute-start | bytes 196616 | tf_op jit(solution)/shard_map/ppermute | solution.py:476
  20.9 14.0 %collective-permute-start.8 = (bf16[8,96,256]{2,1,0:T(8,128)(2,1)S(1)}, bf16[8,96,256]{2,1,0:T(8,128)(2,1)S(1)}, u32[]{:S(2)}, u32[]{:S(2)}) collective-permute-start(bf16[8,96,256]{2,1,0:T(8,128)(2,1)S(1)} %get-tuple-element.53.lift), channel_id=1, source_target_pairs={{0,4},{1,5},{2,6},{3,7},{4,1},{5,0},{6,3},{7,2},{8,12},{9,13},{10,... | collective-permute-start | bytes 1179656 | tf_op jit(solution)/shard_map/ppermute | solution.py:476
  20.9 13.9 %collective-permute-start.7 = (bf16[8,96,256]{2,1,0:T(8,128)(2,1)S(1)}, bf16[8,96,256]{2,1,0:T(8,128)(2,1)S(1)}, u32[]{:S(2)}, u32[]{:S(2)}) collective-permute-start(bf16[8,96,256]{2,1,0:T(8,128)(2,1)S(1)} %get-tuple-element.53.lift), channel_id=1, source_target_pairs={{0,5},{1,4},{2,7},{3,6},{4,0},{5,1},{6,2},{7,3},{8,13},{9,12},{10,... | collective-permute-start | bytes 1179656 | tf_op jit(solution)/shard_map/ppermute | solution.py:476
  24.2 10.7 %collective-permute-start.10 = (bf16[8,96,256]{2,1,0:T(8,128)(2,1)S(1)}, bf16[8,96,256]{2,1,0:T(8,128)(2,1)S(1)}, u32[]{:S(2)}, u32[]{:S(2)}) collective-permute-start(bf16[8,96,256]{2,1,0:T(8,128)(2,1)S(1)} %get-tuple-element.53.lift), channel_id=1, source_target_pairs={{0,2},{1,3},{2,0},{3,1},{4,6},{5,7},{6,4},{7,5},{8,10},{9,11},{10,... | collective-permute-start | bytes 1179656 | tf_op jit(solution)/shard_map/ppermute | solution.py:476
  24.2 9.4 %collective-permute-start.6 = (bf16[4,80,256]{2,1,0:T(8,128)(2,1)S(1)}, bf16[4,80,256]{2,1,0:T(8,128)(2,1)S(1)}, u32[]{:S(2)}, u32[]{:S(2)}) collective-permute-start(bf16[4,80,256]{2,1,0:T(8,128)(2,1)S(1)} %get-tuple-element.46.refs_0_), channel_id=1, source_target_pairs={{0,1},{1,0},{2,3},{3,2},{4,5},{5,4},{6,7},{7,6},{8,9},{9,8},{10,11... | collective-permute-start | bytes 491528 | tf_op jit(solution)/shard_map/ppermute | solution.py:476
  24.3 9.3 %collective-permute-start.9 = (bf16[8,64,256]{2,1,0:T(8,128)(2,1)S(1)}, bf16[8,64,256]{2,1,0:T(8,128)(2,1)S(1)}, u32[]{:S(2)}, u32[]{:S(2)}) collective-permute-start(bf16[8,64,256]{2,1,0:T(8,128)(2,1)S(1)} %get-tuple-element.52.first), channel_id=1, source_target_pairs={{0,2},{1,3},{2,0},{3,1},{4,6},{5,7},{6,4},{7,5},{8,10},{9,11},{10,... | collective-permute-start | bytes 786440 | tf_op jit(solution)/shard_map/ppermute | solution.py:476
  35.0 3.3 %collective-permute-start.11 = (bf16[8,352,256]{2,1,0:T(8,128)(2,1)S(1)}, bf16[8,352,256]{2,1,0:T(8,128)(2,1)S(1)}, u32[]{:S(2)}, u32[]{:S(2)}) collective-permute-start(bf16[8,352,256]{2,1,0:T(8,128)(2,1)S(1)} %assemble.1.late), channel_id=1, source_target_pairs={{0,2},{1,3},{2,0},{3,1},{4,6},{5,7},{6,4},{7,5},{8,10},{9,11},{10,... | collective-permute-start | bytes 4325384 | tf_op jit(solution)/shard_map/ppermute | solution.py:476
  48.0 3.4 %collective-permute-start.13 = (bf16[8,384,256]{2,1,0:T(8,128)(2,1)S(1)}, bf16[8,384,256]{2,1,0:T(8,128)(2,1)S(1)}, u32[]{:S(2)}, u32[]{:S(2)}) collective-permute-start(bf16[8,384,256]{2,1,0:T(8,128)(2,1)S(1)} %get-tuple-element.70), channel_id=1, source_target_pairs={{0,2},{1,3},{2,0},{3,1},{4,6},{5,7},{6,4},{7,5},{8,10},{9,11},{10,... | collective-permute-start | bytes 4718600 | tf_op jit(solution)/shard_map/ppermute | solution.py:476
  50.9 4.8 %collective-permute-start.12 = (bf16[8,128,256]{2,1,0:T(8,128)(2,1)S(1)}, bf16[8,128,256]{2,1,0:T(8,128)(2,1)S(1)}, u32[]{:S(2)}, u32[]{:S(2)}) collective-permute-start(bf16[8,128,256]{2,1,0:T(8,128)(2,1)S(1)} %get-tuple-element.65), channel_id=1, source_target_pairs={{0,2},{1,3},{2,0},{3,1},{4,6},{5,7},{6,4},{7,5},{8,10},{9,11},{10,... | collective-permute-start | bytes 1572872 | tf_op jit(solution)/shard_map/ppermute | solution.py:476
  51.8 8.7 %collective-permute-start.16 = (bf16[4,80,256]{2,1,0:T(8,128)(2,1)S(1)}, bf16[4,80,256]{2,1,0:T(8,128)(2,1)S(1)}, u32[]{:S(2)}, u32[]{:S(2)}) collective-permute-start(bf16[4,80,256]{2,1,0:T(8,128)(2,1)S(1)} %get-tuple-element.75), channel_id=1, source_target_pairs={{0,1},{1,0},{2,3},{3,2},{4,5},{5,4},{6,7},{7,6},{8,9},{9,8},{10,11... | collective-permute-start | bytes 491528 | tf_op jit(solution)/shard_map/ppermute | solution.py:476
  52.5 16.3 %collective-permute-start.14 = (bf16[8,96,256]{2,1,0:T(8,128)(2,1)S(1)}, bf16[8,96,256]{2,1,0:T(8,128)(2,1)S(1)}, u32[]{:S(2)}, u32[]{:S(2)}) collective-permute-start(bf16[8,96,256]{2,1,0:T(8,128)(2,1)S(1)} %get-tuple-element.72), channel_id=1, source_target_pairs={{0,4},{1,5},{2,6},{3,7},{4,1},{5,0},{6,3},{7,2},{8,12},{9,13},{10,... | collective-permute-start | bytes 1179656 | tf_op jit(solution)/shard_map/ppermute | solution.py:476
  55.7 13.5 %collective-permute-start.15 = (bf16[8,96,256]{2,1,0:T(8,128)(2,1)S(1)}, bf16[8,96,256]{2,1,0:T(8,128)(2,1)S(1)}, u32[]{:S(2)}, u32[]{:S(2)}) collective-permute-start(bf16[8,96,256]{2,1,0:T(8,128)(2,1)S(1)} %get-tuple-element.73), channel_id=1, source_target_pairs={{0,5},{1,4},{2,7},{3,6},{4,0},{5,1},{6,2},{7,3},{8,13},{9,12},{10,... | collective-permute-start | bytes 1179656 | tf_op jit(solution)/shard_map/ppermute | solution.py:476
  61.3 18.0 %collective-permute-start.20 = (bf16[8,128,256]{2,1,0:T(8,128)(2,1)S(1)}, bf16[8,128,256]{2,1,0:T(8,128)(2,1)S(1)}, u32[]{:S(2)}, u32[]{:S(2)}) collective-permute-start(bf16[8,128,256]{2,1,0:T(8,128)(2,1)S(1)} %place.1), channel_id=1, source_target_pairs={{0,1},{1,0},{2,3},{3,2},{4,5},{5,4},{6,7},{7,6},{8,9},{9,8},{10,11... | collective-permute-start | bytes 1572872 | tf_op jit(solution)/shard_map/ppermute | solution.py:476
  69.2 7.9 %collective-permute-start.17 = (bf16[8,32,256]{2,1,0:T(8,128)(2,1)S(1)}, bf16[8,32,256]{2,1,0:T(8,128)(2,1)S(1)}, u32[]{:S(2)}, u32[]{:S(2)}) collective-permute-start(bf16[8,32,256]{2,1,0:T(8,128)(2,1)S(1)} %get-tuple-element.76), channel_id=1, source_target_pairs={{0,8},{1,9},{2,10},{3,11},{4,12},{5,13},{6,14},{7,15},{8,0},{9,1},... | collective-permute-start | bytes 393224 | tf_op jit(solution)/shard_map/ppermute | solution.py:476
  70.0 6.1 %collective-permute-start.18 = (bf16[8,16,256]{2,1,0:T(8,128)(2,1)S(1)}, bf16[8,16,256]{2,1,0:T(8,128)(2,1)S(1)}, u32[]{:S(2)}, u32[]{:S(2)}) collective-permute-start(bf16[8,16,256]{2,1,0:T(8,128)(2,1)S(1)} %get-tuple-element.77), channel_id=1, source_target_pairs={{0,16},{1,17},{2,18},{3,19},{4,20},{5,21},{6,22},{7,23},{8,24},{9,... | collective-permute-start | bytes 196616 | tf_op jit(solution)/shard_map/ppermute | solution.py:476
  71.7 5.5 %collective-permute-start.19 = (bf16[8,16,256]{2,1,0:T(8,128)(2,1)S(1)}, bf16[8,16,256]{2,1,0:T(8,128)(2,1)S(1)}, u32[]{:S(2)}, u32[]{:S(2)}) collective-permute-start(bf16[8,16,256]{2,1,0:T(8,128)(2,1)S(1)} %get-tuple-element.78), channel_id=1, source_target_pairs={{0,24},{1,25},{2,26},{3,27},{4,28},{5,29},{6,30},{7,31},{8,16},{9,... | collective-permute-start | bytes 196616 | tf_op jit(solution)/shard_map/ppermute | solution.py:476
